TPU v7x, 32 devices: a whole 2x2x4 slice. The times are simulated.
32 devices in a mesh: grp: 2 (over y), gx: 4 (over z), gy: 2 (over x), gz: 2 (over core).
Axes of the slice: x: 2, y: 2, z: 4, core: 2. Of those that a mesh axis runs over, the one named last changes fastest.
Arguments:
- innovation: float32 [10, 4, 64, 216], P('grp', 'gz', 'gx', 'gy'), parts along dimension 0, may hold values from -36 to 36
- obs_precision: float32 [10, 4, 64, 216], P('grp', 'gz', 'gx', 'gy'), parts along dimension 0, may hold values from 0.3 to 3
- error_scale: float32 [5, 4, 64, 216], P(None, 'gz', 'gx', 'gy'), may hold values from 0.3 to 3
- kappa_x: float32 [4, 64, 216], P('gz', 'gx', 'gy'), may hold values from 0.04 to 0.24
- kappa_y: float32 [4, 64, 216], P('gz', 'gx', 'gy'), may hold values from 0.04 to 0.24
- sea_mask: int32 [4, 64, 216], P('gz', 'gx', 'gy'), may hold values 0 or 1
- members: float32 [32, 5, 4, 64, 216], P('grp', None, 'gz', 'gx', 'gy'), parts along dimension 0, may hold values from -6 to 6
- vertical: float32 [5, 4, 4], replicated, may hold values from -3 to 3
- diffusion_steps: int32 [5], replicated, may hold values from 5 to 10, as said below
Outputs:
- control_field: float32 [10, 4, 64, 216], P('grp', 'gz', 'gx', 'gy'), parts along dimension 0
- control_weights: float32 [32], P('grp'), parts along dimension 0
- residual_field: float32 [10, 4, 64, 216], P('grp', 'gz', 'gx', 'gy'), parts along dimension 0
There are 2 independent parts, one for each index of `grp`. A program takes and returns all parts, laid end to end along the dimension named above; an argument that names none is the same for every part. Nothing has to cross between parts.
Inputs may be any that keep to these rules, and one draw needn't show every extreme that they name: `diffusion_steps`: each field's number of diffusion steps; at least one field takes all 10.
All inputs are finite; a program needn't handle non-finite values. No bound on the sum of `sea_mask` on one device may be relied on, other than what follows from the above.
Results may differ from a plain program's by a relative error of at most 0.0004.
Values sent between devices are 32-bit elements; how exact they have to be, the bound alone decides.
No kernel may reach another device: no remote copies, remote signals or barrier semaphores. Data moves between devices by JAX's collectives and lax.ppermute only.
A program may use at most 64 MiB of HBM per device.

v0:
```python
import math

import jax
import jax.numpy as jnp
from jax import lax
from jax.sharding import PartitionSpec as P

KMAX = 10
ITERS = 2


static_share = 0.6
ensemble_share = 0.4


def extended(cells, sides, width):
    for axis, dim in sides:
        count = lax.axis_size(axis)
        head = lax.slice_in_dim(cells, 0, width, axis=dim)
        tail = lax.slice_in_dim(cells, cells.shape[dim] - width, cells.shape[dim], axis=dim)
        cells = jnp.concatenate(
            [
                lax.ppermute(tail, axis, [(i, (i + 1) % count) for i in range(count)]),
                cells,
                lax.ppermute(head, axis, [((i + 1) % count, i) for i in range(count)]),
            ],
            axis=dim,
        )
    return cells


def level_mix(source, mixing):
    local_levels = source.shape[1]
    gathered = lax.all_gather(source, "gz", axis=1, tiled=True)
    own_rows = lax.dynamic_slice_in_dim(
        mixing, lax.axis_index("gz") * local_levels, local_levels, 1
    )
    return jnp.einsum("flk,fkxy->flxy", own_rows, gathered, precision=lax.Precision.HIGHEST)


def diffuse(source, padded, step_counts, halo_depth):
    current = source
    for segment in range(KMAX // halo_depth):
        current = extended(current, (("gx", 2), ("gy", 3)), halo_depth)
        for substep in range(halo_depth):
            number = segment * halo_depth + substep
            offset = KMAX - halo_depth + substep
            rows_now = current.shape[2]
            cols_now = current.shape[3]
            window = padded[:, :, offset : offset + rows_now, offset : offset + cols_now]
            east_kappa = window[0]
            north_kappa = window[1]
            wet_window = window[2]
            east_coef = east_kappa[:, :-1, :] * wet_window[:, :-1, :] * wet_window[:, 1:, :]
            flux_east = east_coef * (current[:, :, 1:, :] - current[:, :, :-1, :])
            div_east = (flux_east[:, :, 1:, :] - flux_east[:, :, :-1, :])[:, :, :, 1:-1]
            north_coef = north_kappa[:, :, :-1] * wet_window[:, :, :-1] * wet_window[:, :, 1:]
            flux_north = north_coef * (current[:, :, :, 1:] - current[:, :, :, :-1])
            div_north = (flux_north[:, :, :, 1:] - flux_north[:, :, :, :-1])[:, :, 1:-1, :]
            active = (step_counts > number).astype(jnp.float32)[:, None, None, None]
            current = current[:, :, 1:-1, 1:-1] + active * (div_east + div_north)
    return current


def both_sums(terms, partial_value):
    return lax.psum((terms, partial_value), ("gx", "gy", "gz"))


def squares(resid_field):
    return lax.psum(jnp.sum(resid_field * resid_field), ("gx", "gy", "gz"))


def shards(
    innovation,
    obs_precision,
    error_scale,
    kappa_x,
    kappa_y,
    sea_mask,
    members,
    vertical,
    diffusion_steps,
):
    wet_cells = sea_mask.astype(jnp.float32)
    coefficients = jnp.stack([kappa_x, kappa_y, wet_cells])
    padded = extended(coefficients, (("gx", 2), ("gy", 3)), KMAX)
    cols_dev = wet_cells.shape[2]
    y_position = (
        lax.axis_index("gy") * cols_dev + jnp.arange(cols_dev + 2 * KMAX, dtype=jnp.int32) - KMAX
    )
    inside = ((y_position >= 0) & (y_position < cols_dev * lax.axis_size("gy"))).astype(jnp.float32)
    padded = jnp.stack([padded[0], padded[1], padded[2] * inside[None, None, :]])
    halo_depth = 2
    transposed = jnp.swapaxes(vertical, 1, 2)
    sqrt_static = math.sqrt(static_share)
    ens_scale = math.sqrt(ensemble_share / (members.shape[0] - 1))

    def static_back(masked):
        return sqrt_static * diffuse(
            level_mix(error_scale * masked, transposed), padded, diffusion_steps, halo_depth
        )

    def ensemble_terms(masked):
        return jnp.einsum("mflxy,flxy->m", members, masked, precision=lax.Precision.HIGHEST)

    masked = wet_cells * (obs_precision * innovation)
    resid_field = static_back(masked)
    ens_sum, field_norm = both_sums(ensemble_terms(masked), jnp.sum(resid_field * resid_field))
    resid_weights = ens_scale * ens_sum
    norm_now = field_norm + jnp.sum(resid_weights * resid_weights)
    dir_field, dir_weights = (resid_field, resid_weights)
    control_field = jnp.zeros_like(resid_field)
    control_weights = jnp.zeros(resid_weights.shape, jnp.float32)
    for iteration in range(ITERS):
        static = error_scale * level_mix(
            diffuse(dir_field, padded, diffusion_steps, halo_depth), vertical
        )
        ensemble = jnp.einsum(
            "m,mflxy->flxy", dir_weights, members, precision=lax.Precision.HIGHEST
        )
        observed = wet_cells * (sqrt_static * static + ens_scale * ensemble)
        weighted = obs_precision * observed
        masked = wet_cells * weighted
        image_field = dir_field + static_back(masked)
        ens_sum, curve_part = both_sums(ensemble_terms(masked), jnp.sum(dir_field * image_field))
        image_weights = dir_weights + ens_scale * ens_sum
        curvature = curve_part + jnp.sum(dir_weights * image_weights)
        step_length = norm_now / curvature
        control_field = control_field + step_length * dir_field
        control_weights = control_weights + step_length * dir_weights
        resid_field = resid_field - step_length * image_field
        resid_weights = resid_weights - step_length * image_weights
        if iteration + 1 < ITERS:
            norm_next = squares(resid_field) + jnp.sum(resid_weights * resid_weights)
            ratio_next = norm_next / norm_now
            dir_field = resid_field + ratio_next * dir_field
            dir_weights = resid_weights + ratio_next * dir_weights
            norm_now = norm_next
    return (control_field, control_weights, resid_field)


def solution(mesh):
    placed = (
        P("grp", "gz", "gx", "gy"),
        P("grp", "gz", "gx", "gy"),
        P(None, "gz", "gx", "gy"),
        P("gz", "gx", "gy"),
        P("gz", "gx", "gy"),
        P("gz", "gx", "gy"),
        P("grp", None, "gz", "gx", "gy"),
        P(),
        P(),
    )
    return jax.shard_map(
        shards,
        mesh=mesh,
        in_specs=placed,
        out_specs=(P("grp", "gz", "gx", "gy"), P("grp"), P("grp", "gz", "gx", "gy")),
        check_vma=False,
    )
```

profile of v0, /device:TPU:0, one launch (start us, length us, event | category | flops | bytes accessed | tf_op | source)
XLA Modules:
  0.0 489.1 jit_solution(17993200651248399106)
XLA Ops:
  2.3 3.1 collective-permute-start.4
  5.3 2.1 collective-permute-start.5
  9.2 1.9 all_gather.15
  11.7 3.8 collective-permute-start.1
  21.6 2.0 collective-permute-done.2
  23.6 2.6 collective-permute-done.3
  31.1 3.8 collective-permute-start.9
  38.8 2.9 collective-permute-done.10
  45.2 3.0 collective-permute-start.13
  52.0 2.9 collective-permute-done.14
  58.4 2.8 collective-permute-start.17
  65.0 2.9 collective-permute-done.18
  72.5 2.5 collective-permute-start.21
  78.9 4.2 collective-permute-done.22
  83.1 2.5 collective-permute-done.23
  87.4 3.1 collective-permute-start.25
  94.3 3.4 collective-permute-done.26
  100.7 3.2 collective-permute-start.29
  107.8 2.9 collective-permute-done.30
  113.9 3.1 collective-permute-start.33
  120.7 2.9 collective-permute-done.34
  127.1 3.0 collective-permute-start.37
  133.8 2.1 convolution_bitcast_fusion.2
  135.9 29.5 %psum.50 = f32[16]{0:T(128)S(1)} all-reduce(f32[16]{0:T(128)S(1)} %convolution_bitcast_fusion.2), channel_id=1, replica_groups=mesh['grp'=2,'gx'=4,'gy'=2,'gz'=2] {'gx','gy','gz'}, use_global_device_ids=true, to_apply=%region_2.0 | all-reduce | flops 16 | bytes 128 | tf_op jit(solution)/shard_map/psum | solution.py:66
  166.5 3.8 collective-permute-start.41
  172.1 2.0 collective-permute-start.43
  174.3 4.0 collective-permute-done.42
  180.6 1.9 all_gather.16
  183.1 1.9 all_gather.17
  185.5 3.8 collective-permute-start.45
  193.2 3.5 collective-permute-done.46
  199.5 3.4 collective-permute-start.49
  206.8 2.9 collective-permute-done.50
  212.9 3.0 collective-permute-start.53
  219.7 2.9 collective-permute-done.54
  226.1 2.8 collective-permute-start.57
  232.7 2.9 collective-permute-done.58
  239.7 2.7 collective-permute-start.61
  246.0 2.1 convolution_bitcast_fusion.1
  251.8 30.1 %all-reduce.1 = (f32[]{:T(128)}, f32[16]{0:T(128)S(1)}, f32[]{:T(128)}) all-reduce(f32[]{:T(128)} %get-tuple-element.10, f32[16]{0:T(128)S(1)} %convolution_bitcast_fusion.1, f32[]{:T(128)} %get-tuple-element.9), channel_id=1, replica_groups=mesh['grp'=2,'gx'=4,'gy'=2,'gz'=2] {'gx','gy','gz'}, use_global_device_ids=true, to_apply=%region_1.0 | all-reduce | flops 18 | bytes 144 | tf_op jit(solution)/shard_map/psum | solution.py:66
  286.4 30.1 %psum.53 = f32[]{:T(128)} all-reduce(f32[]{:T(128)} %multiply_reduce_fusion.1), channel_id=1, replica_groups=mesh['grp'=2,'gx'=4,'gy'=2,'gz'=2] {'gx','gy','gz'}, use_global_device_ids=true, to_apply=%region_9.0 | all-reduce | flops 1 | bytes 8 | tf_op jit(solution)/shard_map/psum | solution.py:70
  317.9 3.8 collective-permute-start.65
  323.6 2.0 collective-permute-start.67
  325.6 3.2 collective-permute-done.66
  331.3 3.8 collective-permute-start.69
  338.9 2.9 collective-permute-done.70
  345.0 3.0 collective-permute-start.73
  351.9 2.9 collective-permute-done.74
  358.3 2.8 collective-permute-start.77
  364.9 2.9 collective-permute-done.78
  372.4 2.5 collective-permute-start.81
  383.9 1.9 all_gather.18
  386.3 1.9 all_gather.19
  390.3 2.6 collective-permute-start.85
  396.5 3.8 collective-permute-done.86
  403.7 2.8 collective-permute-start.89
  410.4 2.9 collective-permute-done.90
  416.8 2.8 collective-permute-start.93
  423.4 2.9 collective-permute-done.94
  429.9 2.7 collective-permute-start.97
  436.4 2.9 collective-permute-done.98
  443.3 2.5 collective-permute-start.101
  449.7 2.1 convolution_bitcast_fusion
  455.4 30.1 %all-reduce = (f32[]{:T(128)}, f32[16]{0:T(128)S(1)}) all-reduce(f32[]{:T(128)} %get-tuple-element.18, f32[16]{0:T(128)S(1)} %convolution_bitcast_fusion), channel_id=1, replica_groups=mesh['grp'=2,'gx'=4,'gy'=2,'gz'=2] {'gx','gy','gz'}, use_global_device_ids=true, to_apply=%region_12.0 | all-reduce | flops 17 | bytes 136 | tf_op jit(solution)/shard_map/psum | solution.py:66
  (567 shorter events, 188.3 us)
Async XLA Ops:
  2.3 17.1 %collective-permute-start.4 = (f32[3,2,10,108]{3,2,1,0:T(8,128)S(1)}, f32[3,2,10,108]{3,2,1,0:T(8,128)S(1)}, u32[]{:S(2)}, u32[]{:S(2)}) collective-permute-start(f32[3,2,10,108]{3,2,1,0:T(8,128)S(1)} %get-tuple-element.339), channel_id=1, source_target_pairs={{0,4},{4,8},{8,12},{12,0},{1,5},{5,9},{9,13},{13,1},{2,6},{6,10},{... | collective-permute-start | bytes 77768 | tf_op jit(solution)/shard_map/ppermute | solution.py:23
  5.3 14.0 %collective-permute-start.5 = (f32[3,2,10,108]{3,2,1,0:T(8,128)S(1)}, f32[3,2,10,108]{3,2,1,0:T(8,128)S(1)}, u32[]{:S(2)}, u32[]{:S(2)}) collective-permute-start(f32[3,2,10,108]{3,2,1,0:T(8,128)S(1)} %get-tuple-element.340), channel_id=1, source_target_pairs={{4,0},{8,4},{12,8},{0,12},{5,1},{9,5},{13,9},{1,13},{6,2},{10,6},{... | collective-permute-start | bytes 77768 | tf_op jit(solution)/shard_map/ppermute | solution.py:25
  11.6 5.5 %collective-permute-start = (f32[5,2,2,108]{3,2,1,0:T(2,128)S(1)}, f32[5,2,2,108]{3,2,1,0:T(2,128)S(1)}, u32[]{:S(2)}, u32[]{:S(2)}) collective-permute-start(f32[5,2,2,108]{3,2,1,0:T(2,128)S(1)} %get-tuple-element.337), channel_id=1, source_target_pairs={{0,4},{4,8},{8,12},{12,0},{1,5},{5,9},{9,13},{13,1},{2,6},{6,10},{... | collective-permute-start | bytes 25928 | tf_op jit(solution)/shard_map/ppermute | solution.py:23
  11.7 5.5 %collective-permute-start.1 = (f32[5,2,2,108]{3,2,1,0:T(2,128)S(1)}, f32[5,2,2,108]{3,2,1,0:T(2,128)S(1)}, u32[]{:S(2)}, u32[]{:S(2)}) collective-permute-start(f32[5,2,2,108]{3,2,1,0:T(2,128)S(1)} %get-tuple-element.338), channel_id=1, source_target_pairs={{4,0},{8,4},{12,8},{0,12},{5,1},{9,5},{13,9},{1,13},{6,2},{10,6},{... | collective-permute-start | bytes 25928 | tf_op jit(solution)/shard_map/ppermute | solution.py:25
  17.3 6.3 %collective-permute-start.2 = (f32[5,2,20,2]{3,2,1,0:T(8,128)S(1)}, f32[5,2,20,2]{3,2,1,0:T(8,128)S(1)}, u32[]{:S(2)}, u32[]{:S(2)}) collective-permute-start(f32[5,2,20,2]{3,2,1,0:T(8,128)S(1)} %get-tuple-element.285), channel_id=1, source_target_pairs={{0,2},{2,0},{1,3},{3,1},{4,6},{6,4},{5,7},{7,5},{8,10},{10,8},{9,1... | collective-permute-start | bytes 4808 | tf_op jit(solution)/shard_map/ppermute | solution.py:23
  19.0 7.3 %collective-permute-start.3 = (f32[5,2,20,2]{3,2,1,0:T(8,128)S(1)}, f32[5,2,20,2]{3,2,1,0:T(8,128)S(1)}, u32[]{:S(2)}, u32[]{:S(2)}) collective-permute-start(f32[5,2,20,2]{3,2,1,0:T(8,128)S(1)} %get-tuple-element.286), channel_id=1, source_target_pairs={{2,0},{0,2},{3,1},{1,3},{6,4},{4,6},{7,5},{5,7},{10,8},{8,10},{11,... | collective-permute-start | bytes 4808 | tf_op jit(solution)/shard_map/ppermute | solution.py:25
  19.5 8.7 %collective-permute-start.6 = (f32[3,2,36,10]{3,2,1,0:T(8,128)S(1)}, f32[3,2,36,10]{3,2,1,0:T(8,128)S(1)}, u32[]{:S(2)}, u32[]{:S(2)}) collective-permute-start(f32[3,2,36,10]{3,2,1,0:T(8,128)S(1)} %get-tuple-element.283), channel_id=1, source_target_pairs={{0,2},{2,0},{1,3},{3,1},{4,6},{6,4},{5,7},{7,5},{8,10},{10,8},{9,1... | collective-permute-start | bytes 25928 | tf_op jit(solution)/shard_map/ppermute | solution.py:23
  21.2 8.3 %collective-permute-start.7 = (f32[3,2,36,10]{3,2,1,0:T(8,128)S(1)}, f32[3,2,36,10]{3,2,1,0:T(8,128)S(1)}, u32[]{:S(2)}, u32[]{:S(2)}) collective-permute-start(f32[3,2,36,10]{3,2,1,0:T(8,128)S(1)} %get-tuple-element.284), channel_id=1, source_target_pairs={{2,0},{0,2},{3,1},{1,3},{6,4},{4,6},{7,5},{5,7},{10,8},{8,10},{11,... | collective-permute-start | bytes 25928 | tf_op jit(solution)/shard_map/ppermute | solution.py:25
  31.1 5.5 %collective-permute-start.8 = (f32[5,2,2,108]{3,2,1,0:T(2,128)S(1)}, f32[5,2,2,108]{3,2,1,0:T(2,128)S(1)}, u32[]{:S(2)}, u32[]{:S(2)}) collective-permute-start(f32[5,2,2,108]{3,2,1,0:T(2,128)S(1)} %get-tuple-element.335), channel_id=1, source_target_pairs={{0,4},{4,8},{8,12},{12,0},{1,5},{5,9},{9,13},{13,1},{2,6},{6,10},{... | collective-permute-start | bytes 25928 | tf_op jit(solution)/shard_map/ppermute | solution.py:23
  31.1 5.5 %collective-permute-start.9 = (f32[5,2,2,108]{3,2,1,0:T(2,128)S(1)}, f32[5,2,2,108]{3,2,1,0:T(2,128)S(1)}, u32[]{:S(2)}, u32[]{:S(2)}) collective-permute-start(f32[5,2,2,108]{3,2,1,0:T(2,128)S(1)} %get-tuple-element.336), channel_id=1, source_target_pairs={{4,0},{8,4},{12,8},{0,12},{5,1},{9,5},{13,9},{1,13},{6,2},{10,6},{... | collective-permute-start | bytes 25928 | tf_op jit(solution)/shard_map/ppermute | solution.py:25
  44.3 5.5 %collective-permute-start.12 = (f32[5,2,2,108]{3,2,1,0:T(2,128)S(1)}, f32[5,2,2,108]{3,2,1,0:T(2,128)S(1)}, u32[]{:S(2)}, u32[]{:S(2)}) collective-permute-start(f32[5,2,2,108]{3,2,1,0:T(2,128)S(1)} %get-tuple-element.333), channel_id=1, source_target_pairs={{0,4},{4,8},{8,12},{12,0},{1,5},{5,9},{9,13},{13,1},{2,6},{6,10},{... | collective-permute-start | bytes 25928 | tf_op jit(solution)/shard_map/ppermute | solution.py:23
  57.2 5.6 %collective-permute-start.16 = (f32[5,2,2,108]{3,2,1,0:T(2,128)S(1)}, f32[5,2,2,108]{3,2,1,0:T(2,128)S(1)}, u32[]{:S(2)}, u32[]{:S(2)}) collective-permute-start(f32[5,2,2,108]{3,2,1,0:T(2,128)S(1)} %get-tuple-element.331), channel_id=1, source_target_pairs={{0,4},{4,8},{8,12},{12,0},{1,5},{5,9},{9,13},{13,1},{2,6},{6,10},{... | collective-permute-start | bytes 25928 | tf_op jit(solution)/shard_map/ppermute | solution.py:23
  64.3 5.4 %collective-permute-start.19 = (f32[5,2,20,2]{3,2,1,0:T(8,128)S(1)}, f32[5,2,20,2]{3,2,1,0:T(8,128)S(1)}, u32[]{:S(2)}, u32[]{:S(2)}) collective-permute-start(f32[5,2,20,2]{3,2,1,0:T(8,128)S(1)} %get-tuple-element.250), channel_id=1, source_target_pairs={{2,0},{0,2},{3,1},{1,3},{6,4},{4,6},{7,5},{5,7},{10,8},{8,10},{11,... | collective-permute-start | bytes 4808 | tf_op jit(solution)/shard_map/ppermute | solution.py:25
  70.7 6.0 %collective-permute-start.20 = (f32[5,2,2,108]{3,2,1,0:T(2,128)S(1)}, f32[5,2,2,108]{3,2,1,0:T(2,128)S(1)}, u32[]{:S(2)}, u32[]{:S(2)}) collective-permute-start(f32[5,2,2,108]{3,2,1,0:T(2,128)S(1)} %get-tuple-element.329), channel_id=1, source_target_pairs={{0,4},{4,8},{8,12},{12,0},{1,5},{5,9},{9,13},{13,1},{2,6},{6,10},{... | collective-permute-start | bytes 25928 | tf_op jit(solution)/shard_map/ppermute | solution.py:23
  76.8 6.3 %collective-permute-start.22 = (f32[5,2,20,2]{3,2,1,0:T(8,128)S(1)}, f32[5,2,20,2]{3,2,1,0:T(8,128)S(1)}, u32[]{:S(2)}, u32[]{:S(2)}) collective-permute-start(f32[5,2,20,2]{3,2,1,0:T(8,128)S(1)} %get-tuple-element.239), channel_id=1, source_target_pairs={{0,2},{2,0},{1,3},{3,1},{4,6},{6,4},{5,7},{7,5},{8,10},{10,8},{9,1... | collective-permute-start | bytes 4808 | tf_op jit(solution)/shard_map/ppermute | solution.py:23
  77.8 7.7 %collective-permute-start.23 = (f32[5,2,20,2]{3,2,1,0:T(8,128)S(1)}, f32[5,2,20,2]{3,2,1,0:T(8,128)S(1)}, u32[]{:S(2)}, u32[]{:S(2)}) collective-permute-start(f32[5,2,20,2]{3,2,1,0:T(8,128)S(1)} %get-tuple-element.240), channel_id=1, source_target_pairs={{2,0},{0,2},{3,1},{1,3},{6,4},{4,6},{7,5},{5,7},{10,8},{8,10},{11,... | collective-permute-start | bytes 4808 | tf_op jit(solution)/shard_map/ppermute | solution.py:25
  86.6 5.5 %collective-permute-start.24 = (f32[5,2,2,108]{3,2,1,0:T(2,128)S(1)}, f32[5,2,2,108]{3,2,1,0:T(2,128)S(1)}, u32[]{:S(2)}, u32[]{:S(2)}) collective-permute-start(f32[5,2,2,108]{3,2,1,0:T(2,128)S(1)} %get-tuple-element.327), channel_id=1, source_target_pairs={{0,4},{4,8},{8,12},{12,0},{1,5},{5,9},{9,13},{13,1},{2,6},{6,10},{... | collective-permute-start | bytes 25928 | tf_op jit(solution)/shard_map/ppermute | solution.py:23
  92.2 5.5 %collective-permute-start.26 = (f32[5,2,20,2]{3,2,1,0:T(8,128)S(1)}, f32[5,2,20,2]{3,2,1,0:T(8,128)S(1)}, u32[]{:S(2)}, u32[]{:S(2)}) collective-permute-start(f32[5,2,20,2]{3,2,1,0:T(8,128)S(1)} %get-tuple-element.229), channel_id=1, source_target_pairs={{0,2},{2,0},{1,3},{3,1},{4,6},{6,4},{5,7},{7,5},{8,10},{10,8},{9,1... | collective-permute-start | bytes 4808 | tf_op jit(solution)/shard_map/ppermute | solution.py:23
  93.3 5.7 %collective-permute-start.27 = (f32[5,2,20,2]{3,2,1,0:T(8,128)S(1)}, f32[5,2,20,2]{3,2,1,0:T(8,128)S(1)}, u32[]{:S(2)}, u32[]{:S(2)}) collective-permute-start(f32[5,2,20,2]{3,2,1,0:T(8,128)S(1)} %get-tuple-element.230), channel_id=1, source_target_pairs={{2,0},{0,2},{3,1},{1,3},{6,4},{4,6},{7,5},{5,7},{10,8},{8,10},{11,... | collective-permute-start | bytes 4808 | tf_op jit(solution)/shard_map/ppermute | solution.py:25
  100.1 5.5 %collective-permute-start.28 = (f32[5,2,2,108]{3,2,1,0:T(2,128)S(1)}, f32[5,2,2,108]{3,2,1,0:T(2,128)S(1)}, u32[]{:S(2)}, u32[]{:S(2)}) collective-permute-start(f32[5,2,2,108]{3,2,1,0:T(2,128)S(1)} %get-tuple-element.325), channel_id=1, source_target_pairs={{0,4},{4,8},{8,12},{12,0},{1,5},{5,9},{9,13},{13,1},{2,6},{6,10},{... | collective-permute-start | bytes 25928 | tf_op jit(solution)/shard_map/ppermute | solution.py:23
  113.0 5.5 %collective-permute-start.32 = (f32[5,2,2,108]{3,2,1,0:T(2,128)S(1)}, f32[5,2,2,108]{3,2,1,0:T(2,128)S(1)}, u32[]{:S(2)}, u32[]{:S(2)}) collective-permute-start(f32[5,2,2,108]{3,2,1,0:T(2,128)S(1)} %get-tuple-element.323), channel_id=1, source_target_pairs={{0,4},{4,8},{8,12},{12,0},{1,5},{5,9},{9,13},{13,1},{2,6},{6,10},{... | collective-permute-start | bytes 25928 | tf_op jit(solution)/shard_map/ppermute | solution.py:23
  125.9 5.6 %collective-permute-start.36 = (f32[5,2,2,108]{3,2,1,0:T(2,128)S(1)}, f32[5,2,2,108]{3,2,1,0:T(2,128)S(1)}, u32[]{:S(2)}, u32[]{:S(2)}) collective-permute-start(f32[5,2,2,108]{3,2,1,0:T(2,128)S(1)} %get-tuple-element.321), channel_id=1, source_target_pairs={{0,4},{4,8},{8,12},{12,0},{1,5},{5,9},{9,13},{13,1},{2,6},{6,10},{... | collective-permute-start | bytes 25928 | tf_op jit(solution)/shard_map/ppermute | solution.py:23
  131.7 33.7 %collective-permute-start.38 = (f32[5,2,20,2]{3,2,1,0:T(8,128)S(1)}, f32[5,2,20,2]{3,2,1,0:T(8,128)S(1)}, u32[]{:S(2)}, u32[]{:S(2)}) collective-permute-start(f32[5,2,20,2]{3,2,1,0:T(8,128)S(1)} %get-tuple-element.199), channel_id=1, source_target_pairs={{0,2},{2,0},{1,3},{3,1},{4,6},{6,4},{5,7},{7,5},{8,10},{10,8},{9,1... | collective-permute-start | bytes 4808 | tf_op jit(solution)/shard_map/ppermute | solution.py:23
  133.0 32.3 %collective-permute-start.39 = (f32[5,2,20,2]{3,2,1,0:T(8,128)S(1)}, f32[5,2,20,2]{3,2,1,0:T(8,128)S(1)}, u32[]{:S(2)}, u32[]{:S(2)}) collective-permute-start(f32[5,2,20,2]{3,2,1,0:T(8,128)S(1)} %get-tuple-element.200), channel_id=1, source_target_pairs={{2,0},{0,2},{3,1},{1,3},{6,4},{4,6},{7,5},{5,7},{10,8},{8,10},{11,... | collective-permute-start | bytes 4808 | tf_op jit(solution)/shard_map/ppermute | solution.py:25
  166.4 5.5 %collective-permute-start.40 = (f32[5,2,2,108]{3,2,1,0:T(2,128)S(1)}, f32[5,2,2,108]{3,2,1,0:T(2,128)S(1)}, u32[]{:S(2)}, u32[]{:S(2)}) collective-permute-start(f32[5,2,2,108]{3,2,1,0:T(2,128)S(1)} %get-tuple-element.319), channel_id=1, source_target_pairs={{0,4},{4,8},{8,12},{12,0},{1,5},{5,9},{9,13},{13,1},{2,6},{6,10},{... | collective-permute-start | bytes 25928 | tf_op jit(solution)/shard_map/ppermute | solution.py:23
  166.5 5.5 %collective-permute-start.41 = (f32[5,2,2,108]{3,2,1,0:T(2,128)S(1)}, f32[5,2,2,108]{3,2,1,0:T(2,128)S(1)}, u32[]{:S(2)}, u32[]{:S(2)}) collective-permute-start(f32[5,2,2,108]{3,2,1,0:T(2,128)S(1)} %get-tuple-element.320), channel_id=1, source_target_pairs={{4,0},{8,4},{12,8},{0,12},{5,1},{9,5},{13,9},{1,13},{6,2},{10,6},{... | collective-permute-start | bytes 25928 | tf_op jit(solution)/shard_map/ppermute | solution.py:25
  172.1 6.2 %collective-permute-start.42 = (f32[5,2,20,2]{3,2,1,0:T(8,128)S(1)}, f32[5,2,20,2]{3,2,1,0:T(8,128)S(1)}, u32[]{:S(2)}, u32[]{:S(2)}) collective-permute-start(f32[5,2,20,2]{3,2,1,0:T(8,128)S(1)} %get-tuple-element.189), channel_id=1, source_target_pairs={{0,2},{2,0},{1,3},{3,1},{4,6},{6,4},{5,7},{7,5},{8,10},{10,8},{9,1... | collective-permute-start | bytes 4808 | tf_op jit(solution)/shard_map/ppermute | solution.py:23
  172.1 7.4 %collective-permute-start.43 = (f32[5,2,20,2]{3,2,1,0:T(8,128)S(1)}, f32[5,2,20,2]{3,2,1,0:T(8,128)S(1)}, u32[]{:S(2)}, u32[]{:S(2)}) collective-permute-start(f32[5,2,20,2]{3,2,1,0:T(8,128)S(1)} %get-tuple-element.190), channel_id=1, source_target_pairs={{2,0},{0,2},{3,1},{1,3},{6,4},{4,6},{7,5},{5,7},{10,8},{8,10},{11,... | collective-permute-start | bytes 4808 | tf_op jit(solution)/shard_map/ppermute | solution.py:25
  185.4 5.5 %collective-permute-start.44 = (f32[5,2,2,108]{3,2,1,0:T(2,128)S(1)}, f32[5,2,2,108]{3,2,1,0:T(2,128)S(1)}, u32[]{:S(2)}, u32[]{:S(2)}) collective-permute-start(f32[5,2,2,108]{3,2,1,0:T(2,128)S(1)} %get-tuple-element.317), channel_id=1, source_target_pairs={{0,4},{4,8},{8,12},{12,0},{1,5},{5,9},{9,13},{13,1},{2,6},{6,10},{... | collective-permute-start | bytes 25928 | tf_op jit(solution)/shard_map/ppermute | solution.py:23
  185.5 5.5 %collective-permute-start.45 = (f32[5,2,2,108]{3,2,1,0:T(2,128)S(1)}, f32[5,2,2,108]{3,2,1,0:T(2,128)S(1)}, u32[]{:S(2)}, u32[]{:S(2)}) collective-permute-start(f32[5,2,2,108]{3,2,1,0:T(2,128)S(1)} %get-tuple-element.318), channel_id=1, source_target_pairs={{4,0},{8,4},{12,8},{0,12},{5,1},{9,5},{13,9},{1,13},{6,2},{10,6},{... | collective-permute-start | bytes 25928 | tf_op jit(solution)/shard_map/ppermute | solution.py:25
  191.1 5.6 %collective-permute-start.46 = (f32[5,2,20,2]{3,2,1,0:T(8,128)S(1)}, f32[5,2,20,2]{3,2,1,0:T(8,128)S(1)}, u32[]{:S(2)}, u32[]{:S(2)}) collective-permute-start(f32[5,2,20,2]{3,2,1,0:T(8,128)S(1)} %get-tuple-element.179), channel_id=1, source_target_pairs={{0,2},{2,0},{1,3},{3,1},{4,6},{6,4},{5,7},{7,5},{8,10},{10,8},{9,1... | collective-permute-start | bytes 4808 | tf_op jit(solution)/shard_map/ppermute | solution.py:23
  191.4 6.6 %collective-permute-start.47 = (f32[5,2,20,2]{3,2,1,0:T(8,128)S(1)}, f32[5,2,20,2]{3,2,1,0:T(8,128)S(1)}, u32[]{:S(2)}, u32[]{:S(2)}) collective-permute-start(f32[5,2,20,2]{3,2,1,0:T(8,128)S(1)} %get-tuple-element.180), channel_id=1, source_target_pairs={{2,0},{0,2},{3,1},{1,3},{6,4},{4,6},{7,5},{5,7},{10,8},{8,10},{11,... | collective-permute-start | bytes 4808 | tf_op jit(solution)/shard_map/ppermute | solution.py:25
  199.0 5.5 %collective-permute-start.48 = (f32[5,2,2,108]{3,2,1,0:T(2,128)S(1)}, f32[5,2,2,108]{3,2,1,0:T(2,128)S(1)}, u32[]{:S(2)}, u32[]{:S(2)}) collective-permute-start(f32[5,2,2,108]{3,2,1,0:T(2,128)S(1)} %get-tuple-element.315), channel_id=1, source_target_pairs={{0,4},{4,8},{8,12},{12,0},{1,5},{5,9},{9,13},{13,1},{2,6},{6,10},{... | collective-permute-start | bytes 25928 | tf_op jit(solution)/shard_map/ppermute | solution.py:23
  205.2 5.8 %collective-permute-start.51 = (f32[5,2,20,2]{3,2,1,0:T(8,128)S(1)}, f32[5,2,20,2]{3,2,1,0:T(8,128)S(1)}, u32[]{:S(2)}, u32[]{:S(2)}) collective-permute-start(f32[5,2,20,2]{3,2,1,0:T(8,128)S(1)} %get-tuple-element.170), channel_id=1, source_target_pairs={{2,0},{0,2},{3,1},{1,3},{6,4},{4,6},{7,5},{5,7},{10,8},{8,10},{11,... | collective-permute-start | bytes 4808 | tf_op jit(solution)/shard_map/ppermute | solution.py:25
  212.0 5.5 %collective-permute-start.52 = (f32[5,2,2,108]{3,2,1,0:T(2,128)S(1)}, f32[5,2,2,108]{3,2,1,0:T(2,128)S(1)}, u32[]{:S(2)}, u32[]{:S(2)}) collective-permute-start(f32[5,2,2,108]{3,2,1,0:T(2,128)S(1)} %get-tuple-element.313), channel_id=1, source_target_pairs={{0,4},{4,8},{8,12},{12,0},{1,5},{5,9},{9,13},{13,1},{2,6},{6,10},{... | collective-permute-start | bytes 25928 | tf_op jit(solution)/shard_map/ppermute | solution.py:23
  218.4 5.5 %collective-permute-start.55 = (f32[5,2,20,2]{3,2,1,0:T(8,128)S(1)}, f32[5,2,20,2]{3,2,1,0:T(8,128)S(1)}, u32[]{:S(2)}, u32[]{:S(2)}) collective-permute-start(f32[5,2,20,2]{3,2,1,0:T(8,128)S(1)} %get-tuple-element.160), channel_id=1, source_target_pairs={{2,0},{0,2},{3,1},{1,3},{6,4},{4,6},{7,5},{5,7},{10,8},{8,10},{11,... | collective-permute-start | bytes 4808 | tf_op jit(solution)/shard_map/ppermute | solution.py:25
  224.9 5.6 %collective-permute-start.56 = (f32[5,2,2,108]{3,2,1,0:T(2,128)S(1)}, f32[5,2,2,108]{3,2,1,0:T(2,128)S(1)}, u32[]{:S(2)}, u32[]{:S(2)}) collective-permute-start(f32[5,2,2,108]{3,2,1,0:T(2,128)S(1)} %get-tuple-element.311), channel_id=1, source_target_pairs={{0,4},{4,8},{8,12},{12,0},{1,5},{5,9},{9,13},{13,1},{2,6},{6,10},{... | collective-permute-start | bytes 25928 | tf_op jit(solution)/shard_map/ppermute | solution.py:23
  231.4 5.7 %collective-permute-start.59 = (f32[5,2,20,2]{3,2,1,0:T(8,128)S(1)}, f32[5,2,20,2]{3,2,1,0:T(8,128)S(1)}, u32[]{:S(2)}, u32[]{:S(2)}) collective-permute-start(f32[5,2,20,2]{3,2,1,0:T(8,128)S(1)} %get-tuple-element.150), channel_id=1, source_target_pairs={{2,0},{0,2},{3,1},{1,3},{6,4},{4,6},{7,5},{5,7},{10,8},{8,10},{11,... | collective-permute-start | bytes 4808 | tf_op jit(solution)/shard_map/ppermute | solution.py:25
  238.1 5.7 %collective-permute-start.60 = (f32[5,2,2,108]{3,2,1,0:T(2,128)S(1)}, f32[5,2,2,108]{3,2,1,0:T(2,128)S(1)}, u32[]{:S(2)}, u32[]{:S(2)}) collective-permute-start(f32[5,2,2,108]{3,2,1,0:T(2,128)S(1)} %get-tuple-element.309), channel_id=1, source_target_pairs={{0,4},{4,8},{8,12},{12,0},{1,5},{5,9},{9,13},{13,1},{2,6},{6,10},{... | collective-permute-start | bytes 25928 | tf_op jit(solution)/shard_map/ppermute | solution.py:23
  244.8 5.4 %collective-permute-start.63 = (f32[5,2,20,2]{3,2,1,0:T(8,128)S(1)}, f32[5,2,20,2]{3,2,1,0:T(8,128)S(1)}, u32[]{:S(2)}, u32[]{:S(2)}) collective-permute-start(f32[5,2,20,2]{3,2,1,0:T(8,128)S(1)} %get-tuple-element.140), channel_id=1, source_target_pairs={{2,0},{0,2},{3,1},{1,3},{6,4},{4,6},{7,5},{5,7},{10,8},{8,10},{11,... | collective-permute-start | bytes 4808 | tf_op jit(solution)/shard_map/ppermute | solution.py:25
  317.9 5.5 %collective-permute-start.64 = (f32[5,2,2,108]{3,2,1,0:T(2,128)S(1)}, f32[5,2,2,108]{3,2,1,0:T(2,128)S(1)}, u32[]{:S(2)}, u32[]{:S(2)}) collective-permute-start(f32[5,2,2,108]{3,2,1,0:T(2,128)S(1)} %get-tuple-element.307), channel_id=1, source_target_pairs={{0,4},{4,8},{8,12},{12,0},{1,5},{5,9},{9,13},{13,1},{2,6},{6,10},{... | collective-permute-start | bytes 25928 | tf_op jit(solution)/shard_map/ppermute | solution.py:23
  317.9 5.5 %collective-permute-start.65 = (f32[5,2,2,108]{3,2,1,0:T(2,128)S(1)}, f32[5,2,2,108]{3,2,1,0:T(2,128)S(1)}, u32[]{:S(2)}, u32[]{:S(2)}) collective-permute-start(f32[5,2,2,108]{3,2,1,0:T(2,128)S(1)} %get-tuple-element.308), channel_id=1, source_target_pairs={{4,0},{8,4},{12,8},{0,12},{5,1},{9,5},{13,9},{1,13},{6,2},{10,6},{... | collective-permute-start | bytes 25928 | tf_op jit(solution)/shard_map/ppermute | solution.py:25
  323.5 5.3 %collective-permute-start.66 = (f32[5,2,20,2]{3,2,1,0:T(8,128)S(1)}, f32[5,2,20,2]{3,2,1,0:T(8,128)S(1)}, u32[]{:S(2)}, u32[]{:S(2)}) collective-permute-start(f32[5,2,20,2]{3,2,1,0:T(8,128)S(1)} %get-tuple-element.129), channel_id=1, source_target_pairs={{0,2},{2,0},{1,3},{3,1},{4,6},{6,4},{5,7},{7,5},{8,10},{10,8},{9,1... | collective-permute-start | bytes 4808 | tf_op jit(solution)/shard_map/ppermute | solution.py:23
  323.6 6.6 %collective-permute-start.67 = (f32[5,2,20,2]{3,2,1,0:T(8,128)S(1)}, f32[5,2,20,2]{3,2,1,0:T(8,128)S(1)}, u32[]{:S(2)}, u32[]{:S(2)}) collective-permute-start(f32[5,2,20,2]{3,2,1,0:T(8,128)S(1)} %get-tuple-element.130), channel_id=1, source_target_pairs={{2,0},{0,2},{3,1},{1,3},{6,4},{4,6},{7,5},{5,7},{10,8},{8,10},{11,... | collective-permute-start | bytes 4808 | tf_op jit(solution)/shard_map/ppermute | solution.py:25
  331.2 5.5 %collective-permute-start.68 = (f32[5,2,2,108]{3,2,1,0:T(2,128)S(1)}, f32[5,2,2,108]{3,2,1,0:T(2,128)S(1)}, u32[]{:S(2)}, u32[]{:S(2)}) collective-permute-start(f32[5,2,2,108]{3,2,1,0:T(2,128)S(1)} %get-tuple-element.305), channel_id=1, source_target_pairs={{0,4},{4,8},{8,12},{12,0},{1,5},{5,9},{9,13},{13,1},{2,6},{6,10},{... | collective-permute-start | bytes 25928 | tf_op jit(solution)/shard_map/ppermute | solution.py:23
  331.3 5.5 %collective-permute-start.69 = (f32[5,2,2,108]{3,2,1,0:T(2,128)S(1)}, f32[5,2,2,108]{3,2,1,0:T(2,128)S(1)}, u32[]{:S(2)}, u32[]{:S(2)}) collective-permute-start(f32[5,2,2,108]{3,2,1,0:T(2,128)S(1)} %get-tuple-element.306), channel_id=1, source_target_pairs={{4,0},{8,4},{12,8},{0,12},{5,1},{9,5},{13,9},{1,13},{6,2},{10,6},{... | collective-permute-start | bytes 25928 | tf_op jit(solution)/shard_map/ppermute | solution.py:25
  337.3 5.8 %collective-permute-start.71 = (f32[5,2,20,2]{3,2,1,0:T(8,128)S(1)}, f32[5,2,20,2]{3,2,1,0:T(8,128)S(1)}, u32[]{:S(2)}, u32[]{:S(2)}) collective-permute-start(f32[5,2,20,2]{3,2,1,0:T(8,128)S(1)} %get-tuple-element.120), channel_id=1, source_target_pairs={{2,0},{0,2},{3,1},{1,3},{6,4},{4,6},{7,5},{5,7},{10,8},{8,10},{11,... | collective-permute-start | bytes 4808 | tf_op jit(solution)/shard_map/ppermute | solution.py:25
  344.1 5.5 %collective-permute-start.72 = (f32[5,2,2,108]{3,2,1,0:T(2,128)S(1)}, f32[5,2,2,108]{3,2,1,0:T(2,128)S(1)}, u32[]{:S(2)}, u32[]{:S(2)}) collective-permute-start(f32[5,2,2,108]{3,2,1,0:T(2,128)S(1)} %get-tuple-element.303), channel_id=1, source_target_pairs={{0,4},{4,8},{8,12},{12,0},{1,5},{5,9},{9,13},{13,1},{2,6},{6,10},{... | collective-permute-start | bytes 25928 | tf_op jit(solution)/shard_map/ppermute | solution.py:23
  350.6 5.5 %collective-permute-start.75 = (f32[5,2,20,2]{3,2,1,0:T(8,128)S(1)}, f32[5,2,20,2]{3,2,1,0:T(8,128)S(1)}, u32[]{:S(2)}, u32[]{:S(2)}) collective-permute-start(f32[5,2,20,2]{3,2,1,0:T(8,128)S(1)} %get-tuple-element.110), channel_id=1, source_target_pairs={{2,0},{0,2},{3,1},{1,3},{6,4},{4,6},{7,5},{5,7},{10,8},{8,10},{11,... | collective-permute-start | bytes 4808 | tf_op jit(solution)/shard_map/ppermute | solution.py:25
  357.1 5.6 %collective-permute-start.76 = (f32[5,2,2,108]{3,2,1,0:T(2,128)S(1)}, f32[5,2,2,108]{3,2,1,0:T(2,128)S(1)}, u32[]{:S(2)}, u32[]{:S(2)}) collective-permute-start(f32[5,2,2,108]{3,2,1,0:T(2,128)S(1)} %get-tuple-element.301), channel_id=1, source_target_pairs={{0,4},{4,8},{8,12},{12,0},{1,5},{5,9},{9,13},{13,1},{2,6},{6,10},{... | collective-permute-start | bytes 25928 | tf_op jit(solution)/shard_map/ppermute | solution.py:23
  363.6 6.0 %collective-permute-start.79 = (f32[5,2,20,2]{3,2,1,0:T(8,128)S(1)}, f32[5,2,20,2]{3,2,1,0:T(8,128)S(1)}, u32[]{:S(2)}, u32[]{:S(2)}) collective-permute-start(f32[5,2,20,2]{3,2,1,0:T(8,128)S(1)} %get-tuple-element.100), channel_id=1, source_target_pairs={{2,0},{0,2},{3,1},{1,3},{6,4},{4,6},{7,5},{5,7},{10,8},{8,10},{11,... | collective-permute-start | bytes 4808 | tf_op jit(solution)/shard_map/ppermute | solution.py:25
  370.6 5.9 %collective-permute-start.80 = (f32[5,2,2,108]{3,2,1,0:T(2,128)S(1)}, f32[5,2,2,108]{3,2,1,0:T(2,128)S(1)}, u32[]{:S(2)}, u32[]{:S(2)}) collective-permute-start(f32[5,2,2,108]{3,2,1,0:T(2,128)S(1)} %get-tuple-element.299), channel_id=1, source_target_pairs={{0,4},{4,8},{8,12},{12,0},{1,5},{5,9},{9,13},{13,1},{2,6},{6,10},{... | collective-permute-start | bytes 25928 | tf_op jit(solution)/shard_map/ppermute | solution.py:23
  377.2 5.7 %collective-permute-start.83 = (f32[5,2,20,2]{3,2,1,0:T(8,128)S(1)}, f32[5,2,20,2]{3,2,1,0:T(8,128)S(1)}, u32[]{:S(2)}, u32[]{:S(2)}) collective-permute-start(f32[5,2,20,2]{3,2,1,0:T(8,128)S(1)} %get-tuple-element.90), channel_id=1, source_target_pairs={{2,0},{0,2},{3,1},{1,3},{6,4},{4,6},{7,5},{5,7},{10,8},{8,10},{11,... | collective-permute-start | bytes 4808 | tf_op jit(solution)/shard_map/ppermute | solution.py:25
  388.6 5.7 %collective-permute-start.84 = (f32[5,2,2,108]{3,2,1,0:T(2,128)S(1)}, f32[5,2,2,108]{3,2,1,0:T(2,128)S(1)}, u32[]{:S(2)}, u32[]{:S(2)}) collective-permute-start(f32[5,2,2,108]{3,2,1,0:T(2,128)S(1)} %get-tuple-element.297), channel_id=1, source_target_pairs={{0,4},{4,8},{8,12},{12,0},{1,5},{5,9},{9,13},{13,1},{2,6},{6,10},{... | collective-permute-start | bytes 25928 | tf_op jit(solution)/shard_map/ppermute | solution.py:23
  394.5 5.9 %collective-permute-start.86 = (f32[5,2,20,2]{3,2,1,0:T(8,128)S(1)}, f32[5,2,20,2]{3,2,1,0:T(8,128)S(1)}, u32[]{:S(2)}, u32[]{:S(2)}) collective-permute-start(f32[5,2,20,2]{3,2,1,0:T(8,128)S(1)} %get-tuple-element.79), channel_id=1, source_target_pairs={{0,2},{2,0},{1,3},{3,1},{4,6},{6,4},{5,7},{7,5},{8,10},{10,8},{9,1... | collective-permute-start | bytes 4808 | tf_op jit(solution)/shard_map/ppermute | solution.py:23
  395.2 6.4 %collective-permute-start.87 = (f32[5,2,20,2]{3,2,1,0:T(8,128)S(1)}, f32[5,2,20,2]{3,2,1,0:T(8,128)S(1)}, u32[]{:S(2)}, u32[]{:S(2)}) collective-permute-start(f32[5,2,20,2]{3,2,1,0:T(8,128)S(1)} %get-tuple-element.80), channel_id=1, source_target_pairs={{2,0},{0,2},{3,1},{1,3},{6,4},{4,6},{7,5},{5,7},{10,8},{8,10},{11,... | collective-permute-start | bytes 4808 | tf_op jit(solution)/shard_map/ppermute | solution.py:25
  402.7 5.5 %collective-permute-start.88 = (f32[5,2,2,108]{3,2,1,0:T(2,128)S(1)}, f32[5,2,2,108]{3,2,1,0:T(2,128)S(1)}, u32[]{:S(2)}, u32[]{:S(2)}) collective-permute-start(f32[5,2,2,108]{3,2,1,0:T(2,128)S(1)} %get-tuple-element.295), channel_id=1, source_target_pairs={{0,4},{4,8},{8,12},{12,0},{1,5},{5,9},{9,13},{13,1},{2,6},{6,10},{... | collective-permute-start | bytes 25928 | tf_op jit(solution)/shard_map/ppermute | solution.py:23
  409.1 5.5 %collective-permute-start.91 = (f32[5,2,20,2]{3,2,1,0:T(8,128)S(1)}, f32[5,2,20,2]{3,2,1,0:T(8,128)S(1)}, u32[]{:S(2)}, u32[]{:S(2)}) collective-permute-start(f32[5,2,20,2]{3,2,1,0:T(8,128)S(1)} %get-tuple-element.70), channel_id=1, source_target_pairs={{2,0},{0,2},{3,1},{1,3},{6,4},{4,6},{7,5},{5,7},{10,8},{8,10},{11,... | collective-permute-start | bytes 4808 | tf_op jit(solution)/shard_map/ppermute | solution.py:25
  415.6 5.6 %collective-permute-start.92 = (f32[5,2,2,108]{3,2,1,0:T(2,128)S(1)}, f32[5,2,2,108]{3,2,1,0:T(2,128)S(1)}, u32[]{:S(2)}, u32[]{:S(2)}) collective-permute-start(f32[5,2,2,108]{3,2,1,0:T(2,128)S(1)} %get-tuple-element.293), channel_id=1, source_target_pairs={{0,4},{4,8},{8,12},{12,0},{1,5},{5,9},{9,13},{13,1},{2,6},{6,10},{... | collective-permute-start | bytes 25928 | tf_op jit(solution)/shard_map/ppermute | solution.py:23
  422.1 5.5 %collective-permute-start.95 = (f32[5,2,20,2]{3,2,1,0:T(8,128)S(1)}, f32[5,2,20,2]{3,2,1,0:T(8,128)S(1)}, u32[]{:S(2)}, u32[]{:S(2)}) collective-permute-start(f32[5,2,20,2]{3,2,1,0:T(8,128)S(1)} %get-tuple-element.60), channel_id=1, source_target_pairs={{2,0},{0,2},{3,1},{1,3},{6,4},{4,6},{7,5},{5,7},{10,8},{8,10},{11,... | collective-permute-start | bytes 4808 | tf_op jit(solution)/shard_map/ppermute | solution.py:25
  428.6 5.6 %collective-permute-start.96 = (f32[5,2,2,108]{3,2,1,0:T(2,128)S(1)}, f32[5,2,2,108]{3,2,1,0:T(2,128)S(1)}, u32[]{:S(2)}, u32[]{:S(2)}) collective-permute-start(f32[5,2,2,108]{3,2,1,0:T(2,128)S(1)} %get-tuple-element.291), channel_id=1, source_target_pairs={{0,4},{4,8},{8,12},{12,0},{1,5},{5,9},{9,13},{13,1},{2,6},{6,10},{... | collective-permute-start | bytes 25928 | tf_op jit(solution)/shard_map/ppermute | solution.py:23
  435.1 5.5 %collective-permute-start.99 = (f32[5,2,20,2]{3,2,1,0:T(8,128)S(1)}, f32[5,2,20,2]{3,2,1,0:T(8,128)S(1)}, u32[]{:S(2)}, u32[]{:S(2)}) collective-permute-start(f32[5,2,20,2]{3,2,1,0:T(8,128)S(1)} %get-tuple-element.50), channel_id=1, source_target_pairs={{2,0},{0,2},{3,1},{1,3},{6,4},{4,6},{7,5},{5,7},{10,8},{8,10},{11,... | collective-permute-start | bytes 4808 | tf_op jit(solution)/shard_map/ppermute | solution.py:25
  441.6 5.8 %collective-permute-start.100 = (f32[5,2,2,108]{3,2,1,0:T(2,128)S(1)}, f32[5,2,2,108]{3,2,1,0:T(2,128)S(1)}, u32[]{:S(2)}, u32[]{:S(2)}) collective-permute-start(f32[5,2,2,108]{3,2,1,0:T(2,128)S(1)} %get-tuple-element.289), channel_id=1, source_target_pairs={{0,4},{4,8},{8,12},{12,0},{1,5},{5,9},{9,13},{13,1},{2,6},{6,10},{... | collective-permute-start | bytes 25928 | tf_op jit(solution)/shard_map/ppermute | solution.py:23
  448.4 5.4 %collective-permute-start.103 = (f32[5,2,20,2]{3,2,1,0:T(8,128)S(1)}, f32[5,2,20,2]{3,2,1,0:T(8,128)S(1)}, u32[]{:S(2)}, u32[]{:S(2)}) collective-permute-start(f32[5,2,20,2]{3,2,1,0:T(8,128)S(1)} %get-tuple-element.40), channel_id=1, source_target_pairs={{2,0},{0,2},{3,1},{1,3},{6,4},{4,6},{7,5},{5,7},{10,8},{8,10},{11,... | collective-permute-start | bytes 4808 | tf_op jit(solution)/shard_map/ppermute | solution.py:25
  (47 other events, 387.0 us)
where the time goes:
time: 497 us; the launch traced here: 489 us
  starting transfers between devices  160 us (32%)
  waiting for transfers between devices  144 us (29%)
  blocking collectives  129 us (26%)
  other arithmetic  26.6 us (5%)
  matrix products  11.3 us (2%)
  between operations  9.27 us (2%)
  local copies, waits for them, and re-layouts  9.08 us (2%)
    ppermute x52, starting transfers between devices, extended(): lax.ppermute(head, axis, [((i + 1) % count, i) for i in range(count)])  110 us
    ppermute x52, waiting for transfers between devices, extended(): lax.ppermute(tail, axis, [(i, (i + 1) % count) for i in range(count)])  107 us
    psum x3, blocking collectives, both_sums(): return lax.psum((terms, partial_value), ('gx', 'gy', 'gz'))  89.7 us
    ppermute x52, starting transfers between devices, extended(): lax.ppermute(tail, axis, [(i, (i + 1) % count) for i in range(count)])  49.7 us
    ppermute x52, waiting for transfers between devices, extended(): lax.ppermute(head, axis, [((i + 1) % count, i) for i in range(count)])  36.9 us
    psum x1, blocking collectives, squares(): return lax.psum(jnp.sum(resid_field * resid_field), ('gx', 'gy', 'gz'))  30.1 us
  transfers between devices with their start and end apart: 104, of which 75 were waited for; matrix products, arithmetic and copies ran while one was open for 2% of the time, Pallas kernels for 0%

commit v1 on v0

--- a/solution.py
+++ b/solution.py
@@ -1,8 +1,12 @@
+import functools
 import math
+
 
 import jax
 import jax.numpy as jnp
 from jax import lax
+from jax.experimental import pallas as pl
+from jax.experimental.pallas import tpu as pltpu
 from jax.sharding import PartitionSpec as P
 
 KMAX = 10
@@ -70,7 +74,7 @@
     return lax.psum(jnp.sum(resid_field * resid_field), ("gx", "gy", "gz"))
 
 
-def shards(
+def shards_any(
     innovation,
     obs_precision,
     error_scale,
@@ -138,6 +142,410 @@
             norm_now = norm_next
     return (control_field, control_weights, resid_field)
 
+ROWS = 16
+WIN = 56
+LANES = 128
+DEPTH = 2 * KMAX
+GROUP = LANES // DEPTH
+SUMS = 8
+AXES = ("gx", "gy", "gz")
+VMEM = pl.BlockSpec(memory_space=pltpu.VMEM)
+SMEM = pl.BlockSpec(memory_space=pltpu.SMEM)
+SQRT_STATIC = math.sqrt(static_share)
+
+
+def f32(*shape):
+    return jax.ShapeDtypeStruct(shape, jnp.float32)
+
+
+def call(kernel, outs, specs, args, scratch=()):
+    return pl.pallas_call(
+        kernel,
+        out_shape=outs,
+        in_specs=specs,
+        out_specs=[VMEM] * len(outs),
+        scratch_shapes=list(scratch),
+        compiler_params=pltpu.CompilerParams(vmem_limit_bytes=32 * 1024 * 1024),
+    )(*args)
+
+
+def lanes_of(shape):
+    return lax.broadcasted_iota(jnp.int32, shape, len(shape) - 1)
+
+
+def tile(ref, index, size=ROWS):
+    return ref[index * size : (index + 1) * size, :]
+
+
+def pack_edges(out_ref, planes, cols):
+    first = jnp.where(lax.axis_index("gy") == 0, cols - DEPTH, 0)
+    lane = lanes_of((ROWS, LANES))
+    for group in range(-(-len(planes) // GROUP)):
+        packed = jnp.zeros((ROWS, LANES), jnp.float32)
+        for slot, plane in enumerate(planes[group * GROUP : (group + 1) * GROUP]):
+            moved = pltpu.roll(plane, lax.rem(DEPTH * slot - first + LANES, LANES), 1)
+            packed = jnp.where((lane >= DEPTH * slot) & (lane < DEPTH * (slot + 1)), moved, packed)
+        out_ref[group * ROWS : (group + 1) * ROWS, :] = packed
+
+
+def with_edge(own, edge_ref, index, cols):
+    group, slot = divmod(index, GROUP)
+    moved = pltpu.roll(tile(edge_ref, group), (cols - DEPTH * slot) % LANES, 1)
+    return jnp.where(lanes_of(own.shape) < cols, own, moved)
+
+
+def over_rows(values):
+    return jnp.sum(values, axis=0, keepdims=True)
+
+
+def observe(first, planes, levels, cols, members_count, with_weights):
+    ens_scale = math.sqrt(ensemble_share / (members_count - 1))
+    base = planes * ROWS
+
+    def kernel(*refs):
+        if first:
+            innov, prec, scale, mask, kx, ky, members, out_z, out_e, coef = refs
+        elif with_weights:
+            own, other, weights, sums, vert, prec, scale, mask, members, out_z, out_e, out_q = refs
+        else:
+            own, other, weights, sums, vert, prec, scale, mask, members, seen, out_z, out_e = refs
+        out_z[...] = jnp.zeros(out_z.shape, jnp.float32)
+        totals = [jnp.zeros((ROWS, cols), jnp.float32) for _ in range(members_count)]
+        energy = jnp.zeros((ROWS, cols), jnp.float32)
+        cross = jnp.zeros((ROWS, cols), jnp.float32)
+        here = lax.axis_index("gz") * levels
+        there = (1 - lax.axis_index("gz")) * levels
+        for plane in range(planes):
+            field, level = divmod(plane, levels)
+            wet = mask[level].astype(jnp.float32)
+            if first:
+                weighted = wet * (prec[plane] * innov[plane])
+            else:
+                static = jnp.zeros((ROWS, cols), jnp.float32)
+                for k in range(levels):
+                    row = (field * 2 * levels + here + level) * 2 * levels
+                    static += vert[row + here + k] * tile(own, field * levels + k)[:, :cols]
+                    static += vert[row + there + k] * tile(other, field * levels + k)[:, :cols]
+                ensemble = jnp.zeros((ROWS, cols), jnp.float32)
+                for m in range(members_count):
+                    ensemble += weights[m : m + 1, :cols] * members[m, plane]
+                seen_now = wet * (SQRT_STATIC * (scale[plane] * static) + ens_scale * ensemble)
+                weighted = wet * (prec[plane] * seen_now)
+                energy += seen_now * weighted
+                if with_weights:
+                    out_q[plane] = weighted
+                else:
+                    cross += seen_now * seen[plane]
+            if with_weights:
+                for m in range(members_count):
+                    totals[m] += members[m, plane] * weighted
+            out_z[plane * ROWS : (plane + 1) * ROWS, :cols] = scale[plane] * weighted
+        if with_weights:
+            for m in range(members_count):
+                out_z[base + m : base + m + 1, :cols] = ens_scale * over_rows(totals[m])
+        if not first:
+            sums_at = base + ROWS * with_weights
+            out_z[sums_at : sums_at + SUMS, :] = sums[...]
+            out_z[sums_at : sums_at + 1, :cols] = over_rows(energy)
+            if not with_weights:
+                out_z[sums_at + 1 : sums_at + 2, :cols] = over_rows(cross)
+        edges = [tile(out_z, plane) for plane in range(planes)]
+        if first:
+            coef[...] = jnp.zeros(coef.shape, jnp.float32)
+            for level in range(levels):
+                for kind, source in enumerate((kx, ky, mask)):
+                    at = (kind * levels + level) * ROWS
+                    coef[at : at + ROWS, :cols] = source[level].astype(jnp.float32)
+            edges += [tile(coef, index) for index in range(3 * levels)]
+        packed = -(-len(edges) // GROUP) * ROWS
+        pack_edges(out_e, edges, cols)
+        out_e[packed:, :] = out_z[base:, :]
+
+    tail = (ROWS * with_weights) + (0 if first else SUMS)
+    edge_rows = -(-(planes + (3 * levels if first else 0)) // GROUP) * ROWS + tail
+    outs = [f32(base + tail, LANES), f32(edge_rows, LANES)]
+    if first:
+        outs.append(f32(3 * levels * ROWS, LANES))
+    elif with_weights:
+        outs.append(f32(planes, ROWS, cols))
+    return kernel, outs
+
+
+def mix_back(first, planes, levels, cols, tail):
+    base = planes * ROWS
+    coefs = 3 * levels if first else 0
+    fields = planes // levels
+
+    def kernel(*refs):
+        if first:
+            own, other, edge, edge_other, vert, coef, out_all, out_near = refs
+        else:
+            own, other, edge, edge_other, vert, out_all, out_near = refs
+        here = lax.axis_index("gz") * levels
+        there = (1 - lax.axis_index("gz")) * levels
+        upper = lax.broadcasted_iota(jnp.int32, (8, LANES), 0) < 4
+
+        def put(index, values):
+            out_all[index * ROWS : (index + 1) * ROWS, :] = values
+            out_near[index * 8 : (index + 1) * 8, :] = jnp.where(upper, values[:8], values[8:])
+
+        for field in range(fields):
+            mine = [with_edge(tile(own, field * levels + l), edge, field * levels + l, cols) for l in range(levels)]
+            theirs = [
+                with_edge(tile(other, field * levels + l), edge_other, field * levels + l, cols) for l in range(levels)
+            ]
+            for k in range(levels):
+                mixed = jnp.zeros((ROWS, LANES), jnp.float32)
+                for l in range(levels):
+                    block = field * 2 * levels
+                    mixed += vert[(block + here + l) * 2 * levels + here + k] * mine[l]
+                    mixed += vert[(block + there + l) * 2 * levels + here + k] * theirs[l]
+                put(field * levels + k, mixed)
+        for index in range(coefs):
+            put(planes + index, with_edge(tile(coef, index), edge, planes + index, cols))
+        packed = -(-(planes + coefs) // GROUP) * ROWS
+        total = (own[base:, :] + other[base:, :]) + (edge[packed:, :] + edge_other[packed:, :])
+        out_all[(planes + coefs) * ROWS :, :] = total
+        out_near[(planes + coefs) * 8 :, :] = total
+
+    count = planes + coefs
+    return kernel, [f32(count * ROWS + tail, LANES), f32(count * 8 + tail, LANES)]
+
+
+def window(target, index, own, after, near, before, slot):
+    target[index, 0:16, :] = tile(own, slot)
+    target[index, 16:32, :] = tile(after, slot)
+    target[index, 32:40, :] = tile(near, slot, 8)
+    target[index, 40:56, :] = tile(before, slot)
+
+
+def run_steps(start, other, coef, steps, planes, levels):
+    def one(number, source, target):
+        for level in range(levels):
+            for field in range(planes // levels):
+                plane = field * levels + level
+                u = source[plane]
+                rows = u.shape[0]
+                change = (
+                    coef[0, level] * pltpu.roll(u, rows - 1, 0)
+                    + coef[1, level] * pltpu.roll(u, 1, 0)
+                    + coef[2, level] * pltpu.roll(u, LANES - 1, 1)
+                    + coef[3, level] * pltpu.roll(u, 1, 1)
+                    - coef[4, level] * u
+                )
+                active = jnp.where(steps[field] > number, 1.0, 0.0).astype(jnp.float32)
+                target[plane] = u + active * change
+
+    def pair(index, carry):
+        one(2 * index, start, other)
+        one(2 * index + 1, other, start)
+        return carry
+
+    lax.fori_loop(0, KMAX // 2, pair, 0)
+
+
+def make_coefs(coef, kinds, levels, cols):
+    lane = lanes_of((WIN, LANES))
+    last = jnp.where(lax.axis_index("gy") == 0, LANES - 1, cols - 1)
+    for level in range(levels):
+        kx, ky, wet = (kinds[kind * levels + level] for kind in range(3))
+        east = kx * wet * pltpu.roll(wet, WIN - 1, 0)
+        north = ky * wet * pltpu.roll(wet, LANES - 1, 1)
+        north = jnp.where(lane == last, 0.0, north)
+        west = pltpu.roll(east, 1, 0)
+        south = pltpu.roll(north, 1, 1)
+        for index, values in enumerate((east, west, north, south, (east + west) + (north + south))):
+            coef[index, level] = values
+
+
+def own_sum(values, cols):
+    own = values[:ROWS]
+    return over_rows(jnp.where(lanes_of(own.shape) < cols, own, 0.0))
+
+
+def spread(values):
+    return jnp.broadcast_to(jnp.sum(values, axis=1, keepdims=True), values.shape)
+
+
+def first_diffuse(planes, levels, cols):
+    coefs = 3 * levels
+
+    def kernel(own, after, near, before, steps, coef, resid, weights, sums, out_g, buf, kinds):
+        for plane in range(planes):
+            window(buf, plane, own, after, near, before, plane)
+        for index in range(coefs):
+            window(kinds, index, own, after, near, before, planes + index)
+        make_coefs(coef, kinds, levels, cols)
+        at, near_at = (planes + coefs) * ROWS, (planes + coefs) * 8
+        weights[...] = spread((own[at:, :] + after[at:, :]) + (near[near_at:, :] + before[at:, :]))
+        run_steps(buf, resid, coef, steps, planes, levels)
+        squares = jnp.zeros((ROWS, LANES), jnp.float32)
+        for plane in range(planes):
+            value = SQRT_STATIC * buf[plane]
+            resid[plane] = value
+            buf[plane] = value
+            squares += value[:ROWS] * value[:ROWS]
+        sums[...] = jnp.zeros(sums.shape, jnp.float32)
+        sums[2:3, :] = own_sum(squares, cols)
+        run_steps(buf, kinds, coef, steps, planes, levels)
+        for plane in range(planes):
+            out_g[plane * ROWS : (plane + 1) * ROWS, :] = buf[plane, :ROWS, :]
+
+    outs = [
+        f32(5, levels, WIN, LANES),
+        f32(planes, WIN, LANES),
+        f32(ROWS, LANES),
+        f32(SUMS, LANES),
+        f32(planes * ROWS, LANES),
+    ]
+    scratch = [pltpu.VMEM((planes, WIN, LANES), jnp.float32)] * 2
+    return kernel, outs, scratch
+
+
+def second_diffuse(planes, levels, cols):
+    def kernel(own, after, near, before, steps, coef, resid, weights, image, new, new_w, sums, facts, out_g, buf, spare):
+        for plane in range(planes):
+            window(buf, plane, own, after, near, before, plane)
+        at, near_at = planes * ROWS, planes * 8
+        total = spread((own[at:, :] + after[at:, :]) + (near[near_at:, :] + before[at:, :]))
+        energy = total[ROWS : ROWS + 1]
+        rr = total[ROWS + 2 : ROWS + 3] + over_rows(weights[...] * weights[...])
+        curvature = rr + energy
+        step = rr / curvature
+        new_weights = weights[...] - step * (weights[...] + total[:ROWS])
+        new_w[...] = new_weights
+        facts[...] = jnp.zeros(facts.shape, jnp.float32)
+        facts[0:1, :] = rr
+        facts[1:2, :] = energy
+        facts[2:3, :] = step
+        run_steps(buf, spare, coef, steps, planes, levels)
+        squares = jnp.zeros((ROWS, LANES), jnp.float32)
+        cross = jnp.zeros((ROWS, LANES), jnp.float32)
+        for plane in range(planes):
+            direction = resid[plane]
+            image_now = direction + SQRT_STATIC * buf[plane]
+            value = direction - step * image_now
+            image[plane * ROWS : (plane + 1) * ROWS, :] = image_now[:ROWS]
+            new[plane * ROWS : (plane + 1) * ROWS, :] = value[:ROWS]
+            buf[plane] = value
+            squares += value[:ROWS] * value[:ROWS]
+            cross += value[:ROWS] * direction[:ROWS]
+        sums[...] = jnp.zeros(sums.shape, jnp.float32)
+        sums[2:3, :] = own_sum(squares, cols)
+        sums[3:4, :] = own_sum(cross, cols)
+        run_steps(buf, spare, coef, steps, planes, levels)
+        for plane in range(planes):
+            out_g[plane * ROWS : (plane + 1) * ROWS, :] = buf[plane, :ROWS, :]
+
+    block = f32(planes * ROWS, LANES)
+    outs = [block, block, f32(ROWS, LANES), f32(SUMS, LANES), f32(SUMS, LANES), block]
+    scratch = [pltpu.VMEM((planes, WIN, LANES), jnp.float32)] * 2
+    return kernel, outs, scratch
+
+
+def last_diffuse(planes, levels, cols):
+    def kernel(
+        own, after, near, before, steps, coef, resid, weights, image, new, new_w, facts, control, control_w, final, buf, spare
+    ):
+        for plane in range(planes):
+            window(buf, plane, own, after, near, before, plane)
+        at, near_at = planes * ROWS, planes * 8
+        total = spread((own[at:, :] + after[at:, :]) + (near[near_at:, :] + before[at:, :]))
+        rr, energy, step = facts[0:1, :], facts[1:2, :], facts[2:3, :]
+        new_energy, cross_energy = total[0:1], total[1:2]
+        new_rr = total[2:3] + over_rows(new_w[...] * new_w[...])
+        cross_rr = total[3:4] + over_rows(new_w[...] * weights[...])
+        ratio = new_rr / rr
+        squares = new_rr + ratio * (2.0 * cross_rr + ratio * rr)
+        curvature = squares + (new_energy + ratio * (2.0 * cross_energy + ratio * energy))
+        new_step = new_rr / curvature
+        control_w[...] = step * weights[...] + new_step * (new_w[...] + ratio * weights[...])
+        run_steps(buf, spare, coef, steps, planes, levels)
+        for plane in range(planes):
+            value = tile(new, plane)
+            direction = resid[plane, :ROWS, :]
+            new_direction = value + ratio * direction
+            new_image = (value + SQRT_STATIC * buf[plane, :ROWS, :]) + ratio * tile(image, plane)
+            control[plane] = (step * direction + new_step * new_direction)[:, :cols]
+            final[plane] = (value - new_step * new_image)[:, :cols]
+
+    outs = [f32(planes, ROWS, cols), f32(ROWS, LANES), f32(planes, ROWS, cols)]
+    scratch = [pltpu.VMEM((planes, WIN, LANES), jnp.float32)] * 2
+    return kernel, outs, scratch
+
+
+def moved_to(values, dx, dy, dz):
+    sizes = [lax.axis_size(axis) for axis in AXES]
+    pairs = []
+    for x in range(sizes[0]):
+        for y in range(sizes[1]):
+            for z in range(sizes[2]):
+                to = ((x + dx) % sizes[0] * sizes[1] + (y + dy) % sizes[1]) * sizes[2] + (z + dz) % sizes[2]
+                pairs.append(((x * sizes[1] + y) * sizes[2] + z, to))
+    return lax.ppermute(values, AXES, pairs)
+
+
+def across(kernel_of, out_z, out_e, vert, extra):
+    other = moved_to(out_z, 0, 0, 1)
+    edge = moved_to(out_e, 0, 1, 0)
+    edge_other = moved_to(out_e, 0, 1, 1)
+    kernel, outs = kernel_of
+    specs = [VMEM] * 4 + [SMEM] + [VMEM] * len(extra)
+    own, near = call(kernel, outs, specs, (out_z, other, edge, edge_other, vert, *extra))
+    return own, moved_to(own, -1, 0, 0), moved_to(near, 2, 0, 0), moved_to(own, 1, 0, 0)
+
+
+def shards_small(
+    innovation, obs_precision, error_scale, kappa_x, kappa_y, sea_mask, members, vertical, diffusion_steps
+):
+    fields, levels, rows, cols = innovation.shape
+    count = members.shape[0]
+    planes = fields * levels
+    block = (planes, rows, cols)
+    innov, prec, scale = (a.reshape(block) for a in (innovation, obs_precision, error_scale))
+    ens = members.reshape((count,) + block)
+    vert = vertical.reshape(-1)
+
+    kernel, outs = observe(True, planes, levels, cols, count, True)
+    out_z, out_e, coef_own = call(kernel, outs, [VMEM] * 7, (innov, prec, scale, sea_mask, kappa_x, kappa_y, ens))
+    parts = across(mix_back(True, planes, levels, cols, ROWS), out_z, out_e, vert, (coef_own,))
+    kernel, outs, scratch = first_diffuse(planes, levels, cols)
+    specs = [VMEM] * 4 + [SMEM]
+    coef, resid, weights, sums, out_g = call(kernel, outs, specs, (*parts, diffusion_steps), scratch)
+
+    kernel, outs = observe(False, planes, levels, cols, count, True)
+    specs = [VMEM] * 4 + [SMEM] + [VMEM] * 4
+    args = (out_g, moved_to(out_g, 0, 0, 1), weights, sums, vert, prec, scale, sea_mask, ens)
+    out_z, out_e, seen = call(kernel, outs, specs, args)
+    parts = across(mix_back(False, planes, levels, cols, ROWS + SUMS), out_z, out_e, vert, ())
+    kernel, outs, scratch = second_diffuse(planes, levels, cols)
+    specs = [VMEM] * 4 + [SMEM] + [VMEM] * 3
+    image, new, new_w, sums, facts, out_g = call(
+        kernel, outs, specs, (*parts, diffusion_steps, coef, resid, weights), scratch
+    )
+
+    kernel, outs = observe(False, planes, levels, cols, count, False)
+    specs = [VMEM] * 4 + [SMEM] + [VMEM] * 5
+    args = (out_g, moved_to(out_g, 0, 0, 1), new_w, sums, vert, prec, scale, sea_mask, ens, seen)
+    out_z, out_e = call(kernel, outs, specs, args)
+    parts = across(mix_back(False, planes, levels, cols, SUMS), out_z, out_e, vert, ())
+    kernel, outs, scratch = last_diffuse(planes, levels, cols)
+    specs = [VMEM] * 4 + [SMEM] + [VMEM] * 7
+    control, control_w, final = call(
+        kernel, outs, specs, (*parts, diffusion_steps, coef, resid, weights, image, new, new_w, facts), scratch
+    )
+    return control.reshape(innovation.shape), control_w[:, 0], final.reshape(innovation.shape)
+
+
+def shards(innovation, obs_precision, error_scale, kappa_x, kappa_y, sea_mask, members, vertical, diffusion_steps):
+    arrays = (innovation, obs_precision, error_scale, kappa_x, kappa_y, sea_mask, members, vertical, diffusion_steps)
+    sizes = tuple(lax.axis_size(axis) for axis in AXES)
+    rows, cols = innovation.shape[2:]
+    fits = rows == ROWS and members.shape[0] == ROWS and DEPTH <= cols <= LANES - DEPTH and ITERS == 2
+    if sizes == (4, 2, 2) and fits:
+        return shards_small(*arrays)
+    return shards_any(*arrays)
+
 
 def solution(mesh):
     placed = (

time: 497 us -> 74.8 us (0.15); the launches traced: 489 us -> 74.4 us
  starting transfers between devices: 160 us -> 20.1 us
  blocking collectives: 129 us -> 0 us
  waiting for transfers between devices: 144 us -> 30.1 us
  other arithmetic: 26.6 us -> 0 us
  Pallas kernels: 0 us -> 16.5 us
  matrix products: 11.3 us -> 0 us
  between operations: 9.27 us -> 0.77 us
    ppermute x104 -> x20, starting transfers between devices: 160 us -> 20.1 us  [moved_to(): return lax.ppermute(values, AXES, pairs)]
    psum x4 -> x0, blocking collectives: 120 us -> none  [the longest x3 89.7 us: both_sums(): return lax.psum((terms, partial_value), ('gx', 'gy', 'gz'))]
    ppermute x104 -> x20, waiting for transfers between devices: 144 us -> 30.1 us  [moved_to(): return lax.ppermute(values, AXES, pairs)]
    pallas_call x0 -> x9, Pallas kernels: none -> 16.5 us  [call(): pl.pallas_call(kernel, out_shape=outs, in_specs=specs, out_specs=[VMEM] *...]
    dot_general x10 -> x0, matrix products: 11.3 us -> none  [the longest x3 6.32 us: ensemble_terms(): jnp.einsum('mflxy,flxy->m', members, masked, precision=lax.Precision.HIGH...]
    all_gather x5 -> x0, blocking collectives: 9.62 us -> none  [level_mix(): gathered = lax.all_gather(source, 'gz', axis=1, tiled=True)]
    add x50 -> x0, other arithmetic: 8.23 us -> none  [the longest x47 7.69 us: diffuse(): current = current[:, :, 1:-1, 1:-1] + active * (div_east + div_north)]
    mul x109 -> x0, other arithmetic: 7.43 us -> none  [the longest x50 4.87 us: diffuse(): flux_north = north_coef * (current[:, :, :, 1:] - current[:, :, :, :-1])]
  transfers between devices with their start and end apart: 104 -> 20, of which waited for: 75 -> 11; matrix products, arithmetic and copies ran while one was open for 2% -> 0% of each run, Pallas kernels for 0% -> 0%
where the time goes in v1:
time: 74.8 us; the launch traced here: 74.4 us
  waiting for transfers between devices  30.1 us (40%)
  starting transfers between devices  20.1 us (27%)
  Pallas kernels  16.5 us (22%)
  local copies, waits for them, and re-layouts  6.98 us (9%)
  between operations  0.77 us (1%)
    ppermute x20, waiting for transfers between devices, moved_to(): return lax.ppermute(values, AXES, pairs)  30.1 us
    ppermute x20, starting transfers between devices, moved_to(): return lax.ppermute(values, AXES, pairs)  20.1 us
    pallas_call x9, Pallas kernels, call(): pl.pallas_call(kernel, out_shape=outs, in_specs=specs, out_specs=[VMEM] *...  16.5 us
    unnamed x27, local copies, waits for them, and re-layouts  6.26 us
  transfers between devices with their start and end apart: 20, of which 11 were waited for; matrix products, arithmetic and copies ran while one was open for 0% of the time, Pallas kernels for 0%

profile of v1, /device:TPU:0, one launch (start us, length us, event | category | flops | bytes accessed | tf_op | source)
XLA Modules:
  0.0 74.4 jit_solution(18395569957596771738)
XLA Ops:
  0.6 0.0 copy-start.11
  0.6 0.0 copy-start
  0.7 1.3 %copy-done = f32[16,5,2,16,108]{4,3,2,1,0:T(8,128)S(1)} copy-done((f32[16,5,2,16,108]{4,3,2,1,0:T(8,128)S(1)}, f32[16,5,2,16,108]{4,3,2,1,0:T(8,128)}, u32[]{:S(2)}) %copy-start) | copy-done | bytes 1105944
  2.0 0.9 %copy-done.2 = f32[5,2,16,108]{3,2,1,0:T(8,128)S(1)} copy-done((f32[5,2,16,108]{3,2,1,0:T(8,128)S(1)}, f32[5,2,16,108]{3,2,1,0:T(8,128)}, u32[]{:S(2)}) %copy-start.2) | copy-done | bytes 69144
  2.9 0.9 %copy-done.4 = f32[5,2,16,108]{3,2,1,0:T(8,128)S(1)} copy-done((f32[5,2,16,108]{3,2,1,0:T(8,128)S(1)}, f32[5,2,16,108]{3,2,1,0:T(8,128)}, u32[]{:S(2)}) %copy-start.4) | copy-done | bytes 69144
  3.7 0.7 copy-done.6
  4.5 0.9 %copy-done.8 = f32[5,2,16,108]{3,2,1,0:T(8,128)S(1)} copy-done((f32[5,2,16,108]{3,2,1,0:T(8,128)S(1)}, f32[5,2,16,108]{3,2,1,0:T(8,128)}, u32[]{:S(2)}) %copy-start.8) | copy-done | bytes 69144
  5.3 0.7 copy-done.9
  6.1 0.7 copy-done.10
  6.8 0.0 copy-start.7
  6.8 0.2 shard_map.112
  7.0 0.5 collective-permute-start
  7.5 2.6 %collective-permute-start.2 = (f32[64,128]{1,0:T(8,128)S(1)}, f32[64,128]{1,0:T(8,128)S(1)}, u32[]{:S(2)}, u32[]{:S(2)}) collective-permute-start(f32[64,128]{1,0:T(8,128)S(1)} %get-tuple-element.32), channel_id=1, source_target_pairs={{0,3},{1,2},{2,1},{3,0},{4,7},{5,6},{6,5},{7,4},{8,11},{9,10},{10,... | collective-permute-start | bytes 98312 | tf_op jit(solution)/shard_map/ppermute | solution.py:485
  10.1 0.0 collective-permute-start.1
  10.2 0.0 copy-done.12
  10.2 0.1 copy.13
  10.3 0.1 reshape.31.refs_4_
  10.4 1.4 %collective-permute-done.2.refs_3_ = f32[64,128]{1,0:T(8,128)S(1)} collective-permute-done((f32[64,128]{1,0:T(8,128)S(1)}, f32[64,128]{1,0:T(8,128)S(1)}, u32[]{:S(2)}, u32[]{:S(2)}) %collective-permute-start.2) | collective-permute-done | bytes 32800 | tf_op jit(solution)/shard_map/ppermute | solution.py:485
  11.8 2.2 %collective-permute-done.1.refs_2_ = f32[64,128]{1,0:T(8,128)S(1)} collective-permute-done((f32[64,128]{1,0:T(8,128)S(1)}, f32[64,128]{1,0:T(8,128)S(1)}, u32[]{:S(2)}, u32[]{:S(2)}) %collective-permute-start.1) | collective-permute-done | bytes 32800 | tf_op jit(solution)/shard_map/ppermute | solution.py:485
  14.0 0.0 collective-permute-done.refs_1_
  14.0 0.7 shard_map.113
  14.7 1.6 %collective-permute-start.5 = (f32[272,128]{1,0:T(8,128)S(1)}, f32[272,128]{1,0:T(8,128)S(1)}, u32[]{:S(2)}, u32[]{:S(2)}) collective-permute-start(f32[272,128]{1,0:T(8,128)S(1)} %get-tuple-element.34.own), channel_id=1, source_target_pairs={{0,4},{1,5},{2,6},{3,7},{4,8},{5,9},{6,10},{7,11},{8,12},{9,13},{1... | collective-permute-start | bytes 417800 | tf_op jit(solution)/shard_map/ppermute | solution.py:485
  16.3 2.2 %collective-permute-start.3 = (f32[272,128]{1,0:T(8,128)S(1)}, f32[272,128]{1,0:T(8,128)S(1)}, u32[]{:S(2)}, u32[]{:S(2)}) collective-permute-start(f32[272,128]{1,0:T(8,128)S(1)} %get-tuple-element.34.own), channel_id=1, source_target_pairs={{0,12},{1,13},{2,14},{3,15},{4,0},{5,1},{6,2},{7,3},{8,4},{9,5},{1... | collective-permute-start | bytes 417800 | tf_op jit(solution)/shard_map/ppermute | solution.py:485
  18.6 0.8 %collective-permute-start.4 = (f32[144,128]{1,0:T(8,128)S(1)}, f32[144,128]{1,0:T(8,128)S(1)}, u32[]{:S(2)}, u32[]{:S(2)}) collective-permute-start(f32[144,128]{1,0:T(8,128)S(1)} %get-tuple-element.35), channel_id=1, source_target_pairs={{0,8},{1,9},{2,10},{3,11},{4,12},{5,13},{6,14},{7,15},{8,0},{9,1},... | collective-permute-start | bytes 221192 | tf_op jit(solution)/shard_map/ppermute | solution.py:485
  19.4 7.9 %collective-permute-done.4.near = f32[144,128]{1,0:T(8,128)S(1)} collective-permute-done((f32[144,128]{1,0:T(8,128)S(1)}, f32[144,128]{1,0:T(8,128)S(1)}, u32[]{:S(2)}, u32[]{:S(2)}) %collective-permute-start.4) | collective-permute-done | bytes 73760 | tf_op jit(solution)/shard_map/ppermute | solution.py:485
  27.3 0.0 collective-permute-done.5.before
  27.3 0.0 collective-permute-done.3.after
  27.3 0.0 copy-done.11
  27.3 4.6 %shard_map.114 = (f32[5,2,56,128]{3,2,1,0:T(8,128)S(1)}, f32[10,56,128]{2,1,0:T(8,128)S(1)}, f32[16,128]{1,0:T(8,128)S(1)}, f32[8,128]{1,0:T(8,128)S(1)}, f32[160,128]{1,0:T(8,128)S(1)}) custom-call(f32[272,128]{1,0:T(8,128)S(1)} %get-tuple-element.34.own, f32[272,128]{1,0:T(8,128)S(1)} %collective-permute-done.3.after, ...), custom_call_target="tpu_custom_call" | custom-call | tf_op jit(solution)/shard_map/pallas_call | solution.py:162
  31.9 0.1 collective-permute-start.6
  31.9 1.3 %collective-permute-done.6.refs_1_ = f32[160,128]{1,0:T(8,128)S(1)} collective-permute-done((f32[160,128]{1,0:T(8,128)S(1)}, f32[160,128]{1,0:T(8,128)S(1)}, u32[]{:S(2)}, u32[]{:S(2)}) %collective-permute-start.6) | collective-permute-done | bytes 81952 | tf_op jit(solution)/shard_map/ppermute | solution.py:485
  33.2 0.8 %shard_map.115 = (f32[184,128]{1,0:T(8,128)S(1)}, f32[56,128]{1,0:T(8,128)S(1)}, f32[10,16,108]{2,1,0:T(8,128)S(1)}) custom-call(f32[160,128]{1,0:T(8,128)S(1)} %get-tuple-element.36.refs_0_, f32[160,128]{1,0:T(8,128)S(1)} %collective-permute-done.6.refs_1_, f32[16,128]{1,0:T(8,128)S(1)} %get-tuple-element.37.refs_2_.weights, ...), custom_call_target="tpu_custom_call" | custom-call | tf_op jit(solution)/shard_map/pallas_call | solution.py:162
  34.1 0.2 collective-permute-start.7
  34.3 1.0 %collective-permute-start.9 = (f32[56,128]{1,0:T(8,128)S(1)}, f32[56,128]{1,0:T(8,128)S(1)}, u32[]{:S(2)}, u32[]{:S(2)}) collective-permute-start(f32[56,128]{1,0:T(8,128)S(1)} %get-tuple-element.40), channel_id=1, source_target_pairs={{0,3},{1,2},{2,1},{3,0},{4,7},{5,6},{6,5},{7,4},{8,11},{9,10},{10,... | collective-permute-start | bytes 86024 | tf_op jit(solution)/shard_map/ppermute | solution.py:485
  35.2 1.0 %collective-permute-start.8 = (f32[56,128]{1,0:T(8,128)S(1)}, f32[56,128]{1,0:T(8,128)S(1)}, u32[]{:S(2)}, u32[]{:S(2)}) collective-permute-start(f32[56,128]{1,0:T(8,128)S(1)} %get-tuple-element.40), channel_id=1, source_target_pairs={{0,2},{1,3},{2,0},{3,1},{4,6},{5,7},{6,4},{7,5},{8,10},{9,11},{10,... | collective-permute-start | bytes 86024 | tf_op jit(solution)/shard_map/ppermute | solution.py:485
  36.3 1.3 %collective-permute-done.9.refs_3_ = f32[56,128]{1,0:T(8,128)S(1)} collective-permute-done((f32[56,128]{1,0:T(8,128)S(1)}, f32[56,128]{1,0:T(8,128)S(1)}, u32[]{:S(2)}, u32[]{:S(2)}) %collective-permute-start.9) | collective-permute-done | bytes 28704 | tf_op jit(solution)/shard_map/ppermute | solution.py:485
  37.6 1.5 %collective-permute-done.8.refs_2_ = f32[56,128]{1,0:T(8,128)S(1)} collective-permute-done((f32[56,128]{1,0:T(8,128)S(1)}, f32[56,128]{1,0:T(8,128)S(1)}, u32[]{:S(2)}, u32[]{:S(2)}) %collective-permute-start.8) | collective-permute-done | bytes 28704 | tf_op jit(solution)/shard_map/ppermute | solution.py:485
  39.1 0.0 collective-permute-done.7.refs_1_
  39.1 0.7 shard_map.116
  39.8 0.1 collective-permute-start.12
  39.8 3.8 %collective-permute-start.10 = (f32[184,128]{1,0:T(8,128)S(1)}, f32[184,128]{1,0:T(8,128)S(1)}, u32[]{:S(2)}, u32[]{:S(2)}) collective-permute-start(f32[184,128]{1,0:T(8,128)S(1)} %get-tuple-element.41.own), channel_id=1, source_target_pairs={{0,12},{1,13},{2,14},{3,15},{4,0},{5,1},{6,2},{7,3},{8,4},{9,5},{1... | collective-permute-start | bytes 282632 | tf_op jit(solution)/shard_map/ppermute | solution.py:485
  43.7 0.0 collective-permute-start.11
  43.7 5.5 %collective-permute-done.11.near = f32[104,128]{1,0:T(8,128)S(1)} collective-permute-done((f32[104,128]{1,0:T(8,128)S(1)}, f32[104,128]{1,0:T(8,128)S(1)}, u32[]{:S(2)}, u32[]{:S(2)}) %collective-permute-start.11) | collective-permute-done | bytes 53280 | tf_op jit(solution)/shard_map/ppermute | solution.py:485
  49.1 0.0 collective-permute-done.12.before
  49.1 0.0 collective-permute-done.10.after
  49.1 4.5 %shard_map.117 = (f32[160,128]{1,0:T(8,128)S(1)}, f32[160,128]{1,0:T(8,128)S(1)}, f32[16,128]{1,0:T(8,128)S(1)}, f32[8,128]{1,0:T(8,128)S(1)}, f32[8,128]{1,0:T(8,128)S(1)}, /*index=5*/f32[160,128]{1,0:T(8,128)S(1)}) custom-call(f32[184,128]{1,0:T(8,128)S(1)} %get-tuple-element.41.own, f32[184,128]{1,0:T(8,128)S(1)} %collective-permute-done.10.after, ...), custom_call_target="tpu_custom_call" | custom-call | tf_op jit(solution)/shard_map/pallas_call | solution.py:162
  53.7 0.1 collective-permute-start.13
  53.7 1.3 %collective-permute-done.13.refs_1_ = f32[160,128]{1,0:T(8,128)S(1)} collective-permute-done((f32[160,128]{1,0:T(8,128)S(1)}, f32[160,128]{1,0:T(8,128)S(1)}, u32[]{:S(2)}, u32[]{:S(2)}) %collective-permute-start.13) | collective-permute-done | bytes 81952 | tf_op jit(solution)/shard_map/ppermute | solution.py:485
  55.0 0.8 %shard_map.118 = (f32[168,128]{1,0:T(8,128)S(1)}, f32[40,128]{1,0:T(8,128)S(1)}) custom-call(f32[160,128]{1,0:T(8,128)S(1)} %get-tuple-element.45.refs_0_, f32[160,128]{1,0:T(8,128)S(1)} %collective-permute-done.13.refs_1_, f32[16,128]{1,0:T(8,128)S(1)} %get-tuple-element.46.refs_2_.new_w, f32[8,128]{1,0:T(8,128)S(1)} %get-tuple-element.47.refs_3_, ...), custom_call_target="tpu_custom_call" | custom-call | tf_op jit(solution)/shard_map/pallas_call | solution.py:162
  55.8 0.2 collective-permute-start.14
  56.0 0.9 %collective-permute-start.16 = (f32[40,128]{1,0:T(8,128)S(1)}, f32[40,128]{1,0:T(8,128)S(1)}, u32[]{:S(2)}, u32[]{:S(2)}) collective-permute-start(f32[40,128]{1,0:T(8,128)S(1)} %get-tuple-element.50), channel_id=1, source_target_pairs={{0,3},{1,2},{2,1},{3,0},{4,7},{5,6},{6,5},{7,4},{8,11},{9,10},{10,... | collective-permute-start | bytes 61448 | tf_op jit(solution)/shard_map/ppermute | solution.py:485
  56.9 1.0 %collective-permute-start.15 = (f32[40,128]{1,0:T(8,128)S(1)}, f32[40,128]{1,0:T(8,128)S(1)}, u32[]{:S(2)}, u32[]{:S(2)}) collective-permute-start(f32[40,128]{1,0:T(8,128)S(1)} %get-tuple-element.50), channel_id=1, source_target_pairs={{0,2},{1,3},{2,0},{3,1},{4,6},{5,7},{6,4},{7,5},{8,10},{9,11},{10,... | collective-permute-start | bytes 61448 | tf_op jit(solution)/shard_map/ppermute | solution.py:485
  58.0 1.2 %collective-permute-done.16.refs_3_ = f32[40,128]{1,0:T(8,128)S(1)} collective-permute-done((f32[40,128]{1,0:T(8,128)S(1)}, f32[40,128]{1,0:T(8,128)S(1)}, u32[]{:S(2)}, u32[]{:S(2)}) %collective-permute-start.16) | collective-permute-done | bytes 20512 | tf_op jit(solution)/shard_map/ppermute | solution.py:485
  59.2 1.5 %collective-permute-done.15.refs_2_ = f32[40,128]{1,0:T(8,128)S(1)} collective-permute-done((f32[40,128]{1,0:T(8,128)S(1)}, f32[40,128]{1,0:T(8,128)S(1)}, u32[]{:S(2)}, u32[]{:S(2)}) %collective-permute-start.15) | collective-permute-done | bytes 20512 | tf_op jit(solution)/shard_map/ppermute | solution.py:485
  60.7 0.0 collective-permute-done.14.refs_1_
  60.7 0.7 shard_map.119
  61.4 0.1 collective-permute-start.19
  61.5 3.8 %collective-permute-start.17 = (f32[168,128]{1,0:T(8,128)S(1)}, f32[168,128]{1,0:T(8,128)S(1)}, u32[]{:S(2)}, u32[]{:S(2)}) collective-permute-start(f32[168,128]{1,0:T(8,128)S(1)} %get-tuple-element.51.own), channel_id=1, source_target_pairs={{0,12},{1,13},{2,14},{3,15},{4,0},{5,1},{6,2},{7,3},{8,4},{9,5},{1... | collective-permute-start | bytes 258056 | tf_op jit(solution)/shard_map/ppermute | solution.py:485
  65.3 0.0 collective-permute-start.18
  65.3 4.9 %collective-permute-done.18.near = f32[88,128]{1,0:T(8,128)S(1)} collective-permute-done((f32[88,128]{1,0:T(8,128)S(1)}, f32[88,128]{1,0:T(8,128)S(1)}, u32[]{:S(2)}, u32[]{:S(2)}) %collective-permute-start.18) | collective-permute-done | bytes 45088 | tf_op jit(solution)/shard_map/ppermute | solution.py:485
  70.2 0.0 collective-permute-done.19.before
  70.2 0.0 collective-permute-done.17.after
  70.2 3.6 %shard_map.120 = (f32[10,16,108]{2,1,0:T(8,128)}, f32[16,128]{1,0:T(8,128)S(1)}, f32[10,16,108]{2,1,0:T(8,128)}) custom-call(f32[168,128]{1,0:T(8,128)S(1)} %get-tuple-element.51.own, f32[168,128]{1,0:T(8,128)S(1)} %collective-permute-done.17.after, f32[88,128]{1,0:T(8,128)S(1)} %collective-permute-done.18.near, ...), custom_call_target="tpu_custom_call" | custom-call | tf_op jit(solution)/shard_map/pallas_call | solution.py:162
  73.8 0.6 slice_reduce_fusion
  (14 shorter events, 0.0 us)
Async XLA Ops:
  0.6 26.6 %copy-start.11 = (s32[5]{0:T(128)S(1)}, s32[5]{0:T(128)}, u32[]{:S(2)}) copy-start(s32[5]{0:T(128)} %steps.5) | copy-start | bytes 64
  0.6 1.3 %copy-start = (f32[16,5,2,16,108]{4,3,2,1,0:T(8,128)S(1)}, f32[16,5,2,16,108]{4,3,2,1,0:T(8,128)}, u32[]{:S(2)}) copy-start(f32[16,5,2,16,108]{4,3,2,1,0:T(8,128)} %param.15) | copy-start | bytes 3317764
  2.0 0.9 %copy-start.2 = (f32[5,2,16,108]{3,2,1,0:T(8,128)S(1)}, f32[5,2,16,108]{3,2,1,0:T(8,128)}, u32[]{:S(2)}) copy-start(f32[5,2,16,108]{3,2,1,0:T(8,128)} %param.10) | copy-start | bytes 207364
  2.9 0.9 %copy-start.4 = (f32[5,2,16,108]{3,2,1,0:T(8,128)S(1)}, f32[5,2,16,108]{3,2,1,0:T(8,128)}, u32[]{:S(2)}) copy-start(f32[5,2,16,108]{3,2,1,0:T(8,128)} %param.11) | copy-start | bytes 207364
  3.7 0.7 copy-start.6
  4.5 0.9 %copy-start.8 = (f32[5,2,16,108]{3,2,1,0:T(8,128)S(1)}, f32[5,2,16,108]{3,2,1,0:T(8,128)}, u32[]{:S(2)}) copy-start(f32[5,2,16,108]{3,2,1,0:T(8,128)} %param.9) | copy-start | bytes 207364
  5.3 0.7 copy-start.9
  6.1 0.7 copy-start.10
  6.8 3.4 %copy-start.12 = (f32[5,4,4]{0,2,1:T(4,128)S(1)}, f32[5,4,4]{0,2,1:T(4,128)}, u32[]{:S(2)}) copy-start(f32[5,4,4]{0,2,1:T(4,128)} %param.16) | copy-start | bytes 964
  6.8 26.4 %copy-start.1 = (f32[16,5,2,16,108]{4,3,2,1,0:T(8,128)S(1)}, f32[16,5,2,16,108]{4,3,2,1,0:T(8,128)}, u32[]{:S(2)}) copy-start(f32[16,5,2,16,108]{4,3,2,1,0:T(8,128)} %param.15) | copy-start | bytes 3317764
  6.8 26.4 %copy-start.3 = (f32[5,2,16,108]{3,2,1,0:T(8,128)S(1)}, f32[5,2,16,108]{3,2,1,0:T(8,128)}, u32[]{:S(2)}) copy-start(f32[5,2,16,108]{3,2,1,0:T(8,128)} %param.10) | copy-start | bytes 207364
  6.8 26.4 %copy-start.5 = (f32[5,2,16,108]{3,2,1,0:T(8,128)S(1)}, f32[5,2,16,108]{3,2,1,0:T(8,128)}, u32[]{:S(2)}) copy-start(f32[5,2,16,108]{3,2,1,0:T(8,128)} %param.11) | copy-start | bytes 207364
  6.8 26.4 %copy-start.7 = (s32[2,16,108]{2,1,0:T(8,128)S(1)}, s32[2,16,108]{2,1,0:T(8,128)}, u32[]{:S(2)}) copy-start(s32[2,16,108]{2,1,0:T(8,128)} %refs_7_.3) | copy-start | bytes 41476
  7.0 7.1 %collective-permute-start = (f32[176,128]{1,0:T(8,128)S(1)}, f32[176,128]{1,0:T(8,128)S(1)}, u32[]{:S(2)}, u32[]{:S(2)}) collective-permute-start(f32[176,128]{1,0:T(8,128)S(1)} %get-tuple-element.31.refs_0_), channel_id=1, source_target_pairs={{0,1},{1,0},{2,3},{3,2},{4,5},{5,4},{6,7},{7,6},{8,9},{9,8},{10,11... | collective-permute-start | bytes 270344 | tf_op jit(solution)/shard_map/ppermute | solution.py:485
  7.5 4.3 %collective-permute-start.2 = (f32[64,128]{1,0:T(8,128)S(1)}, f32[64,128]{1,0:T(8,128)S(1)}, u32[]{:S(2)}, u32[]{:S(2)}) collective-permute-start(f32[64,128]{1,0:T(8,128)S(1)} %get-tuple-element.32), channel_id=1, source_target_pairs={{0,3},{1,2},{2,1},{3,0},{4,7},{5,6},{6,5},{7,4},{8,11},{9,10},{10,... | collective-permute-start | bytes 98312 | tf_op jit(solution)/shard_map/ppermute | solution.py:485
  10.1 3.9 %collective-permute-start.1 = (f32[64,128]{1,0:T(8,128)S(1)}, f32[64,128]{1,0:T(8,128)S(1)}, u32[]{:S(2)}, u32[]{:S(2)}) collective-permute-start(f32[64,128]{1,0:T(8,128)S(1)} %get-tuple-element.32), channel_id=1, source_target_pairs={{0,2},{1,3},{2,0},{3,1},{4,6},{5,7},{6,4},{7,5},{8,10},{9,11},{10,... | collective-permute-start | bytes 98312 | tf_op jit(solution)/shard_map/ppermute | solution.py:485
  14.7 12.6 %collective-permute-start.5 = (f32[272,128]{1,0:T(8,128)S(1)}, f32[272,128]{1,0:T(8,128)S(1)}, u32[]{:S(2)}, u32[]{:S(2)}) collective-permute-start(f32[272,128]{1,0:T(8,128)S(1)} %get-tuple-element.34.own), channel_id=1, source_target_pairs={{0,4},{1,5},{2,6},{3,7},{4,8},{5,9},{6,10},{7,11},{8,12},{9,13},{1... | collective-permute-start | bytes 417800 | tf_op jit(solution)/shard_map/ppermute | solution.py:485
  16.3 10.9 %collective-permute-start.3 = (f32[272,128]{1,0:T(8,128)S(1)}, f32[272,128]{1,0:T(8,128)S(1)}, u32[]{:S(2)}, u32[]{:S(2)}) collective-permute-start(f32[272,128]{1,0:T(8,128)S(1)} %get-tuple-element.34.own), channel_id=1, source_target_pairs={{0,12},{1,13},{2,14},{3,15},{4,0},{5,1},{6,2},{7,3},{8,4},{9,5},{1... | collective-permute-start | bytes 417800 | tf_op jit(solution)/shard_map/ppermute | solution.py:485
  18.6 8.7 %collective-permute-start.4 = (f32[144,128]{1,0:T(8,128)S(1)}, f32[144,128]{1,0:T(8,128)S(1)}, u32[]{:S(2)}, u32[]{:S(2)}) collective-permute-start(f32[144,128]{1,0:T(8,128)S(1)} %get-tuple-element.35), channel_id=1, source_target_pairs={{0,8},{1,9},{2,10},{3,11},{4,12},{5,13},{6,14},{7,15},{8,0},{9,1},... | collective-permute-start | bytes 221192 | tf_op jit(solution)/shard_map/ppermute | solution.py:485
  31.9 1.3 %collective-permute-start.6 = (f32[160,128]{1,0:T(8,128)S(1)}, f32[160,128]{1,0:T(8,128)S(1)}, u32[]{:S(2)}, u32[]{:S(2)}) collective-permute-start(f32[160,128]{1,0:T(8,128)S(1)} %get-tuple-element.36.refs_0_), channel_id=1, source_target_pairs={{0,1},{1,0},{2,3},{3,2},{4,5},{5,4},{6,7},{7,6},{8,9},{9,8},{10,11... | collective-permute-start | bytes 245768 | tf_op jit(solution)/shard_map/ppermute | solution.py:485
  34.1 5.0 %collective-permute-start.7 = (f32[184,128]{1,0:T(8,128)S(1)}, f32[184,128]{1,0:T(8,128)S(1)}, u32[]{:S(2)}, u32[]{:S(2)}) collective-permute-start(f32[184,128]{1,0:T(8,128)S(1)} %get-tuple-element.39.refs_0_), channel_id=1, source_target_pairs={{0,1},{1,0},{2,3},{3,2},{4,5},{5,4},{6,7},{7,6},{8,9},{9,8},{10,11... | collective-permute-start | bytes 282632 | tf_op jit(solution)/shard_map/ppermute | solution.py:485
  34.3 3.3 %collective-permute-start.9 = (f32[56,128]{1,0:T(8,128)S(1)}, f32[56,128]{1,0:T(8,128)S(1)}, u32[]{:S(2)}, u32[]{:S(2)}) collective-permute-start(f32[56,128]{1,0:T(8,128)S(1)} %get-tuple-element.40), channel_id=1, source_target_pairs={{0,3},{1,2},{2,1},{3,0},{4,7},{5,6},{6,5},{7,4},{8,11},{9,10},{10,... | collective-permute-start | bytes 86024 | tf_op jit(solution)/shard_map/ppermute | solution.py:485
  35.2 3.9 %collective-permute-start.8 = (f32[56,128]{1,0:T(8,128)S(1)}, f32[56,128]{1,0:T(8,128)S(1)}, u32[]{:S(2)}, u32[]{:S(2)}) collective-permute-start(f32[56,128]{1,0:T(8,128)S(1)} %get-tuple-element.40), channel_id=1, source_target_pairs={{0,2},{1,3},{2,0},{3,1},{4,6},{5,7},{6,4},{7,5},{8,10},{9,11},{10,... | collective-permute-start | bytes 86024 | tf_op jit(solution)/shard_map/ppermute | solution.py:485
  39.8 9.3 %collective-permute-start.12 = (f32[184,128]{1,0:T(8,128)S(1)}, f32[184,128]{1,0:T(8,128)S(1)}, u32[]{:S(2)}, u32[]{:S(2)}) collective-permute-start(f32[184,128]{1,0:T(8,128)S(1)} %get-tuple-element.41.own), channel_id=1, source_target_pairs={{0,4},{1,5},{2,6},{3,7},{4,8},{5,9},{6,10},{7,11},{8,12},{9,13},{1... | collective-permute-start | bytes 282632 | tf_op jit(solution)/shard_map/ppermute | solution.py:485
  39.8 9.3 %collective-permute-start.10 = (f32[184,128]{1,0:T(8,128)S(1)}, f32[184,128]{1,0:T(8,128)S(1)}, u32[]{:S(2)}, u32[]{:S(2)}) collective-permute-start(f32[184,128]{1,0:T(8,128)S(1)} %get-tuple-element.41.own), channel_id=1, source_target_pairs={{0,12},{1,13},{2,14},{3,15},{4,0},{5,1},{6,2},{7,3},{8,4},{9,5},{1... | collective-permute-start | bytes 282632 | tf_op jit(solution)/shard_map/ppermute | solution.py:485
  43.7 5.5 %collective-permute-start.11 = (f32[104,128]{1,0:T(8,128)S(1)}, f32[104,128]{1,0:T(8,128)S(1)}, u32[]{:S(2)}, u32[]{:S(2)}) collective-permute-start(f32[104,128]{1,0:T(8,128)S(1)} %get-tuple-element.42), channel_id=1, source_target_pairs={{0,8},{1,9},{2,10},{3,11},{4,12},{5,13},{6,14},{7,15},{8,0},{9,1},... | collective-permute-start | bytes 159752 | tf_op jit(solution)/shard_map/ppermute | solution.py:485
  53.7 1.3 %collective-permute-start.13 = (f32[160,128]{1,0:T(8,128)S(1)}, f32[160,128]{1,0:T(8,128)S(1)}, u32[]{:S(2)}, u32[]{:S(2)}) collective-permute-start(f32[160,128]{1,0:T(8,128)S(1)} %get-tuple-element.45.refs_0_), channel_id=1, source_target_pairs={{0,1},{1,0},{2,3},{3,2},{4,5},{5,4},{6,7},{7,6},{8,9},{9,8},{10,11... | collective-permute-start | bytes 245768 | tf_op jit(solution)/shard_map/ppermute | solution.py:485
  55.8 4.9 %collective-permute-start.14 = (f32[168,128]{1,0:T(8,128)S(1)}, f32[168,128]{1,0:T(8,128)S(1)}, u32[]{:S(2)}, u32[]{:S(2)}) collective-permute-start(f32[168,128]{1,0:T(8,128)S(1)} %get-tuple-element.49.refs_0_), channel_id=1, source_target_pairs={{0,1},{1,0},{2,3},{3,2},{4,5},{5,4},{6,7},{7,6},{8,9},{9,8},{10,11... | collective-permute-start | bytes 258056 | tf_op jit(solution)/shard_map/ppermute | solution.py:485
  56.0 3.2 %collective-permute-start.16 = (f32[40,128]{1,0:T(8,128)S(1)}, f32[40,128]{1,0:T(8,128)S(1)}, u32[]{:S(2)}, u32[]{:S(2)}) collective-permute-start(f32[40,128]{1,0:T(8,128)S(1)} %get-tuple-element.50), channel_id=1, source_target_pairs={{0,3},{1,2},{2,1},{3,0},{4,7},{5,6},{6,5},{7,4},{8,11},{9,10},{10,... | collective-permute-start | bytes 61448 | tf_op jit(solution)/shard_map/ppermute | solution.py:485
  56.9 3.8 %collective-permute-start.15 = (f32[40,128]{1,0:T(8,128)S(1)}, f32[40,128]{1,0:T(8,128)S(1)}, u32[]{:S(2)}, u32[]{:S(2)}) collective-permute-start(f32[40,128]{1,0:T(8,128)S(1)} %get-tuple-element.50), channel_id=1, source_target_pairs={{0,2},{1,3},{2,0},{3,1},{4,6},{5,7},{6,4},{7,5},{8,10},{9,11},{10,... | collective-permute-start | bytes 61448 | tf_op jit(solution)/shard_map/ppermute | solution.py:485
  61.4 8.8 %collective-permute-start.19 = (f32[168,128]{1,0:T(8,128)S(1)}, f32[168,128]{1,0:T(8,128)S(1)}, u32[]{:S(2)}, u32[]{:S(2)}) collective-permute-start(f32[168,128]{1,0:T(8,128)S(1)} %get-tuple-element.51.own), channel_id=1, source_target_pairs={{0,4},{1,5},{2,6},{3,7},{4,8},{5,9},{6,10},{7,11},{8,12},{9,13},{1... | collective-permute-start | bytes 258056 | tf_op jit(solution)/shard_map/ppermute | solution.py:485
  61.5 8.7 %collective-permute-start.17 = (f32[168,128]{1,0:T(8,128)S(1)}, f32[168,128]{1,0:T(8,128)S(1)}, u32[]{:S(2)}, u32[]{:S(2)}) collective-permute-start(f32[168,128]{1,0:T(8,128)S(1)} %get-tuple-element.51.own), channel_id=1, source_target_pairs={{0,12},{1,13},{2,14},{3,15},{4,0},{5,1},{6,2},{7,3},{8,4},{9,5},{1... | collective-permute-start | bytes 258056 | tf_op jit(solution)/shard_map/ppermute | solution.py:485
  65.3 4.9 %collective-permute-start.18 = (f32[88,128]{1,0:T(8,128)S(1)}, f32[88,128]{1,0:T(8,128)S(1)}, u32[]{:S(2)}, u32[]{:S(2)}) collective-permute-start(f32[88,128]{1,0:T(8,128)S(1)} %get-tuple-element.52), channel_id=1, source_target_pairs={{0,8},{1,9},{2,10},{3,11},{4,12},{5,13},{6,14},{7,15},{8,0},{9,1},... | collective-permute-start | bytes 135176 | tf_op jit(solution)/shard_map/ppermute | solution.py:485

commit v2 on v1

--- a/solution.py
+++ b/solution.py
@@ -150,7 +150,7 @@
 SUMS = 8
 AXES = ("gx", "gy", "gz")
 VMEM = pl.BlockSpec(memory_space=pltpu.VMEM)
-SMEM = pl.BlockSpec(memory_space=pltpu.SMEM)
+HBM = pl.BlockSpec(memory_space=pltpu.HBM)
 SQRT_STATIC = math.sqrt(static_share)
 
 
@@ -158,14 +158,14 @@
     return jax.ShapeDtypeStruct(shape, jnp.float32)
 
 
-def call(kernel, outs, specs, args, scratch=()):
+def call(kernel, outs, specs, args, scratch=(), grant=32):
     return pl.pallas_call(
         kernel,
         out_shape=outs,
         in_specs=specs,
         out_specs=[VMEM] * len(outs),
         scratch_shapes=list(scratch),
-        compiler_params=pltpu.CompilerParams(vmem_limit_bytes=32 * 1024 * 1024),
+        compiler_params=pltpu.CompilerParams(vmem_limit_bytes=grant * 1024 * 1024),
     )(*args)
 
 
@@ -198,19 +198,68 @@
     return jnp.sum(values, axis=0, keepdims=True)
 
 
-def observe(first, planes, levels, cols, members_count, with_weights):
-    ens_scale = math.sqrt(ensemble_share / (members_count - 1))
+def coefficient_planes(coef, sources, levels, cols):
+    coef[...] = jnp.zeros(coef.shape, jnp.float32)
+    for level in range(levels):
+        for kind, source in enumerate(sources):
+            at = (kind * levels + level) * ROWS
+            coef[at : at + ROWS, :cols] = source[level].astype(jnp.float32)
+
+
+def project(out_z, at, totals, scale):
+    for m, total in enumerate(totals):
+        out_z[at + m : at + m + 1, : total.shape[1]] = scale * over_rows(total)
+
+
+def start(planes, levels, cols, count):
+    ens_scale = math.sqrt(ensemble_share / (count - 1))
     base = planes * ROWS
+    edge_rows = -(-(planes + 3 * levels) // GROUP) * ROWS
 
     def kernel(*refs):
-        if first:
-            innov, prec, scale, mask, kx, ky, members, out_z, out_e, coef = refs
-        elif with_weights:
-            own, other, weights, sums, vert, prec, scale, mask, members, out_z, out_e, out_q = refs
+        sources, (out_z, out_e, coef), copies, weighted, sems = refs[:7], refs[7:10], refs[10:17], refs[17], refs[18]
+        moves = [pltpu.make_async_copy(a, b, sems.at[i]) for i, (a, b) in enumerate(zip(sources, copies, strict=True))]
+        for move in moves:
+            move.start()
+        innov, prec, scale, mask, kx, ky, members = copies
+        out_z[...] = jnp.zeros(out_z.shape, jnp.float32)
+        for move in moves[:6]:
+            move.wait()
+        coefficient_planes(coef, (kx, ky, mask), levels, cols)
+        for plane in range(planes):
+            weighted[plane] = mask[plane % levels].astype(jnp.float32) * (prec[plane] * innov[plane])
+            out_z[plane * ROWS : (plane + 1) * ROWS, :cols] = scale[plane] * weighted[plane]
+        edges = [tile(out_z, plane) for plane in range(planes)]
+        pack_edges(out_e, edges + [tile(coef, index) for index in range(3 * levels)], cols)
+        moves[6].wait()
+        totals = [jnp.zeros((ROWS, cols), jnp.float32) for _ in range(count)]
+        for plane in range(planes):
+            for m in range(count):
+                totals[m] += members[m, plane] * weighted[plane]
+        project(out_z, base, totals, ens_scale)
+        out_e[edge_rows:, :] = out_z[base:, :]
+
+    outs = [f32(base + ROWS, LANES), f32(edge_rows + ROWS, LANES), f32(3 * levels * ROWS, LANES)]
+    field, flat = (planes, ROWS, cols), (levels, ROWS, cols)
+    kept = [(field, jnp.float32)] * 3 + [(flat, jnp.int32)] + [(flat, jnp.float32)] * 2 + [((count,) + field, jnp.float32)]
+    scratch = [pltpu.VMEM(*one) for one in kept] + [pltpu.VMEM(field, jnp.float32), pltpu.SemaphoreType.DMA((7,))]
+    return kernel, outs, scratch
+
+
+def observe(planes, levels, cols, count, with_weights):
+    ens_scale = math.sqrt(ensemble_share / (count - 1))
+    base = planes * ROWS
+    edge_rows = -(-planes // GROUP) * ROWS
+    sums_at = base + ROWS * with_weights
+
+    def kernel(*refs):
+        own, other, weights, sums, vert, prec, scale, mask, members = refs[:9]
+        if with_weights:
+            out_z, out_e, out_q = refs[9:]
         else:
-            own, other, weights, sums, vert, prec, scale, mask, members, seen, out_z, out_e = refs
+            seen, out_z, out_e = refs[9:]
         out_z[...] = jnp.zeros(out_z.shape, jnp.float32)
-        totals = [jnp.zeros((ROWS, cols), jnp.float32) for _ in range(members_count)]
+        totals = [jnp.zeros((ROWS, cols), jnp.float32) for _ in range(count)]
         energy = jnp.zeros((ROWS, cols), jnp.float32)
         cross = jnp.zeros((ROWS, cols), jnp.float32)
         here = lax.axis_index("gz") * levels
@@ -218,55 +267,36 @@
         for plane in range(planes):
             field, level = divmod(plane, levels)
             wet = mask[level].astype(jnp.float32)
-            if first:
-                weighted = wet * (prec[plane] * innov[plane])
+            static = jnp.zeros((ROWS, cols), jnp.float32)
+            for k in range(levels):
+                row = (field * 2 * levels + here + level) * 2 * levels
+                static += vert[pl.ds(row + here + k, 1), :cols] * tile(own, field * levels + k)[:, :cols]
+                static += vert[pl.ds(row + there + k, 1), :cols] * tile(other, field * levels + k)[:, :cols]
+            ensemble = jnp.zeros((ROWS, cols), jnp.float32)
+            for m in range(count):
+                ensemble += weights[m : m + 1, :cols] * members[m, plane]
+            seen_now = wet * (SQRT_STATIC * (scale[plane] * static) + ens_scale * ensemble)
+            weighted = wet * (prec[plane] * seen_now)
+            energy += seen_now * weighted
+            if with_weights:
+                out_q[plane] = weighted
+                for m in range(count):
+                    totals[m] += members[m, plane] * weighted
             else:
-                static = jnp.zeros((ROWS, cols), jnp.float32)
-                for k in range(levels):
-                    row = (field * 2 * levels + here + level) * 2 * levels
-                    static += vert[row + here + k] * tile(own, field * levels + k)[:, :cols]
-                    static += vert[row + there + k] * tile(other, field * levels + k)[:, :cols]
-                ensemble = jnp.zeros((ROWS, cols), jnp.float32)
-                for m in range(members_count):
-                    ensemble += weights[m : m + 1, :cols] * members[m, plane]
-                seen_now = wet * (SQRT_STATIC * (scale[plane] * static) + ens_scale * ensemble)
-                weighted = wet * (prec[plane] * seen_now)
-                energy += seen_now * weighted
-                if with_weights:
-                    out_q[plane] = weighted
-                else:
-                    cross += seen_now * seen[plane]
-            if with_weights:
-                for m in range(members_count):
-                    totals[m] += members[m, plane] * weighted
+                cross += seen_now * seen[plane]
             out_z[plane * ROWS : (plane + 1) * ROWS, :cols] = scale[plane] * weighted
         if with_weights:
-            for m in range(members_count):
-                out_z[base + m : base + m + 1, :cols] = ens_scale * over_rows(totals[m])
-        if not first:
-            sums_at = base + ROWS * with_weights
-            out_z[sums_at : sums_at + SUMS, :] = sums[...]
-            out_z[sums_at : sums_at + 1, :cols] = over_rows(energy)
-            if not with_weights:
-                out_z[sums_at + 1 : sums_at + 2, :cols] = over_rows(cross)
-        edges = [tile(out_z, plane) for plane in range(planes)]
-        if first:
-            coef[...] = jnp.zeros(coef.shape, jnp.float32)
-            for level in range(levels):
-                for kind, source in enumerate((kx, ky, mask)):
-                    at = (kind * levels + level) * ROWS
-                    coef[at : at + ROWS, :cols] = source[level].astype(jnp.float32)
-            edges += [tile(coef, index) for index in range(3 * levels)]
-        packed = -(-len(edges) // GROUP) * ROWS
-        pack_edges(out_e, edges, cols)
-        out_e[packed:, :] = out_z[base:, :]
-
-    tail = (ROWS * with_weights) + (0 if first else SUMS)
-    edge_rows = -(-(planes + (3 * levels if first else 0)) // GROUP) * ROWS + tail
-    outs = [f32(base + tail, LANES), f32(edge_rows, LANES)]
-    if first:
-        outs.append(f32(3 * levels * ROWS, LANES))
-    elif with_weights:
+            project(out_z, base, totals, ens_scale)
+        out_z[sums_at : sums_at + SUMS, :] = sums[...]
+        out_z[sums_at : sums_at + 1, :cols] = over_rows(energy)
+        if not with_weights:
+            out_z[sums_at + 1 : sums_at + 2, :cols] = over_rows(cross)
+        pack_edges(out_e, [tile(out_z, plane) for plane in range(planes)], cols)
+        out_e[edge_rows:, :] = out_z[base:, :]
+
+    tail = (ROWS * with_weights) + SUMS
+    outs = [f32(base + tail, LANES), f32(edge_rows + tail, LANES)]
+    if with_weights:
         outs.append(f32(planes, ROWS, cols))
     return kernel, outs
 
@@ -298,8 +328,8 @@
                 mixed = jnp.zeros((ROWS, LANES), jnp.float32)
                 for l in range(levels):
                     block = field * 2 * levels
-                    mixed += vert[(block + here + l) * 2 * levels + here + k] * mine[l]
-                    mixed += vert[(block + there + l) * 2 * levels + here + k] * theirs[l]
+                    mixed += vert[pl.ds((block + here + l) * 2 * levels + here + k, 1), :] * mine[l]
+                    mixed += vert[pl.ds((block + there + l) * 2 * levels + here + k, 1), :] * theirs[l]
                 put(field * levels + k, mixed)
         for index in range(coefs):
             put(planes + index, with_edge(tile(coef, index), edge, planes + index, cols))
@@ -312,15 +342,18 @@
     return kernel, [f32(count * ROWS + tail, LANES), f32(count * 8 + tail, LANES)]
 
 
-def window(target, index, own, after, near, before, slot):
+def window(target, index, own, first, near, third, slot):
+    even = lax.rem(lax.axis_index("gx"), 2) == 0
+    one, three = tile(first, slot), tile(third, slot)
     target[index, 0:16, :] = tile(own, slot)
-    target[index, 16:32, :] = tile(after, slot)
+    target[index, 16:32, :] = jnp.where(even, one, three)
     target[index, 32:40, :] = tile(near, slot, 8)
-    target[index, 40:56, :] = tile(before, slot)
+    target[index, 40:56, :] = jnp.where(even, three, one)
 
 
 def run_steps(start, other, coef, steps, planes, levels):
     def one(number, source, target):
+        number = number.astype(jnp.float32)
         for level in range(levels):
             for field in range(planes // levels):
                 plane = field * levels + level
@@ -333,7 +366,7 @@
                     + coef[3, level] * pltpu.roll(u, 1, 1)
                     - coef[4, level] * u
                 )
-                active = jnp.where(steps[field] > number, 1.0, 0.0).astype(jnp.float32)
+                active = jnp.where(steps[field : field + 1, :] > number, 1.0, 0.0).astype(jnp.float32)
                 target[plane] = u + active * change
 
     def pair(index, carry):
@@ -370,14 +403,14 @@
 def first_diffuse(planes, levels, cols):
     coefs = 3 * levels
 
-    def kernel(own, after, near, before, steps, coef, resid, weights, sums, out_g, buf, kinds):
-        for plane in range(planes):
-            window(buf, plane, own, after, near, before, plane)
+    def kernel(own, first, near, third, steps, coef, resid, weights, sums, out_g, buf, kinds):
+        for plane in range(planes):
+            window(buf, plane, own, first, near, third, plane)
         for index in range(coefs):
-            window(kinds, index, own, after, near, before, planes + index)
+            window(kinds, index, own, first, near, third, planes + index)
         make_coefs(coef, kinds, levels, cols)
         at, near_at = (planes + coefs) * ROWS, (planes + coefs) * 8
-        weights[...] = spread((own[at:, :] + after[at:, :]) + (near[near_at:, :] + before[at:, :]))
+        weights[...] = spread((own[at:, :] + first[at:, :]) + (near[near_at:, :] + third[at:, :]))
         run_steps(buf, resid, coef, steps, planes, levels)
         squares = jnp.zeros((ROWS, LANES), jnp.float32)
         for plane in range(planes):
@@ -403,11 +436,11 @@
 
 
 def second_diffuse(planes, levels, cols):
-    def kernel(own, after, near, before, steps, coef, resid, weights, image, new, new_w, sums, facts, out_g, buf, spare):
-        for plane in range(planes):
-            window(buf, plane, own, after, near, before, plane)
+    def kernel(own, first, near, third, steps, coef, resid, weights, image, new, new_w, sums, facts, out_g, buf, spare):
+        for plane in range(planes):
+            window(buf, plane, own, first, near, third, plane)
         at, near_at = planes * ROWS, planes * 8
-        total = spread((own[at:, :] + after[at:, :]) + (near[near_at:, :] + before[at:, :]))
+        total = spread((own[at:, :] + first[at:, :]) + (near[near_at:, :] + third[at:, :]))
         energy = total[ROWS : ROWS + 1]
         rr = total[ROWS + 2 : ROWS + 3] + over_rows(weights[...] * weights[...])
         curvature = rr + energy
@@ -445,12 +478,12 @@
 
 def last_diffuse(planes, levels, cols):
     def kernel(
-        own, after, near, before, steps, coef, resid, weights, image, new, new_w, facts, control, control_w, final, buf, spare
+        own, first, near, third, steps, coef, resid, weights, image, new, new_w, facts, control, control_w, final, buf, spare
     ):
         for plane in range(planes):
-            window(buf, plane, own, after, near, before, plane)
+            window(buf, plane, own, first, near, third, plane)
         at, near_at = planes * ROWS, planes * 8
-        total = spread((own[at:, :] + after[at:, :]) + (near[near_at:, :] + before[at:, :]))
+        total = spread((own[at:, :] + first[at:, :]) + (near[near_at:, :] + third[at:, :]))
         rr, energy, step = facts[0:1, :], facts[1:2, :], facts[2:3, :]
         new_energy, cross_energy = total[0:1], total[1:2]
         new_rr = total[2:3] + over_rows(new_w[...] * new_w[...])
@@ -459,7 +492,9 @@
         squares = new_rr + ratio * (2.0 * cross_rr + ratio * rr)
         curvature = squares + (new_energy + ratio * (2.0 * cross_energy + ratio * energy))
         new_step = new_rr / curvature
-        control_w[...] = step * weights[...] + new_step * (new_w[...] + ratio * weights[...])
+        combined = step * weights[...] + new_step * (new_w[...] + ratio * weights[...])
+        diagonal = lax.broadcasted_iota(jnp.int32, combined.shape, 0) == lanes_of(combined.shape)
+        control_w[...] = over_rows(jnp.where(diagonal, combined, 0.0))[:, :ROWS]
         run_steps(buf, spare, coef, steps, planes, levels)
         for plane in range(planes):
             value = tile(new, plane)
@@ -469,20 +504,16 @@
             control[plane] = (step * direction + new_step * new_direction)[:, :cols]
             final[plane] = (value - new_step * new_image)[:, :cols]
 
-    outs = [f32(planes, ROWS, cols), f32(ROWS, LANES), f32(planes, ROWS, cols)]
+    outs = [f32(planes, ROWS, cols), f32(1, ROWS), f32(planes, ROWS, cols)]
     scratch = [pltpu.VMEM((planes, WIN, LANES), jnp.float32)] * 2
     return kernel, outs, scratch
 
 
-def moved_to(values, dx, dy, dz):
+def moved_to(values, x, y, z):
     sizes = [lax.axis_size(axis) for axis in AXES]
-    pairs = []
-    for x in range(sizes[0]):
-        for y in range(sizes[1]):
-            for z in range(sizes[2]):
-                to = ((x + dx) % sizes[0] * sizes[1] + (y + dy) % sizes[1]) * sizes[2] + (z + dz) % sizes[2]
-                pairs.append(((x * sizes[1] + y) * sizes[2] + z, to))
-    return lax.ppermute(values, AXES, pairs)
+    here = [(a, b, c) for a in range(sizes[0]) for b in range(sizes[1]) for c in range(sizes[2])]
+    number = {place: index for index, place in enumerate(here)}
+    return lax.ppermute(values, AXES, [(number[a, b, c], number[a ^ x, b ^ y, c ^ z]) for a, b, c in here])
 
 
 def across(kernel_of, out_z, out_e, vert, extra):
@@ -490,9 +521,8 @@
     edge = moved_to(out_e, 0, 1, 0)
     edge_other = moved_to(out_e, 0, 1, 1)
     kernel, outs = kernel_of
-    specs = [VMEM] * 4 + [SMEM] + [VMEM] * len(extra)
-    own, near = call(kernel, outs, specs, (out_z, other, edge, edge_other, vert, *extra))
-    return own, moved_to(own, -1, 0, 0), moved_to(near, 2, 0, 0), moved_to(own, 1, 0, 0)
+    own, near = call(kernel, outs, [VMEM] * (5 + len(extra)), (out_z, other, edge, edge_other, vert, *extra))
+    return own, moved_to(own, 1, 0, 0), moved_to(near, 2, 0, 0), moved_to(own, 3, 0, 0)
 
 
 def shards_small(
@@ -504,37 +534,32 @@
     block = (planes, rows, cols)
     innov, prec, scale = (a.reshape(block) for a in (innovation, obs_precision, error_scale))
     ens = members.reshape((count,) + block)
-    vert = vertical.reshape(-1)
-
-    kernel, outs = observe(True, planes, levels, cols, count, True)
-    out_z, out_e, coef_own = call(kernel, outs, [VMEM] * 7, (innov, prec, scale, sea_mask, kappa_x, kappa_y, ens))
+    vert = jnp.broadcast_to(vertical.reshape(-1, 1), (vertical.size, LANES))
+    steps = jnp.broadcast_to(diffusion_steps.astype(jnp.float32)[:, None], (fields, LANES))
+
+    kernel, outs, scratch = start(planes, levels, cols, count)
+    args = (innov, prec, scale, sea_mask, kappa_x, kappa_y, ens)
+    out_z, out_e, coef_own = call(kernel, outs, [HBM] * 7, args, scratch, 56)
     parts = across(mix_back(True, planes, levels, cols, ROWS), out_z, out_e, vert, (coef_own,))
     kernel, outs, scratch = first_diffuse(planes, levels, cols)
-    specs = [VMEM] * 4 + [SMEM]
-    coef, resid, weights, sums, out_g = call(kernel, outs, specs, (*parts, diffusion_steps), scratch)
-
-    kernel, outs = observe(False, planes, levels, cols, count, True)
-    specs = [VMEM] * 4 + [SMEM] + [VMEM] * 4
+    coef, resid, weights, sums, out_g = call(kernel, outs, [VMEM] * 5, (*parts, steps), scratch)
+
+    kernel, outs = observe(planes, levels, cols, count, True)
     args = (out_g, moved_to(out_g, 0, 0, 1), weights, sums, vert, prec, scale, sea_mask, ens)
-    out_z, out_e, seen = call(kernel, outs, specs, args)
+    out_z, out_e, seen = call(kernel, outs, [VMEM] * 9, args)
     parts = across(mix_back(False, planes, levels, cols, ROWS + SUMS), out_z, out_e, vert, ())
     kernel, outs, scratch = second_diffuse(planes, levels, cols)
-    specs = [VMEM] * 4 + [SMEM] + [VMEM] * 3
-    image, new, new_w, sums, facts, out_g = call(
-        kernel, outs, specs, (*parts, diffusion_steps, coef, resid, weights), scratch
-    )
-
-    kernel, outs = observe(False, planes, levels, cols, count, False)
-    specs = [VMEM] * 4 + [SMEM] + [VMEM] * 5
+    args = (*parts, steps, coef, resid, weights)
+    image, new, new_w, sums, facts, out_g = call(kernel, outs, [VMEM] * 8, args, scratch)
+
+    kernel, outs = observe(planes, levels, cols, count, False)
     args = (out_g, moved_to(out_g, 0, 0, 1), new_w, sums, vert, prec, scale, sea_mask, ens, seen)
-    out_z, out_e = call(kernel, outs, specs, args)
+    out_z, out_e = call(kernel, outs, [VMEM] * 10, args)
     parts = across(mix_back(False, planes, levels, cols, SUMS), out_z, out_e, vert, ())
     kernel, outs, scratch = last_diffuse(planes, levels, cols)
-    specs = [VMEM] * 4 + [SMEM] + [VMEM] * 7
-    control, control_w, final = call(
-        kernel, outs, specs, (*parts, diffusion_steps, coef, resid, weights, image, new, new_w, facts), scratch
-    )
-    return control.reshape(innovation.shape), control_w[:, 0], final.reshape(innovation.shape)
+    args = (*parts, steps, coef, resid, weights, image, new, new_w, facts)
+    control, control_w, final = call(kernel, outs, [VMEM] * 12, args, scratch)
+    return control.reshape(innovation.shape), control_w.reshape(count), final.reshape(innovation.shape)
 
 
 def shards(innovation, obs_precision, error_scale, kappa_x, kappa_y, sea_mask, members, vertical, diffusion_steps):

time: 74.8 us -> 65.9 us (0.88)
  local copies, waits for them, and re-layouts: 6.98 us -> 2.07 us
  waiting for transfers between devices: 30.1 us -> 27.2 us
  Pallas kernels: 16.5 us -> 14.5 us
  starting transfers between devices: 20.1 us -> 21 us
    unnamed x27 -> x17, local copies, waits for them, and re-layouts: 6.26 us -> 1.83 us
    ppermute x20, waiting for transfers between devices: 30.1 us -> 27.2 us  [moved_to(): lax.ppermute(values, AXES, [(number[a, b, c], number[a ^ x, b ^ y, c ^ z]...]
    pallas_call x9, Pallas kernels: 16.5 us -> 14.5 us  [call(): pl.pallas_call(kernel, out_shape=outs, in_specs=specs, out_specs=[VMEM] *...]
    ppermute x20, starting transfers between devices: 20.1 us -> 21 us  [moved_to(): lax.ppermute(values, AXES, [(number[a, b, c], number[a ^ x, b ^ y, c ^ z]...]
  transfers between devices with their start and end apart: 20 -> 20, of which waited for: 11 -> 13; matrix products, arithmetic and copies ran while one was open for 0% -> 0% of each run, Pallas kernels for 0% -> 0%
where the time goes in v2:
time: 65.9 us; the launch traced here: 65.6 us
  waiting for transfers between devices  27.2 us (41%)
  starting transfers between devices  21 us (32%)
  Pallas kernels  14.5 us (22%)
  local copies, waits for them, and re-layouts  2.07 us (3%)
  between operations  0.78 us (1%)
    ppermute x20, waiting for transfers between devices, moved_to(): lax.ppermute(values, AXES, [(number[a, b, c], number[a ^ x, b ^ y, c ^ z]...  27.2 us
    ppermute x20, starting transfers between devices, moved_to(): lax.ppermute(values, AXES, [(number[a, b, c], number[a ^ x, b ^ y, c ^ z]...  21 us
    pallas_call x9, Pallas kernels, call(): pl.pallas_call(kernel, out_shape=outs, in_specs=specs, out_specs=[VMEM] *...  14.5 us
    unnamed x17, local copies, waits for them, and re-layouts  1.83 us
  transfers between devices with their start and end apart: 20, of which 13 were waited for; matrix products, arithmetic and copies ran while one was open for 0% of the time, Pallas kernels for 0%

profile of v2, /device:TPU:0, one launch (start us, length us, event | category | flops | bytes accessed | tf_op | source)
XLA Modules:
  0.0 65.6 jit_solution(10784342339697421523)
XLA Ops:
  0.6 0.0 copy-start.3
  0.6 0.0 copy-start
  0.7 0.0 copy-start.2
  0.7 0.0 copy-start.1
  0.7 0.0 copy-start.6
  0.7 0.0 copy-start.7
  0.7 2.4 %shard_map.112 = (f32[176,128]{1,0:T(8,128)}, f32[64,128]{1,0:T(8,128)}, f32[96,128]{1,0:T(8,128)}) custom-call(f32[10,16,108]{2,1,0:T(8,128)} %bitcast.16, f32[10,16,108]{2,1,0:T(8,128)} %bitcast.10, f32[10,16,108]{2,1,0:T(8,128)} %bitcast.13, s32[2,16,108]{2,1,0:T(8,128)} %refs_7_.3, f32[2,16,108]{2,1,0:T(8,128)} %refs_4_.1, f32[2,16,108]{2,1,0:T(8,128)} %refs_5_.1, ...), custom_call_target="tpu_custom_call" | custom-call | tf_op jit(solution)/shard_map/pallas_call | solution.py:162
  3.1 0.5 collective-permute-start
  3.6 2.6 %collective-permute-start.2 = (f32[64,128]{1,0:T(8,128)}, f32[64,128]{1,0:T(8,128)S(1)}, u32[]{:S(2)}, u32[]{:S(2)}) collective-permute-start(f32[64,128]{1,0:T(8,128)} %get-tuple-element.32), channel_id=1, source_target_pairs={{0,3},{1,2},{2,1},{3,0},{4,7},{5,6},{6,5},{7,4},{8,11},{9,10},{10,... | collective-permute-start | bytes 98312 | tf_op jit(solution)/shard_map/ppermute | solution.py:516
  6.2 0.0 collective-permute-start.1
  6.3 0.0 copy-done.6
  6.3 0.1 copy.13
  6.4 0.1 broadcast_in_dim.6
  6.5 1.7 %collective-permute-done.2.refs_3_ = f32[64,128]{1,0:T(8,128)S(1)} collective-permute-done((f32[64,128]{1,0:T(8,128)}, f32[64,128]{1,0:T(8,128)S(1)}, u32[]{:S(2)}, u32[]{:S(2)}) %collective-permute-start.2) | collective-permute-done | bytes 32800 | tf_op jit(solution)/shard_map/ppermute | solution.py:516
  8.1 2.2 %collective-permute-done.1.refs_2_ = f32[64,128]{1,0:T(8,128)S(1)} collective-permute-done((f32[64,128]{1,0:T(8,128)}, f32[64,128]{1,0:T(8,128)S(1)}, u32[]{:S(2)}, u32[]{:S(2)}) %collective-permute-start.1) | collective-permute-done | bytes 32800 | tf_op jit(solution)/shard_map/ppermute | solution.py:516
  10.3 0.0 collective-permute-done.refs_1_
  10.3 0.1 broadcast_in_dim.14.refs_4_
  10.4 0.9 %copy-done.4 = f32[176,128]{1,0:T(8,128)S(1)} copy-done((f32[176,128]{1,0:T(8,128)S(1)}, f32[176,128]{1,0:T(8,128)}, u32[]{:S(2)}) %copy-start.4) | copy-done | bytes 90136
  11.3 0.8 %copy-done.5 = f32[96,128]{1,0:T(8,128)S(1)} copy-done((f32[96,128]{1,0:T(8,128)S(1)}, f32[96,128]{1,0:T(8,128)}, u32[]{:S(2)}) %copy-start.5) | copy-done | bytes 49176
  12.1 0.1 shard_map.113
  12.2 3.7 %collective-permute-start.5 = (f32[272,128]{1,0:T(8,128)S(1)}, f32[272,128]{1,0:T(8,128)S(1)}, u32[]{:S(2)}, u32[]{:S(2)}) collective-permute-start(f32[272,128]{1,0:T(8,128)S(1)} %get-tuple-element.34.own), channel_id=1, source_target_pairs={{0,12},{1,13},{2,14},{3,15},{4,8},{5,9},{6,10},{7,11},{8,4},{9,5},... | collective-permute-start | bytes 417800 | tf_op jit(solution)/shard_map/ppermute | solution.py:516
  15.9 0.0 collective-permute-start.3
  15.9 0.8 %collective-permute-start.4 = (f32[144,128]{1,0:T(8,128)S(1)}, f32[144,128]{1,0:T(8,128)S(1)}, u32[]{:S(2)}, u32[]{:S(2)}) collective-permute-start(f32[144,128]{1,0:T(8,128)S(1)} %get-tuple-element.35), channel_id=1, source_target_pairs={{0,8},{1,9},{2,10},{3,11},{4,12},{5,13},{6,14},{7,15},{8,0},{9,1},... | collective-permute-start | bytes 221192 | tf_op jit(solution)/shard_map/ppermute | solution.py:516
  16.7 0.0 copy-done.7
  16.7 7.3 %collective-permute-done.4.near = f32[144,128]{1,0:T(8,128)S(1)} collective-permute-done((f32[144,128]{1,0:T(8,128)S(1)}, f32[144,128]{1,0:T(8,128)S(1)}, u32[]{:S(2)}, u32[]{:S(2)}) %collective-permute-start.4) | collective-permute-done | bytes 73760 | tf_op jit(solution)/shard_map/ppermute | solution.py:516
  24.0 0.0 collective-permute-done.5.third
  24.0 0.0 collective-permute-done.3.first
  24.0 0.1 broadcast_in_dim.15.steps
  24.0 4.1 %shard_map.114 = (f32[5,2,56,128]{3,2,1,0:T(8,128)S(1)}, f32[10,56,128]{2,1,0:T(8,128)S(1)}, f32[16,128]{1,0:T(8,128)S(1)}, f32[8,128]{1,0:T(8,128)S(1)}, f32[160,128]{1,0:T(8,128)S(1)}) custom-call(f32[272,128]{1,0:T(8,128)S(1)} %get-tuple-element.34.own, f32[272,128]{1,0:T(8,128)S(1)} %collective-permute-done.3.first, ...), custom_call_target="tpu_custom_call" | custom-call | tf_op jit(solution)/shard_map/pallas_call | solution.py:162
  28.1 0.1 collective-permute-start.6
  28.2 1.3 %collective-permute-done.6.refs_1_ = f32[160,128]{1,0:T(8,128)S(1)} collective-permute-done((f32[160,128]{1,0:T(8,128)S(1)}, f32[160,128]{1,0:T(8,128)S(1)}, u32[]{:S(2)}, u32[]{:S(2)}) %collective-permute-start.6) | collective-permute-done | bytes 81952 | tf_op jit(solution)/shard_map/ppermute | solution.py:516
  29.5 0.0 copy-done
  29.5 0.3 shard_map.115
  29.8 0.2 collective-permute-start.7
  30.0 0.9 %collective-permute-start.9 = (f32[56,128]{1,0:T(8,128)S(1)}, f32[56,128]{1,0:T(8,128)S(1)}, u32[]{:S(2)}, u32[]{:S(2)}) collective-permute-start(f32[56,128]{1,0:T(8,128)S(1)} %get-tuple-element.40), channel_id=1, source_target_pairs={{0,3},{1,2},{2,1},{3,0},{4,7},{5,6},{6,5},{7,4},{8,11},{9,10},{10,... | collective-permute-start | bytes 86024 | tf_op jit(solution)/shard_map/ppermute | solution.py:516
  31.0 1.0 %collective-permute-start.8 = (f32[56,128]{1,0:T(8,128)S(1)}, f32[56,128]{1,0:T(8,128)S(1)}, u32[]{:S(2)}, u32[]{:S(2)}) collective-permute-start(f32[56,128]{1,0:T(8,128)S(1)} %get-tuple-element.40), channel_id=1, source_target_pairs={{0,2},{1,3},{2,0},{3,1},{4,6},{5,7},{6,4},{7,5},{8,10},{9,11},{10,... | collective-permute-start | bytes 86024 | tf_op jit(solution)/shard_map/ppermute | solution.py:516
  32.0 1.3 %collective-permute-done.9.refs_3_ = f32[56,128]{1,0:T(8,128)S(1)} collective-permute-done((f32[56,128]{1,0:T(8,128)S(1)}, f32[56,128]{1,0:T(8,128)S(1)}, u32[]{:S(2)}, u32[]{:S(2)}) %collective-permute-start.9) | collective-permute-done | bytes 28704 | tf_op jit(solution)/shard_map/ppermute | solution.py:516
  33.3 1.5 %collective-permute-done.8.refs_2_ = f32[56,128]{1,0:T(8,128)S(1)} collective-permute-done((f32[56,128]{1,0:T(8,128)S(1)}, f32[56,128]{1,0:T(8,128)S(1)}, u32[]{:S(2)}, u32[]{:S(2)}) %collective-permute-start.8) | collective-permute-done | bytes 28704 | tf_op jit(solution)/shard_map/ppermute | solution.py:516
  34.9 0.0 collective-permute-done.7.refs_1_
  34.9 0.1 shard_map.116
  35.0 1.9 %collective-permute-start.12 = (f32[184,128]{1,0:T(8,128)S(1)}, f32[184,128]{1,0:T(8,128)S(1)}, u32[]{:S(2)}, u32[]{:S(2)}) collective-permute-start(f32[184,128]{1,0:T(8,128)S(1)} %get-tuple-element.41.own), channel_id=1, source_target_pairs={{0,12},{1,13},{2,14},{3,15},{4,8},{5,9},{6,10},{7,11},{8,4},{9,5},... | collective-permute-start | bytes 282632 | tf_op jit(solution)/shard_map/ppermute | solution.py:516
  36.8 0.7 %collective-permute-start.10 = (f32[184,128]{1,0:T(8,128)S(1)}, f32[184,128]{1,0:T(8,128)S(1)}, u32[]{:S(2)}, u32[]{:S(2)}) collective-permute-start(f32[184,128]{1,0:T(8,128)S(1)} %get-tuple-element.41.own), channel_id=1, source_target_pairs={{0,4},{1,5},{2,6},{3,7},{4,0},{5,1},{6,2},{7,3},{8,12},{9,13},{10,... | collective-permute-start | bytes 282632 | tf_op jit(solution)/shard_map/ppermute | solution.py:516
  37.6 1.9 %collective-permute-start.11 = (f32[104,128]{1,0:T(8,128)S(1)}, f32[104,128]{1,0:T(8,128)S(1)}, u32[]{:S(2)}, u32[]{:S(2)}) collective-permute-start(f32[104,128]{1,0:T(8,128)S(1)} %get-tuple-element.42), channel_id=1, source_target_pairs={{0,8},{1,9},{2,10},{3,11},{4,12},{5,13},{6,14},{7,15},{8,0},{9,1},... | collective-permute-start | bytes 159752 | tf_op jit(solution)/shard_map/ppermute | solution.py:516
  39.4 3.9 %collective-permute-done.11.near = f32[104,128]{1,0:T(8,128)S(1)} collective-permute-done((f32[104,128]{1,0:T(8,128)S(1)}, f32[104,128]{1,0:T(8,128)S(1)}, u32[]{:S(2)}, u32[]{:S(2)}) %collective-permute-start.11) | collective-permute-done | bytes 53280 | tf_op jit(solution)/shard_map/ppermute | solution.py:516
  43.3 0.0 collective-permute-done.12.third
  43.3 0.3 collective-permute-done.10.first
  43.7 4.1 %shard_map.117 = (f32[160,128]{1,0:T(8,128)S(1)}, f32[160,128]{1,0:T(8,128)S(1)}, f32[16,128]{1,0:T(8,128)S(1)}, f32[8,128]{1,0:T(8,128)S(1)}, f32[8,128]{1,0:T(8,128)S(1)}, /*index=5*/f32[160,128]{1,0:T(8,128)S(1)}) custom-call(f32[184,128]{1,0:T(8,128)S(1)} %get-tuple-element.41.own, f32[184,128]{1,0:T(8,128)S(1)} %collective-permute-done.10.first, ...), custom_call_target="tpu_custom_call" | custom-call | tf_op jit(solution)/shard_map/pallas_call | solution.py:162
  47.7 0.1 collective-permute-start.13
  47.8 1.3 %collective-permute-done.13.refs_1_ = f32[160,128]{1,0:T(8,128)S(1)} collective-permute-done((f32[160,128]{1,0:T(8,128)S(1)}, f32[160,128]{1,0:T(8,128)S(1)}, u32[]{:S(2)}, u32[]{:S(2)}) %collective-permute-start.13) | collective-permute-done | bytes 81952 | tf_op jit(solution)/shard_map/ppermute | solution.py:516
  49.1 0.3 shard_map.118
  49.3 0.2 collective-permute-start.14
  49.5 1.0 %collective-permute-start.16 = (f32[40,128]{1,0:T(8,128)S(1)}, f32[40,128]{1,0:T(8,128)S(1)}, u32[]{:S(2)}, u32[]{:S(2)}) collective-permute-start(f32[40,128]{1,0:T(8,128)S(1)} %get-tuple-element.50), channel_id=1, source_target_pairs={{0,3},{1,2},{2,1},{3,0},{4,7},{5,6},{6,5},{7,4},{8,11},{9,10},{10,... | collective-permute-start | bytes 61448 | tf_op jit(solution)/shard_map/ppermute | solution.py:516
  50.5 1.0 %collective-permute-start.15 = (f32[40,128]{1,0:T(8,128)S(1)}, f32[40,128]{1,0:T(8,128)S(1)}, u32[]{:S(2)}, u32[]{:S(2)}) collective-permute-start(f32[40,128]{1,0:T(8,128)S(1)} %get-tuple-element.50), channel_id=1, source_target_pairs={{0,2},{1,3},{2,0},{3,1},{4,6},{5,7},{6,4},{7,5},{8,10},{9,11},{10,... | collective-permute-start | bytes 61448 | tf_op jit(solution)/shard_map/ppermute | solution.py:516
  51.5 1.2 %collective-permute-done.16.refs_3_ = f32[40,128]{1,0:T(8,128)S(1)} collective-permute-done((f32[40,128]{1,0:T(8,128)S(1)}, f32[40,128]{1,0:T(8,128)S(1)}, u32[]{:S(2)}, u32[]{:S(2)}) %collective-permute-start.16) | collective-permute-done | bytes 20512 | tf_op jit(solution)/shard_map/ppermute | solution.py:516
  52.7 1.6 %collective-permute-done.15.refs_2_ = f32[40,128]{1,0:T(8,128)S(1)} collective-permute-done((f32[40,128]{1,0:T(8,128)S(1)}, f32[40,128]{1,0:T(8,128)S(1)}, u32[]{:S(2)}, u32[]{:S(2)}) %collective-permute-start.15) | collective-permute-done | bytes 20512 | tf_op jit(solution)/shard_map/ppermute | solution.py:516
  54.3 0.0 collective-permute-done.14.refs_1_
  54.3 0.1 shard_map.119
  54.5 2.3 %collective-permute-start.19 = (f32[168,128]{1,0:T(8,128)S(1)}, f32[168,128]{1,0:T(8,128)S(1)}, u32[]{:S(2)}, u32[]{:S(2)}) collective-permute-start(f32[168,128]{1,0:T(8,128)S(1)} %get-tuple-element.51.own), channel_id=1, source_target_pairs={{0,12},{1,13},{2,14},{3,15},{4,8},{5,9},{6,10},{7,11},{8,4},{9,5},... | collective-permute-start | bytes 258056 | tf_op jit(solution)/shard_map/ppermute | solution.py:516
  56.8 0.0 collective-permute-start.17
  56.8 2.1 %collective-permute-start.18 = (f32[88,128]{1,0:T(8,128)S(1)}, f32[88,128]{1,0:T(8,128)S(1)}, u32[]{:S(2)}, u32[]{:S(2)}) collective-permute-start(f32[88,128]{1,0:T(8,128)S(1)} %get-tuple-element.52), channel_id=1, source_target_pairs={{0,8},{1,9},{2,10},{3,11},{4,12},{5,13},{6,14},{7,15},{8,0},{9,1},... | collective-permute-start | bytes 135176 | tf_op jit(solution)/shard_map/ppermute | solution.py:516
  58.9 3.3 %collective-permute-done.18.near = f32[88,128]{1,0:T(8,128)S(1)} collective-permute-done((f32[88,128]{1,0:T(8,128)S(1)}, f32[88,128]{1,0:T(8,128)S(1)}, u32[]{:S(2)}, u32[]{:S(2)}) %collective-permute-start.18) | collective-permute-done | bytes 45088 | tf_op jit(solution)/shard_map/ppermute | solution.py:516
  62.2 0.0 collective-permute-done.19.third
  62.2 0.4 collective-permute-done.17.first
  62.6 3.1 %shard_map.120 = (f32[10,16,108]{2,1,0:T(8,128)}, f32[1,16]{1,0:T(1,128)}, f32[10,16,108]{2,1,0:T(8,128)}) custom-call(f32[168,128]{1,0:T(8,128)S(1)} %get-tuple-element.51.own, f32[168,128]{1,0:T(8,128)S(1)} %collective-permute-done.17.first, f32[88,128]{1,0:T(8,128)S(1)} %collective-permute-done.18.near, f32[168,128]{1,0:T(8,128)S(1)} %collective-permute-done.19.third, ...), custom_call_target="tpu_custom_call" | custom-call | tf_op jit(solution)/shard_map/pallas_call | solution.py:162
  (6 shorter events, 0.0 us)
Async XLA Ops:
  0.6 28.8 %copy-start.3 = (s32[2,16,108]{2,1,0:T(8,128)S(1)}, s32[2,16,108]{2,1,0:T(8,128)}, u32[]{:S(2)}) copy-start(s32[2,16,108]{2,1,0:T(8,128)} %refs_7_.3) | copy-start | bytes 41476
  0.6 28.8 %copy-start = (f32[16,5,2,16,108]{4,3,2,1,0:T(8,128)S(1)}, f32[16,5,2,16,108]{4,3,2,1,0:T(8,128)}, u32[]{:S(2)}) copy-start(f32[16,5,2,16,108]{4,3,2,1,0:T(8,128)} %param.15) | copy-start | bytes 3317764
  0.7 28.8 %copy-start.2 = (f32[5,2,16,108]{3,2,1,0:T(8,128)S(1)}, f32[5,2,16,108]{3,2,1,0:T(8,128)}, u32[]{:S(2)}) copy-start(f32[5,2,16,108]{3,2,1,0:T(8,128)} %param.11) | copy-start | bytes 207364
  0.7 28.8 %copy-start.1 = (f32[5,2,16,108]{3,2,1,0:T(8,128)S(1)}, f32[5,2,16,108]{3,2,1,0:T(8,128)}, u32[]{:S(2)}) copy-start(f32[5,2,16,108]{3,2,1,0:T(8,128)} %param.10) | copy-start | bytes 207364
  0.7 5.6 %copy-start.6 = (f32[5,4,4]{0,2,1:T(4,128)S(1)}, f32[5,4,4]{0,2,1:T(4,128)}, u32[]{:S(2)}) copy-start(f32[5,4,4]{0,2,1:T(4,128)} %param.16) | copy-start | bytes 964
  0.7 16.0 %copy-start.7 = (s32[5]{0:T(128)S(1)}, s32[5]{0:T(128)}, u32[]{:S(2)}) copy-start(s32[5]{0:T(128)} %param.17) | copy-start | bytes 64
  3.1 7.3 %collective-permute-start = (f32[176,128]{1,0:T(8,128)}, f32[176,128]{1,0:T(8,128)S(1)}, u32[]{:S(2)}, u32[]{:S(2)}) collective-permute-start(f32[176,128]{1,0:T(8,128)} %get-tuple-element.31.refs_0_), channel_id=1, source_target_pairs={{0,1},{1,0},{2,3},{3,2},{4,5},{5,4},{6,7},{7,6},{8,9},{9,8},{10,11... | collective-permute-start | bytes 270344 | tf_op jit(solution)/shard_map/ppermute | solution.py:516
  3.6 4.5 %collective-permute-start.2 = (f32[64,128]{1,0:T(8,128)}, f32[64,128]{1,0:T(8,128)S(1)}, u32[]{:S(2)}, u32[]{:S(2)}) collective-permute-start(f32[64,128]{1,0:T(8,128)} %get-tuple-element.32), channel_id=1, source_target_pairs={{0,3},{1,2},{2,1},{3,0},{4,7},{5,6},{6,5},{7,4},{8,11},{9,10},{10,... | collective-permute-start | bytes 98312 | tf_op jit(solution)/shard_map/ppermute | solution.py:516
  6.2 4.1 %collective-permute-start.1 = (f32[64,128]{1,0:T(8,128)}, f32[64,128]{1,0:T(8,128)S(1)}, u32[]{:S(2)}, u32[]{:S(2)}) collective-permute-start(f32[64,128]{1,0:T(8,128)} %get-tuple-element.32), channel_id=1, source_target_pairs={{0,2},{1,3},{2,0},{3,1},{4,6},{5,7},{6,4},{7,5},{8,10},{9,11},{10,... | collective-permute-start | bytes 98312 | tf_op jit(solution)/shard_map/ppermute | solution.py:516
  10.4 0.9 %copy-start.4 = (f32[176,128]{1,0:T(8,128)S(1)}, f32[176,128]{1,0:T(8,128)}, u32[]{:S(2)}) copy-start(f32[176,128]{1,0:T(8,128)} %get-tuple-element.31.refs_0_) | copy-start | bytes 270340
  11.3 0.8 %copy-start.5 = (f32[96,128]{1,0:T(8,128)S(1)}, f32[96,128]{1,0:T(8,128)}, u32[]{:S(2)}) copy-start(f32[96,128]{1,0:T(8,128)} %get-tuple-element.33.refs_5_) | copy-start | bytes 147460
  12.2 11.7 %collective-permute-start.5 = (f32[272,128]{1,0:T(8,128)S(1)}, f32[272,128]{1,0:T(8,128)S(1)}, u32[]{:S(2)}, u32[]{:S(2)}) collective-permute-start(f32[272,128]{1,0:T(8,128)S(1)} %get-tuple-element.34.own), channel_id=1, source_target_pairs={{0,12},{1,13},{2,14},{3,15},{4,8},{5,9},{6,10},{7,11},{8,4},{9,5},... | collective-permute-start | bytes 417800 | tf_op jit(solution)/shard_map/ppermute | solution.py:516
  15.9 8.1 %collective-permute-start.3 = (f32[272,128]{1,0:T(8,128)S(1)}, f32[272,128]{1,0:T(8,128)S(1)}, u32[]{:S(2)}, u32[]{:S(2)}) collective-permute-start(f32[272,128]{1,0:T(8,128)S(1)} %get-tuple-element.34.own), channel_id=1, source_target_pairs={{0,4},{1,5},{2,6},{3,7},{4,0},{5,1},{6,2},{7,3},{8,12},{9,13},{10,... | collective-permute-start | bytes 417800 | tf_op jit(solution)/shard_map/ppermute | solution.py:516
  15.9 8.0 %collective-permute-start.4 = (f32[144,128]{1,0:T(8,128)S(1)}, f32[144,128]{1,0:T(8,128)S(1)}, u32[]{:S(2)}, u32[]{:S(2)}) collective-permute-start(f32[144,128]{1,0:T(8,128)S(1)} %get-tuple-element.35), channel_id=1, source_target_pairs={{0,8},{1,9},{2,10},{3,11},{4,12},{5,13},{6,14},{7,15},{8,0},{9,1},... | collective-permute-start | bytes 221192 | tf_op jit(solution)/shard_map/ppermute | solution.py:516
  28.1 1.3 %collective-permute-start.6 = (f32[160,128]{1,0:T(8,128)S(1)}, f32[160,128]{1,0:T(8,128)S(1)}, u32[]{:S(2)}, u32[]{:S(2)}) collective-permute-start(f32[160,128]{1,0:T(8,128)S(1)} %get-tuple-element.36.refs_0_), channel_id=1, source_target_pairs={{0,1},{1,0},{2,3},{3,2},{4,5},{5,4},{6,7},{7,6},{8,9},{9,8},{10,11... | collective-permute-start | bytes 245768 | tf_op jit(solution)/shard_map/ppermute | solution.py:516
  29.8 5.0 %collective-permute-start.7 = (f32[184,128]{1,0:T(8,128)S(1)}, f32[184,128]{1,0:T(8,128)S(1)}, u32[]{:S(2)}, u32[]{:S(2)}) collective-permute-start(f32[184,128]{1,0:T(8,128)S(1)} %get-tuple-element.39.refs_0_), channel_id=1, source_target_pairs={{0,1},{1,0},{2,3},{3,2},{4,5},{5,4},{6,7},{7,6},{8,9},{9,8},{10,11... | collective-permute-start | bytes 282632 | tf_op jit(solution)/shard_map/ppermute | solution.py:516
  30.0 3.3 %collective-permute-start.9 = (f32[56,128]{1,0:T(8,128)S(1)}, f32[56,128]{1,0:T(8,128)S(1)}, u32[]{:S(2)}, u32[]{:S(2)}) collective-permute-start(f32[56,128]{1,0:T(8,128)S(1)} %get-tuple-element.40), channel_id=1, source_target_pairs={{0,3},{1,2},{2,1},{3,0},{4,7},{5,6},{6,5},{7,4},{8,11},{9,10},{10,... | collective-permute-start | bytes 86024 | tf_op jit(solution)/shard_map/ppermute | solution.py:516
  31.0 3.9 %collective-permute-start.8 = (f32[56,128]{1,0:T(8,128)S(1)}, f32[56,128]{1,0:T(8,128)S(1)}, u32[]{:S(2)}, u32[]{:S(2)}) collective-permute-start(f32[56,128]{1,0:T(8,128)S(1)} %get-tuple-element.40), channel_id=1, source_target_pairs={{0,2},{1,3},{2,0},{3,1},{4,6},{5,7},{6,4},{7,5},{8,10},{9,11},{10,... | collective-permute-start | bytes 86024 | tf_op jit(solution)/shard_map/ppermute | solution.py:516
  35.0 8.4 %collective-permute-start.12 = (f32[184,128]{1,0:T(8,128)S(1)}, f32[184,128]{1,0:T(8,128)S(1)}, u32[]{:S(2)}, u32[]{:S(2)}) collective-permute-start(f32[184,128]{1,0:T(8,128)S(1)} %get-tuple-element.41.own), channel_id=1, source_target_pairs={{0,12},{1,13},{2,14},{3,15},{4,8},{5,9},{6,10},{7,11},{8,4},{9,5},... | collective-permute-start | bytes 282632 | tf_op jit(solution)/shard_map/ppermute | solution.py:516
  36.8 6.8 %collective-permute-start.10 = (f32[184,128]{1,0:T(8,128)S(1)}, f32[184,128]{1,0:T(8,128)S(1)}, u32[]{:S(2)}, u32[]{:S(2)}) collective-permute-start(f32[184,128]{1,0:T(8,128)S(1)} %get-tuple-element.41.own), channel_id=1, source_target_pairs={{0,4},{1,5},{2,6},{3,7},{4,0},{5,1},{6,2},{7,3},{8,12},{9,13},{10,... | collective-permute-start | bytes 282632 | tf_op jit(solution)/shard_map/ppermute | solution.py:516
  37.6 5.8 %collective-permute-start.11 = (f32[104,128]{1,0:T(8,128)S(1)}, f32[104,128]{1,0:T(8,128)S(1)}, u32[]{:S(2)}, u32[]{:S(2)}) collective-permute-start(f32[104,128]{1,0:T(8,128)S(1)} %get-tuple-element.42), channel_id=1, source_target_pairs={{0,8},{1,9},{2,10},{3,11},{4,12},{5,13},{6,14},{7,15},{8,0},{9,1},... | collective-permute-start | bytes 159752 | tf_op jit(solution)/shard_map/ppermute | solution.py:516
  47.7 1.3 %collective-permute-start.13 = (f32[160,128]{1,0:T(8,128)S(1)}, f32[160,128]{1,0:T(8,128)S(1)}, u32[]{:S(2)}, u32[]{:S(2)}) collective-permute-start(f32[160,128]{1,0:T(8,128)S(1)} %get-tuple-element.45.refs_0_), channel_id=1, source_target_pairs={{0,1},{1,0},{2,3},{3,2},{4,5},{5,4},{6,7},{7,6},{8,9},{9,8},{10,11... | collective-permute-start | bytes 245768 | tf_op jit(solution)/shard_map/ppermute | solution.py:516
  49.3 5.0 %collective-permute-start.14 = (f32[168,128]{1,0:T(8,128)S(1)}, f32[168,128]{1,0:T(8,128)S(1)}, u32[]{:S(2)}, u32[]{:S(2)}) collective-permute-start(f32[168,128]{1,0:T(8,128)S(1)} %get-tuple-element.49.refs_0_), channel_id=1, source_target_pairs={{0,1},{1,0},{2,3},{3,2},{4,5},{5,4},{6,7},{7,6},{8,9},{9,8},{10,11... | collective-permute-start | bytes 258056 | tf_op jit(solution)/shard_map/ppermute | solution.py:516
  49.5 3.2 %collective-permute-start.16 = (f32[40,128]{1,0:T(8,128)S(1)}, f32[40,128]{1,0:T(8,128)S(1)}, u32[]{:S(2)}, u32[]{:S(2)}) collective-permute-start(f32[40,128]{1,0:T(8,128)S(1)} %get-tuple-element.50), channel_id=1, source_target_pairs={{0,3},{1,2},{2,1},{3,0},{4,7},{5,6},{6,5},{7,4},{8,11},{9,10},{10,... | collective-permute-start | bytes 61448 | tf_op jit(solution)/shard_map/ppermute | solution.py:516
  50.5 3.8 %collective-permute-start.15 = (f32[40,128]{1,0:T(8,128)S(1)}, f32[40,128]{1,0:T(8,128)S(1)}, u32[]{:S(2)}, u32[]{:S(2)}) collective-permute-start(f32[40,128]{1,0:T(8,128)S(1)} %get-tuple-element.50), channel_id=1, source_target_pairs={{0,2},{1,3},{2,0},{3,1},{4,6},{5,7},{6,4},{7,5},{8,10},{9,11},{10,... | collective-permute-start | bytes 61448 | tf_op jit(solution)/shard_map/ppermute | solution.py:516
  54.5 7.7 %collective-permute-start.19 = (f32[168,128]{1,0:T(8,128)S(1)}, f32[168,128]{1,0:T(8,128)S(1)}, u32[]{:S(2)}, u32[]{:S(2)}) collective-permute-start(f32[168,128]{1,0:T(8,128)S(1)} %get-tuple-element.51.own), channel_id=1, source_target_pairs={{0,12},{1,13},{2,14},{3,15},{4,8},{5,9},{6,10},{7,11},{8,4},{9,5},... | collective-permute-start | bytes 258056 | tf_op jit(solution)/shard_map/ppermute | solution.py:516
  56.8 5.8 %collective-permute-start.17 = (f32[168,128]{1,0:T(8,128)S(1)}, f32[168,128]{1,0:T(8,128)S(1)}, u32[]{:S(2)}, u32[]{:S(2)}) collective-permute-start(f32[168,128]{1,0:T(8,128)S(1)} %get-tuple-element.51.own), channel_id=1, source_target_pairs={{0,4},{1,5},{2,6},{3,7},{4,0},{5,1},{6,2},{7,3},{8,12},{9,13},{10,... | collective-permute-start | bytes 258056 | tf_op jit(solution)/shard_map/ppermute | solution.py:516
  56.8 5.4 %collective-permute-start.18 = (f32[88,128]{1,0:T(8,128)S(1)}, f32[88,128]{1,0:T(8,128)S(1)}, u32[]{:S(2)}, u32[]{:S(2)}) collective-permute-start(f32[88,128]{1,0:T(8,128)S(1)} %get-tuple-element.52), channel_id=1, source_target_pairs={{0,8},{1,9},{2,10},{3,11},{4,12},{5,13},{6,14},{7,15},{8,0},{9,1},... | collective-permute-start | bytes 135176 | tf_op jit(solution)/shard_map/ppermute | solution.py:516

commit v3 on v2

--- a/solution.py
+++ b/solution.py
@@ -144,6 +144,7 @@
 
 ROWS = 16
 WIN = 56
+TILES = WIN // 8
 LANES = 128
 DEPTH = 2 * KMAX
 GROUP = LANES // DEPTH
@@ -196,6 +197,10 @@
 
 def over_rows(values):
     return jnp.sum(values, axis=0, keepdims=True)
+
+
+def whole(values):
+    return jnp.sum(over_rows(values), axis=1, keepdims=True)
 
 
 def coefficient_planes(coef, sources, levels, cols):
@@ -255,9 +260,9 @@
     def kernel(*refs):
         own, other, weights, sums, vert, prec, scale, mask, members = refs[:9]
         if with_weights:
-            out_z, out_e, out_q = refs[9:]
+            out_z, out_e, seen = refs[9:]
         else:
-            seen, out_z, out_e = refs[9:]
+            seen, out_z, out_e, now = refs[9:]
         out_z[...] = jnp.zeros(out_z.shape, jnp.float32)
         totals = [jnp.zeros((ROWS, cols), jnp.float32) for _ in range(count)]
         energy = jnp.zeros((ROWS, cols), jnp.float32)
@@ -277,31 +282,47 @@
                 ensemble += weights[m : m + 1, :cols] * members[m, plane]
             seen_now = wet * (SQRT_STATIC * (scale[plane] * static) + ens_scale * ensemble)
             weighted = wet * (prec[plane] * seen_now)
-            energy += seen_now * weighted
             if with_weights:
-                out_q[plane] = weighted
+                seen[plane] = seen_now
+                energy += seen_now * weighted
                 for m in range(count):
                     totals[m] += members[m, plane] * weighted
             else:
-                cross += seen_now * seen[plane]
+                now[plane] = seen_now
+                before = seen[plane]
+                energy += before * (prec[plane] * before)
+                cross += before * weighted
             out_z[plane * ROWS : (plane + 1) * ROWS, :cols] = scale[plane] * weighted
         if with_weights:
             project(out_z, base, totals, ens_scale)
         out_z[sums_at : sums_at + SUMS, :] = sums[...]
-        out_z[sums_at : sums_at + 1, :cols] = over_rows(energy)
-        if not with_weights:
-            out_z[sums_at + 1 : sums_at + 2, :cols] = over_rows(cross)
+        if with_weights:
+            out_z[sums_at : sums_at + 1, :cols] = over_rows(energy)
+        else:
+            energy, cross = whole(energy), whole(cross)
+            share = jnp.where(energy > 0.0, -cross / jnp.where(energy > 0.0, energy, 1.0), 0.0)
+            rest = jnp.zeros((ROWS, cols), jnp.float32)
+            left = jnp.zeros((ROWS, cols), jnp.float32)
+            for plane in range(planes):
+                before = seen[plane]
+                gap = now[plane] + share * before
+                rest += gap * (prec[plane] * gap)
+                left += before * (prec[plane] * gap)
+            place = (lax.axis_index("gx") * 2 + lax.axis_index("gy")) * 2 + lax.axis_index("gz")
+            own_lane = lanes_of((1, LANES)) == place
+            for index, value in enumerate((whole(rest), whole(left), share, energy)):
+                out_z[sums_at + index : sums_at + index + 1, :] = jnp.where(own_lane, value, 0.0)
         pack_edges(out_e, [tile(out_z, plane) for plane in range(planes)], cols)
         out_e[edge_rows:, :] = out_z[base:, :]
 
     tail = (ROWS * with_weights) + SUMS
     outs = [f32(base + tail, LANES), f32(edge_rows + tail, LANES)]
     if with_weights:
-        outs.append(f32(planes, ROWS, cols))
-    return kernel, outs
-
-
-def mix_back(first, planes, levels, cols, tail):
+        return kernel, outs + [f32(planes, ROWS, cols)], ()
+    return kernel, outs, [pltpu.VMEM((planes, ROWS, cols), jnp.float32)]
+
+
+def mix_back(first, far, planes, levels, cols, tail):
     base = planes * ROWS
     coefs = 3 * levels if first else 0
     fields = planes // levels
@@ -317,7 +338,8 @@
 
         def put(index, values):
             out_all[index * ROWS : (index + 1) * ROWS, :] = values
-            out_near[index * 8 : (index + 1) * 8, :] = jnp.where(upper, values[:8], values[8:])
+            if far:
+                out_near[index * 8 : (index + 1) * 8, :] = jnp.where(upper, values[:8], values[8:])
 
         for field in range(fields):
             mine = [with_edge(tile(own, field * levels + l), edge, field * levels + l, cols) for l in range(levels)]
@@ -336,177 +358,179 @@
         packed = -(-(planes + coefs) // GROUP) * ROWS
         total = (own[base:, :] + other[base:, :]) + (edge[packed:, :] + edge_other[packed:, :])
         out_all[(planes + coefs) * ROWS :, :] = total
-        out_near[(planes + coefs) * 8 :, :] = total
+        out_near[far * (planes + coefs) * 8 :, :] = total
 
     count = planes + coefs
-    return kernel, [f32(count * ROWS + tail, LANES), f32(count * 8 + tail, LANES)]
-
-
-def window(target, index, own, first, near, third, slot):
+    return kernel, [f32(count * ROWS + tail, LANES), f32(far * count * 8 + tail, LANES)]
+
+
+def fetch_window(target, nat, index, own, first, near, third, slot):
     even = lax.rem(lax.axis_index("gx"), 2) == 0
     one, three = tile(first, slot), tile(third, slot)
-    target[index, 0:16, :] = tile(own, slot)
-    target[index, 16:32, :] = jnp.where(even, one, three)
-    target[index, 32:40, :] = tile(near, slot, 8)
-    target[index, 40:56, :] = jnp.where(even, three, one)
-
-
-def run_steps(start, other, coef, steps, planes, levels):
-    def one(number, source, target):
-        number = number.astype(jnp.float32)
+    nat[index, 0:16, :] = tile(own, slot)
+    nat[index, 16:32, :] = jnp.where(even, one, three)
+    nat[index, 32:40, :] = jnp.zeros((8, LANES), jnp.float32) if near is None else tile(near, slot, 8)
+    nat[index, 40:56, :] = jnp.where(even, three, one)
+    for t in range(TILES):
+        target[index, t * 8 : (t + 1) * 8, :] = nat[index, pl.ds(t, 8, stride=TILES), :]
+
+
+def own_rows(values, nat, index):
+    for t in range(TILES):
+        nat[index, pl.ds(t, 8, stride=TILES), :] = values[t * 8 : (t + 1) * 8]
+    return nat[index, 0:ROWS, :]
+
+
+def eight(ref, *index):
+    return [ref[(*index, pl.ds(t * 8, 8), slice(None))] for t in range(TILES)]
+
+
+def after(tiles):
+    return tiles[1:] + [pltpu.roll(tiles[0], 7, 0)]
+
+
+def run_steps(buf, coef, steps, planes, levels):
+    for number in range(KMAX):
         for level in range(levels):
+            east, north = eight(coef, 0, level), eight(coef, 1, level)
             for field in range(planes // levels):
                 plane = field * levels + level
-                u = source[plane]
-                rows = u.shape[0]
-                change = (
-                    coef[0, level] * pltpu.roll(u, rows - 1, 0)
-                    + coef[1, level] * pltpu.roll(u, 1, 0)
-                    + coef[2, level] * pltpu.roll(u, LANES - 1, 1)
-                    + coef[3, level] * pltpu.roll(u, 1, 1)
-                    - coef[4, level] * u
-                )
-                active = jnp.where(steps[field : field + 1, :] > number, 1.0, 0.0).astype(jnp.float32)
-                target[plane] = u + active * change
-
-    def pair(index, carry):
-        one(2 * index, start, other)
-        one(2 * index + 1, other, start)
-        return carry
-
-    lax.fori_loop(0, KMAX // 2, pair, 0)
+                active = jnp.where(steps[field : field + 1, :] > float(number), 1.0, 0.0).astype(jnp.float32)
+                u = eight(buf, plane)
+                flux_east = [c * (v - w) for c, v, w in zip(east, after(u), u, strict=True)]
+                flux_west = [pltpu.roll(flux_east[-1], 1, 0)] + flux_east[:-1]
+                for t in range(TILES):
+                    flux_north = north[t] * (pltpu.roll(u[t], LANES - 1, 1) - u[t])
+                    change = (flux_east[t] - flux_west[t]) + (flux_north - pltpu.roll(flux_north, 1, 1))
+                    buf[plane, t * 8 : (t + 1) * 8, :] = u[t] + active * change
 
 
 def make_coefs(coef, kinds, levels, cols):
-    lane = lanes_of((WIN, LANES))
     last = jnp.where(lax.axis_index("gy") == 0, LANES - 1, cols - 1)
+    inside = lanes_of((8, LANES)) != last
     for level in range(levels):
-        kx, ky, wet = (kinds[kind * levels + level] for kind in range(3))
-        east = kx * wet * pltpu.roll(wet, WIN - 1, 0)
-        north = ky * wet * pltpu.roll(wet, LANES - 1, 1)
-        north = jnp.where(lane == last, 0.0, north)
-        west = pltpu.roll(east, 1, 0)
-        south = pltpu.roll(north, 1, 1)
-        for index, values in enumerate((east, west, north, south, (east + west) + (north + south))):
-            coef[index, level] = values
-
-
-def own_sum(values, cols):
-    own = values[:ROWS]
-    return over_rows(jnp.where(lanes_of(own.shape) < cols, own, 0.0))
+        kx, ky, wet = (eight(kinds, kind * levels + level) for kind in range(3))
+        for t, beyond in enumerate(after(wet)):
+            rows = slice(t * 8, (t + 1) * 8)
+            coef[0, level, rows, :] = kx[t] * wet[t] * beyond
+            coef[1, level, rows, :] = jnp.where(inside, ky[t] * wet[t] * pltpu.roll(wet[t], LANES - 1, 1), 0.0)
+
+
+def own_cells(cols):
+    row = lax.broadcasted_iota(jnp.int32, (WIN, LANES), 0)
+    row = lax.rem(row, 8) * TILES + lax.div(row, 8)
+    return jnp.where((row < ROWS) & (lanes_of((WIN, LANES)) < cols), 1.0, 0.0).astype(jnp.float32)
 
 
 def spread(values):
     return jnp.broadcast_to(jnp.sum(values, axis=1, keepdims=True), values.shape)
 
 
+def window_scratch(planes):
+    return [pltpu.VMEM((planes, WIN, LANES), jnp.float32)] * 2
+
+
 def first_diffuse(planes, levels, cols):
     coefs = 3 * levels
 
-    def kernel(own, first, near, third, steps, coef, resid, weights, sums, out_g, buf, kinds):
-        for plane in range(planes):
-            window(buf, plane, own, first, near, third, plane)
+    def kernel(own, first, near, third, steps, coef, resid, weights, sums, out_g, buf, nat):
         for index in range(coefs):
-            window(kinds, index, own, first, near, third, planes + index)
-        make_coefs(coef, kinds, levels, cols)
+            fetch_window(buf, nat, index, own, first, near, third, planes + index)
+        make_coefs(coef, buf, levels, cols)
+        for plane in range(planes):
+            fetch_window(buf, nat, plane, own, first, near, third, plane)
         at, near_at = (planes + coefs) * ROWS, (planes + coefs) * 8
         weights[...] = spread((own[at:, :] + first[at:, :]) + (near[near_at:, :] + third[at:, :]))
-        run_steps(buf, resid, coef, steps, planes, levels)
-        squares = jnp.zeros((ROWS, LANES), jnp.float32)
+        run_steps(buf, coef, steps, planes, levels)
+        squares = jnp.zeros((WIN, LANES), jnp.float32)
         for plane in range(planes):
             value = SQRT_STATIC * buf[plane]
             resid[plane] = value
             buf[plane] = value
-            squares += value[:ROWS] * value[:ROWS]
+            squares += value * value
         sums[...] = jnp.zeros(sums.shape, jnp.float32)
-        sums[2:3, :] = own_sum(squares, cols)
-        run_steps(buf, kinds, coef, steps, planes, levels)
-        for plane in range(planes):
-            out_g[plane * ROWS : (plane + 1) * ROWS, :] = buf[plane, :ROWS, :]
+        sums[4:5, :] = over_rows(own_cells(cols) * squares)
+        run_steps(buf, coef, steps, planes, levels)
+        for plane in range(planes):
+            out_g[plane * ROWS : (plane + 1) * ROWS, :] = own_rows(buf[plane], nat, plane)
 
     outs = [
-        f32(5, levels, WIN, LANES),
+        f32(2, levels, WIN, LANES),
         f32(planes, WIN, LANES),
         f32(ROWS, LANES),
         f32(SUMS, LANES),
         f32(planes * ROWS, LANES),
     ]
-    scratch = [pltpu.VMEM((planes, WIN, LANES), jnp.float32)] * 2
-    return kernel, outs, scratch
+    return kernel, outs, window_scratch(planes)
 
 
 def second_diffuse(planes, levels, cols):
-    def kernel(own, first, near, third, steps, coef, resid, weights, image, new, new_w, sums, facts, out_g, buf, spare):
-        for plane in range(planes):
-            window(buf, plane, own, first, near, third, plane)
+    def kernel(own, first, near, third, steps, coef, resid, weights, image, new, new_w, sums, facts, out_g, buf, nat):
+        for plane in range(planes):
+            fetch_window(buf, nat, plane, own, first, near, third, plane)
         at, near_at = planes * ROWS, planes * 8
         total = spread((own[at:, :] + first[at:, :]) + (near[near_at:, :] + third[at:, :]))
         energy = total[ROWS : ROWS + 1]
-        rr = total[ROWS + 2 : ROWS + 3] + over_rows(weights[...] * weights[...])
-        curvature = rr + energy
-        step = rr / curvature
-        new_weights = weights[...] - step * (weights[...] + total[:ROWS])
-        new_w[...] = new_weights
+        rr = total[ROWS + 4 : ROWS + 5] + over_rows(weights[...] * weights[...])
+        step = rr / (rr + energy)
+        new_w[...] = weights[...] - step * (weights[...] + total[:ROWS])
         facts[...] = jnp.zeros(facts.shape, jnp.float32)
         facts[0:1, :] = rr
-        facts[1:2, :] = energy
-        facts[2:3, :] = step
-        run_steps(buf, spare, coef, steps, planes, levels)
-        squares = jnp.zeros((ROWS, LANES), jnp.float32)
-        cross = jnp.zeros((ROWS, LANES), jnp.float32)
+        facts[1:2, :] = step
+        run_steps(buf, coef, steps, planes, levels)
+        squares = jnp.zeros((WIN, LANES), jnp.float32)
+        cross = jnp.zeros((WIN, LANES), jnp.float32)
         for plane in range(planes):
             direction = resid[plane]
             image_now = direction + SQRT_STATIC * buf[plane]
             value = direction - step * image_now
-            image[plane * ROWS : (plane + 1) * ROWS, :] = image_now[:ROWS]
-            new[plane * ROWS : (plane + 1) * ROWS, :] = value[:ROWS]
+            image[plane] = image_now
+            new[plane] = value
             buf[plane] = value
-            squares += value[:ROWS] * value[:ROWS]
-            cross += value[:ROWS] * direction[:ROWS]
+            squares += value * value
+            cross += value * direction
         sums[...] = jnp.zeros(sums.shape, jnp.float32)
-        sums[2:3, :] = own_sum(squares, cols)
-        sums[3:4, :] = own_sum(cross, cols)
-        run_steps(buf, spare, coef, steps, planes, levels)
-        for plane in range(planes):
-            out_g[plane * ROWS : (plane + 1) * ROWS, :] = buf[plane, :ROWS, :]
-
-    block = f32(planes * ROWS, LANES)
-    outs = [block, block, f32(ROWS, LANES), f32(SUMS, LANES), f32(SUMS, LANES), block]
-    scratch = [pltpu.VMEM((planes, WIN, LANES), jnp.float32)] * 2
-    return kernel, outs, scratch
+        sums[4:5, :] = over_rows(own_cells(cols) * squares)
+        sums[5:6, :] = over_rows(own_cells(cols) * cross)
+        run_steps(buf, coef, steps, planes, levels)
+        for plane in range(planes):
+            out_g[plane * ROWS : (plane + 1) * ROWS, :] = own_rows(buf[plane], nat, plane)
+
+    block = f32(planes, WIN, LANES)
+    outs = [block, block, f32(ROWS, LANES), f32(SUMS, LANES), f32(SUMS, LANES), f32(planes * ROWS, LANES)]
+    return kernel, outs, window_scratch(planes)
 
 
 def last_diffuse(planes, levels, cols):
     def kernel(
-        own, first, near, third, steps, coef, resid, weights, image, new, new_w, facts, control, control_w, final, buf, spare
+        own, first, near, third, steps, coef, resid, weights, image, new, new_w, facts, control, control_w, final, buf, nat
     ):
         for plane in range(planes):
-            window(buf, plane, own, first, near, third, plane)
-        at, near_at = planes * ROWS, planes * 8
-        total = spread((own[at:, :] + first[at:, :]) + (near[near_at:, :] + third[at:, :]))
-        rr, energy, step = facts[0:1, :], facts[1:2, :], facts[2:3, :]
-        new_energy, cross_energy = total[0:1], total[1:2]
-        new_rr = total[2:3] + over_rows(new_w[...] * new_w[...])
-        cross_rr = total[3:4] + over_rows(new_w[...] * weights[...])
+            fetch_window(buf, nat, plane, own, first, None, third, plane)
+        at = planes * ROWS
+        lanes = (own[at:, :] + first[at:, :]) + (near[...] + third[at:, :])
+        total = spread(lanes)
+        rr, step = facts[0:1, :], facts[1:2, :]
+        new_rr = total[4:5] + over_rows(new_w[...] * new_w[...])
+        cross_rr = total[5:6] + over_rows(new_w[...] * weights[...])
         ratio = new_rr / rr
+        gap = ratio - lanes[2:3]
+        energy = spread(lanes[0:1] + gap * (2.0 * lanes[1:2] + gap * lanes[3:4]))
         squares = new_rr + ratio * (2.0 * cross_rr + ratio * rr)
-        curvature = squares + (new_energy + ratio * (2.0 * cross_energy + ratio * energy))
-        new_step = new_rr / curvature
+        new_step = new_rr / (squares + energy)
         combined = step * weights[...] + new_step * (new_w[...] + ratio * weights[...])
         diagonal = lax.broadcasted_iota(jnp.int32, combined.shape, 0) == lanes_of(combined.shape)
         control_w[...] = over_rows(jnp.where(diagonal, combined, 0.0))[:, :ROWS]
-        run_steps(buf, spare, coef, steps, planes, levels)
-        for plane in range(planes):
-            value = tile(new, plane)
-            direction = resid[plane, :ROWS, :]
+        run_steps(buf, coef, steps, planes, levels)
+        for plane in range(planes):
+            direction, value = resid[plane], new[plane]
             new_direction = value + ratio * direction
-            new_image = (value + SQRT_STATIC * buf[plane, :ROWS, :]) + ratio * tile(image, plane)
-            control[plane] = (step * direction + new_step * new_direction)[:, :cols]
-            final[plane] = (value - new_step * new_image)[:, :cols]
+            new_image = (value + SQRT_STATIC * buf[plane]) + ratio * image[plane]
+            control[plane] = own_rows(step * direction + new_step * new_direction, nat, plane)[:, :cols]
+            final[plane] = own_rows(value - new_step * new_image, nat, plane)[:, :cols]
 
     outs = [f32(planes, ROWS, cols), f32(1, ROWS), f32(planes, ROWS, cols)]
-    scratch = [pltpu.VMEM((planes, WIN, LANES), jnp.float32)] * 2
-    return kernel, outs, scratch
+    return kernel, outs, window_scratch(planes)
 
 
 def moved_to(values, x, y, z):
@@ -540,22 +564,22 @@
     kernel, outs, scratch = start(planes, levels, cols, count)
     args = (innov, prec, scale, sea_mask, kappa_x, kappa_y, ens)
     out_z, out_e, coef_own = call(kernel, outs, [HBM] * 7, args, scratch, 56)
-    parts = across(mix_back(True, planes, levels, cols, ROWS), out_z, out_e, vert, (coef_own,))
+    parts = across(mix_back(True, True, planes, levels, cols, ROWS), out_z, out_e, vert, (coef_own,))
     kernel, outs, scratch = first_diffuse(planes, levels, cols)
     coef, resid, weights, sums, out_g = call(kernel, outs, [VMEM] * 5, (*parts, steps), scratch)
 
-    kernel, outs = observe(planes, levels, cols, count, True)
+    kernel, outs, scratch = observe(planes, levels, cols, count, True)
     args = (out_g, moved_to(out_g, 0, 0, 1), weights, sums, vert, prec, scale, sea_mask, ens)
-    out_z, out_e, seen = call(kernel, outs, [VMEM] * 9, args)
-    parts = across(mix_back(False, planes, levels, cols, ROWS + SUMS), out_z, out_e, vert, ())
+    out_z, out_e, seen = call(kernel, outs, [VMEM] * 9, args, scratch)
+    parts = across(mix_back(False, True, planes, levels, cols, ROWS + SUMS), out_z, out_e, vert, ())
     kernel, outs, scratch = second_diffuse(planes, levels, cols)
     args = (*parts, steps, coef, resid, weights)
     image, new, new_w, sums, facts, out_g = call(kernel, outs, [VMEM] * 8, args, scratch)
 
-    kernel, outs = observe(planes, levels, cols, count, False)
+    kernel, outs, scratch = observe(planes, levels, cols, count, False)
     args = (out_g, moved_to(out_g, 0, 0, 1), new_w, sums, vert, prec, scale, sea_mask, ens, seen)
-    out_z, out_e = call(kernel, outs, [VMEM] * 10, args)
-    parts = across(mix_back(False, planes, levels, cols, SUMS), out_z, out_e, vert, ())
+    out_z, out_e = call(kernel, outs, [VMEM] * 10, args, scratch)
+    parts = across(mix_back(False, False, planes, levels, cols, SUMS), out_z, out_e, vert, ())
     kernel, outs, scratch = last_diffuse(planes, levels, cols)
     args = (*parts, steps, coef, resid, weights, image, new, new_w, facts)
     control, control_w, final = call(kernel, outs, [VMEM] * 12, args, scratch)

time: 65.9 us -> 63.2 us (0.959)
  Pallas kernels: 14.5 us -> 12.7 us
  waiting for transfers between devices: 27.2 us -> 26.4 us
    pallas_call x9, Pallas kernels: 14.5 us -> 12.7 us  [call(): pl.pallas_call(kernel, out_shape=outs, in_specs=specs, out_specs=[VMEM] *...]
    ppermute x20, waiting for transfers between devices: 27.2 us -> 26.4 us  [moved_to(): lax.ppermute(values, AXES, [(number[a, b, c], number[a ^ x, b ^ y, c ^ z]...]
where the time goes in v3:
time: 63.2 us; the launch traced here: 63 us
  waiting for transfers between devices  26.4 us (42%)
  starting transfers between devices  21 us (33%)
  Pallas kernels  12.7 us (20%)
  local copies, waits for them, and re-layouts  2.07 us (3%)
  between operations  0.77 us (1%)
    ppermute x20, waiting for transfers between devices, moved_to(): lax.ppermute(values, AXES, [(number[a, b, c], number[a ^ x, b ^ y, c ^ z]...  26.4 us
    ppermute x20, starting transfers between devices, moved_to(): lax.ppermute(values, AXES, [(number[a, b, c], number[a ^ x, b ^ y, c ^ z]...  21 us
    pallas_call x9, Pallas kernels, call(): pl.pallas_call(kernel, out_shape=outs, in_specs=specs, out_specs=[VMEM] *...  12.7 us
    unnamed x17, local copies, waits for them, and re-layouts  1.83 us
  transfers between devices with their start and end apart: 20, of which 13 were waited for; matrix products, arithmetic and copies ran while one was open for 0% of the time, Pallas kernels for 0%

profile of v3, /device:TPU:0, one launch (start us, length us, event | category | flops | bytes accessed | tf_op | source)
XLA Modules:
  0.0 63.0 jit_solution(999843832500267675)
XLA Ops:
  0.6 0.0 copy-start.3
  0.6 0.0 copy-start
  0.7 0.0 copy-start.2
  0.7 0.0 copy-start.1
  0.7 0.0 copy-start.6
  0.7 0.0 copy-start.7
  0.7 2.4 %shard_map.112 = (f32[176,128]{1,0:T(8,128)}, f32[64,128]{1,0:T(8,128)}, f32[96,128]{1,0:T(8,128)}) custom-call(f32[10,16,108]{2,1,0:T(8,128)} %bitcast.16, f32[10,16,108]{2,1,0:T(8,128)} %bitcast.10, f32[10,16,108]{2,1,0:T(8,128)} %bitcast.13, s32[2,16,108]{2,1,0:T(8,128)} %refs_7_.3, f32[2,16,108]{2,1,0:T(8,128)} %refs_4_.1, f32[2,16,108]{2,1,0:T(8,128)} %refs_5_.1, ...), custom_call_target="tpu_custom_call" | custom-call | tf_op jit(solution)/shard_map/pallas_call | solution.py:163
  3.1 0.5 collective-permute-start
  3.6 2.6 %collective-permute-start.2 = (f32[64,128]{1,0:T(8,128)}, f32[64,128]{1,0:T(8,128)S(1)}, u32[]{:S(2)}, u32[]{:S(2)}) collective-permute-start(f32[64,128]{1,0:T(8,128)} %get-tuple-element.32), channel_id=1, source_target_pairs={{0,3},{1,2},{2,1},{3,0},{4,7},{5,6},{6,5},{7,4},{8,11},{9,10},{10,... | collective-permute-start | bytes 98312 | tf_op jit(solution)/shard_map/ppermute | solution.py:540
  6.2 0.0 collective-permute-start.1
  6.3 0.0 copy-done.6
  6.3 0.1 copy.13
  6.4 0.1 broadcast_in_dim.6
  6.5 1.7 %collective-permute-done.2.refs_3_ = f32[64,128]{1,0:T(8,128)S(1)} collective-permute-done((f32[64,128]{1,0:T(8,128)}, f32[64,128]{1,0:T(8,128)S(1)}, u32[]{:S(2)}, u32[]{:S(2)}) %collective-permute-start.2) | collective-permute-done | bytes 32800 | tf_op jit(solution)/shard_map/ppermute | solution.py:540
  8.1 2.2 %collective-permute-done.1.refs_2_ = f32[64,128]{1,0:T(8,128)S(1)} collective-permute-done((f32[64,128]{1,0:T(8,128)}, f32[64,128]{1,0:T(8,128)S(1)}, u32[]{:S(2)}, u32[]{:S(2)}) %collective-permute-start.1) | collective-permute-done | bytes 32800 | tf_op jit(solution)/shard_map/ppermute | solution.py:540
  10.3 0.0 collective-permute-done.refs_1_
  10.3 0.1 broadcast_in_dim.14.refs_4_
  10.4 0.9 %copy-done.4 = f32[176,128]{1,0:T(8,128)S(1)} copy-done((f32[176,128]{1,0:T(8,128)S(1)}, f32[176,128]{1,0:T(8,128)}, u32[]{:S(2)}) %copy-start.4) | copy-done | bytes 90136
  11.3 0.8 %copy-done.5 = f32[96,128]{1,0:T(8,128)S(1)} copy-done((f32[96,128]{1,0:T(8,128)S(1)}, f32[96,128]{1,0:T(8,128)}, u32[]{:S(2)}) %copy-start.5) | copy-done | bytes 49176
  12.1 0.1 shard_map.113
  12.2 3.7 %collective-permute-start.5 = (f32[272,128]{1,0:T(8,128)S(1)}, f32[272,128]{1,0:T(8,128)S(1)}, u32[]{:S(2)}, u32[]{:S(2)}) collective-permute-start(f32[272,128]{1,0:T(8,128)S(1)} %get-tuple-element.34.own), channel_id=1, source_target_pairs={{0,12},{1,13},{2,14},{3,15},{4,8},{5,9},{6,10},{7,11},{8,4},{9,5},... | collective-permute-start | bytes 417800 | tf_op jit(solution)/shard_map/ppermute | solution.py:540
  15.9 0.0 collective-permute-start.3
  15.9 0.8 %collective-permute-start.4 = (f32[144,128]{1,0:T(8,128)S(1)}, f32[144,128]{1,0:T(8,128)S(1)}, u32[]{:S(2)}, u32[]{:S(2)}) collective-permute-start(f32[144,128]{1,0:T(8,128)S(1)} %get-tuple-element.35), channel_id=1, source_target_pairs={{0,8},{1,9},{2,10},{3,11},{4,12},{5,13},{6,14},{7,15},{8,0},{9,1},... | collective-permute-start | bytes 221192 | tf_op jit(solution)/shard_map/ppermute | solution.py:540
  16.7 0.0 copy-done.7
  16.7 7.3 %collective-permute-done.4.near = f32[144,128]{1,0:T(8,128)S(1)} collective-permute-done((f32[144,128]{1,0:T(8,128)S(1)}, f32[144,128]{1,0:T(8,128)S(1)}, u32[]{:S(2)}, u32[]{:S(2)}) %collective-permute-start.4) | collective-permute-done | bytes 73760 | tf_op jit(solution)/shard_map/ppermute | solution.py:540
  24.0 0.0 collective-permute-done.5.third
  24.0 0.0 collective-permute-done.3.first
  24.0 0.1 broadcast_in_dim.15.steps
  24.0 3.4 %shard_map.114 = (f32[2,2,56,128]{3,2,1,0:T(8,128)S(1)}, f32[10,56,128]{2,1,0:T(8,128)S(1)}, f32[16,128]{1,0:T(8,128)S(1)}, f32[8,128]{1,0:T(8,128)S(1)}, f32[160,128]{1,0:T(8,128)S(1)}) custom-call(f32[272,128]{1,0:T(8,128)S(1)} %get-tuple-element.34.own, f32[272,128]{1,0:T(8,128)S(1)} %collective-permute-done.3.first, ...), custom_call_target="tpu_custom_call" | custom-call | tf_op jit(solution)/shard_map/pallas_call | solution.py:163
  27.4 0.1 collective-permute-start.6
  27.5 1.3 %collective-permute-done.6.refs_1_ = f32[160,128]{1,0:T(8,128)S(1)} collective-permute-done((f32[160,128]{1,0:T(8,128)S(1)}, f32[160,128]{1,0:T(8,128)S(1)}, u32[]{:S(2)}, u32[]{:S(2)}) %collective-permute-start.6) | collective-permute-done | bytes 81952 | tf_op jit(solution)/shard_map/ppermute | solution.py:540
  28.8 0.0 copy-done.3
  28.8 0.3 shard_map.115
  29.1 0.2 collective-permute-start.7
  29.3 1.0 %collective-permute-start.9 = (f32[56,128]{1,0:T(8,128)S(1)}, f32[56,128]{1,0:T(8,128)S(1)}, u32[]{:S(2)}, u32[]{:S(2)}) collective-permute-start(f32[56,128]{1,0:T(8,128)S(1)} %get-tuple-element.40), channel_id=1, source_target_pairs={{0,3},{1,2},{2,1},{3,0},{4,7},{5,6},{6,5},{7,4},{8,11},{9,10},{10,... | collective-permute-start | bytes 86024 | tf_op jit(solution)/shard_map/ppermute | solution.py:540
  30.3 1.0 %collective-permute-start.8 = (f32[56,128]{1,0:T(8,128)S(1)}, f32[56,128]{1,0:T(8,128)S(1)}, u32[]{:S(2)}, u32[]{:S(2)}) collective-permute-start(f32[56,128]{1,0:T(8,128)S(1)} %get-tuple-element.40), channel_id=1, source_target_pairs={{0,2},{1,3},{2,0},{3,1},{4,6},{5,7},{6,4},{7,5},{8,10},{9,11},{10,... | collective-permute-start | bytes 86024 | tf_op jit(solution)/shard_map/ppermute | solution.py:540
  31.3 1.3 %collective-permute-done.9.refs_3_ = f32[56,128]{1,0:T(8,128)S(1)} collective-permute-done((f32[56,128]{1,0:T(8,128)S(1)}, f32[56,128]{1,0:T(8,128)S(1)}, u32[]{:S(2)}, u32[]{:S(2)}) %collective-permute-start.9) | collective-permute-done | bytes 28704 | tf_op jit(solution)/shard_map/ppermute | solution.py:540
  32.6 1.5 %collective-permute-done.8.refs_2_ = f32[56,128]{1,0:T(8,128)S(1)} collective-permute-done((f32[56,128]{1,0:T(8,128)S(1)}, f32[56,128]{1,0:T(8,128)S(1)}, u32[]{:S(2)}, u32[]{:S(2)}) %collective-permute-start.8) | collective-permute-done | bytes 28704 | tf_op jit(solution)/shard_map/ppermute | solution.py:540
  34.2 0.0 collective-permute-done.7.refs_1_
  34.2 0.1 shard_map.116
  34.3 1.9 %collective-permute-start.12 = (f32[184,128]{1,0:T(8,128)S(1)}, f32[184,128]{1,0:T(8,128)S(1)}, u32[]{:S(2)}, u32[]{:S(2)}) collective-permute-start(f32[184,128]{1,0:T(8,128)S(1)} %get-tuple-element.41.own), channel_id=1, source_target_pairs={{0,12},{1,13},{2,14},{3,15},{4,8},{5,9},{6,10},{7,11},{8,4},{9,5},... | collective-permute-start | bytes 282632 | tf_op jit(solution)/shard_map/ppermute | solution.py:540
  36.1 0.7 %collective-permute-start.10 = (f32[184,128]{1,0:T(8,128)S(1)}, f32[184,128]{1,0:T(8,128)S(1)}, u32[]{:S(2)}, u32[]{:S(2)}) collective-permute-start(f32[184,128]{1,0:T(8,128)S(1)} %get-tuple-element.41.own), channel_id=1, source_target_pairs={{0,4},{1,5},{2,6},{3,7},{4,0},{5,1},{6,2},{7,3},{8,12},{9,13},{10,... | collective-permute-start | bytes 282632 | tf_op jit(solution)/shard_map/ppermute | solution.py:540
  36.9 1.9 %collective-permute-start.11 = (f32[104,128]{1,0:T(8,128)S(1)}, f32[104,128]{1,0:T(8,128)S(1)}, u32[]{:S(2)}, u32[]{:S(2)}) collective-permute-start(f32[104,128]{1,0:T(8,128)S(1)} %get-tuple-element.42), channel_id=1, source_target_pairs={{0,8},{1,9},{2,10},{3,11},{4,12},{5,13},{6,14},{7,15},{8,0},{9,1},... | collective-permute-start | bytes 159752 | tf_op jit(solution)/shard_map/ppermute | solution.py:540
  38.7 3.9 %collective-permute-done.11.near = f32[104,128]{1,0:T(8,128)S(1)} collective-permute-done((f32[104,128]{1,0:T(8,128)S(1)}, f32[104,128]{1,0:T(8,128)S(1)}, u32[]{:S(2)}, u32[]{:S(2)}) %collective-permute-start.11) | collective-permute-done | bytes 53280 | tf_op jit(solution)/shard_map/ppermute | solution.py:540
  42.7 0.0 collective-permute-done.12.third
  42.7 0.3 collective-permute-done.10.first
  43.0 3.4 %shard_map.117 = (f32[10,56,128]{2,1,0:T(8,128)S(1)}, f32[10,56,128]{2,1,0:T(8,128)S(1)}, f32[16,128]{1,0:T(8,128)S(1)}, f32[8,128]{1,0:T(8,128)S(1)}, f32[8,128]{1,0:T(8,128)S(1)}, /*index=5*/f32[160,128]{1,0:T(8,128)S(1)}) custom-call(f32[184,128]{1,0:T(8,128)S(1)} %get-tuple-element.41.own, f32[184,128]{1,0:T(8,128)S(1)} %collective-permute-done.10.first, ...), custom_call_target="tpu_custom_call" | custom-call | tf_op jit(solution)/shard_map/pallas_call | solution.py:163
  46.4 0.1 collective-permute-start.13
  46.4 1.3 %collective-permute-done.13.refs_1_ = f32[160,128]{1,0:T(8,128)S(1)} collective-permute-done((f32[160,128]{1,0:T(8,128)S(1)}, f32[160,128]{1,0:T(8,128)S(1)}, u32[]{:S(2)}, u32[]{:S(2)}) %collective-permute-start.13) | collective-permute-done | bytes 81952 | tf_op jit(solution)/shard_map/ppermute | solution.py:540
  47.7 0.4 shard_map.118
  48.1 0.2 collective-permute-start.14
  48.2 1.0 %collective-permute-start.16 = (f32[40,128]{1,0:T(8,128)S(1)}, f32[40,128]{1,0:T(8,128)S(1)}, u32[]{:S(2)}, u32[]{:S(2)}) collective-permute-start(f32[40,128]{1,0:T(8,128)S(1)} %get-tuple-element.50), channel_id=1, source_target_pairs={{0,3},{1,2},{2,1},{3,0},{4,7},{5,6},{6,5},{7,4},{8,11},{9,10},{10,... | collective-permute-start | bytes 61448 | tf_op jit(solution)/shard_map/ppermute | solution.py:540
  49.2 1.0 %collective-permute-start.15 = (f32[40,128]{1,0:T(8,128)S(1)}, f32[40,128]{1,0:T(8,128)S(1)}, u32[]{:S(2)}, u32[]{:S(2)}) collective-permute-start(f32[40,128]{1,0:T(8,128)S(1)} %get-tuple-element.50), channel_id=1, source_target_pairs={{0,2},{1,3},{2,0},{3,1},{4,6},{5,7},{6,4},{7,5},{8,10},{9,11},{10,... | collective-permute-start | bytes 61448 | tf_op jit(solution)/shard_map/ppermute | solution.py:540
  50.2 1.2 %collective-permute-done.16.refs_3_ = f32[40,128]{1,0:T(8,128)S(1)} collective-permute-done((f32[40,128]{1,0:T(8,128)S(1)}, f32[40,128]{1,0:T(8,128)S(1)}, u32[]{:S(2)}, u32[]{:S(2)}) %collective-permute-start.16) | collective-permute-done | bytes 20512 | tf_op jit(solution)/shard_map/ppermute | solution.py:540
  51.5 1.6 %collective-permute-done.15.refs_2_ = f32[40,128]{1,0:T(8,128)S(1)} collective-permute-done((f32[40,128]{1,0:T(8,128)S(1)}, f32[40,128]{1,0:T(8,128)S(1)}, u32[]{:S(2)}, u32[]{:S(2)}) %collective-permute-start.15) | collective-permute-done | bytes 20512 | tf_op jit(solution)/shard_map/ppermute | solution.py:540
  53.0 0.0 collective-permute-done.14.refs_1_
  53.0 0.1 shard_map.119
  53.2 2.3 %collective-permute-start.19 = (f32[168,128]{1,0:T(8,128)S(1)}, f32[168,128]{1,0:T(8,128)S(1)}, u32[]{:S(2)}, u32[]{:S(2)}) collective-permute-start(f32[168,128]{1,0:T(8,128)S(1)} %get-tuple-element.51.own), channel_id=1, source_target_pairs={{0,12},{1,13},{2,14},{3,15},{4,8},{5,9},{6,10},{7,11},{8,4},{9,5},... | collective-permute-start | bytes 258056 | tf_op jit(solution)/shard_map/ppermute | solution.py:540
  55.5 0.0 collective-permute-start.17
  55.5 2.1 %collective-permute-start.18 = (f32[8,128]{1,0:T(8,128)S(1)}, f32[8,128]{1,0:T(8,128)S(1)}, u32[]{:S(2)}, u32[]{:S(2)}) collective-permute-start(f32[8,128]{1,0:T(8,128)S(1)} %get-tuple-element.52), channel_id=1, source_target_pairs={{0,8},{1,9},{2,10},{3,11},{4,12},{5,13},{6,14},{7,15},{8,0},{9,1},... | collective-permute-start | bytes 12296 | tf_op jit(solution)/shard_map/ppermute | solution.py:540
  57.6 2.4 %collective-permute-done.18.near = f32[8,128]{1,0:T(8,128)S(1)} collective-permute-done((f32[8,128]{1,0:T(8,128)S(1)}, f32[8,128]{1,0:T(8,128)S(1)}, u32[]{:S(2)}, u32[]{:S(2)}) %collective-permute-start.18) | collective-permute-done | bytes 4128 | tf_op jit(solution)/shard_map/ppermute | solution.py:540
  60.0 0.0 collective-permute-done.19.third
  60.0 0.5 collective-permute-done.17.first
  60.5 2.5 %shard_map.120 = (f32[10,16,108]{2,1,0:T(8,128)}, f32[1,16]{1,0:T(1,128)}, f32[10,16,108]{2,1,0:T(8,128)}) custom-call(f32[168,128]{1,0:T(8,128)S(1)} %get-tuple-element.51.own, f32[168,128]{1,0:T(8,128)S(1)} %collective-permute-done.17.first, f32[8,128]{1,0:T(8,128)S(1)} %collective-permute-done.18.near, f32[168,128]{1,0:T(8,128)S(1)} %collective-permute-done.19.third, ...), custom_call_target="tpu_custom_call" | custom-call | tf_op jit(solution)/shard_map/pallas_call | solution.py:163
  (6 shorter events, 0.0 us)
Async XLA Ops:
  0.6 28.1 %copy-start.3 = (s32[2,16,108]{2,1,0:T(8,128)S(1)}, s32[2,16,108]{2,1,0:T(8,128)}, u32[]{:S(2)}) copy-start(s32[2,16,108]{2,1,0:T(8,128)} %refs_7_.3) | copy-start | bytes 41476
  0.6 28.1 %copy-start = (f32[16,5,2,16,108]{4,3,2,1,0:T(8,128)S(1)}, f32[16,5,2,16,108]{4,3,2,1,0:T(8,128)}, u32[]{:S(2)}) copy-start(f32[16,5,2,16,108]{4,3,2,1,0:T(8,128)} %param.15) | copy-start | bytes 3317764
  0.7 28.1 %copy-start.2 = (f32[5,2,16,108]{3,2,1,0:T(8,128)S(1)}, f32[5,2,16,108]{3,2,1,0:T(8,128)}, u32[]{:S(2)}) copy-start(f32[5,2,16,108]{3,2,1,0:T(8,128)} %param.11) | copy-start | bytes 207364
  0.7 28.1 %copy-start.1 = (f32[5,2,16,108]{3,2,1,0:T(8,128)S(1)}, f32[5,2,16,108]{3,2,1,0:T(8,128)}, u32[]{:S(2)}) copy-start(f32[5,2,16,108]{3,2,1,0:T(8,128)} %param.10) | copy-start | bytes 207364
  0.7 5.6 %copy-start.6 = (f32[5,4,4]{0,2,1:T(4,128)S(1)}, f32[5,4,4]{0,2,1:T(4,128)}, u32[]{:S(2)}) copy-start(f32[5,4,4]{0,2,1:T(4,128)} %param.16) | copy-start | bytes 964
  0.7 16.0 %copy-start.7 = (s32[5]{0:T(128)S(1)}, s32[5]{0:T(128)}, u32[]{:S(2)}) copy-start(s32[5]{0:T(128)} %param.17) | copy-start | bytes 64
  3.1 7.3 %collective-permute-start = (f32[176,128]{1,0:T(8,128)}, f32[176,128]{1,0:T(8,128)S(1)}, u32[]{:S(2)}, u32[]{:S(2)}) collective-permute-start(f32[176,128]{1,0:T(8,128)} %get-tuple-element.31.refs_0_), channel_id=1, source_target_pairs={{0,1},{1,0},{2,3},{3,2},{4,5},{5,4},{6,7},{7,6},{8,9},{9,8},{10,11... | collective-permute-start | bytes 270344 | tf_op jit(solution)/shard_map/ppermute | solution.py:540
  3.6 4.5 %collective-permute-start.2 = (f32[64,128]{1,0:T(8,128)}, f32[64,128]{1,0:T(8,128)S(1)}, u32[]{:S(2)}, u32[]{:S(2)}) collective-permute-start(f32[64,128]{1,0:T(8,128)} %get-tuple-element.32), channel_id=1, source_target_pairs={{0,3},{1,2},{2,1},{3,0},{4,7},{5,6},{6,5},{7,4},{8,11},{9,10},{10,... | collective-permute-start | bytes 98312 | tf_op jit(solution)/shard_map/ppermute | solution.py:540
  6.2 4.1 %collective-permute-start.1 = (f32[64,128]{1,0:T(8,128)}, f32[64,128]{1,0:T(8,128)S(1)}, u32[]{:S(2)}, u32[]{:S(2)}) collective-permute-start(f32[64,128]{1,0:T(8,128)} %get-tuple-element.32), channel_id=1, source_target_pairs={{0,2},{1,3},{2,0},{3,1},{4,6},{5,7},{6,4},{7,5},{8,10},{9,11},{10,... | collective-permute-start | bytes 98312 | tf_op jit(solution)/shard_map/ppermute | solution.py:540
  10.4 0.9 %copy-start.4 = (f32[176,128]{1,0:T(8,128)S(1)}, f32[176,128]{1,0:T(8,128)}, u32[]{:S(2)}) copy-start(f32[176,128]{1,0:T(8,128)} %get-tuple-element.31.refs_0_) | copy-start | bytes 270340
  11.3 0.8 %copy-start.5 = (f32[96,128]{1,0:T(8,128)S(1)}, f32[96,128]{1,0:T(8,128)}, u32[]{:S(2)}) copy-start(f32[96,128]{1,0:T(8,128)} %get-tuple-element.33.refs_5_) | copy-start | bytes 147460
  12.2 11.7 %collective-permute-start.5 = (f32[272,128]{1,0:T(8,128)S(1)}, f32[272,128]{1,0:T(8,128)S(1)}, u32[]{:S(2)}, u32[]{:S(2)}) collective-permute-start(f32[272,128]{1,0:T(8,128)S(1)} %get-tuple-element.34.own), channel_id=1, source_target_pairs={{0,12},{1,13},{2,14},{3,15},{4,8},{5,9},{6,10},{7,11},{8,4},{9,5},... | collective-permute-start | bytes 417800 | tf_op jit(solution)/shard_map/ppermute | solution.py:540
  15.9 8.1 %collective-permute-start.3 = (f32[272,128]{1,0:T(8,128)S(1)}, f32[272,128]{1,0:T(8,128)S(1)}, u32[]{:S(2)}, u32[]{:S(2)}) collective-permute-start(f32[272,128]{1,0:T(8,128)S(1)} %get-tuple-element.34.own), channel_id=1, source_target_pairs={{0,4},{1,5},{2,6},{3,7},{4,0},{5,1},{6,2},{7,3},{8,12},{9,13},{10,... | collective-permute-start | bytes 417800 | tf_op jit(solution)/shard_map/ppermute | solution.py:540
  15.9 8.0 %collective-permute-start.4 = (f32[144,128]{1,0:T(8,128)S(1)}, f32[144,128]{1,0:T(8,128)S(1)}, u32[]{:S(2)}, u32[]{:S(2)}) collective-permute-start(f32[144,128]{1,0:T(8,128)S(1)} %get-tuple-element.35), channel_id=1, source_target_pairs={{0,8},{1,9},{2,10},{3,11},{4,12},{5,13},{6,14},{7,15},{8,0},{9,1},... | collective-permute-start | bytes 221192 | tf_op jit(solution)/shard_map/ppermute | solution.py:540
  27.4 1.3 %collective-permute-start.6 = (f32[160,128]{1,0:T(8,128)S(1)}, f32[160,128]{1,0:T(8,128)S(1)}, u32[]{:S(2)}, u32[]{:S(2)}) collective-permute-start(f32[160,128]{1,0:T(8,128)S(1)} %get-tuple-element.36.refs_0_), channel_id=1, source_target_pairs={{0,1},{1,0},{2,3},{3,2},{4,5},{5,4},{6,7},{7,6},{8,9},{9,8},{10,11... | collective-permute-start | bytes 245768 | tf_op jit(solution)/shard_map/ppermute | solution.py:540
  29.1 5.0 %collective-permute-start.7 = (f32[184,128]{1,0:T(8,128)S(1)}, f32[184,128]{1,0:T(8,128)S(1)}, u32[]{:S(2)}, u32[]{:S(2)}) collective-permute-start(f32[184,128]{1,0:T(8,128)S(1)} %get-tuple-element.39.refs_0_), channel_id=1, source_target_pairs={{0,1},{1,0},{2,3},{3,2},{4,5},{5,4},{6,7},{7,6},{8,9},{9,8},{10,11... | collective-permute-start | bytes 282632 | tf_op jit(solution)/shard_map/ppermute | solution.py:540
  29.3 3.3 %collective-permute-start.9 = (f32[56,128]{1,0:T(8,128)S(1)}, f32[56,128]{1,0:T(8,128)S(1)}, u32[]{:S(2)}, u32[]{:S(2)}) collective-permute-start(f32[56,128]{1,0:T(8,128)S(1)} %get-tuple-element.40), channel_id=1, source_target_pairs={{0,3},{1,2},{2,1},{3,0},{4,7},{5,6},{6,5},{7,4},{8,11},{9,10},{10,... | collective-permute-start | bytes 86024 | tf_op jit(solution)/shard_map/ppermute | solution.py:540
  30.3 3.9 %collective-permute-start.8 = (f32[56,128]{1,0:T(8,128)S(1)}, f32[56,128]{1,0:T(8,128)S(1)}, u32[]{:S(2)}, u32[]{:S(2)}) collective-permute-start(f32[56,128]{1,0:T(8,128)S(1)} %get-tuple-element.40), channel_id=1, source_target_pairs={{0,2},{1,3},{2,0},{3,1},{4,6},{5,7},{6,4},{7,5},{8,10},{9,11},{10,... | collective-permute-start | bytes 86024 | tf_op jit(solution)/shard_map/ppermute | solution.py:540
  34.3 8.4 %collective-permute-start.12 = (f32[184,128]{1,0:T(8,128)S(1)}, f32[184,128]{1,0:T(8,128)S(1)}, u32[]{:S(2)}, u32[]{:S(2)}) collective-permute-start(f32[184,128]{1,0:T(8,128)S(1)} %get-tuple-element.41.own), channel_id=1, source_target_pairs={{0,12},{1,13},{2,14},{3,15},{4,8},{5,9},{6,10},{7,11},{8,4},{9,5},... | collective-permute-start | bytes 282632 | tf_op jit(solution)/shard_map/ppermute | solution.py:540
  36.1 6.8 %collective-permute-start.10 = (f32[184,128]{1,0:T(8,128)S(1)}, f32[184,128]{1,0:T(8,128)S(1)}, u32[]{:S(2)}, u32[]{:S(2)}) collective-permute-start(f32[184,128]{1,0:T(8,128)S(1)} %get-tuple-element.41.own), channel_id=1, source_target_pairs={{0,4},{1,5},{2,6},{3,7},{4,0},{5,1},{6,2},{7,3},{8,12},{9,13},{10,... | collective-permute-start | bytes 282632 | tf_op jit(solution)/shard_map/ppermute | solution.py:540
  36.9 5.8 %collective-permute-start.11 = (f32[104,128]{1,0:T(8,128)S(1)}, f32[104,128]{1,0:T(8,128)S(1)}, u32[]{:S(2)}, u32[]{:S(2)}) collective-permute-start(f32[104,128]{1,0:T(8,128)S(1)} %get-tuple-element.42), channel_id=1, source_target_pairs={{0,8},{1,9},{2,10},{3,11},{4,12},{5,13},{6,14},{7,15},{8,0},{9,1},... | collective-permute-start | bytes 159752 | tf_op jit(solution)/shard_map/ppermute | solution.py:540
  46.4 1.3 %collective-permute-start.13 = (f32[160,128]{1,0:T(8,128)S(1)}, f32[160,128]{1,0:T(8,128)S(1)}, u32[]{:S(2)}, u32[]{:S(2)}) collective-permute-start(f32[160,128]{1,0:T(8,128)S(1)} %get-tuple-element.45.refs_0_), channel_id=1, source_target_pairs={{0,1},{1,0},{2,3},{3,2},{4,5},{5,4},{6,7},{7,6},{8,9},{9,8},{10,11... | collective-permute-start | bytes 245768 | tf_op jit(solution)/shard_map/ppermute | solution.py:540
  48.1 5.0 %collective-permute-start.14 = (f32[168,128]{1,0:T(8,128)S(1)}, f32[168,128]{1,0:T(8,128)S(1)}, u32[]{:S(2)}, u32[]{:S(2)}) collective-permute-start(f32[168,128]{1,0:T(8,128)S(1)} %get-tuple-element.49.refs_0_), channel_id=1, source_target_pairs={{0,1},{1,0},{2,3},{3,2},{4,5},{5,4},{6,7},{7,6},{8,9},{9,8},{10,11... | collective-permute-start | bytes 258056 | tf_op jit(solution)/shard_map/ppermute | solution.py:540
  48.2 3.2 %collective-permute-start.16 = (f32[40,128]{1,0:T(8,128)S(1)}, f32[40,128]{1,0:T(8,128)S(1)}, u32[]{:S(2)}, u32[]{:S(2)}) collective-permute-start(f32[40,128]{1,0:T(8,128)S(1)} %get-tuple-element.50), channel_id=1, source_target_pairs={{0,3},{1,2},{2,1},{3,0},{4,7},{5,6},{6,5},{7,4},{8,11},{9,10},{10,... | collective-permute-start | bytes 61448 | tf_op jit(solution)/shard_map/ppermute | solution.py:540
  49.2 3.8 %collective-permute-start.15 = (f32[40,128]{1,0:T(8,128)S(1)}, f32[40,128]{1,0:T(8,128)S(1)}, u32[]{:S(2)}, u32[]{:S(2)}) collective-permute-start(f32[40,128]{1,0:T(8,128)S(1)} %get-tuple-element.50), channel_id=1, source_target_pairs={{0,2},{1,3},{2,0},{3,1},{4,6},{5,7},{6,4},{7,5},{8,10},{9,11},{10,... | collective-permute-start | bytes 61448 | tf_op jit(solution)/shard_map/ppermute | solution.py:540
  53.2 6.8 %collective-permute-start.19 = (f32[168,128]{1,0:T(8,128)S(1)}, f32[168,128]{1,0:T(8,128)S(1)}, u32[]{:S(2)}, u32[]{:S(2)}) collective-permute-start(f32[168,128]{1,0:T(8,128)S(1)} %get-tuple-element.51.own), channel_id=1, source_target_pairs={{0,12},{1,13},{2,14},{3,15},{4,8},{5,9},{6,10},{7,11},{8,4},{9,5},... | collective-permute-start | bytes 258056 | tf_op jit(solution)/shard_map/ppermute | solution.py:540
  55.5 5.0 %collective-permute-start.17 = (f32[168,128]{1,0:T(8,128)S(1)}, f32[168,128]{1,0:T(8,128)S(1)}, u32[]{:S(2)}, u32[]{:S(2)}) collective-permute-start(f32[168,128]{1,0:T(8,128)S(1)} %get-tuple-element.51.own), channel_id=1, source_target_pairs={{0,4},{1,5},{2,6},{3,7},{4,0},{5,1},{6,2},{7,3},{8,12},{9,13},{10,... | collective-permute-start | bytes 258056 | tf_op jit(solution)/shard_map/ppermute | solution.py:540
  55.5 4.5 %collective-permute-start.18 = (f32[8,128]{1,0:T(8,128)S(1)}, f32[8,128]{1,0:T(8,128)S(1)}, u32[]{:S(2)}, u32[]{:S(2)}) collective-permute-start(f32[8,128]{1,0:T(8,128)S(1)} %get-tuple-element.52), channel_id=1, source_target_pairs={{0,8},{1,9},{2,10},{3,11},{4,12},{5,13},{6,14},{7,15},{8,0},{9,1},... | collective-permute-start | bytes 12296 | tf_op jit(solution)/shard_map/ppermute | solution.py:540

commit v4 on v3

--- a/solution.py
+++ b/solution.py
@@ -145,10 +145,12 @@
 ROWS = 16
 WIN = 56
 TILES = WIN // 8
+NEAR_TILES = 5
 LANES = 128
 DEPTH = 2 * KMAX
 GROUP = LANES // DEPTH
 SUMS = 8
+FETCHES = 4
 AXES = ("gx", "gy", "gz")
 VMEM = pl.BlockSpec(memory_space=pltpu.VMEM)
 HBM = pl.BlockSpec(memory_space=pltpu.HBM)
@@ -223,7 +225,11 @@
 
     def kernel(*refs):
         sources, (out_z, out_e, coef), copies, weighted, sems = refs[:7], refs[7:10], refs[10:17], refs[17], refs[18]
-        moves = [pltpu.make_async_copy(a, b, sems.at[i]) for i, (a, b) in enumerate(zip(sources, copies, strict=True))]
+        pairs = list(zip(sources[:6], copies[:6], strict=True))
+        for part in range(FETCHES):
+            rows = pl.ds(part * (count // FETCHES), count // FETCHES)
+            pairs.append((sources[6].at[rows], copies[6].at[rows]))
+        moves = [pltpu.make_async_copy(a, b, sems.at[i]) for i, (a, b) in enumerate(pairs)]
         for move in moves:
             move.start()
         innov, prec, scale, mask, kx, ky, members = copies
@@ -236,7 +242,8 @@
             out_z[plane * ROWS : (plane + 1) * ROWS, :cols] = scale[plane] * weighted[plane]
         edges = [tile(out_z, plane) for plane in range(planes)]
         pack_edges(out_e, edges + [tile(coef, index) for index in range(3 * levels)], cols)
-        moves[6].wait()
+        for move in moves[6:]:
+            move.wait()
         totals = [jnp.zeros((ROWS, cols), jnp.float32) for _ in range(count)]
         for plane in range(planes):
             for m in range(count):
@@ -247,7 +254,7 @@
     outs = [f32(base + ROWS, LANES), f32(edge_rows + ROWS, LANES), f32(3 * levels * ROWS, LANES)]
     field, flat = (planes, ROWS, cols), (levels, ROWS, cols)
     kept = [(field, jnp.float32)] * 3 + [(flat, jnp.int32)] + [(flat, jnp.float32)] * 2 + [((count,) + field, jnp.float32)]
-    scratch = [pltpu.VMEM(*one) for one in kept] + [pltpu.VMEM(field, jnp.float32), pltpu.SemaphoreType.DMA((7,))]
+    scratch = [pltpu.VMEM(*one) for one in kept] + [pltpu.VMEM(field, jnp.float32), pltpu.SemaphoreType.DMA((6 + FETCHES,))]
     return kernel, outs, scratch
 
 
@@ -324,22 +331,32 @@
 
 def mix_back(first, far, planes, levels, cols, tail):
     base = planes * ROWS
-    coefs = 3 * levels if first else 0
+    coefs = 2 * levels if first else 0
     fields = planes // levels
+    count = planes + coefs
+    sent = -(-planes * KMAX // 8) * 8
 
     def kernel(*refs):
         if first:
-            own, other, edge, edge_other, vert, coef, out_all, out_near = refs
+            own, other, edge, edge_other, vert, raw, out_all, out_near = refs
+        elif far:
+            own, other, edge, edge_other, vert, out_all, out_near = refs
         else:
-            own, other, edge, edge_other, vert, out_all, out_near = refs
+            own, other, edge, edge_other, vert, out_own, out_one, out_three, out_sums = refs
         here = lax.axis_index("gz") * levels
         there = (1 - lax.axis_index("gz")) * levels
+        even = lax.rem(lax.axis_index("gx"), 2) == 0
         upper = lax.broadcasted_iota(jnp.int32, (8, LANES), 0) < 4
 
         def put(index, values):
-            out_all[index * ROWS : (index + 1) * ROWS, :] = values
             if far:
+                out_all[index * ROWS : (index + 1) * ROWS, :] = values
                 out_near[index * 8 : (index + 1) * 8, :] = jnp.where(upper, values[:8], values[8:])
+            else:
+                out_own[index * ROWS : (index + 1) * ROWS, :] = values
+                head, end = values[:KMAX], values[ROWS - KMAX :]
+                out_one[index * KMAX : (index + 1) * KMAX, :] = jnp.where(even, end, head)
+                out_three[index * KMAX : (index + 1) * KMAX, :] = jnp.where(even, head, end)
 
         for field in range(fields):
             mine = [with_edge(tile(own, field * levels + l), edge, field * levels + l, cols) for l in range(levels)]
@@ -353,73 +370,100 @@
                     mixed += vert[pl.ds((block + here + l) * 2 * levels + here + k, 1), :] * mine[l]
                     mixed += vert[pl.ds((block + there + l) * 2 * levels + here + k, 1), :] * theirs[l]
                 put(field * levels + k, mixed)
-        for index in range(coefs):
-            put(planes + index, with_edge(tile(coef, index), edge, planes + index, cols))
-        packed = -(-(planes + coefs) // GROUP) * ROWS
+        packed = -(-(planes + (3 * levels if first else 0)) // GROUP) * ROWS
         total = (own[base:, :] + other[base:, :]) + (edge[packed:, :] + edge_other[packed:, :])
-        out_all[(planes + coefs) * ROWS :, :] = total
-        out_near[far * (planes + coefs) * 8 :, :] = total
-
-    count = planes + coefs
-    return kernel, [f32(count * ROWS + tail, LANES), f32(far * count * 8 + tail, LANES)]
-
-
-def fetch_window(target, nat, index, own, first, near, third, slot):
-    even = lax.rem(lax.axis_index("gx"), 2) == 0
+        if not far:
+            out_sums[...] = total
+            out_one[sent:, :] = total
+            out_three[sent:, :] = total
+            return
+        at, near_at = count * ROWS, count * 8
+        out_all[at : at + tail, :] = total
+        out_near[near_at : near_at + tail, :] = total
+        if first:
+            last = jnp.where(lax.axis_index("gy") == 0, LANES - 1, cols - 1)
+            lane = lanes_of((ROWS, LANES))
+            bottom = lax.broadcasted_iota(jnp.int32, (ROWS, LANES), 0) == ROWS - 1
+            wets = jnp.zeros((8, LANES), jnp.float32)
+            for level in range(levels):
+                kx, ky, wet = (
+                    with_edge(tile(raw, kind * levels + level), edge, planes + kind * levels + level, cols) for kind in range(3)
+                )
+                put(planes + level, kx * wet * jnp.where(bottom, 1.0, pltpu.roll(wet, ROWS - 1, 0)))
+                put(planes + levels + level, jnp.where(lane == last, 0.0, ky * wet * pltpu.roll(wet, LANES - 1, 1)))
+                wets = jnp.where(lax.broadcasted_iota(jnp.int32, (8, LANES), 0) == level, wet[:1], wets)
+            out_all[at + tail :, :] = wets
+            out_near[near_at + tail :, :] = wets
+
+    if not far:
+        return kernel, [f32(base, LANES)] + [f32(sent + tail, LANES)] * 2 + [f32(tail, LANES)]
+    tail_all = tail + (8 if first else 0)
+    return kernel, [f32(count * ROWS + tail_all, LANES), f32(count * 8 + tail_all, LANES)]
+
+
+def pass_on(*refs):
+    half = len(refs) // 2
+    for source, target in zip(refs[:half], refs[half:], strict=True):
+        target[...] = source[...]
+
+
+def is_even():
+    return lax.rem(lax.axis_index("gx"), 2) == 0
+
+
+def far_window(nat, index, own, first, near, third, slot):
+    even = is_even()
     one, three = tile(first, slot), tile(third, slot)
     nat[index, 0:16, :] = tile(own, slot)
     nat[index, 16:32, :] = jnp.where(even, one, three)
-    nat[index, 32:40, :] = jnp.zeros((8, LANES), jnp.float32) if near is None else tile(near, slot, 8)
+    nat[index, 32:40, :] = tile(near, slot, 8)
     nat[index, 40:56, :] = jnp.where(even, three, one)
-    for t in range(TILES):
-        target[index, t * 8 : (t + 1) * 8, :] = nat[index, pl.ds(t, 8, stride=TILES), :]
-
-
-def own_rows(values, nat, index):
-    for t in range(TILES):
-        nat[index, pl.ds(t, 8, stride=TILES), :] = values[t * 8 : (t + 1) * 8]
-    return nat[index, 0:ROWS, :]
-
-
-def eight(ref, *index):
-    return [ref[(*index, pl.ds(t * 8, 8), slice(None))] for t in range(TILES)]
+
+
+def shorten(nat, index):
+    return jnp.concatenate([nat[index, 0:28, :], nat[index, 44:56, :]], axis=0)
+
+
+def dealt(nat, index, tiles):
+    return [nat[index, pl.ds(t, 8, stride=tiles), :] for t in range(tiles)]
+
+
+def deal(buf, nat, index, tiles):
+    for t, values in enumerate(dealt(nat, index, tiles)):
+        buf[index, t * 8 : (t + 1) * 8, :] = values
+
+
+def undeal(nat, buf, index, tiles):
+    for t in range(tiles):
+        nat[index, pl.ds(t, 8, stride=tiles), :] = buf[index, t * 8 : (t + 1) * 8, :]
+
+
+def eight(ref, tiles, *index):
+    return [ref[(*index, pl.ds(t * 8, 8), slice(None))] for t in range(tiles)]
 
 
 def after(tiles):
     return tiles[1:] + [pltpu.roll(tiles[0], 7, 0)]
 
 
-def run_steps(buf, coef, steps, planes, levels):
+def run_steps(buf, coef, steps, planes, levels, tiles):
     for number in range(KMAX):
         for level in range(levels):
-            east, north = eight(coef, 0, level), eight(coef, 1, level)
+            east, north = eight(coef, tiles, 0, level), eight(coef, tiles, 1, level)
             for field in range(planes // levels):
                 plane = field * levels + level
                 active = jnp.where(steps[field : field + 1, :] > float(number), 1.0, 0.0).astype(jnp.float32)
-                u = eight(buf, plane)
+                u = eight(buf, tiles, plane)
                 flux_east = [c * (v - w) for c, v, w in zip(east, after(u), u, strict=True)]
                 flux_west = [pltpu.roll(flux_east[-1], 1, 0)] + flux_east[:-1]
-                for t in range(TILES):
+                for t in range(tiles):
                     flux_north = north[t] * (pltpu.roll(u[t], LANES - 1, 1) - u[t])
                     change = (flux_east[t] - flux_west[t]) + (flux_north - pltpu.roll(flux_north, 1, 1))
                     buf[plane, t * 8 : (t + 1) * 8, :] = u[t] + active * change
 
 
-def make_coefs(coef, kinds, levels, cols):
-    last = jnp.where(lax.axis_index("gy") == 0, LANES - 1, cols - 1)
-    inside = lanes_of((8, LANES)) != last
-    for level in range(levels):
-        kx, ky, wet = (eight(kinds, kind * levels + level) for kind in range(3))
-        for t, beyond in enumerate(after(wet)):
-            rows = slice(t * 8, (t + 1) * 8)
-            coef[0, level, rows, :] = kx[t] * wet[t] * beyond
-            coef[1, level, rows, :] = jnp.where(inside, ky[t] * wet[t] * pltpu.roll(wet[t], LANES - 1, 1), 0.0)
-
-
-def own_cells(cols):
-    row = lax.broadcasted_iota(jnp.int32, (WIN, LANES), 0)
-    row = lax.rem(row, 8) * TILES + lax.div(row, 8)
-    return jnp.where((row < ROWS) & (lanes_of((WIN, LANES)) < cols), 1.0, 0.0).astype(jnp.float32)
+def own_sum(values, cols):
+    return over_rows(jnp.where(lanes_of(values.shape) < cols, values, 0.0))
 
 
 def spread(values):
@@ -430,33 +474,57 @@
     return [pltpu.VMEM((planes, WIN, LANES), jnp.float32)] * 2
 
 
+def diffuse_own(out_g, field, buf, nat, coef, steps, planes, levels):
+    for plane in range(planes):
+        for t, values in enumerate(dealt(field, plane, NEAR_TILES)):
+            buf[plane, t * 8 : (t + 1) * 8, :] = values
+    run_steps(buf, coef, steps, planes, levels, NEAR_TILES)
+    for plane in range(planes):
+        undeal(nat, buf, plane, NEAR_TILES)
+        out_g[plane * ROWS : (plane + 1) * ROWS, :] = nat[plane, :ROWS, :]
+
+
 def first_diffuse(planes, levels, cols):
-    coefs = 3 * levels
-
-    def kernel(own, first, near, third, steps, coef, resid, weights, sums, out_g, buf, nat):
+    coefs = 2 * levels
+
+    def kernel(own, first, near, third, steps, coef, coef_near, resid, weights, sums, out_g, buf, nat):
+        even = is_even()
+        at, near_at = (planes + coefs) * ROWS, (planes + coefs) * 8
         for index in range(coefs):
-            fetch_window(buf, nat, index, own, first, near, third, planes + index)
-        make_coefs(coef, buf, levels, cols)
-        for plane in range(planes):
-            fetch_window(buf, nat, plane, own, first, near, third, plane)
-        at, near_at = (planes + coefs) * ROWS, (planes + coefs) * 8
-        weights[...] = spread((own[at:, :] + first[at:, :]) + (near[near_at:, :] + third[at:, :]))
-        run_steps(buf, coef, steps, planes, levels)
-        squares = jnp.zeros((WIN, LANES), jnp.float32)
-        for plane in range(planes):
-            value = SQRT_STATIC * buf[plane]
+            far_window(nat, index, own, first, near, third, planes + index)
+            if index < levels:
+                row, near_row = at + ROWS + index, near_at + ROWS + index
+                one, three = first[row : row + 1, :], third[row : row + 1, :]
+                nat[index, 15:16, :] = nat[index, 15:16, :] * jnp.where(even, one, three)
+                nat[index, 31:32, :] = nat[index, 31:32, :] * near[near_row : near_row + 1, :]
+                nat[index, 39:40, :] = nat[index, 39:40, :] * jnp.where(even, three, one)
+                nat[index, 55:56, :] = nat[index, 55:56, :] * own[row : row + 1, :]
+            kind, level = divmod(index, levels)
+            for t, values in enumerate(dealt(nat, index, TILES)):
+                coef[kind, level, t * 8 : (t + 1) * 8, :] = values
+            buf[index, : 8 * NEAR_TILES, :] = shorten(nat, index)
+            for t, values in enumerate(dealt(buf, index, NEAR_TILES)):
+                coef_near[kind, level, t * 8 : (t + 1) * 8, :] = values
+        for plane in range(planes):
+            far_window(nat, plane, own, first, near, third, plane)
+            deal(buf, nat, plane, TILES)
+        sent = slice(at, at + ROWS)
+        weights[...] = spread((own[sent, :] + first[sent, :]) + (near[near_at : near_at + ROWS, :] + third[sent, :]))
+        run_steps(buf, coef, steps, planes, levels, TILES)
+        squares = jnp.zeros((ROWS, LANES), jnp.float32)
+        for plane in range(planes):
+            undeal(nat, buf, plane, TILES)
+            value = SQRT_STATIC * shorten(nat, plane)
             resid[plane] = value
-            buf[plane] = value
-            squares += value * value
+            squares += value[:ROWS] * value[:ROWS]
         sums[...] = jnp.zeros(sums.shape, jnp.float32)
-        sums[4:5, :] = over_rows(own_cells(cols) * squares)
-        run_steps(buf, coef, steps, planes, levels)
-        for plane in range(planes):
-            out_g[plane * ROWS : (plane + 1) * ROWS, :] = own_rows(buf[plane], nat, plane)
+        sums[4:5, :] = own_sum(squares, cols)
+        diffuse_own(out_g, resid, buf, nat, coef_near, steps, planes, levels)
 
     outs = [
         f32(2, levels, WIN, LANES),
-        f32(planes, WIN, LANES),
+        f32(2, levels, 8 * NEAR_TILES, LANES),
+        f32(planes, 8 * NEAR_TILES, LANES),
         f32(ROWS, LANES),
         f32(SUMS, LANES),
         f32(planes * ROWS, LANES),
@@ -465,9 +533,12 @@
 
 
 def second_diffuse(planes, levels, cols):
-    def kernel(own, first, near, third, steps, coef, resid, weights, image, new, new_w, sums, facts, out_g, buf, nat):
-        for plane in range(planes):
-            fetch_window(buf, nat, plane, own, first, near, third, plane)
+    def kernel(
+        own, first, near, third, steps, coef, coef_near, resid, weights, image, new, new_w, sums, facts, out_g, buf, nat, field
+    ):
+        for plane in range(planes):
+            far_window(nat, plane, own, first, near, third, plane)
+            deal(buf, nat, plane, TILES)
         at, near_at = planes * ROWS, planes * 8
         total = spread((own[at:, :] + first[at:, :]) + (near[near_at:, :] + third[at:, :]))
         energy = total[ROWS : ROWS + 1]
@@ -477,38 +548,45 @@
         facts[...] = jnp.zeros(facts.shape, jnp.float32)
         facts[0:1, :] = rr
         facts[1:2, :] = step
-        run_steps(buf, coef, steps, planes, levels)
-        squares = jnp.zeros((WIN, LANES), jnp.float32)
-        cross = jnp.zeros((WIN, LANES), jnp.float32)
-        for plane in range(planes):
+        run_steps(buf, coef, steps, planes, levels, TILES)
+        squares = jnp.zeros((ROWS, LANES), jnp.float32)
+        cross = jnp.zeros((ROWS, LANES), jnp.float32)
+        for plane in range(planes):
+            undeal(nat, buf, plane, TILES)
             direction = resid[plane]
-            image_now = direction + SQRT_STATIC * buf[plane]
+            image_now = direction + SQRT_STATIC * shorten(nat, plane)
             value = direction - step * image_now
-            image[plane] = image_now
-            new[plane] = value
-            buf[plane] = value
-            squares += value * value
-            cross += value * direction
+            field[plane] = value
+            image[plane] = image_now[:ROWS]
+            new[plane] = value[:ROWS]
+            squares += value[:ROWS] * value[:ROWS]
+            cross += value[:ROWS] * direction[:ROWS]
         sums[...] = jnp.zeros(sums.shape, jnp.float32)
-        sums[4:5, :] = over_rows(own_cells(cols) * squares)
-        sums[5:6, :] = over_rows(own_cells(cols) * cross)
-        run_steps(buf, coef, steps, planes, levels)
-        for plane in range(planes):
-            out_g[plane * ROWS : (plane + 1) * ROWS, :] = own_rows(buf[plane], nat, plane)
-
-    block = f32(planes, WIN, LANES)
+        sums[4:5, :] = own_sum(squares, cols)
+        sums[5:6, :] = own_sum(cross, cols)
+        diffuse_own(out_g, field, buf, nat, coef_near, steps, planes, levels)
+
+    block = f32(planes, ROWS, LANES)
     outs = [block, block, f32(ROWS, LANES), f32(SUMS, LANES), f32(SUMS, LANES), f32(planes * ROWS, LANES)]
-    return kernel, outs, window_scratch(planes)
+    return kernel, outs, window_scratch(planes) + [pltpu.VMEM((planes, 8 * NEAR_TILES, LANES), jnp.float32)]
 
 
 def last_diffuse(planes, levels, cols):
     def kernel(
-        own, first, near, third, steps, coef, resid, weights, image, new, new_w, facts, control, control_w, final, buf, nat
+        own, one, three, sums, sums_two, steps, coef, resid, weights, image, new, new_w, facts,
+        control, control_w, final, buf, nat,
     ):
-        for plane in range(planes):
-            fetch_window(buf, nat, plane, own, first, None, third, plane)
-        at = planes * ROWS
-        lanes = (own[at:, :] + first[at:, :]) + (near[...] + third[at:, :])
+        even = is_even()
+        gap_rows = jnp.zeros((4, LANES), jnp.float32)
+        for plane in range(planes):
+            first, third = tile(one, plane, KMAX), tile(three, plane, KMAX)
+            nat[plane, 0:16, :] = tile(own, plane)
+            nat[plane, 16:26, :] = jnp.where(even, first, third)
+            nat[plane, 26:30, :] = gap_rows
+            nat[plane, 30:40, :] = jnp.where(even, third, first)
+            deal(buf, nat, plane, NEAR_TILES)
+        sent = one.shape[0] - SUMS
+        lanes = (sums[...] + one[sent:, :]) + (sums_two[...] + three[sent:, :])
         total = spread(lanes)
         rr, step = facts[0:1, :], facts[1:2, :]
         new_rr = total[4:5] + over_rows(new_w[...] * new_w[...])
@@ -521,13 +599,14 @@
         combined = step * weights[...] + new_step * (new_w[...] + ratio * weights[...])
         diagonal = lax.broadcasted_iota(jnp.int32, combined.shape, 0) == lanes_of(combined.shape)
         control_w[...] = over_rows(jnp.where(diagonal, combined, 0.0))[:, :ROWS]
-        run_steps(buf, coef, steps, planes, levels)
-        for plane in range(planes):
-            direction, value = resid[plane], new[plane]
+        run_steps(buf, coef, steps, planes, levels, NEAR_TILES)
+        for plane in range(planes):
+            undeal(nat, buf, plane, NEAR_TILES)
+            direction, value = resid[plane, :ROWS, :], new[plane]
             new_direction = value + ratio * direction
-            new_image = (value + SQRT_STATIC * buf[plane]) + ratio * image[plane]
-            control[plane] = own_rows(step * direction + new_step * new_direction, nat, plane)[:, :cols]
-            final[plane] = own_rows(value - new_step * new_image, nat, plane)[:, :cols]
+            new_image = (value + SQRT_STATIC * nat[plane, :ROWS, :]) + ratio * image[plane]
+            control[plane] = (step * direction + new_step * new_direction)[:, :cols]
+            final[plane] = (value - new_step * new_image)[:, :cols]
 
     outs = [f32(planes, ROWS, cols), f32(1, ROWS), f32(planes, ROWS, cols)]
     return kernel, outs, window_scratch(planes)
@@ -540,12 +619,19 @@
     return lax.ppermute(values, AXES, [(number[a, b, c], number[a ^ x, b ^ y, c ^ z]) for a, b, c in here])
 
 
-def across(kernel_of, out_z, out_e, vert, extra):
+def mix_round(kernel_of, out_z, out_e, vert, raw=None):
     other = moved_to(out_z, 0, 0, 1)
     edge = moved_to(out_e, 0, 1, 0)
     edge_other = moved_to(out_e, 0, 1, 1)
     kernel, outs = kernel_of
-    own, near = call(kernel, outs, [VMEM] * (5 + len(extra)), (out_z, other, edge, edge_other, vert, *extra))
+    args = (out_z, other, edge, edge_other, vert)
+    if raw is not None:
+        own, raw = call(pass_on, [f32(*out_z.shape), f32(*raw.shape)], [VMEM] * 2, (out_z, raw))
+        args = (own, *args[1:], raw)
+    return call(kernel, outs, [VMEM] * len(args), args)
+
+
+def far_round(own, near):
     return own, moved_to(own, 1, 0, 0), moved_to(near, 2, 0, 0), moved_to(own, 3, 0, 0)
 
 
@@ -563,26 +649,27 @@
 
     kernel, outs, scratch = start(planes, levels, cols, count)
     args = (innov, prec, scale, sea_mask, kappa_x, kappa_y, ens)
-    out_z, out_e, coef_own = call(kernel, outs, [HBM] * 7, args, scratch, 56)
-    parts = across(mix_back(True, True, planes, levels, cols, ROWS), out_z, out_e, vert, (coef_own,))
+    out_z, out_e, raw = call(kernel, outs, [HBM] * 7, args, scratch, 56)
+    parts = far_round(*mix_round(mix_back(True, True, planes, levels, cols, ROWS), out_z, out_e, vert, raw))
     kernel, outs, scratch = first_diffuse(planes, levels, cols)
-    coef, resid, weights, sums, out_g = call(kernel, outs, [VMEM] * 5, (*parts, steps), scratch)
+    coef, coef_near, resid, weights, sums, out_g = call(kernel, outs, [VMEM] * 5, (*parts, steps), scratch)
 
     kernel, outs, scratch = observe(planes, levels, cols, count, True)
     args = (out_g, moved_to(out_g, 0, 0, 1), weights, sums, vert, prec, scale, sea_mask, ens)
     out_z, out_e, seen = call(kernel, outs, [VMEM] * 9, args, scratch)
-    parts = across(mix_back(False, True, planes, levels, cols, ROWS + SUMS), out_z, out_e, vert, ())
+    parts = far_round(*mix_round(mix_back(False, True, planes, levels, cols, ROWS + SUMS), out_z, out_e, vert))
     kernel, outs, scratch = second_diffuse(planes, levels, cols)
-    args = (*parts, steps, coef, resid, weights)
-    image, new, new_w, sums, facts, out_g = call(kernel, outs, [VMEM] * 8, args, scratch)
+    args = (*parts, steps, coef, coef_near, resid, weights)
+    image, new, new_w, sums, facts, out_g = call(kernel, outs, [VMEM] * 9, args, scratch)
 
     kernel, outs, scratch = observe(planes, levels, cols, count, False)
     args = (out_g, moved_to(out_g, 0, 0, 1), new_w, sums, vert, prec, scale, sea_mask, ens, seen)
     out_z, out_e = call(kernel, outs, [VMEM] * 10, args, scratch)
-    parts = across(mix_back(False, False, planes, levels, cols, SUMS), out_z, out_e, vert, ())
+    own, one, three, sums = mix_round(mix_back(False, False, planes, levels, cols, SUMS), out_z, out_e, vert)
+    parts = (own, moved_to(one, 1, 0, 0), moved_to(three, 3, 0, 0), sums, moved_to(sums, 2, 0, 0))
     kernel, outs, scratch = last_diffuse(planes, levels, cols)
-    args = (*parts, steps, coef, resid, weights, image, new, new_w, facts)
-    control, control_w, final = call(kernel, outs, [VMEM] * 12, args, scratch)
+    args = (*parts, steps, coef_near, resid, weights, image, new, new_w, facts)
+    control, control_w, final = call(kernel, outs, [VMEM] * 13, args, scratch)
     return control.reshape(innovation.shape), control_w.reshape(count), final.reshape(innovation.shape)
 
 

time: 63.2 us -> 61.3 us (0.970)
  waiting for transfers between devices: 26.4 us -> 25.1 us
  starting transfers between devices: 21 us -> 20.1 us
    ppermute x20, waiting for transfers between devices: 26.4 us -> 25.1 us  [moved_to(): lax.ppermute(values, AXES, [(number[a, b, c], number[a ^ x, b ^ y, c ^ z]...]
    ppermute x20, starting transfers between devices: 21 us -> 20.1 us  [moved_to(): lax.ppermute(values, AXES, [(number[a, b, c], number[a ^ x, b ^ y, c ^ z]...]
    pallas_call x9 -> x10, Pallas kernels: 12.7 us -> 13 us  [call(): pl.pallas_call(kernel, out_shape=outs, in_specs=specs, out_specs=[VMEM] *...]
  transfers between devices with their start and end apart: 20 -> 20, of which waited for: 13 -> 11; matrix products, arithmetic and copies ran while one was open for 0% -> 0% of each run, Pallas kernels for 0% -> 0%
where the time goes in v4:
time: 61.3 us; the launch traced here: 61.1 us
  waiting for transfers between devices  25.1 us (41%)
  starting transfers between devices  20.1 us (33%)
  Pallas kernels  13 us (21%)
  local copies, waits for them, and re-layouts  2.06 us (3%)
  between operations  0.78 us (1%)
    ppermute x20, waiting for transfers between devices, moved_to(): lax.ppermute(values, AXES, [(number[a, b, c], number[a ^ x, b ^ y, c ^ z]...  25.1 us
    ppermute x20, starting transfers between devices, moved_to(): lax.ppermute(values, AXES, [(number[a, b, c], number[a ^ x, b ^ y, c ^ z]...  20.1 us
    pallas_call x10, Pallas kernels, call(): pl.pallas_call(kernel, out_shape=outs, in_specs=specs, out_specs=[VMEM] *...  13 us
    unnamed x17, local copies, waits for them, and re-layouts  1.82 us
  transfers between devices with their start and end apart: 20, of which 11 were waited for; matrix products, arithmetic and copies ran while one was open for 0% of the time, Pallas kernels for 0%

profile of v4, /device:TPU:0, one launch (start us, length us, event | category | flops | bytes accessed | tf_op | source)
XLA Modules:
  0.0 61.1 jit_solution(2952891385583440820)
XLA Ops:
  0.6 0.0 copy-start.6
  0.6 0.0 copy-start.7
  0.7 0.0 copy-start
  0.7 0.0 copy-start.1
  0.7 0.0 copy-start.2
  0.7 0.0 copy-start.3
  0.7 2.4 %shard_map.112 = (f32[176,128]{1,0:T(8,128)}, f32[64,128]{1,0:T(8,128)}, f32[96,128]{1,0:T(8,128)}) custom-call(f32[10,16,108]{2,1,0:T(8,128)} %bitcast.16, f32[10,16,108]{2,1,0:T(8,128)} %bitcast.10, f32[10,16,108]{2,1,0:T(8,128)} %bitcast.13, s32[2,16,108]{2,1,0:T(8,128)} %refs_7_.3, f32[2,16,108]{2,1,0:T(8,128)} %refs_4_.1, f32[2,16,108]{2,1,0:T(8,128)} %refs_5_.1, ...), custom_call_target="tpu_custom_call" | custom-call | tf_op jit(solution)/shard_map/pallas_call | solution.py:165
  3.1 0.5 collective-permute-start
  3.6 2.6 %collective-permute-start.2 = (f32[64,128]{1,0:T(8,128)}, f32[64,128]{1,0:T(8,128)S(1)}, u32[]{:S(2)}, u32[]{:S(2)}) collective-permute-start(f32[64,128]{1,0:T(8,128)} %get-tuple-element.39), channel_id=1, source_target_pairs={{0,3},{1,2},{2,1},{3,0},{4,7},{5,6},{6,5},{7,4},{8,11},{9,10},{10,... | collective-permute-start | bytes 98312 | tf_op jit(solution)/shard_map/ppermute | solution.py:619
  6.2 0.0 collective-permute-start.1
  6.3 0.0 copy-done.6
  6.3 0.1 copy.13
  6.4 0.1 broadcast_in_dim.6
  6.5 0.0 copy-start.4
  6.5 0.9 %copy-done.4 = f32[176,128]{1,0:T(8,128)S(1)} copy-done((f32[176,128]{1,0:T(8,128)S(1)}, f32[176,128]{1,0:T(8,128)}, u32[]{:S(2)}) %copy-start.4) | copy-done | bytes 90136
  7.4 0.8 %copy-done.5 = f32[96,128]{1,0:T(8,128)S(1)} copy-done((f32[96,128]{1,0:T(8,128)S(1)}, f32[96,128]{1,0:T(8,128)}, u32[]{:S(2)}) %copy-start.5) | copy-done | bytes 49176
  8.2 0.0 collective-permute-done.2.refs_3_
  8.2 2.2 %collective-permute-done.1.refs_2_ = f32[64,128]{1,0:T(8,128)S(1)} collective-permute-done((f32[64,128]{1,0:T(8,128)}, f32[64,128]{1,0:T(8,128)S(1)}, u32[]{:S(2)}, u32[]{:S(2)}) %collective-permute-start.1) | collective-permute-done | bytes 32800 | tf_op jit(solution)/shard_map/ppermute | solution.py:619
  10.3 0.0 collective-permute-done.refs_1_
  10.3 0.1 broadcast_in_dim.14.refs_4_
  10.4 0.1 shard_map.114
  10.6 3.7 %collective-permute-start.5 = (f32[248,128]{1,0:T(8,128)S(1)}, f32[248,128]{1,0:T(8,128)S(1)}, u32[]{:S(2)}, u32[]{:S(2)}) collective-permute-start(f32[248,128]{1,0:T(8,128)S(1)} %get-tuple-element.41.own), channel_id=1, source_target_pairs={{0,12},{1,13},{2,14},{3,15},{4,8},{5,9},{6,10},{7,11},{8,4},{9,5},... | collective-permute-start | bytes 380936 | tf_op jit(solution)/shard_map/ppermute | solution.py:619
  14.2 0.0 collective-permute-start.3
  14.2 0.8 %collective-permute-start.4 = (f32[136,128]{1,0:T(8,128)S(1)}, f32[136,128]{1,0:T(8,128)S(1)}, u32[]{:S(2)}, u32[]{:S(2)}) collective-permute-start(f32[136,128]{1,0:T(8,128)S(1)} %get-tuple-element.42), channel_id=1, source_target_pairs={{0,8},{1,9},{2,10},{3,11},{4,12},{5,13},{6,14},{7,15},{8,0},{9,1},... | collective-permute-start | bytes 208904 | tf_op jit(solution)/shard_map/ppermute | solution.py:619
  15.0 0.0 copy-done.7
  15.0 6.6 %collective-permute-done.4.near = f32[136,128]{1,0:T(8,128)S(1)} collective-permute-done((f32[136,128]{1,0:T(8,128)S(1)}, f32[136,128]{1,0:T(8,128)S(1)}, u32[]{:S(2)}, u32[]{:S(2)}) %collective-permute-start.4) | collective-permute-done | bytes 69664 | tf_op jit(solution)/shard_map/ppermute | solution.py:619
  21.6 0.0 collective-permute-done.5.third
  21.6 0.0 collective-permute-done.3.first
  21.6 0.1 broadcast_in_dim.15.steps
  21.6 4.1 %shard_map.115 = (f32[2,2,56,128]{3,2,1,0:T(8,128)S(1)}, f32[2,2,40,128]{3,2,1,0:T(8,128)S(1)}, f32[10,40,128]{2,1,0:T(8,128)S(1)}, f32[16,128]{1,0:T(8,128)S(1)...) custom-call(f32[248,128]{1,0:T(8,128)S(1)} %get-tuple-element.41.own, f32[248,128]{1,0:T(8,128)S(1)} %collective-permute-done.3.first, ...), custom_call_target="tpu_custom_call" | custom-call | tf_op jit(solution)/shard_map/pallas_call | solution.py:165
  25.7 0.1 collective-permute-start.6
  25.8 1.3 %collective-permute-done.6.refs_1_ = f32[160,128]{1,0:T(8,128)S(1)} collective-permute-done((f32[160,128]{1,0:T(8,128)S(1)}, f32[160,128]{1,0:T(8,128)S(1)}, u32[]{:S(2)}, u32[]{:S(2)}) %collective-permute-start.6) | collective-permute-done | bytes 81952 | tf_op jit(solution)/shard_map/ppermute | solution.py:619
  27.1 0.3 shard_map.116
  27.4 0.2 collective-permute-start.7
  27.6 1.0 %collective-permute-start.9 = (f32[56,128]{1,0:T(8,128)S(1)}, f32[56,128]{1,0:T(8,128)S(1)}, u32[]{:S(2)}, u32[]{:S(2)}) collective-permute-start(f32[56,128]{1,0:T(8,128)S(1)} %get-tuple-element.47), channel_id=1, source_target_pairs={{0,3},{1,2},{2,1},{3,0},{4,7},{5,6},{6,5},{7,4},{8,11},{9,10},{10,... | collective-permute-start | bytes 86024 | tf_op jit(solution)/shard_map/ppermute | solution.py:619
  28.6 1.0 %collective-permute-start.8 = (f32[56,128]{1,0:T(8,128)S(1)}, f32[56,128]{1,0:T(8,128)S(1)}, u32[]{:S(2)}, u32[]{:S(2)}) collective-permute-start(f32[56,128]{1,0:T(8,128)S(1)} %get-tuple-element.47), channel_id=1, source_target_pairs={{0,2},{1,3},{2,0},{3,1},{4,6},{5,7},{6,4},{7,5},{8,10},{9,11},{10,... | collective-permute-start | bytes 86024 | tf_op jit(solution)/shard_map/ppermute | solution.py:619
  29.6 1.3 %collective-permute-done.9.refs_3_ = f32[56,128]{1,0:T(8,128)S(1)} collective-permute-done((f32[56,128]{1,0:T(8,128)S(1)}, f32[56,128]{1,0:T(8,128)S(1)}, u32[]{:S(2)}, u32[]{:S(2)}) %collective-permute-start.9) | collective-permute-done | bytes 28704 | tf_op jit(solution)/shard_map/ppermute | solution.py:619
  31.0 1.5 %collective-permute-done.8.refs_2_ = f32[56,128]{1,0:T(8,128)S(1)} collective-permute-done((f32[56,128]{1,0:T(8,128)S(1)}, f32[56,128]{1,0:T(8,128)S(1)}, u32[]{:S(2)}, u32[]{:S(2)}) %collective-permute-start.8) | collective-permute-done | bytes 28704 | tf_op jit(solution)/shard_map/ppermute | solution.py:619
  32.5 0.0 collective-permute-done.7.refs_1_
  32.5 0.1 shard_map.117
  32.6 2.0 %collective-permute-start.12 = (f32[184,128]{1,0:T(8,128)S(1)}, f32[184,128]{1,0:T(8,128)S(1)}, u32[]{:S(2)}, u32[]{:S(2)}) collective-permute-start(f32[184,128]{1,0:T(8,128)S(1)} %get-tuple-element.48.own), channel_id=1, source_target_pairs={{0,12},{1,13},{2,14},{3,15},{4,8},{5,9},{6,10},{7,11},{8,4},{9,5},... | collective-permute-start | bytes 282632 | tf_op jit(solution)/shard_map/ppermute | solution.py:619
  34.6 0.6 %collective-permute-start.10 = (f32[184,128]{1,0:T(8,128)S(1)}, f32[184,128]{1,0:T(8,128)S(1)}, u32[]{:S(2)}, u32[]{:S(2)}) collective-permute-start(f32[184,128]{1,0:T(8,128)S(1)} %get-tuple-element.48.own), channel_id=1, source_target_pairs={{0,4},{1,5},{2,6},{3,7},{4,0},{5,1},{6,2},{7,3},{8,12},{9,13},{10,... | collective-permute-start | bytes 282632 | tf_op jit(solution)/shard_map/ppermute | solution.py:619
  35.3 1.8 %collective-permute-start.11 = (f32[104,128]{1,0:T(8,128)S(1)}, f32[104,128]{1,0:T(8,128)S(1)}, u32[]{:S(2)}, u32[]{:S(2)}) collective-permute-start(f32[104,128]{1,0:T(8,128)S(1)} %get-tuple-element.49), channel_id=1, source_target_pairs={{0,8},{1,9},{2,10},{3,11},{4,12},{5,13},{6,14},{7,15},{8,0},{9,1},... | collective-permute-start | bytes 159752 | tf_op jit(solution)/shard_map/ppermute | solution.py:619
  37.0 3.9 %collective-permute-done.11.near = f32[104,128]{1,0:T(8,128)S(1)} collective-permute-done((f32[104,128]{1,0:T(8,128)S(1)}, f32[104,128]{1,0:T(8,128)S(1)}, u32[]{:S(2)}, u32[]{:S(2)}) %collective-permute-start.11) | collective-permute-done | bytes 53280 | tf_op jit(solution)/shard_map/ppermute | solution.py:619
  41.0 0.0 collective-permute-done.12.third
  41.0 0.4 collective-permute-done.10.first
  41.4 3.2 %shard_map.118 = (f32[10,16,128]{2,1,0:T(8,128)S(1)}, f32[10,16,128]{2,1,0:T(8,128)S(1)}, f32[16,128]{1,0:T(8,128)S(1)}, f32[8,128]{1,0:T(8,128)S(1)}, f32[8,128]{1,0:T(8,128)S(1)}, /*index=5*/f32[160,128]{1,0:T(8,128)S(1)}) custom-call(f32[184,128]{1,0:T(8,128)S(1)} %get-tuple-element.48.own, f32[184,128]{1,0:T(8,128)S(1)} %collective-permute-done.10.first, ...), custom_call_target="tpu_custom_call" | custom-call | tf_op jit(solution)/shard_map/pallas_call | solution.py:165
  44.6 0.1 collective-permute-start.13
  44.7 1.3 %collective-permute-done.13.refs_1_ = f32[160,128]{1,0:T(8,128)S(1)} collective-permute-done((f32[160,128]{1,0:T(8,128)S(1)}, f32[160,128]{1,0:T(8,128)S(1)}, u32[]{:S(2)}, u32[]{:S(2)}) %collective-permute-start.13) | collective-permute-done | bytes 81952 | tf_op jit(solution)/shard_map/ppermute | solution.py:619
  45.9 0.4 shard_map.119
  46.3 0.2 collective-permute-start.14
  46.4 0.9 %collective-permute-start.16 = (f32[40,128]{1,0:T(8,128)S(1)}, f32[40,128]{1,0:T(8,128)S(1)}, u32[]{:S(2)}, u32[]{:S(2)}) collective-permute-start(f32[40,128]{1,0:T(8,128)S(1)} %get-tuple-element.58), channel_id=1, source_target_pairs={{0,3},{1,2},{2,1},{3,0},{4,7},{5,6},{6,5},{7,4},{8,11},{9,10},{10,... | collective-permute-start | bytes 61448 | tf_op jit(solution)/shard_map/ppermute | solution.py:619
  47.4 1.0 %collective-permute-start.15 = (f32[40,128]{1,0:T(8,128)S(1)}, f32[40,128]{1,0:T(8,128)S(1)}, u32[]{:S(2)}, u32[]{:S(2)}) collective-permute-start(f32[40,128]{1,0:T(8,128)S(1)} %get-tuple-element.58), channel_id=1, source_target_pairs={{0,2},{1,3},{2,0},{3,1},{4,6},{5,7},{6,4},{7,5},{8,10},{9,11},{10,... | collective-permute-start | bytes 61448 | tf_op jit(solution)/shard_map/ppermute | solution.py:619
  48.4 1.2 %collective-permute-done.16.refs_3_ = f32[40,128]{1,0:T(8,128)S(1)} collective-permute-done((f32[40,128]{1,0:T(8,128)S(1)}, f32[40,128]{1,0:T(8,128)S(1)}, u32[]{:S(2)}, u32[]{:S(2)}) %collective-permute-start.16) | collective-permute-done | bytes 20512 | tf_op jit(solution)/shard_map/ppermute | solution.py:619
  49.7 1.5 %collective-permute-done.15.refs_2_ = f32[40,128]{1,0:T(8,128)S(1)} collective-permute-done((f32[40,128]{1,0:T(8,128)S(1)}, f32[40,128]{1,0:T(8,128)S(1)}, u32[]{:S(2)}, u32[]{:S(2)}) %collective-permute-start.15) | collective-permute-done | bytes 20512 | tf_op jit(solution)/shard_map/ppermute | solution.py:619
  51.2 0.0 collective-permute-done.14.refs_1_
  51.2 0.1 shard_map.120
  51.3 0.8 %collective-permute-start.17 = (f32[112,128]{1,0:T(8,128)S(1)}, f32[112,128]{1,0:T(8,128)S(1)}, u32[]{:S(2)}, u32[]{:S(2)}) collective-permute-start(f32[112,128]{1,0:T(8,128)S(1)} %get-tuple-element.60), channel_id=1, source_target_pairs={{0,4},{1,5},{2,6},{3,7},{4,0},{5,1},{6,2},{7,3},{8,12},{9,13},{10,... | collective-permute-start | bytes 172040 | tf_op jit(solution)/shard_map/ppermute | solution.py:619
  52.1 2.2 %collective-permute-start.18 = (f32[112,128]{1,0:T(8,128)S(1)}, f32[112,128]{1,0:T(8,128)S(1)}, u32[]{:S(2)}, u32[]{:S(2)}) collective-permute-start(f32[112,128]{1,0:T(8,128)S(1)} %get-tuple-element.61), channel_id=1, source_target_pairs={{0,12},{1,13},{2,14},{3,15},{4,8},{5,9},{6,10},{7,11},{8,4},{9,5},... | collective-permute-start | bytes 172040 | tf_op jit(solution)/shard_map/ppermute | solution.py:619
  54.3 0.6 collective-permute-start.19
  54.9 4.0 %collective-permute-done.19.sums_two = f32[8,128]{1,0:T(8,128)S(1)} collective-permute-done((f32[8,128]{1,0:T(8,128)S(1)}, f32[8,128]{1,0:T(8,128)S(1)}, u32[]{:S(2)}, u32[]{:S(2)}) %collective-permute-start.19) | collective-permute-done | bytes 4128 | tf_op jit(solution)/shard_map/ppermute | solution.py:619
  58.8 0.0 collective-permute-done.17.one
  58.8 0.0 collective-permute-done.18.three
  58.8 2.3 %shard_map.121 = (f32[10,16,108]{2,1,0:T(8,128)}, f32[1,16]{1,0:T(1,128)}, f32[10,16,108]{2,1,0:T(8,128)}) custom-call(f32[160,128]{1,0:T(8,128)S(1)} %get-tuple-element.59.own, f32[112,128]{1,0:T(8,128)S(1)} %collective-permute-done.17.one, f32[112,128]{1,0:T(8,128)S(1)} %collective-permute-done.18.three, f32[8,128]{1,0:T(8,128)S(1)} %get-tuple-element.62.sums, ...), custom_call_target="tpu_custom_call" | custom-call | tf_op jit(solution)/shard_map/pallas_call | solution.py:165
  (7 shorter events, 0.0 us)
Async XLA Ops:
  0.6 5.6 %copy-start.6 = (f32[5,4,4]{0,2,1:T(4,128)S(1)}, f32[5,4,4]{0,2,1:T(4,128)}, u32[]{:S(2)}) copy-start(f32[5,4,4]{0,2,1:T(4,128)} %param.16) | copy-start | bytes 964
  0.6 14.4 %copy-start.7 = (s32[5]{0:T(128)S(1)}, s32[5]{0:T(128)}, u32[]{:S(2)}) copy-start(s32[5]{0:T(128)} %param.17) | copy-start | bytes 64
  0.7 26.4 %copy-start = (f32[16,5,2,16,108]{4,3,2,1,0:T(8,128)S(1)}, f32[16,5,2,16,108]{4,3,2,1,0:T(8,128)}, u32[]{:S(2)}) copy-start(f32[16,5,2,16,108]{4,3,2,1,0:T(8,128)} %param.15) | copy-start | bytes 3317764
  0.7 26.4 %copy-start.1 = (f32[5,2,16,108]{3,2,1,0:T(8,128)S(1)}, f32[5,2,16,108]{3,2,1,0:T(8,128)}, u32[]{:S(2)}) copy-start(f32[5,2,16,108]{3,2,1,0:T(8,128)} %param.10) | copy-start | bytes 207364
  0.7 26.4 %copy-start.2 = (f32[5,2,16,108]{3,2,1,0:T(8,128)S(1)}, f32[5,2,16,108]{3,2,1,0:T(8,128)}, u32[]{:S(2)}) copy-start(f32[5,2,16,108]{3,2,1,0:T(8,128)} %param.11) | copy-start | bytes 207364
  0.7 26.4 %copy-start.3 = (s32[2,16,108]{2,1,0:T(8,128)S(1)}, s32[2,16,108]{2,1,0:T(8,128)}, u32[]{:S(2)}) copy-start(s32[2,16,108]{2,1,0:T(8,128)} %refs_7_.3) | copy-start | bytes 41476
  3.1 7.3 %collective-permute-start = (f32[176,128]{1,0:T(8,128)}, f32[176,128]{1,0:T(8,128)S(1)}, u32[]{:S(2)}, u32[]{:S(2)}) collective-permute-start(f32[176,128]{1,0:T(8,128)} %get-tuple-element.36.refs_0_), channel_id=1, source_target_pairs={{0,1},{1,0},{2,3},{3,2},{4,5},{5,4},{6,7},{7,6},{8,9},{9,8},{10,11... | collective-permute-start | bytes 270344 | tf_op jit(solution)/shard_map/ppermute | solution.py:619
  3.6 4.6 %collective-permute-start.2 = (f32[64,128]{1,0:T(8,128)}, f32[64,128]{1,0:T(8,128)S(1)}, u32[]{:S(2)}, u32[]{:S(2)}) collective-permute-start(f32[64,128]{1,0:T(8,128)} %get-tuple-element.39), channel_id=1, source_target_pairs={{0,3},{1,2},{2,1},{3,0},{4,7},{5,6},{6,5},{7,4},{8,11},{9,10},{10,... | collective-permute-start | bytes 98312 | tf_op jit(solution)/shard_map/ppermute | solution.py:619
  6.2 4.1 %collective-permute-start.1 = (f32[64,128]{1,0:T(8,128)}, f32[64,128]{1,0:T(8,128)S(1)}, u32[]{:S(2)}, u32[]{:S(2)}) collective-permute-start(f32[64,128]{1,0:T(8,128)} %get-tuple-element.39), channel_id=1, source_target_pairs={{0,2},{1,3},{2,0},{3,1},{4,6},{5,7},{6,4},{7,5},{8,10},{9,11},{10,... | collective-permute-start | bytes 98312 | tf_op jit(solution)/shard_map/ppermute | solution.py:619
  6.5 0.9 %copy-start.4 = (f32[176,128]{1,0:T(8,128)S(1)}, f32[176,128]{1,0:T(8,128)}, u32[]{:S(2)}) copy-start(f32[176,128]{1,0:T(8,128)} %get-tuple-element.36.refs_0_) | copy-start | bytes 270340
  7.4 0.8 %copy-start.5 = (f32[96,128]{1,0:T(8,128)S(1)}, f32[96,128]{1,0:T(8,128)}, u32[]{:S(2)}) copy-start(f32[96,128]{1,0:T(8,128)} %get-tuple-element.37.refs_1_) | copy-start | bytes 147460
  10.6 11.0 %collective-permute-start.5 = (f32[248,128]{1,0:T(8,128)S(1)}, f32[248,128]{1,0:T(8,128)S(1)}, u32[]{:S(2)}, u32[]{:S(2)}) collective-permute-start(f32[248,128]{1,0:T(8,128)S(1)} %get-tuple-element.41.own), channel_id=1, source_target_pairs={{0,12},{1,13},{2,14},{3,15},{4,8},{5,9},{6,10},{7,11},{8,4},{9,5},... | collective-permute-start | bytes 380936 | tf_op jit(solution)/shard_map/ppermute | solution.py:619
  14.2 7.4 %collective-permute-start.3 = (f32[248,128]{1,0:T(8,128)S(1)}, f32[248,128]{1,0:T(8,128)S(1)}, u32[]{:S(2)}, u32[]{:S(2)}) collective-permute-start(f32[248,128]{1,0:T(8,128)S(1)} %get-tuple-element.41.own), channel_id=1, source_target_pairs={{0,4},{1,5},{2,6},{3,7},{4,0},{5,1},{6,2},{7,3},{8,12},{9,13},{10,... | collective-permute-start | bytes 380936 | tf_op jit(solution)/shard_map/ppermute | solution.py:619
  14.2 7.3 %collective-permute-start.4 = (f32[136,128]{1,0:T(8,128)S(1)}, f32[136,128]{1,0:T(8,128)S(1)}, u32[]{:S(2)}, u32[]{:S(2)}) collective-permute-start(f32[136,128]{1,0:T(8,128)S(1)} %get-tuple-element.42), channel_id=1, source_target_pairs={{0,8},{1,9},{2,10},{3,11},{4,12},{5,13},{6,14},{7,15},{8,0},{9,1},... | collective-permute-start | bytes 208904 | tf_op jit(solution)/shard_map/ppermute | solution.py:619
  25.7 1.3 %collective-permute-start.6 = (f32[160,128]{1,0:T(8,128)S(1)}, f32[160,128]{1,0:T(8,128)S(1)}, u32[]{:S(2)}, u32[]{:S(2)}) collective-permute-start(f32[160,128]{1,0:T(8,128)S(1)} %get-tuple-element.43.refs_0_), channel_id=1, source_target_pairs={{0,1},{1,0},{2,3},{3,2},{4,5},{5,4},{6,7},{7,6},{8,9},{9,8},{10,11... | collective-permute-start | bytes 245768 | tf_op jit(solution)/shard_map/ppermute | solution.py:619
  27.4 5.0 %collective-permute-start.7 = (f32[184,128]{1,0:T(8,128)S(1)}, f32[184,128]{1,0:T(8,128)S(1)}, u32[]{:S(2)}, u32[]{:S(2)}) collective-permute-start(f32[184,128]{1,0:T(8,128)S(1)} %get-tuple-element.46.refs_0_), channel_id=1, source_target_pairs={{0,1},{1,0},{2,3},{3,2},{4,5},{5,4},{6,7},{7,6},{8,9},{9,8},{10,11... | collective-permute-start | bytes 282632 | tf_op jit(solution)/shard_map/ppermute | solution.py:619
  27.6 3.3 %collective-permute-start.9 = (f32[56,128]{1,0:T(8,128)S(1)}, f32[56,128]{1,0:T(8,128)S(1)}, u32[]{:S(2)}, u32[]{:S(2)}) collective-permute-start(f32[56,128]{1,0:T(8,128)S(1)} %get-tuple-element.47), channel_id=1, source_target_pairs={{0,3},{1,2},{2,1},{3,0},{4,7},{5,6},{6,5},{7,4},{8,11},{9,10},{10,... | collective-permute-start | bytes 86024 | tf_op jit(solution)/shard_map/ppermute | solution.py:619
  28.6 3.9 %collective-permute-start.8 = (f32[56,128]{1,0:T(8,128)S(1)}, f32[56,128]{1,0:T(8,128)S(1)}, u32[]{:S(2)}, u32[]{:S(2)}) collective-permute-start(f32[56,128]{1,0:T(8,128)S(1)} %get-tuple-element.47), channel_id=1, source_target_pairs={{0,2},{1,3},{2,0},{3,1},{4,6},{5,7},{6,4},{7,5},{8,10},{9,11},{10,... | collective-permute-start | bytes 86024 | tf_op jit(solution)/shard_map/ppermute | solution.py:619
  32.6 8.4 %collective-permute-start.12 = (f32[184,128]{1,0:T(8,128)S(1)}, f32[184,128]{1,0:T(8,128)S(1)}, u32[]{:S(2)}, u32[]{:S(2)}) collective-permute-start(f32[184,128]{1,0:T(8,128)S(1)} %get-tuple-element.48.own), channel_id=1, source_target_pairs={{0,12},{1,13},{2,14},{3,15},{4,8},{5,9},{6,10},{7,11},{8,4},{9,5},... | collective-permute-start | bytes 282632 | tf_op jit(solution)/shard_map/ppermute | solution.py:619
  34.6 6.7 %collective-permute-start.10 = (f32[184,128]{1,0:T(8,128)S(1)}, f32[184,128]{1,0:T(8,128)S(1)}, u32[]{:S(2)}, u32[]{:S(2)}) collective-permute-start(f32[184,128]{1,0:T(8,128)S(1)} %get-tuple-element.48.own), channel_id=1, source_target_pairs={{0,4},{1,5},{2,6},{3,7},{4,0},{5,1},{6,2},{7,3},{8,12},{9,13},{10,... | collective-permute-start | bytes 282632 | tf_op jit(solution)/shard_map/ppermute | solution.py:619
  35.3 5.7 %collective-permute-start.11 = (f32[104,128]{1,0:T(8,128)S(1)}, f32[104,128]{1,0:T(8,128)S(1)}, u32[]{:S(2)}, u32[]{:S(2)}) collective-permute-start(f32[104,128]{1,0:T(8,128)S(1)} %get-tuple-element.49), channel_id=1, source_target_pairs={{0,8},{1,9},{2,10},{3,11},{4,12},{5,13},{6,14},{7,15},{8,0},{9,1},... | collective-permute-start | bytes 159752 | tf_op jit(solution)/shard_map/ppermute | solution.py:619
  44.6 1.3 %collective-permute-start.13 = (f32[160,128]{1,0:T(8,128)S(1)}, f32[160,128]{1,0:T(8,128)S(1)}, u32[]{:S(2)}, u32[]{:S(2)}) collective-permute-start(f32[160,128]{1,0:T(8,128)S(1)} %get-tuple-element.53.refs_0_), channel_id=1, source_target_pairs={{0,1},{1,0},{2,3},{3,2},{4,5},{5,4},{6,7},{7,6},{8,9},{9,8},{10,11... | collective-permute-start | bytes 245768 | tf_op jit(solution)/shard_map/ppermute | solution.py:619
  46.3 4.9 %collective-permute-start.14 = (f32[168,128]{1,0:T(8,128)S(1)}, f32[168,128]{1,0:T(8,128)S(1)}, u32[]{:S(2)}, u32[]{:S(2)}) collective-permute-start(f32[168,128]{1,0:T(8,128)S(1)} %get-tuple-element.57.refs_0_), channel_id=1, source_target_pairs={{0,1},{1,0},{2,3},{3,2},{4,5},{5,4},{6,7},{7,6},{8,9},{9,8},{10,11... | collective-permute-start | bytes 258056 | tf_op jit(solution)/shard_map/ppermute | solution.py:619
  46.4 3.2 %collective-permute-start.16 = (f32[40,128]{1,0:T(8,128)S(1)}, f32[40,128]{1,0:T(8,128)S(1)}, u32[]{:S(2)}, u32[]{:S(2)}) collective-permute-start(f32[40,128]{1,0:T(8,128)S(1)} %get-tuple-element.58), channel_id=1, source_target_pairs={{0,3},{1,2},{2,1},{3,0},{4,7},{5,6},{6,5},{7,4},{8,11},{9,10},{10,... | collective-permute-start | bytes 61448 | tf_op jit(solution)/shard_map/ppermute | solution.py:619
  47.4 3.8 %collective-permute-start.15 = (f32[40,128]{1,0:T(8,128)S(1)}, f32[40,128]{1,0:T(8,128)S(1)}, u32[]{:S(2)}, u32[]{:S(2)}) collective-permute-start(f32[40,128]{1,0:T(8,128)S(1)} %get-tuple-element.58), channel_id=1, source_target_pairs={{0,2},{1,3},{2,0},{3,1},{4,6},{5,7},{6,4},{7,5},{8,10},{9,11},{10,... | collective-permute-start | bytes 61448 | tf_op jit(solution)/shard_map/ppermute | solution.py:619
  51.3 7.5 %collective-permute-start.17 = (f32[112,128]{1,0:T(8,128)S(1)}, f32[112,128]{1,0:T(8,128)S(1)}, u32[]{:S(2)}, u32[]{:S(2)}) collective-permute-start(f32[112,128]{1,0:T(8,128)S(1)} %get-tuple-element.60), channel_id=1, source_target_pairs={{0,4},{1,5},{2,6},{3,7},{4,0},{5,1},{6,2},{7,3},{8,12},{9,13},{10,... | collective-permute-start | bytes 172040 | tf_op jit(solution)/shard_map/ppermute | solution.py:619
  52.1 6.8 %collective-permute-start.18 = (f32[112,128]{1,0:T(8,128)S(1)}, f32[112,128]{1,0:T(8,128)S(1)}, u32[]{:S(2)}, u32[]{:S(2)}) collective-permute-start(f32[112,128]{1,0:T(8,128)S(1)} %get-tuple-element.61), channel_id=1, source_target_pairs={{0,12},{1,13},{2,14},{3,15},{4,8},{5,9},{6,10},{7,11},{8,4},{9,5},... | collective-permute-start | bytes 172040 | tf_op jit(solution)/shard_map/ppermute | solution.py:619
  54.3 4.5 %collective-permute-start.19 = (f32[8,128]{1,0:T(8,128)S(1)}, f32[8,128]{1,0:T(8,128)S(1)}, u32[]{:S(2)}, u32[]{:S(2)}) collective-permute-start(f32[8,128]{1,0:T(8,128)S(1)} %get-tuple-element.62.sums), channel_id=1, source_target_pairs={{0,8},{1,9},{2,10},{3,11},{4,12},{5,13},{6,14},{7,15},{8,0},{9,1},... | collective-permute-start | bytes 12296 | tf_op jit(solution)/shard_map/ppermute | solution.py:619

commit v5 on v4

--- a/solution.py
+++ b/solution.py
@@ -446,20 +446,22 @@
     return tiles[1:] + [pltpu.roll(tiles[0], 7, 0)]
 
 
-def run_steps(buf, coef, steps, planes, levels, tiles):
+def run_steps(buf, spare, coef, steps, planes, levels, tiles):
     for number in range(KMAX):
+        source, target = (buf, spare)[number % 2], (spare, buf)[number % 2]
         for level in range(levels):
-            east, north = eight(coef, tiles, 0, level), eight(coef, tiles, 1, level)
+            east, north, south = (eight(coef, tiles, kind, level) for kind in range(3))
             for field in range(planes // levels):
                 plane = field * levels + level
                 active = jnp.where(steps[field : field + 1, :] > float(number), 1.0, 0.0).astype(jnp.float32)
-                u = eight(buf, tiles, plane)
+                u = eight(source, tiles, plane)
                 flux_east = [c * (v - w) for c, v, w in zip(east, after(u), u, strict=True)]
                 flux_west = [pltpu.roll(flux_east[-1], 1, 0)] + flux_east[:-1]
                 for t in range(tiles):
-                    flux_north = north[t] * (pltpu.roll(u[t], LANES - 1, 1) - u[t])
-                    change = (flux_east[t] - flux_west[t]) + (flux_north - pltpu.roll(flux_north, 1, 1))
-                    buf[plane, t * 8 : (t + 1) * 8, :] = u[t] + active * change
+                    to_north = north[t] * (pltpu.roll(u[t], LANES - 1, 1) - u[t])
+                    to_south = south[t] * (pltpu.roll(u[t], 1, 1) - u[t])
+                    change = (flux_east[t] - flux_west[t]) + (to_north + to_south)
+                    target[plane, t * 8 : (t + 1) * 8, :] = u[t] + active * change
 
 
 def own_sum(values, cols):
@@ -478,7 +480,7 @@
     for plane in range(planes):
         for t, values in enumerate(dealt(field, plane, NEAR_TILES)):
             buf[plane, t * 8 : (t + 1) * 8, :] = values
-    run_steps(buf, coef, steps, planes, levels, NEAR_TILES)
+    run_steps(buf, nat, coef, steps, planes, levels, NEAR_TILES)
     for plane in range(planes):
         undeal(nat, buf, plane, NEAR_TILES)
         out_g[plane * ROWS : (plane + 1) * ROWS, :] = nat[plane, :ROWS, :]
@@ -499,18 +501,19 @@
                 nat[index, 31:32, :] = nat[index, 31:32, :] * near[near_row : near_row + 1, :]
                 nat[index, 39:40, :] = nat[index, 39:40, :] * jnp.where(even, three, one)
                 nat[index, 55:56, :] = nat[index, 55:56, :] * own[row : row + 1, :]
+            buf[index, : 8 * NEAR_TILES, :] = shorten(nat, index)
             kind, level = divmod(index, levels)
-            for t, values in enumerate(dealt(nat, index, TILES)):
-                coef[kind, level, t * 8 : (t + 1) * 8, :] = values
-            buf[index, : 8 * NEAR_TILES, :] = shorten(nat, index)
-            for t, values in enumerate(dealt(buf, index, NEAR_TILES)):
-                coef_near[kind, level, t * 8 : (t + 1) * 8, :] = values
+            for target, window, tiles in ((coef, nat, TILES), (coef_near, buf, NEAR_TILES)):
+                for t, values in enumerate(dealt(window, index, tiles)):
+                    target[kind, level, t * 8 : (t + 1) * 8, :] = values
+                    if kind == 1:
+                        target[2, level, t * 8 : (t + 1) * 8, :] = pltpu.roll(values, 1, 1)
         for plane in range(planes):
             far_window(nat, plane, own, first, near, third, plane)
             deal(buf, nat, plane, TILES)
         sent = slice(at, at + ROWS)
         weights[...] = spread((own[sent, :] + first[sent, :]) + (near[near_at : near_at + ROWS, :] + third[sent, :]))
-        run_steps(buf, coef, steps, planes, levels, TILES)
+        run_steps(buf, nat, coef, steps, planes, levels, TILES)
         squares = jnp.zeros((ROWS, LANES), jnp.float32)
         for plane in range(planes):
             undeal(nat, buf, plane, TILES)
@@ -522,8 +525,8 @@
         diffuse_own(out_g, resid, buf, nat, coef_near, steps, planes, levels)
 
     outs = [
-        f32(2, levels, WIN, LANES),
-        f32(2, levels, 8 * NEAR_TILES, LANES),
+        f32(3, levels, WIN, LANES),
+        f32(3, levels, 8 * NEAR_TILES, LANES),
         f32(planes, 8 * NEAR_TILES, LANES),
         f32(ROWS, LANES),
         f32(SUMS, LANES),
@@ -548,7 +551,7 @@
         facts[...] = jnp.zeros(facts.shape, jnp.float32)
         facts[0:1, :] = rr
         facts[1:2, :] = step
-        run_steps(buf, coef, steps, planes, levels, TILES)
+        run_steps(buf, nat, coef, steps, planes, levels, TILES)
         squares = jnp.zeros((ROWS, LANES), jnp.float32)
         cross = jnp.zeros((ROWS, LANES), jnp.float32)
         for plane in range(planes):
@@ -599,7 +602,7 @@
         combined = step * weights[...] + new_step * (new_w[...] + ratio * weights[...])
         diagonal = lax.broadcasted_iota(jnp.int32, combined.shape, 0) == lanes_of(combined.shape)
         control_w[...] = over_rows(jnp.where(diagonal, combined, 0.0))[:, :ROWS]
-        run_steps(buf, coef, steps, planes, levels, NEAR_TILES)
+        run_steps(buf, nat, coef, steps, planes, levels, NEAR_TILES)
         for plane in range(planes):
             undeal(nat, buf, plane, NEAR_TILES)
             direction, value = resid[plane, :ROWS, :], new[plane]

time: 61.3 us -> 59.3 us (0.967)
  Pallas kernels: 13 us -> 11 us
    pallas_call x10, Pallas kernels: 13 us -> 11 us  [call(): pl.pallas_call(kernel, out_shape=outs, in_specs=specs, out_specs=[VMEM] *...]
where the time goes in v5:
time: 59.3 us; the launch traced here: 59.1 us
  waiting for transfers between devices  25.1 us (42%)
  starting transfers between devices  20.1 us (34%)
  Pallas kernels  11 us (19%)
  local copies, waits for them, and re-layouts  2.06 us (3%)
  between operations  0.78 us (1%)
    ppermute x20, waiting for transfers between devices, moved_to(): lax.ppermute(values, AXES, [(number[a, b, c], number[a ^ x, b ^ y, c ^ z]...  25.1 us
    ppermute x20, starting transfers between devices, moved_to(): lax.ppermute(values, AXES, [(number[a, b, c], number[a ^ x, b ^ y, c ^ z]...  20.1 us
    pallas_call x10, Pallas kernels, call(): pl.pallas_call(kernel, out_shape=outs, in_specs=specs, out_specs=[VMEM] *...  11 us
    unnamed x17, local copies, waits for them, and re-layouts  1.82 us
  transfers between devices with their start and end apart: 20, of which 11 were waited for; matrix products, arithmetic and copies ran while one was open for 0% of the time, Pallas kernels for 0%

profile of v5, /device:TPU:0, one launch (start us, length us, event | category | flops | bytes accessed | tf_op | source)
XLA Modules:
  0.0 59.1 jit_solution(13608099334741479957)
XLA Ops:
  0.6 0.0 copy-start.6
  0.6 0.0 copy-start.7
  0.7 0.0 copy-start
  0.7 0.0 copy-start.1
  0.7 0.0 copy-start.2
  0.7 0.0 copy-start.3
  0.7 2.4 %shard_map.112 = (f32[176,128]{1,0:T(8,128)}, f32[64,128]{1,0:T(8,128)}, f32[96,128]{1,0:T(8,128)}) custom-call(f32[10,16,108]{2,1,0:T(8,128)} %bitcast.16, f32[10,16,108]{2,1,0:T(8,128)} %bitcast.10, f32[10,16,108]{2,1,0:T(8,128)} %bitcast.13, s32[2,16,108]{2,1,0:T(8,128)} %refs_7_.3, f32[2,16,108]{2,1,0:T(8,128)} %refs_4_.1, f32[2,16,108]{2,1,0:T(8,128)} %refs_5_.1, ...), custom_call_target="tpu_custom_call" | custom-call | tf_op jit(solution)/shard_map/pallas_call | solution.py:165
  3.1 0.5 collective-permute-start
  3.6 2.6 %collective-permute-start.2 = (f32[64,128]{1,0:T(8,128)}, f32[64,128]{1,0:T(8,128)S(1)}, u32[]{:S(2)}, u32[]{:S(2)}) collective-permute-start(f32[64,128]{1,0:T(8,128)} %get-tuple-element.39), channel_id=1, source_target_pairs={{0,3},{1,2},{2,1},{3,0},{4,7},{5,6},{6,5},{7,4},{8,11},{9,10},{10,... | collective-permute-start | bytes 98312 | tf_op jit(solution)/shard_map/ppermute | solution.py:622
  6.2 0.0 collective-permute-start.1
  6.3 0.0 copy-done.6
  6.3 0.1 copy.13
  6.4 0.1 broadcast_in_dim.6
  6.5 0.9 %copy-done.4 = f32[176,128]{1,0:T(8,128)S(1)} copy-done((f32[176,128]{1,0:T(8,128)S(1)}, f32[176,128]{1,0:T(8,128)}, u32[]{:S(2)}) %copy-start.4) | copy-done | bytes 90136
  7.4 0.8 %copy-done.5 = f32[96,128]{1,0:T(8,128)S(1)} copy-done((f32[96,128]{1,0:T(8,128)S(1)}, f32[96,128]{1,0:T(8,128)}, u32[]{:S(2)}) %copy-start.5) | copy-done | bytes 49176
  8.2 0.0 collective-permute-done.2.refs_3_
  8.2 2.2 %collective-permute-done.1.refs_2_ = f32[64,128]{1,0:T(8,128)S(1)} collective-permute-done((f32[64,128]{1,0:T(8,128)}, f32[64,128]{1,0:T(8,128)S(1)}, u32[]{:S(2)}, u32[]{:S(2)}) %collective-permute-start.1) | collective-permute-done | bytes 32800 | tf_op jit(solution)/shard_map/ppermute | solution.py:622
  10.3 0.0 collective-permute-done.refs_1_
  10.3 0.1 broadcast_in_dim.14.refs_4_
  10.4 0.1 shard_map.114
  10.6 3.7 %collective-permute-start.5 = (f32[248,128]{1,0:T(8,128)S(1)}, f32[248,128]{1,0:T(8,128)S(1)}, u32[]{:S(2)}, u32[]{:S(2)}) collective-permute-start(f32[248,128]{1,0:T(8,128)S(1)} %get-tuple-element.41.own), channel_id=1, source_target_pairs={{0,12},{1,13},{2,14},{3,15},{4,8},{5,9},{6,10},{7,11},{8,4},{9,5},... | collective-permute-start | bytes 380936 | tf_op jit(solution)/shard_map/ppermute | solution.py:622
  14.2 0.0 collective-permute-start.3
  14.2 0.8 %collective-permute-start.4 = (f32[136,128]{1,0:T(8,128)S(1)}, f32[136,128]{1,0:T(8,128)S(1)}, u32[]{:S(2)}, u32[]{:S(2)}) collective-permute-start(f32[136,128]{1,0:T(8,128)S(1)} %get-tuple-element.42), channel_id=1, source_target_pairs={{0,8},{1,9},{2,10},{3,11},{4,12},{5,13},{6,14},{7,15},{8,0},{9,1},... | collective-permute-start | bytes 208904 | tf_op jit(solution)/shard_map/ppermute | solution.py:622
  15.0 6.6 %collective-permute-done.4.near = f32[136,128]{1,0:T(8,128)S(1)} collective-permute-done((f32[136,128]{1,0:T(8,128)S(1)}, f32[136,128]{1,0:T(8,128)S(1)}, u32[]{:S(2)}, u32[]{:S(2)}) %collective-permute-start.4) | collective-permute-done | bytes 69664 | tf_op jit(solution)/shard_map/ppermute | solution.py:622
  21.6 0.0 collective-permute-done.5.third
  21.6 0.0 collective-permute-done.3.first
  21.6 0.1 broadcast_in_dim.15.steps
  21.6 2.8 %shard_map.115 = (f32[3,2,56,128]{3,2,1,0:T(8,128)S(1)}, f32[3,2,40,128]{3,2,1,0:T(8,128)S(1)}, f32[10,40,128]{2,1,0:T(8,128)S(1)}, f32[16,128]{1,0:T(8,128)S(1)...) custom-call(f32[248,128]{1,0:T(8,128)S(1)} %get-tuple-element.41.own, f32[248,128]{1,0:T(8,128)S(1)} %collective-permute-done.3.first, ...), custom_call_target="tpu_custom_call" | custom-call | tf_op jit(solution)/shard_map/pallas_call | solution.py:165
  24.5 0.1 collective-permute-start.6
  24.5 1.3 %collective-permute-done.6.refs_1_ = f32[160,128]{1,0:T(8,128)S(1)} collective-permute-done((f32[160,128]{1,0:T(8,128)S(1)}, f32[160,128]{1,0:T(8,128)S(1)}, u32[]{:S(2)}, u32[]{:S(2)}) %collective-permute-start.6) | collective-permute-done | bytes 81952 | tf_op jit(solution)/shard_map/ppermute | solution.py:622
  25.8 0.0 copy-done
  25.8 0.0 copy-done.2
  25.8 0.3 shard_map.116
  26.1 0.2 collective-permute-start.7
  26.4 1.0 %collective-permute-start.9 = (f32[56,128]{1,0:T(8,128)S(1)}, f32[56,128]{1,0:T(8,128)S(1)}, u32[]{:S(2)}, u32[]{:S(2)}) collective-permute-start(f32[56,128]{1,0:T(8,128)S(1)} %get-tuple-element.47), channel_id=1, source_target_pairs={{0,3},{1,2},{2,1},{3,0},{4,7},{5,6},{6,5},{7,4},{8,11},{9,10},{10,... | collective-permute-start | bytes 86024 | tf_op jit(solution)/shard_map/ppermute | solution.py:622
  27.3 1.0 %collective-permute-start.8 = (f32[56,128]{1,0:T(8,128)S(1)}, f32[56,128]{1,0:T(8,128)S(1)}, u32[]{:S(2)}, u32[]{:S(2)}) collective-permute-start(f32[56,128]{1,0:T(8,128)S(1)} %get-tuple-element.47), channel_id=1, source_target_pairs={{0,2},{1,3},{2,0},{3,1},{4,6},{5,7},{6,4},{7,5},{8,10},{9,11},{10,... | collective-permute-start | bytes 86024 | tf_op jit(solution)/shard_map/ppermute | solution.py:622
  28.4 1.3 %collective-permute-done.9.refs_3_ = f32[56,128]{1,0:T(8,128)S(1)} collective-permute-done((f32[56,128]{1,0:T(8,128)S(1)}, f32[56,128]{1,0:T(8,128)S(1)}, u32[]{:S(2)}, u32[]{:S(2)}) %collective-permute-start.9) | collective-permute-done | bytes 28704 | tf_op jit(solution)/shard_map/ppermute | solution.py:622
  29.7 1.5 %collective-permute-done.8.refs_2_ = f32[56,128]{1,0:T(8,128)S(1)} collective-permute-done((f32[56,128]{1,0:T(8,128)S(1)}, f32[56,128]{1,0:T(8,128)S(1)}, u32[]{:S(2)}, u32[]{:S(2)}) %collective-permute-start.8) | collective-permute-done | bytes 28704 | tf_op jit(solution)/shard_map/ppermute | solution.py:622
  31.2 0.0 collective-permute-done.7.refs_1_
  31.2 0.1 shard_map.117
  31.3 2.0 %collective-permute-start.12 = (f32[184,128]{1,0:T(8,128)S(1)}, f32[184,128]{1,0:T(8,128)S(1)}, u32[]{:S(2)}, u32[]{:S(2)}) collective-permute-start(f32[184,128]{1,0:T(8,128)S(1)} %get-tuple-element.48.own), channel_id=1, source_target_pairs={{0,12},{1,13},{2,14},{3,15},{4,8},{5,9},{6,10},{7,11},{8,4},{9,5},... | collective-permute-start | bytes 282632 | tf_op jit(solution)/shard_map/ppermute | solution.py:622
  33.3 0.6 %collective-permute-start.10 = (f32[184,128]{1,0:T(8,128)S(1)}, f32[184,128]{1,0:T(8,128)S(1)}, u32[]{:S(2)}, u32[]{:S(2)}) collective-permute-start(f32[184,128]{1,0:T(8,128)S(1)} %get-tuple-element.48.own), channel_id=1, source_target_pairs={{0,4},{1,5},{2,6},{3,7},{4,0},{5,1},{6,2},{7,3},{8,12},{9,13},{10,... | collective-permute-start | bytes 282632 | tf_op jit(solution)/shard_map/ppermute | solution.py:622
  34.0 1.8 %collective-permute-start.11 = (f32[104,128]{1,0:T(8,128)S(1)}, f32[104,128]{1,0:T(8,128)S(1)}, u32[]{:S(2)}, u32[]{:S(2)}) collective-permute-start(f32[104,128]{1,0:T(8,128)S(1)} %get-tuple-element.49), channel_id=1, source_target_pairs={{0,8},{1,9},{2,10},{3,11},{4,12},{5,13},{6,14},{7,15},{8,0},{9,1},... | collective-permute-start | bytes 159752 | tf_op jit(solution)/shard_map/ppermute | solution.py:622
  35.8 3.9 %collective-permute-done.11.near = f32[104,128]{1,0:T(8,128)S(1)} collective-permute-done((f32[104,128]{1,0:T(8,128)S(1)}, f32[104,128]{1,0:T(8,128)S(1)}, u32[]{:S(2)}, u32[]{:S(2)}) %collective-permute-start.11) | collective-permute-done | bytes 53280 | tf_op jit(solution)/shard_map/ppermute | solution.py:622
  39.7 0.0 collective-permute-done.12.third
  39.7 0.4 collective-permute-done.10.first
  40.1 2.9 %shard_map.118 = (f32[10,16,128]{2,1,0:T(8,128)S(1)}, f32[10,16,128]{2,1,0:T(8,128)S(1)}, f32[16,128]{1,0:T(8,128)S(1)}, f32[8,128]{1,0:T(8,128)S(1)}, f32[8,128]{1,0:T(8,128)S(1)}, /*index=5*/f32[160,128]{1,0:T(8,128)S(1)}) custom-call(f32[184,128]{1,0:T(8,128)S(1)} %get-tuple-element.48.own, f32[184,128]{1,0:T(8,128)S(1)} %collective-permute-done.10.first, ...), custom_call_target="tpu_custom_call" | custom-call | tf_op jit(solution)/shard_map/pallas_call | solution.py:165
  42.9 0.1 collective-permute-start.13
  43.0 1.3 %collective-permute-done.13.refs_1_ = f32[160,128]{1,0:T(8,128)S(1)} collective-permute-done((f32[160,128]{1,0:T(8,128)S(1)}, f32[160,128]{1,0:T(8,128)S(1)}, u32[]{:S(2)}, u32[]{:S(2)}) %collective-permute-start.13) | collective-permute-done | bytes 81952 | tf_op jit(solution)/shard_map/ppermute | solution.py:622
  44.3 0.4 shard_map.119
  44.6 0.2 collective-permute-start.14
  44.8 0.9 %collective-permute-start.16 = (f32[40,128]{1,0:T(8,128)S(1)}, f32[40,128]{1,0:T(8,128)S(1)}, u32[]{:S(2)}, u32[]{:S(2)}) collective-permute-start(f32[40,128]{1,0:T(8,128)S(1)} %get-tuple-element.58), channel_id=1, source_target_pairs={{0,3},{1,2},{2,1},{3,0},{4,7},{5,6},{6,5},{7,4},{8,11},{9,10},{10,... | collective-permute-start | bytes 61448 | tf_op jit(solution)/shard_map/ppermute | solution.py:622
  45.8 1.0 %collective-permute-start.15 = (f32[40,128]{1,0:T(8,128)S(1)}, f32[40,128]{1,0:T(8,128)S(1)}, u32[]{:S(2)}, u32[]{:S(2)}) collective-permute-start(f32[40,128]{1,0:T(8,128)S(1)} %get-tuple-element.58), channel_id=1, source_target_pairs={{0,2},{1,3},{2,0},{3,1},{4,6},{5,7},{6,4},{7,5},{8,10},{9,11},{10,... | collective-permute-start | bytes 61448 | tf_op jit(solution)/shard_map/ppermute | solution.py:622
  46.8 1.2 %collective-permute-done.16.refs_3_ = f32[40,128]{1,0:T(8,128)S(1)} collective-permute-done((f32[40,128]{1,0:T(8,128)S(1)}, f32[40,128]{1,0:T(8,128)S(1)}, u32[]{:S(2)}, u32[]{:S(2)}) %collective-permute-start.16) | collective-permute-done | bytes 20512 | tf_op jit(solution)/shard_map/ppermute | solution.py:622
  48.0 1.5 %collective-permute-done.15.refs_2_ = f32[40,128]{1,0:T(8,128)S(1)} collective-permute-done((f32[40,128]{1,0:T(8,128)S(1)}, f32[40,128]{1,0:T(8,128)S(1)}, u32[]{:S(2)}, u32[]{:S(2)}) %collective-permute-start.15) | collective-permute-done | bytes 20512 | tf_op jit(solution)/shard_map/ppermute | solution.py:622
  49.5 0.0 collective-permute-done.14.refs_1_
  49.5 0.1 shard_map.120
  49.7 0.8 %collective-permute-start.17 = (f32[112,128]{1,0:T(8,128)S(1)}, f32[112,128]{1,0:T(8,128)S(1)}, u32[]{:S(2)}, u32[]{:S(2)}) collective-permute-start(f32[112,128]{1,0:T(8,128)S(1)} %get-tuple-element.60), channel_id=1, source_target_pairs={{0,4},{1,5},{2,6},{3,7},{4,0},{5,1},{6,2},{7,3},{8,12},{9,13},{10,... | collective-permute-start | bytes 172040 | tf_op jit(solution)/shard_map/ppermute | solution.py:622
  50.4 2.2 %collective-permute-start.18 = (f32[112,128]{1,0:T(8,128)S(1)}, f32[112,128]{1,0:T(8,128)S(1)}, u32[]{:S(2)}, u32[]{:S(2)}) collective-permute-start(f32[112,128]{1,0:T(8,128)S(1)} %get-tuple-element.61), channel_id=1, source_target_pairs={{0,12},{1,13},{2,14},{3,15},{4,8},{5,9},{6,10},{7,11},{8,4},{9,5},... | collective-permute-start | bytes 172040 | tf_op jit(solution)/shard_map/ppermute | solution.py:622
  52.7 0.6 collective-permute-start.19
  53.2 4.0 %collective-permute-done.19.sums_two = f32[8,128]{1,0:T(8,128)S(1)} collective-permute-done((f32[8,128]{1,0:T(8,128)S(1)}, f32[8,128]{1,0:T(8,128)S(1)}, u32[]{:S(2)}, u32[]{:S(2)}) %collective-permute-start.19) | collective-permute-done | bytes 4128 | tf_op jit(solution)/shard_map/ppermute | solution.py:622
  57.2 0.0 collective-permute-done.17.one
  57.2 0.0 collective-permute-done.18.three
  57.2 1.9 %shard_map.121 = (f32[10,16,108]{2,1,0:T(8,128)}, f32[1,16]{1,0:T(1,128)}, f32[10,16,108]{2,1,0:T(8,128)}) custom-call(f32[160,128]{1,0:T(8,128)S(1)} %get-tuple-element.59.own, f32[112,128]{1,0:T(8,128)S(1)} %collective-permute-done.17.one, f32[112,128]{1,0:T(8,128)S(1)} %collective-permute-done.18.three, f32[8,128]{1,0:T(8,128)S(1)} %get-tuple-element.62.sums, ...), custom_call_target="tpu_custom_call" | custom-call | tf_op jit(solution)/shard_map/pallas_call | solution.py:165
  (7 shorter events, 0.0 us)
Async XLA Ops:
  0.6 5.6 %copy-start.6 = (f32[5,4,4]{0,2,1:T(4,128)S(1)}, f32[5,4,4]{0,2,1:T(4,128)}, u32[]{:S(2)}) copy-start(f32[5,4,4]{0,2,1:T(4,128)} %param.16) | copy-start | bytes 964
  0.6 14.4 %copy-start.7 = (s32[5]{0:T(128)S(1)}, s32[5]{0:T(128)}, u32[]{:S(2)}) copy-start(s32[5]{0:T(128)} %param.17) | copy-start | bytes 64
  0.7 25.2 %copy-start = (f32[16,5,2,16,108]{4,3,2,1,0:T(8,128)S(1)}, f32[16,5,2,16,108]{4,3,2,1,0:T(8,128)}, u32[]{:S(2)}) copy-start(f32[16,5,2,16,108]{4,3,2,1,0:T(8,128)} %param.15) | copy-start | bytes 3317764
  0.7 25.1 %copy-start.1 = (f32[5,2,16,108]{3,2,1,0:T(8,128)S(1)}, f32[5,2,16,108]{3,2,1,0:T(8,128)}, u32[]{:S(2)}) copy-start(f32[5,2,16,108]{3,2,1,0:T(8,128)} %param.10) | copy-start | bytes 207364
  0.7 25.1 %copy-start.2 = (f32[5,2,16,108]{3,2,1,0:T(8,128)S(1)}, f32[5,2,16,108]{3,2,1,0:T(8,128)}, u32[]{:S(2)}) copy-start(f32[5,2,16,108]{3,2,1,0:T(8,128)} %param.11) | copy-start | bytes 207364
  0.7 25.1 %copy-start.3 = (s32[2,16,108]{2,1,0:T(8,128)S(1)}, s32[2,16,108]{2,1,0:T(8,128)}, u32[]{:S(2)}) copy-start(s32[2,16,108]{2,1,0:T(8,128)} %refs_7_.3) | copy-start | bytes 41476
  3.1 7.3 %collective-permute-start = (f32[176,128]{1,0:T(8,128)}, f32[176,128]{1,0:T(8,128)S(1)}, u32[]{:S(2)}, u32[]{:S(2)}) collective-permute-start(f32[176,128]{1,0:T(8,128)} %get-tuple-element.36.refs_0_), channel_id=1, source_target_pairs={{0,1},{1,0},{2,3},{3,2},{4,5},{5,4},{6,7},{7,6},{8,9},{9,8},{10,11... | collective-permute-start | bytes 270344 | tf_op jit(solution)/shard_map/ppermute | solution.py:622
  3.6 4.6 %collective-permute-start.2 = (f32[64,128]{1,0:T(8,128)}, f32[64,128]{1,0:T(8,128)S(1)}, u32[]{:S(2)}, u32[]{:S(2)}) collective-permute-start(f32[64,128]{1,0:T(8,128)} %get-tuple-element.39), channel_id=1, source_target_pairs={{0,3},{1,2},{2,1},{3,0},{4,7},{5,6},{6,5},{7,4},{8,11},{9,10},{10,... | collective-permute-start | bytes 98312 | tf_op jit(solution)/shard_map/ppermute | solution.py:622
  6.2 4.1 %collective-permute-start.1 = (f32[64,128]{1,0:T(8,128)}, f32[64,128]{1,0:T(8,128)S(1)}, u32[]{:S(2)}, u32[]{:S(2)}) collective-permute-start(f32[64,128]{1,0:T(8,128)} %get-tuple-element.39), channel_id=1, source_target_pairs={{0,2},{1,3},{2,0},{3,1},{4,6},{5,7},{6,4},{7,5},{8,10},{9,11},{10,... | collective-permute-start | bytes 98312 | tf_op jit(solution)/shard_map/ppermute | solution.py:622
  6.5 0.9 %copy-start.4 = (f32[176,128]{1,0:T(8,128)S(1)}, f32[176,128]{1,0:T(8,128)}, u32[]{:S(2)}) copy-start(f32[176,128]{1,0:T(8,128)} %get-tuple-element.36.refs_0_) | copy-start | bytes 270340
  7.4 0.8 %copy-start.5 = (f32[96,128]{1,0:T(8,128)S(1)}, f32[96,128]{1,0:T(8,128)}, u32[]{:S(2)}) copy-start(f32[96,128]{1,0:T(8,128)} %get-tuple-element.37.refs_1_) | copy-start | bytes 147460
  10.6 11.0 %collective-permute-start.5 = (f32[248,128]{1,0:T(8,128)S(1)}, f32[248,128]{1,0:T(8,128)S(1)}, u32[]{:S(2)}, u32[]{:S(2)}) collective-permute-start(f32[248,128]{1,0:T(8,128)S(1)} %get-tuple-element.41.own), channel_id=1, source_target_pairs={{0,12},{1,13},{2,14},{3,15},{4,8},{5,9},{6,10},{7,11},{8,4},{9,5},... | collective-permute-start | bytes 380936 | tf_op jit(solution)/shard_map/ppermute | solution.py:622
  14.2 7.4 %collective-permute-start.3 = (f32[248,128]{1,0:T(8,128)S(1)}, f32[248,128]{1,0:T(8,128)S(1)}, u32[]{:S(2)}, u32[]{:S(2)}) collective-permute-start(f32[248,128]{1,0:T(8,128)S(1)} %get-tuple-element.41.own), channel_id=1, source_target_pairs={{0,4},{1,5},{2,6},{3,7},{4,0},{5,1},{6,2},{7,3},{8,12},{9,13},{10,... | collective-permute-start | bytes 380936 | tf_op jit(solution)/shard_map/ppermute | solution.py:622
  14.2 7.3 %collective-permute-start.4 = (f32[136,128]{1,0:T(8,128)S(1)}, f32[136,128]{1,0:T(8,128)S(1)}, u32[]{:S(2)}, u32[]{:S(2)}) collective-permute-start(f32[136,128]{1,0:T(8,128)S(1)} %get-tuple-element.42), channel_id=1, source_target_pairs={{0,8},{1,9},{2,10},{3,11},{4,12},{5,13},{6,14},{7,15},{8,0},{9,1},... | collective-permute-start | bytes 208904 | tf_op jit(solution)/shard_map/ppermute | solution.py:622
  24.5 1.3 %collective-permute-start.6 = (f32[160,128]{1,0:T(8,128)S(1)}, f32[160,128]{1,0:T(8,128)S(1)}, u32[]{:S(2)}, u32[]{:S(2)}) collective-permute-start(f32[160,128]{1,0:T(8,128)S(1)} %get-tuple-element.43.refs_0_), channel_id=1, source_target_pairs={{0,1},{1,0},{2,3},{3,2},{4,5},{5,4},{6,7},{7,6},{8,9},{9,8},{10,11... | collective-permute-start | bytes 245768 | tf_op jit(solution)/shard_map/ppermute | solution.py:622
  26.1 5.0 %collective-permute-start.7 = (f32[184,128]{1,0:T(8,128)S(1)}, f32[184,128]{1,0:T(8,128)S(1)}, u32[]{:S(2)}, u32[]{:S(2)}) collective-permute-start(f32[184,128]{1,0:T(8,128)S(1)} %get-tuple-element.46.refs_0_), channel_id=1, source_target_pairs={{0,1},{1,0},{2,3},{3,2},{4,5},{5,4},{6,7},{7,6},{8,9},{9,8},{10,11... | collective-permute-start | bytes 282632 | tf_op jit(solution)/shard_map/ppermute | solution.py:622
  26.4 3.3 %collective-permute-start.9 = (f32[56,128]{1,0:T(8,128)S(1)}, f32[56,128]{1,0:T(8,128)S(1)}, u32[]{:S(2)}, u32[]{:S(2)}) collective-permute-start(f32[56,128]{1,0:T(8,128)S(1)} %get-tuple-element.47), channel_id=1, source_target_pairs={{0,3},{1,2},{2,1},{3,0},{4,7},{5,6},{6,5},{7,4},{8,11},{9,10},{10,... | collective-permute-start | bytes 86024 | tf_op jit(solution)/shard_map/ppermute | solution.py:622
  27.3 3.9 %collective-permute-start.8 = (f32[56,128]{1,0:T(8,128)S(1)}, f32[56,128]{1,0:T(8,128)S(1)}, u32[]{:S(2)}, u32[]{:S(2)}) collective-permute-start(f32[56,128]{1,0:T(8,128)S(1)} %get-tuple-element.47), channel_id=1, source_target_pairs={{0,2},{1,3},{2,0},{3,1},{4,6},{5,7},{6,4},{7,5},{8,10},{9,11},{10,... | collective-permute-start | bytes 86024 | tf_op jit(solution)/shard_map/ppermute | solution.py:622
  31.3 8.4 %collective-permute-start.12 = (f32[184,128]{1,0:T(8,128)S(1)}, f32[184,128]{1,0:T(8,128)S(1)}, u32[]{:S(2)}, u32[]{:S(2)}) collective-permute-start(f32[184,128]{1,0:T(8,128)S(1)} %get-tuple-element.48.own), channel_id=1, source_target_pairs={{0,12},{1,13},{2,14},{3,15},{4,8},{5,9},{6,10},{7,11},{8,4},{9,5},... | collective-permute-start | bytes 282632 | tf_op jit(solution)/shard_map/ppermute | solution.py:622
  33.3 6.7 %collective-permute-start.10 = (f32[184,128]{1,0:T(8,128)S(1)}, f32[184,128]{1,0:T(8,128)S(1)}, u32[]{:S(2)}, u32[]{:S(2)}) collective-permute-start(f32[184,128]{1,0:T(8,128)S(1)} %get-tuple-element.48.own), channel_id=1, source_target_pairs={{0,4},{1,5},{2,6},{3,7},{4,0},{5,1},{6,2},{7,3},{8,12},{9,13},{10,... | collective-permute-start | bytes 282632 | tf_op jit(solution)/shard_map/ppermute | solution.py:622
  34.0 5.7 %collective-permute-start.11 = (f32[104,128]{1,0:T(8,128)S(1)}, f32[104,128]{1,0:T(8,128)S(1)}, u32[]{:S(2)}, u32[]{:S(2)}) collective-permute-start(f32[104,128]{1,0:T(8,128)S(1)} %get-tuple-element.49), channel_id=1, source_target_pairs={{0,8},{1,9},{2,10},{3,11},{4,12},{5,13},{6,14},{7,15},{8,0},{9,1},... | collective-permute-start | bytes 159752 | tf_op jit(solution)/shard_map/ppermute | solution.py:622
  42.9 1.3 %collective-permute-start.13 = (f32[160,128]{1,0:T(8,128)S(1)}, f32[160,128]{1,0:T(8,128)S(1)}, u32[]{:S(2)}, u32[]{:S(2)}) collective-permute-start(f32[160,128]{1,0:T(8,128)S(1)} %get-tuple-element.53.refs_0_), channel_id=1, source_target_pairs={{0,1},{1,0},{2,3},{3,2},{4,5},{5,4},{6,7},{7,6},{8,9},{9,8},{10,11... | collective-permute-start | bytes 245768 | tf_op jit(solution)/shard_map/ppermute | solution.py:622
  44.6 4.9 %collective-permute-start.14 = (f32[168,128]{1,0:T(8,128)S(1)}, f32[168,128]{1,0:T(8,128)S(1)}, u32[]{:S(2)}, u32[]{:S(2)}) collective-permute-start(f32[168,128]{1,0:T(8,128)S(1)} %get-tuple-element.57.refs_0_), channel_id=1, source_target_pairs={{0,1},{1,0},{2,3},{3,2},{4,5},{5,4},{6,7},{7,6},{8,9},{9,8},{10,11... | collective-permute-start | bytes 258056 | tf_op jit(solution)/shard_map/ppermute | solution.py:622
  44.8 3.2 %collective-permute-start.16 = (f32[40,128]{1,0:T(8,128)S(1)}, f32[40,128]{1,0:T(8,128)S(1)}, u32[]{:S(2)}, u32[]{:S(2)}) collective-permute-start(f32[40,128]{1,0:T(8,128)S(1)} %get-tuple-element.58), channel_id=1, source_target_pairs={{0,3},{1,2},{2,1},{3,0},{4,7},{5,6},{6,5},{7,4},{8,11},{9,10},{10,... | collective-permute-start | bytes 61448 | tf_op jit(solution)/shard_map/ppermute | solution.py:622
  45.8 3.8 %collective-permute-start.15 = (f32[40,128]{1,0:T(8,128)S(1)}, f32[40,128]{1,0:T(8,128)S(1)}, u32[]{:S(2)}, u32[]{:S(2)}) collective-permute-start(f32[40,128]{1,0:T(8,128)S(1)} %get-tuple-element.58), channel_id=1, source_target_pairs={{0,2},{1,3},{2,0},{3,1},{4,6},{5,7},{6,4},{7,5},{8,10},{9,11},{10,... | collective-permute-start | bytes 61448 | tf_op jit(solution)/shard_map/ppermute | solution.py:622
  49.7 7.5 %collective-permute-start.17 = (f32[112,128]{1,0:T(8,128)S(1)}, f32[112,128]{1,0:T(8,128)S(1)}, u32[]{:S(2)}, u32[]{:S(2)}) collective-permute-start(f32[112,128]{1,0:T(8,128)S(1)} %get-tuple-element.60), channel_id=1, source_target_pairs={{0,4},{1,5},{2,6},{3,7},{4,0},{5,1},{6,2},{7,3},{8,12},{9,13},{10,... | collective-permute-start | bytes 172040 | tf_op jit(solution)/shard_map/ppermute | solution.py:622
  50.4 6.8 %collective-permute-start.18 = (f32[112,128]{1,0:T(8,128)S(1)}, f32[112,128]{1,0:T(8,128)S(1)}, u32[]{:S(2)}, u32[]{:S(2)}) collective-permute-start(f32[112,128]{1,0:T(8,128)S(1)} %get-tuple-element.61), channel_id=1, source_target_pairs={{0,12},{1,13},{2,14},{3,15},{4,8},{5,9},{6,10},{7,11},{8,4},{9,5},... | collective-permute-start | bytes 172040 | tf_op jit(solution)/shard_map/ppermute | solution.py:622
  52.7 4.5 %collective-permute-start.19 = (f32[8,128]{1,0:T(8,128)S(1)}, f32[8,128]{1,0:T(8,128)S(1)}, u32[]{:S(2)}, u32[]{:S(2)}) collective-permute-start(f32[8,128]{1,0:T(8,128)S(1)} %get-tuple-element.62.sums), channel_id=1, source_target_pairs={{0,8},{1,9},{2,10},{3,11},{4,12},{5,13},{6,14},{7,15},{8,0},{9,1},... | collective-permute-start | bytes 12296 | tf_op jit(solution)/shard_map/ppermute | solution.py:622

commit v6 on v5

--- a/solution.py
+++ b/solution.py
@@ -242,13 +242,14 @@
             out_z[plane * ROWS : (plane + 1) * ROWS, :cols] = scale[plane] * weighted[plane]
         edges = [tile(out_z, plane) for plane in range(planes)]
         pack_edges(out_e, edges + [tile(coef, index) for index in range(3 * levels)], cols)
-        for move in moves[6:]:
-            move.wait()
-        totals = [jnp.zeros((ROWS, cols), jnp.float32) for _ in range(count)]
-        for plane in range(planes):
-            for m in range(count):
-                totals[m] += members[m, plane] * weighted[plane]
-        project(out_z, base, totals, ens_scale)
+        each = count // FETCHES
+        for part in range(FETCHES):
+            moves[6 + part].wait()
+            totals = [jnp.zeros((ROWS, cols), jnp.float32) for _ in range(each)]
+            for plane in range(planes):
+                for m in range(each):
+                    totals[m] += members[part * each + m, plane] * weighted[plane]
+            project(out_z, base + part * each, totals, ens_scale)
         out_e[edge_rows:, :] = out_z[base:, :]
 
     outs = [f32(base + ROWS, LANES), f32(edge_rows + ROWS, LANES), f32(3 * levels * ROWS, LANES)]
@@ -575,10 +576,7 @@
 
 
 def last_diffuse(planes, levels, cols):
-    def kernel(
-        own, one, three, sums, sums_two, steps, coef, resid, weights, image, new, new_w, facts,
-        control, control_w, final, buf, nat,
-    ):
+    def kernel(own, one, three, sums, steps, coef, out_g, out_sums, buf, nat):
         even = is_even()
         gap_rows = jnp.zeros((4, LANES), jnp.float32)
         for plane in range(planes):
@@ -589,7 +587,19 @@
             nat[plane, 30:40, :] = jnp.where(even, third, first)
             deal(buf, nat, plane, NEAR_TILES)
         sent = one.shape[0] - SUMS
-        lanes = (sums[...] + one[sent:, :]) + (sums_two[...] + three[sent:, :])
+        out_sums[0] = sums[...] + one[sent:, :]
+        out_sums[1] = three[sent:, :]
+        run_steps(buf, nat, coef, steps, planes, levels, NEAR_TILES)
+        for plane in range(planes):
+            undeal(nat, buf, plane, NEAR_TILES)
+            out_g[plane] = nat[plane, :ROWS, :]
+
+    return kernel, [f32(planes, ROWS, LANES), f32(2, SUMS, LANES)], window_scratch(planes)
+
+
+def finish(planes, cols):
+    def kernel(diffused, sums, sums_two, resid, weights, image, new, new_w, facts, control, control_w, final):
+        lanes = sums[0] + (sums_two[...] + sums[1])
         total = spread(lanes)
         rr, step = facts[0:1, :], facts[1:2, :]
         new_rr = total[4:5] + over_rows(new_w[...] * new_w[...])
@@ -602,17 +612,14 @@
         combined = step * weights[...] + new_step * (new_w[...] + ratio * weights[...])
         diagonal = lax.broadcasted_iota(jnp.int32, combined.shape, 0) == lanes_of(combined.shape)
         control_w[...] = over_rows(jnp.where(diagonal, combined, 0.0))[:, :ROWS]
-        run_steps(buf, nat, coef, steps, planes, levels, NEAR_TILES)
-        for plane in range(planes):
-            undeal(nat, buf, plane, NEAR_TILES)
+        for plane in range(planes):
             direction, value = resid[plane, :ROWS, :], new[plane]
             new_direction = value + ratio * direction
-            new_image = (value + SQRT_STATIC * nat[plane, :ROWS, :]) + ratio * image[plane]
+            new_image = (value + SQRT_STATIC * diffused[plane]) + ratio * image[plane]
             control[plane] = (step * direction + new_step * new_direction)[:, :cols]
             final[plane] = (value - new_step * new_image)[:, :cols]
 
-    outs = [f32(planes, ROWS, cols), f32(1, ROWS), f32(planes, ROWS, cols)]
-    return kernel, outs, window_scratch(planes)
+    return kernel, [f32(planes, ROWS, cols), f32(1, ROWS), f32(planes, ROWS, cols)]
 
 
 def moved_to(values, x, y, z):
@@ -669,10 +676,13 @@
     args = (out_g, moved_to(out_g, 0, 0, 1), new_w, sums, vert, prec, scale, sea_mask, ens, seen)
     out_z, out_e = call(kernel, outs, [VMEM] * 10, args, scratch)
     own, one, three, sums = mix_round(mix_back(False, False, planes, levels, cols, SUMS), out_z, out_e, vert)
-    parts = (own, moved_to(one, 1, 0, 0), moved_to(three, 3, 0, 0), sums, moved_to(sums, 2, 0, 0))
+    sums_two = moved_to(sums, 2, 0, 0)
     kernel, outs, scratch = last_diffuse(planes, levels, cols)
-    args = (*parts, steps, coef_near, resid, weights, image, new, new_w, facts)
-    control, control_w, final = call(kernel, outs, [VMEM] * 13, args, scratch)
+    args = (own, moved_to(one, 1, 0, 0), moved_to(three, 3, 0, 0), sums, steps, coef_near)
+    diffused, sums = call(kernel, outs, [VMEM] * 6, args, scratch)
+    kernel, outs = finish(planes, cols)
+    args = (diffused, sums, sums_two, resid, weights, image, new, new_w, facts)
+    control, control_w, final = call(kernel, outs, [VMEM] * 9, args)
     return control.reshape(innovation.shape), control_w.reshape(count), final.reshape(innovation.shape)
 
 

time: 59.3 us -> 58.7 us (0.990)
  waiting for transfers between devices: 25.1 us -> 24.3 us
    ppermute x20, waiting for transfers between devices: 25.1 us -> 24.3 us  [moved_to(): lax.ppermute(values, AXES, [(number[a, b, c], number[a ^ x, b ^ y, c ^ z]...]
    pallas_call x10 -> x11, Pallas kernels: 11 us -> 11.1 us  [call(): pl.pallas_call(kernel, out_shape=outs, in_specs=specs, out_specs=[VMEM] *...]
  transfers between devices with their start and end apart: 20 -> 20, of which waited for: 11 -> 12; matrix products, arithmetic and copies ran while one was open for 0% -> 0% of each run, Pallas kernels for 0% -> 2%
where the time goes in v6:
time: 58.7 us; the launch traced here: 58.4 us
  waiting for transfers between devices  24.3 us (41%)
  starting transfers between devices  20.1 us (34%)
  Pallas kernels  11.1 us (19%)
  local copies, waits for them, and re-layouts  2.06 us (4%)
  between operations  0.79 us (1%)
    ppermute x20, waiting for transfers between devices, moved_to(): lax.ppermute(values, AXES, [(number[a, b, c], number[a ^ x, b ^ y, c ^ z]...  24.3 us
    ppermute x20, starting transfers between devices, moved_to(): lax.ppermute(values, AXES, [(number[a, b, c], number[a ^ x, b ^ y, c ^ z]...  20.1 us
    pallas_call x11, Pallas kernels, call(): pl.pallas_call(kernel, out_shape=outs, in_specs=specs, out_specs=[VMEM] *...  11.1 us
    unnamed x17, local copies, waits for them, and re-layouts  1.82 us
  transfers between devices with their start and end apart: 20, of which 12 were waited for; matrix products, arithmetic and copies ran while one was open for 0% of the time, Pallas kernels for 2%

profile of v6, /device:TPU:0, one launch (start us, length us, event | category | flops | bytes accessed | tf_op | source)
XLA Modules:
  0.0 58.4 jit_solution(7165245464376206531)
XLA Ops:
  0.6 0.0 copy-start.6
  0.6 0.0 copy-start.7
  0.7 0.0 copy-start
  0.7 0.0 copy-start.1
  0.7 0.0 copy-start.2
  0.7 0.0 copy-start.3
  0.7 2.3 %shard_map.112 = (f32[176,128]{1,0:T(8,128)}, f32[64,128]{1,0:T(8,128)}, f32[96,128]{1,0:T(8,128)}) custom-call(f32[10,16,108]{2,1,0:T(8,128)} %bitcast.16, f32[10,16,108]{2,1,0:T(8,128)} %bitcast.10, f32[10,16,108]{2,1,0:T(8,128)} %bitcast.13, s32[2,16,108]{2,1,0:T(8,128)} %refs_7_.3, f32[2,16,108]{2,1,0:T(8,128)} %refs_4_.1, f32[2,16,108]{2,1,0:T(8,128)} %refs_5_.1, ...), custom_call_target="tpu_custom_call" | custom-call | tf_op jit(solution)/shard_map/pallas_call | solution.py:165
  3.0 0.5 collective-permute-start
  3.5 2.6 %collective-permute-start.2 = (f32[64,128]{1,0:T(8,128)}, f32[64,128]{1,0:T(8,128)S(1)}, u32[]{:S(2)}, u32[]{:S(2)}) collective-permute-start(f32[64,128]{1,0:T(8,128)} %get-tuple-element.41), channel_id=1, source_target_pairs={{0,3},{1,2},{2,1},{3,0},{4,7},{5,6},{6,5},{7,4},{8,11},{9,10},{10,... | collective-permute-start | bytes 98312 | tf_op jit(solution)/shard_map/ppermute | solution.py:629
  6.1 0.0 collective-permute-start.1
  6.2 0.1 copy.13
  6.3 0.1 broadcast_in_dim.6
  6.4 0.0 copy-start.4
  6.4 0.9 %copy-done.4 = f32[176,128]{1,0:T(8,128)S(1)} copy-done((f32[176,128]{1,0:T(8,128)S(1)}, f32[176,128]{1,0:T(8,128)}, u32[]{:S(2)}) %copy-start.4) | copy-done | bytes 90136
  7.3 0.8 %copy-done.5 = f32[96,128]{1,0:T(8,128)S(1)} copy-done((f32[96,128]{1,0:T(8,128)S(1)}, f32[96,128]{1,0:T(8,128)}, u32[]{:S(2)}) %copy-start.5) | copy-done | bytes 49176
  8.1 0.0 collective-permute-done.2.refs_3_
  8.1 2.2 %collective-permute-done.1.refs_2_ = f32[64,128]{1,0:T(8,128)S(1)} collective-permute-done((f32[64,128]{1,0:T(8,128)}, f32[64,128]{1,0:T(8,128)S(1)}, u32[]{:S(2)}, u32[]{:S(2)}) %collective-permute-start.1) | collective-permute-done | bytes 32800 | tf_op jit(solution)/shard_map/ppermute | solution.py:629
  10.3 0.0 collective-permute-done.refs_1_
  10.3 0.1 broadcast_in_dim.14.refs_4_
  10.3 0.1 shard_map.114
  10.5 3.7 %collective-permute-start.5 = (f32[248,128]{1,0:T(8,128)S(1)}, f32[248,128]{1,0:T(8,128)S(1)}, u32[]{:S(2)}, u32[]{:S(2)}) collective-permute-start(f32[248,128]{1,0:T(8,128)S(1)} %get-tuple-element.43.own), channel_id=1, source_target_pairs={{0,12},{1,13},{2,14},{3,15},{4,8},{5,9},{6,10},{7,11},{8,4},{9,5},... | collective-permute-start | bytes 380936 | tf_op jit(solution)/shard_map/ppermute | solution.py:629
  14.1 0.0 collective-permute-start.3
  14.2 0.8 %collective-permute-start.4 = (f32[136,128]{1,0:T(8,128)S(1)}, f32[136,128]{1,0:T(8,128)S(1)}, u32[]{:S(2)}, u32[]{:S(2)}) collective-permute-start(f32[136,128]{1,0:T(8,128)S(1)} %get-tuple-element.44), channel_id=1, source_target_pairs={{0,8},{1,9},{2,10},{3,11},{4,12},{5,13},{6,14},{7,15},{8,0},{9,1},... | collective-permute-start | bytes 208904 | tf_op jit(solution)/shard_map/ppermute | solution.py:629
  14.9 6.6 %collective-permute-done.4.near = f32[136,128]{1,0:T(8,128)S(1)} collective-permute-done((f32[136,128]{1,0:T(8,128)S(1)}, f32[136,128]{1,0:T(8,128)S(1)}, u32[]{:S(2)}, u32[]{:S(2)}) %collective-permute-start.4) | collective-permute-done | bytes 69664 | tf_op jit(solution)/shard_map/ppermute | solution.py:629
  21.5 0.0 collective-permute-done.5.third
  21.5 0.0 collective-permute-done.3.first
  21.5 0.1 broadcast_in_dim.15.steps
  21.6 2.8 %shard_map.115 = (f32[3,2,56,128]{3,2,1,0:T(8,128)S(1)}, f32[3,2,40,128]{3,2,1,0:T(8,128)S(1)}, f32[10,40,128]{2,1,0:T(8,128)S(1)}, f32[16,128]{1,0:T(8,128)S(1)...) custom-call(f32[248,128]{1,0:T(8,128)S(1)} %get-tuple-element.43.own, f32[248,128]{1,0:T(8,128)S(1)} %collective-permute-done.3.first, ...), custom_call_target="tpu_custom_call" | custom-call | tf_op jit(solution)/shard_map/pallas_call | solution.py:165
  24.4 0.1 collective-permute-start.6
  24.5 1.3 %collective-permute-done.6.refs_1_ = f32[160,128]{1,0:T(8,128)S(1)} collective-permute-done((f32[160,128]{1,0:T(8,128)S(1)}, f32[160,128]{1,0:T(8,128)S(1)}, u32[]{:S(2)}, u32[]{:S(2)}) %collective-permute-start.6) | collective-permute-done | bytes 81952 | tf_op jit(solution)/shard_map/ppermute | solution.py:629
  25.7 0.0 copy-done
  25.7 0.3 shard_map.116
  26.1 0.2 collective-permute-start.7
  26.3 1.0 %collective-permute-start.9 = (f32[56,128]{1,0:T(8,128)S(1)}, f32[56,128]{1,0:T(8,128)S(1)}, u32[]{:S(2)}, u32[]{:S(2)}) collective-permute-start(f32[56,128]{1,0:T(8,128)S(1)} %get-tuple-element.49), channel_id=1, source_target_pairs={{0,3},{1,2},{2,1},{3,0},{4,7},{5,6},{6,5},{7,4},{8,11},{9,10},{10,... | collective-permute-start | bytes 86024 | tf_op jit(solution)/shard_map/ppermute | solution.py:629
  27.2 1.0 %collective-permute-start.8 = (f32[56,128]{1,0:T(8,128)S(1)}, f32[56,128]{1,0:T(8,128)S(1)}, u32[]{:S(2)}, u32[]{:S(2)}) collective-permute-start(f32[56,128]{1,0:T(8,128)S(1)} %get-tuple-element.49), channel_id=1, source_target_pairs={{0,2},{1,3},{2,0},{3,1},{4,6},{5,7},{6,4},{7,5},{8,10},{9,11},{10,... | collective-permute-start | bytes 86024 | tf_op jit(solution)/shard_map/ppermute | solution.py:629
  28.3 1.3 %collective-permute-done.9.refs_3_ = f32[56,128]{1,0:T(8,128)S(1)} collective-permute-done((f32[56,128]{1,0:T(8,128)S(1)}, f32[56,128]{1,0:T(8,128)S(1)}, u32[]{:S(2)}, u32[]{:S(2)}) %collective-permute-start.9) | collective-permute-done | bytes 28704 | tf_op jit(solution)/shard_map/ppermute | solution.py:629
  29.6 1.5 %collective-permute-done.8.refs_2_ = f32[56,128]{1,0:T(8,128)S(1)} collective-permute-done((f32[56,128]{1,0:T(8,128)S(1)}, f32[56,128]{1,0:T(8,128)S(1)}, u32[]{:S(2)}, u32[]{:S(2)}) %collective-permute-start.8) | collective-permute-done | bytes 28704 | tf_op jit(solution)/shard_map/ppermute | solution.py:629
  31.1 0.0 collective-permute-done.7.refs_1_
  31.1 0.1 shard_map.117
  31.2 2.0 %collective-permute-start.12 = (f32[184,128]{1,0:T(8,128)S(1)}, f32[184,128]{1,0:T(8,128)S(1)}, u32[]{:S(2)}, u32[]{:S(2)}) collective-permute-start(f32[184,128]{1,0:T(8,128)S(1)} %get-tuple-element.50.own), channel_id=1, source_target_pairs={{0,12},{1,13},{2,14},{3,15},{4,8},{5,9},{6,10},{7,11},{8,4},{9,5},... | collective-permute-start | bytes 282632 | tf_op jit(solution)/shard_map/ppermute | solution.py:629
  33.3 0.6 %collective-permute-start.10 = (f32[184,128]{1,0:T(8,128)S(1)}, f32[184,128]{1,0:T(8,128)S(1)}, u32[]{:S(2)}, u32[]{:S(2)}) collective-permute-start(f32[184,128]{1,0:T(8,128)S(1)} %get-tuple-element.50.own), channel_id=1, source_target_pairs={{0,4},{1,5},{2,6},{3,7},{4,0},{5,1},{6,2},{7,3},{8,12},{9,13},{10,... | collective-permute-start | bytes 282632 | tf_op jit(solution)/shard_map/ppermute | solution.py:629
  33.9 1.8 %collective-permute-start.11 = (f32[104,128]{1,0:T(8,128)S(1)}, f32[104,128]{1,0:T(8,128)S(1)}, u32[]{:S(2)}, u32[]{:S(2)}) collective-permute-start(f32[104,128]{1,0:T(8,128)S(1)} %get-tuple-element.51), channel_id=1, source_target_pairs={{0,8},{1,9},{2,10},{3,11},{4,12},{5,13},{6,14},{7,15},{8,0},{9,1},... | collective-permute-start | bytes 159752 | tf_op jit(solution)/shard_map/ppermute | solution.py:629
  35.7 3.9 %collective-permute-done.11.near = f32[104,128]{1,0:T(8,128)S(1)} collective-permute-done((f32[104,128]{1,0:T(8,128)S(1)}, f32[104,128]{1,0:T(8,128)S(1)}, u32[]{:S(2)}, u32[]{:S(2)}) %collective-permute-start.11) | collective-permute-done | bytes 53280 | tf_op jit(solution)/shard_map/ppermute | solution.py:629
  39.6 0.0 collective-permute-done.12.third
  39.6 0.4 collective-permute-done.10.first
  40.0 2.9 %shard_map.118 = (f32[10,16,128]{2,1,0:T(8,128)S(1)}, f32[10,16,128]{2,1,0:T(8,128)S(1)}, f32[16,128]{1,0:T(8,128)S(1)}, f32[8,128]{1,0:T(8,128)S(1)}, f32[8,128]{1,0:T(8,128)S(1)}, /*index=5*/f32[160,128]{1,0:T(8,128)S(1)}) custom-call(f32[184,128]{1,0:T(8,128)S(1)} %get-tuple-element.50.own, f32[184,128]{1,0:T(8,128)S(1)} %collective-permute-done.10.first, ...), custom_call_target="tpu_custom_call" | custom-call | tf_op jit(solution)/shard_map/pallas_call | solution.py:165
  42.9 0.1 collective-permute-start.13
  42.9 1.3 %collective-permute-done.13.refs_1_ = f32[160,128]{1,0:T(8,128)S(1)} collective-permute-done((f32[160,128]{1,0:T(8,128)S(1)}, f32[160,128]{1,0:T(8,128)S(1)}, u32[]{:S(2)}, u32[]{:S(2)}) %collective-permute-start.13) | collective-permute-done | bytes 81952 | tf_op jit(solution)/shard_map/ppermute | solution.py:629
  44.2 0.4 shard_map.119
  44.6 0.2 collective-permute-start.14
  44.7 0.9 %collective-permute-start.16 = (f32[40,128]{1,0:T(8,128)S(1)}, f32[40,128]{1,0:T(8,128)S(1)}, u32[]{:S(2)}, u32[]{:S(2)}) collective-permute-start(f32[40,128]{1,0:T(8,128)S(1)} %get-tuple-element.60), channel_id=1, source_target_pairs={{0,3},{1,2},{2,1},{3,0},{4,7},{5,6},{6,5},{7,4},{8,11},{9,10},{10,... | collective-permute-start | bytes 61448 | tf_op jit(solution)/shard_map/ppermute | solution.py:629
  45.7 1.0 %collective-permute-start.15 = (f32[40,128]{1,0:T(8,128)S(1)}, f32[40,128]{1,0:T(8,128)S(1)}, u32[]{:S(2)}, u32[]{:S(2)}) collective-permute-start(f32[40,128]{1,0:T(8,128)S(1)} %get-tuple-element.60), channel_id=1, source_target_pairs={{0,2},{1,3},{2,0},{3,1},{4,6},{5,7},{6,4},{7,5},{8,10},{9,11},{10,... | collective-permute-start | bytes 61448 | tf_op jit(solution)/shard_map/ppermute | solution.py:629
  46.7 1.2 %collective-permute-done.16.refs_3_ = f32[40,128]{1,0:T(8,128)S(1)} collective-permute-done((f32[40,128]{1,0:T(8,128)S(1)}, f32[40,128]{1,0:T(8,128)S(1)}, u32[]{:S(2)}, u32[]{:S(2)}) %collective-permute-start.16) | collective-permute-done | bytes 20512 | tf_op jit(solution)/shard_map/ppermute | solution.py:629
  48.0 1.5 %collective-permute-done.15.refs_2_ = f32[40,128]{1,0:T(8,128)S(1)} collective-permute-done((f32[40,128]{1,0:T(8,128)S(1)}, f32[40,128]{1,0:T(8,128)S(1)}, u32[]{:S(2)}, u32[]{:S(2)}) %collective-permute-start.15) | collective-permute-done | bytes 20512 | tf_op jit(solution)/shard_map/ppermute | solution.py:629
  49.5 0.0 collective-permute-done.14.refs_1_
  49.5 0.1 shard_map.120
  49.6 0.8 %collective-permute-start.17 = (f32[112,128]{1,0:T(8,128)S(1)}, f32[112,128]{1,0:T(8,128)S(1)}, u32[]{:S(2)}, u32[]{:S(2)}) collective-permute-start(f32[112,128]{1,0:T(8,128)S(1)} %get-tuple-element.62), channel_id=1, source_target_pairs={{0,4},{1,5},{2,6},{3,7},{4,0},{5,1},{6,2},{7,3},{8,12},{9,13},{10,... | collective-permute-start | bytes 172040 | tf_op jit(solution)/shard_map/ppermute | solution.py:629
  50.4 2.2 %collective-permute-start.18 = (f32[112,128]{1,0:T(8,128)S(1)}, f32[112,128]{1,0:T(8,128)S(1)}, u32[]{:S(2)}, u32[]{:S(2)}) collective-permute-start(f32[112,128]{1,0:T(8,128)S(1)} %get-tuple-element.63), channel_id=1, source_target_pairs={{0,12},{1,13},{2,14},{3,15},{4,8},{5,9},{6,10},{7,11},{8,4},{9,5},... | collective-permute-start | bytes 172040 | tf_op jit(solution)/shard_map/ppermute | solution.py:629
  52.6 0.6 collective-permute-start.19
  53.2 1.3 %collective-permute-done.17.one = f32[112,128]{1,0:T(8,128)S(1)} collective-permute-done((f32[112,128]{1,0:T(8,128)S(1)}, f32[112,128]{1,0:T(8,128)S(1)}, u32[]{:S(2)}, u32[]{:S(2)}) %collective-permute-start.17) | collective-permute-done | bytes 57376 | tf_op jit(solution)/shard_map/ppermute | solution.py:629
  54.5 1.9 %collective-permute-done.18.three = f32[112,128]{1,0:T(8,128)S(1)} collective-permute-done((f32[112,128]{1,0:T(8,128)S(1)}, f32[112,128]{1,0:T(8,128)S(1)}, u32[]{:S(2)}, u32[]{:S(2)}) %collective-permute-start.18) | collective-permute-done | bytes 57376 | tf_op jit(solution)/shard_map/ppermute | solution.py:629
  56.4 1.2 %shard_map.121 = (f32[10,16,128]{2,1,0:T(8,128)S(1)}, f32[2,8,128]{2,1,0:T(8,128)S(1)}) custom-call(f32[160,128]{1,0:T(8,128)S(1)} %get-tuple-element.61.own, f32[112,128]{1,0:T(8,128)S(1)} %collective-permute-done.17.one, f32[112,128]{1,0:T(8,128)S(1)} %collective-permute-done.18.three, f32[8,128]{1,0:T(8,128)S(1)} %get-tuple-element.64.sums, ...), custom_call_target="tpu_custom_call" | custom-call | tf_op jit(solution)/shard_map/pallas_call | solution.py:165
  57.5 0.0 collective-permute-done.19.sums_two
  57.6 0.9 %shard_map.122 = (f32[10,16,108]{2,1,0:T(8,128)}, f32[1,16]{1,0:T(1,128)}, f32[10,16,108]{2,1,0:T(8,128)}) custom-call(f32[10,16,128]{2,1,0:T(8,128)S(1)} %get-tuple-element.65.diffused, f32[2,8,128]{2,1,0:T(8,128)S(1)} %get-tuple-element.66.sums, f32[8,128]{1,0:T(8,128)S(1)} %collective-permute-done.19.sums_two, ...), custom_call_target="tpu_custom_call" | custom-call | tf_op jit(solution)/shard_map/pallas_call | solution.py:165
  (8 shorter events, 0.0 us)
Async XLA Ops:
  0.6 5.5 %copy-start.6 = (f32[5,4,4]{0,2,1:T(4,128)S(1)}, f32[5,4,4]{0,2,1:T(4,128)}, u32[]{:S(2)}) copy-start(f32[5,4,4]{0,2,1:T(4,128)} %param.16) | copy-start | bytes 964
  0.6 14.3 %copy-start.7 = (s32[5]{0:T(128)S(1)}, s32[5]{0:T(128)}, u32[]{:S(2)}) copy-start(s32[5]{0:T(128)} %param.17) | copy-start | bytes 64
  0.7 25.1 %copy-start = (f32[16,5,2,16,108]{4,3,2,1,0:T(8,128)S(1)}, f32[16,5,2,16,108]{4,3,2,1,0:T(8,128)}, u32[]{:S(2)}) copy-start(f32[16,5,2,16,108]{4,3,2,1,0:T(8,128)} %param.15) | copy-start | bytes 3317764
  0.7 25.1 %copy-start.1 = (f32[5,2,16,108]{3,2,1,0:T(8,128)S(1)}, f32[5,2,16,108]{3,2,1,0:T(8,128)}, u32[]{:S(2)}) copy-start(f32[5,2,16,108]{3,2,1,0:T(8,128)} %param.10) | copy-start | bytes 207364
  0.7 25.1 %copy-start.2 = (f32[5,2,16,108]{3,2,1,0:T(8,128)S(1)}, f32[5,2,16,108]{3,2,1,0:T(8,128)}, u32[]{:S(2)}) copy-start(f32[5,2,16,108]{3,2,1,0:T(8,128)} %param.11) | copy-start | bytes 207364
  0.7 25.1 %copy-start.3 = (s32[2,16,108]{2,1,0:T(8,128)S(1)}, s32[2,16,108]{2,1,0:T(8,128)}, u32[]{:S(2)}) copy-start(s32[2,16,108]{2,1,0:T(8,128)} %refs_7_.3) | copy-start | bytes 41476
  3.0 7.3 %collective-permute-start = (f32[176,128]{1,0:T(8,128)}, f32[176,128]{1,0:T(8,128)S(1)}, u32[]{:S(2)}, u32[]{:S(2)}) collective-permute-start(f32[176,128]{1,0:T(8,128)} %get-tuple-element.38.refs_0_), channel_id=1, source_target_pairs={{0,1},{1,0},{2,3},{3,2},{4,5},{5,4},{6,7},{7,6},{8,9},{9,8},{10,11... | collective-permute-start | bytes 270344 | tf_op jit(solution)/shard_map/ppermute | solution.py:629
  3.5 4.6 %collective-permute-start.2 = (f32[64,128]{1,0:T(8,128)}, f32[64,128]{1,0:T(8,128)S(1)}, u32[]{:S(2)}, u32[]{:S(2)}) collective-permute-start(f32[64,128]{1,0:T(8,128)} %get-tuple-element.41), channel_id=1, source_target_pairs={{0,3},{1,2},{2,1},{3,0},{4,7},{5,6},{6,5},{7,4},{8,11},{9,10},{10,... | collective-permute-start | bytes 98312 | tf_op jit(solution)/shard_map/ppermute | solution.py:629
  6.1 4.1 %collective-permute-start.1 = (f32[64,128]{1,0:T(8,128)}, f32[64,128]{1,0:T(8,128)S(1)}, u32[]{:S(2)}, u32[]{:S(2)}) collective-permute-start(f32[64,128]{1,0:T(8,128)} %get-tuple-element.41), channel_id=1, source_target_pairs={{0,2},{1,3},{2,0},{3,1},{4,6},{5,7},{6,4},{7,5},{8,10},{9,11},{10,... | collective-permute-start | bytes 98312 | tf_op jit(solution)/shard_map/ppermute | solution.py:629
  6.4 0.9 %copy-start.4 = (f32[176,128]{1,0:T(8,128)S(1)}, f32[176,128]{1,0:T(8,128)}, u32[]{:S(2)}) copy-start(f32[176,128]{1,0:T(8,128)} %get-tuple-element.38.refs_0_) | copy-start | bytes 270340
  7.3 0.8 %copy-start.5 = (f32[96,128]{1,0:T(8,128)S(1)}, f32[96,128]{1,0:T(8,128)}, u32[]{:S(2)}) copy-start(f32[96,128]{1,0:T(8,128)} %get-tuple-element.39.refs_1_) | copy-start | bytes 147460
  10.5 11.0 %collective-permute-start.5 = (f32[248,128]{1,0:T(8,128)S(1)}, f32[248,128]{1,0:T(8,128)S(1)}, u32[]{:S(2)}, u32[]{:S(2)}) collective-permute-start(f32[248,128]{1,0:T(8,128)S(1)} %get-tuple-element.43.own), channel_id=1, source_target_pairs={{0,12},{1,13},{2,14},{3,15},{4,8},{5,9},{6,10},{7,11},{8,4},{9,5},... | collective-permute-start | bytes 380936 | tf_op jit(solution)/shard_map/ppermute | solution.py:629
  14.1 7.4 %collective-permute-start.3 = (f32[248,128]{1,0:T(8,128)S(1)}, f32[248,128]{1,0:T(8,128)S(1)}, u32[]{:S(2)}, u32[]{:S(2)}) collective-permute-start(f32[248,128]{1,0:T(8,128)S(1)} %get-tuple-element.43.own), channel_id=1, source_target_pairs={{0,4},{1,5},{2,6},{3,7},{4,0},{5,1},{6,2},{7,3},{8,12},{9,13},{10,... | collective-permute-start | bytes 380936 | tf_op jit(solution)/shard_map/ppermute | solution.py:629
  14.2 7.3 %collective-permute-start.4 = (f32[136,128]{1,0:T(8,128)S(1)}, f32[136,128]{1,0:T(8,128)S(1)}, u32[]{:S(2)}, u32[]{:S(2)}) collective-permute-start(f32[136,128]{1,0:T(8,128)S(1)} %get-tuple-element.44), channel_id=1, source_target_pairs={{0,8},{1,9},{2,10},{3,11},{4,12},{5,13},{6,14},{7,15},{8,0},{9,1},... | collective-permute-start | bytes 208904 | tf_op jit(solution)/shard_map/ppermute | solution.py:629
  24.4 1.3 %collective-permute-start.6 = (f32[160,128]{1,0:T(8,128)S(1)}, f32[160,128]{1,0:T(8,128)S(1)}, u32[]{:S(2)}, u32[]{:S(2)}) collective-permute-start(f32[160,128]{1,0:T(8,128)S(1)} %get-tuple-element.45.refs_0_), channel_id=1, source_target_pairs={{0,1},{1,0},{2,3},{3,2},{4,5},{5,4},{6,7},{7,6},{8,9},{9,8},{10,11... | collective-permute-start | bytes 245768 | tf_op jit(solution)/shard_map/ppermute | solution.py:629
  26.1 5.0 %collective-permute-start.7 = (f32[184,128]{1,0:T(8,128)S(1)}, f32[184,128]{1,0:T(8,128)S(1)}, u32[]{:S(2)}, u32[]{:S(2)}) collective-permute-start(f32[184,128]{1,0:T(8,128)S(1)} %get-tuple-element.48.refs_0_), channel_id=1, source_target_pairs={{0,1},{1,0},{2,3},{3,2},{4,5},{5,4},{6,7},{7,6},{8,9},{9,8},{10,11... | collective-permute-start | bytes 282632 | tf_op jit(solution)/shard_map/ppermute | solution.py:629
  26.3 3.3 %collective-permute-start.9 = (f32[56,128]{1,0:T(8,128)S(1)}, f32[56,128]{1,0:T(8,128)S(1)}, u32[]{:S(2)}, u32[]{:S(2)}) collective-permute-start(f32[56,128]{1,0:T(8,128)S(1)} %get-tuple-element.49), channel_id=1, source_target_pairs={{0,3},{1,2},{2,1},{3,0},{4,7},{5,6},{6,5},{7,4},{8,11},{9,10},{10,... | collective-permute-start | bytes 86024 | tf_op jit(solution)/shard_map/ppermute | solution.py:629
  27.2 3.9 %collective-permute-start.8 = (f32[56,128]{1,0:T(8,128)S(1)}, f32[56,128]{1,0:T(8,128)S(1)}, u32[]{:S(2)}, u32[]{:S(2)}) collective-permute-start(f32[56,128]{1,0:T(8,128)S(1)} %get-tuple-element.49), channel_id=1, source_target_pairs={{0,2},{1,3},{2,0},{3,1},{4,6},{5,7},{6,4},{7,5},{8,10},{9,11},{10,... | collective-permute-start | bytes 86024 | tf_op jit(solution)/shard_map/ppermute | solution.py:629
  31.2 8.4 %collective-permute-start.12 = (f32[184,128]{1,0:T(8,128)S(1)}, f32[184,128]{1,0:T(8,128)S(1)}, u32[]{:S(2)}, u32[]{:S(2)}) collective-permute-start(f32[184,128]{1,0:T(8,128)S(1)} %get-tuple-element.50.own), channel_id=1, source_target_pairs={{0,12},{1,13},{2,14},{3,15},{4,8},{5,9},{6,10},{7,11},{8,4},{9,5},... | collective-permute-start | bytes 282632 | tf_op jit(solution)/shard_map/ppermute | solution.py:629
  33.3 6.7 %collective-permute-start.10 = (f32[184,128]{1,0:T(8,128)S(1)}, f32[184,128]{1,0:T(8,128)S(1)}, u32[]{:S(2)}, u32[]{:S(2)}) collective-permute-start(f32[184,128]{1,0:T(8,128)S(1)} %get-tuple-element.50.own), channel_id=1, source_target_pairs={{0,4},{1,5},{2,6},{3,7},{4,0},{5,1},{6,2},{7,3},{8,12},{9,13},{10,... | collective-permute-start | bytes 282632 | tf_op jit(solution)/shard_map/ppermute | solution.py:629
  33.9 5.7 %collective-permute-start.11 = (f32[104,128]{1,0:T(8,128)S(1)}, f32[104,128]{1,0:T(8,128)S(1)}, u32[]{:S(2)}, u32[]{:S(2)}) collective-permute-start(f32[104,128]{1,0:T(8,128)S(1)} %get-tuple-element.51), channel_id=1, source_target_pairs={{0,8},{1,9},{2,10},{3,11},{4,12},{5,13},{6,14},{7,15},{8,0},{9,1},... | collective-permute-start | bytes 159752 | tf_op jit(solution)/shard_map/ppermute | solution.py:629
  42.9 1.3 %collective-permute-start.13 = (f32[160,128]{1,0:T(8,128)S(1)}, f32[160,128]{1,0:T(8,128)S(1)}, u32[]{:S(2)}, u32[]{:S(2)}) collective-permute-start(f32[160,128]{1,0:T(8,128)S(1)} %get-tuple-element.55.refs_0_), channel_id=1, source_target_pairs={{0,1},{1,0},{2,3},{3,2},{4,5},{5,4},{6,7},{7,6},{8,9},{9,8},{10,11... | collective-permute-start | bytes 245768 | tf_op jit(solution)/shard_map/ppermute | solution.py:629
  44.6 4.9 %collective-permute-start.14 = (f32[168,128]{1,0:T(8,128)S(1)}, f32[168,128]{1,0:T(8,128)S(1)}, u32[]{:S(2)}, u32[]{:S(2)}) collective-permute-start(f32[168,128]{1,0:T(8,128)S(1)} %get-tuple-element.59.refs_0_), channel_id=1, source_target_pairs={{0,1},{1,0},{2,3},{3,2},{4,5},{5,4},{6,7},{7,6},{8,9},{9,8},{10,11... | collective-permute-start | bytes 258056 | tf_op jit(solution)/shard_map/ppermute | solution.py:629
  44.7 3.2 %collective-permute-start.16 = (f32[40,128]{1,0:T(8,128)S(1)}, f32[40,128]{1,0:T(8,128)S(1)}, u32[]{:S(2)}, u32[]{:S(2)}) collective-permute-start(f32[40,128]{1,0:T(8,128)S(1)} %get-tuple-element.60), channel_id=1, source_target_pairs={{0,3},{1,2},{2,1},{3,0},{4,7},{5,6},{6,5},{7,4},{8,11},{9,10},{10,... | collective-permute-start | bytes 61448 | tf_op jit(solution)/shard_map/ppermute | solution.py:629
  45.7 3.8 %collective-permute-start.15 = (f32[40,128]{1,0:T(8,128)S(1)}, f32[40,128]{1,0:T(8,128)S(1)}, u32[]{:S(2)}, u32[]{:S(2)}) collective-permute-start(f32[40,128]{1,0:T(8,128)S(1)} %get-tuple-element.60), channel_id=1, source_target_pairs={{0,2},{1,3},{2,0},{3,1},{4,6},{5,7},{6,4},{7,5},{8,10},{9,11},{10,... | collective-permute-start | bytes 61448 | tf_op jit(solution)/shard_map/ppermute | solution.py:629
  49.6 4.9 %collective-permute-start.17 = (f32[112,128]{1,0:T(8,128)S(1)}, f32[112,128]{1,0:T(8,128)S(1)}, u32[]{:S(2)}, u32[]{:S(2)}) collective-permute-start(f32[112,128]{1,0:T(8,128)S(1)} %get-tuple-element.62), channel_id=1, source_target_pairs={{0,4},{1,5},{2,6},{3,7},{4,0},{5,1},{6,2},{7,3},{8,12},{9,13},{10,... | collective-permute-start | bytes 172040 | tf_op jit(solution)/shard_map/ppermute | solution.py:629
  50.4 6.0 %collective-permute-start.18 = (f32[112,128]{1,0:T(8,128)S(1)}, f32[112,128]{1,0:T(8,128)S(1)}, u32[]{:S(2)}, u32[]{:S(2)}) collective-permute-start(f32[112,128]{1,0:T(8,128)S(1)} %get-tuple-element.63), channel_id=1, source_target_pairs={{0,12},{1,13},{2,14},{3,15},{4,8},{5,9},{6,10},{7,11},{8,4},{9,5},... | collective-permute-start | bytes 172040 | tf_op jit(solution)/shard_map/ppermute | solution.py:629
  52.6 4.9 %collective-permute-start.19 = (f32[8,128]{1,0:T(8,128)S(1)}, f32[8,128]{1,0:T(8,128)S(1)}, u32[]{:S(2)}, u32[]{:S(2)}) collective-permute-start(f32[8,128]{1,0:T(8,128)S(1)} %get-tuple-element.64.sums), channel_id=1, source_target_pairs={{0,8},{1,9},{2,10},{3,11},{4,12},{5,13},{6,14},{7,15},{8,0},{9,1},... | collective-permute-start | bytes 12296 | tf_op jit(solution)/shard_map/ppermute | solution.py:629

commit v7 on v6

--- a/solution.py
+++ b/solution.py
@@ -205,6 +205,21 @@
     return jnp.sum(over_rows(values), axis=1, keepdims=True)
 
 
+def on_diagonal(values):
+    rows = lax.broadcasted_iota(jnp.int32, values.shape, 0)
+    return over_rows(jnp.where(rows == lanes_of(values.shape), values, 0.0))
+
+
+def off_diagonal(row, count):
+    shape = (count, LANES)
+    rows = lax.broadcasted_iota(jnp.int32, shape, 0)
+    return spread(jnp.where(rows == lanes_of(shape), jnp.broadcast_to(row, shape), 0.0))
+
+
+def spread(values):
+    return jnp.broadcast_to(jnp.sum(values, axis=1, keepdims=True), values.shape)
+
+
 def coefficient_planes(coef, sources, levels, cols):
     coef[...] = jnp.zeros(coef.shape, jnp.float32)
     for level in range(levels):
@@ -213,9 +228,9 @@
             coef[at : at + ROWS, :cols] = source[level].astype(jnp.float32)
 
 
-def project(out_z, at, totals, scale):
+def project(stack, at, totals, scale):
     for m, total in enumerate(totals):
-        out_z[at + m : at + m + 1, : total.shape[1]] = scale * over_rows(total)
+        stack[at + m : at + m + 1, : total.shape[1]] = scale * over_rows(total)
 
 
 def start(planes, levels, cols, count):
@@ -224,7 +239,7 @@
     edge_rows = -(-(planes + 3 * levels) // GROUP) * ROWS
 
     def kernel(*refs):
-        sources, (out_z, out_e, coef), copies, weighted, sems = refs[:7], refs[7:10], refs[10:17], refs[17], refs[18]
+        sources, (out_z, out_e, coef), copies, (weighted, stack, sems) = refs[:7], refs[7:10], refs[10:17], refs[17:]
         pairs = list(zip(sources[:6], copies[:6], strict=True))
         for part in range(FETCHES):
             rows = pl.ds(part * (count // FETCHES), count // FETCHES)
@@ -234,6 +249,7 @@
             move.start()
         innov, prec, scale, mask, kx, ky, members = copies
         out_z[...] = jnp.zeros(out_z.shape, jnp.float32)
+        stack[...] = jnp.zeros(stack.shape, jnp.float32)
         for move in moves[:6]:
             move.wait()
         coefficient_planes(coef, (kx, ky, mask), levels, cols)
@@ -249,13 +265,15 @@
             for plane in range(planes):
                 for m in range(each):
                     totals[m] += members[part * each + m, plane] * weighted[plane]
-            project(out_z, base + part * each, totals, ens_scale)
+            project(stack, part * each, totals, ens_scale)
+        out_z[base : base + 1, :] = on_diagonal(spread(stack[...]))
         out_e[edge_rows:, :] = out_z[base:, :]
 
-    outs = [f32(base + ROWS, LANES), f32(edge_rows + ROWS, LANES), f32(3 * levels * ROWS, LANES)]
+    outs = [f32(base + SUMS, LANES), f32(edge_rows + SUMS, LANES), f32(3 * levels * ROWS, LANES)]
     field, flat = (planes, ROWS, cols), (levels, ROWS, cols)
     kept = [(field, jnp.float32)] * 3 + [(flat, jnp.int32)] + [(flat, jnp.float32)] * 2 + [((count,) + field, jnp.float32)]
-    scratch = [pltpu.VMEM(*one) for one in kept] + [pltpu.VMEM(field, jnp.float32), pltpu.SemaphoreType.DMA((6 + FETCHES,))]
+    scratch = [pltpu.VMEM(*one) for one in kept] + [pltpu.VMEM(field, jnp.float32), pltpu.VMEM((ROWS, LANES), jnp.float32)]
+    scratch.append(pltpu.SemaphoreType.DMA((6 + FETCHES,)))
     return kernel, outs, scratch
 
 
@@ -263,12 +281,11 @@
     ens_scale = math.sqrt(ensemble_share / (count - 1))
     base = planes * ROWS
     edge_rows = -(-planes // GROUP) * ROWS
-    sums_at = base + ROWS * with_weights
 
     def kernel(*refs):
         own, other, weights, sums, vert, prec, scale, mask, members = refs[:9]
         if with_weights:
-            out_z, out_e, seen = refs[9:]
+            out_z, out_e, seen, stack = refs[9:]
         else:
             seen, out_z, out_e, now = refs[9:]
         out_z[...] = jnp.zeros(out_z.shape, jnp.float32)
@@ -302,11 +319,13 @@
                 cross += before * weighted
             out_z[plane * ROWS : (plane + 1) * ROWS, :cols] = scale[plane] * weighted
         if with_weights:
-            project(out_z, base, totals, ens_scale)
-        out_z[sums_at : sums_at + SUMS, :] = sums[...]
-        if with_weights:
-            out_z[sums_at : sums_at + 1, :cols] = over_rows(energy)
+            stack[:ROWS, :] = jnp.zeros((ROWS, LANES), jnp.float32)
+            project(stack, 0, totals, ens_scale)
+            stack[ROWS:, :] = sums[...]
+            stack[ROWS : ROWS + 1, :cols] = over_rows(energy)
+            out_z[base : base + 1, :] = on_diagonal(spread(stack[...]))
         else:
+            out_z[base:, :] = sums[...]
             energy, cross = whole(energy), whole(cross)
             share = jnp.where(energy > 0.0, -cross / jnp.where(energy > 0.0, energy, 1.0), 0.0)
             rest = jnp.zeros((ROWS, cols), jnp.float32)
@@ -319,18 +338,17 @@
             place = (lax.axis_index("gx") * 2 + lax.axis_index("gy")) * 2 + lax.axis_index("gz")
             own_lane = lanes_of((1, LANES)) == place
             for index, value in enumerate((whole(rest), whole(left), share, energy)):
-                out_z[sums_at + index : sums_at + index + 1, :] = jnp.where(own_lane, value, 0.0)
+                out_z[base + index : base + index + 1, :] = jnp.where(own_lane, value, 0.0)
         pack_edges(out_e, [tile(out_z, plane) for plane in range(planes)], cols)
         out_e[edge_rows:, :] = out_z[base:, :]
 
-    tail = (ROWS * with_weights) + SUMS
-    outs = [f32(base + tail, LANES), f32(edge_rows + tail, LANES)]
+    outs = [f32(base + SUMS, LANES), f32(edge_rows + SUMS, LANES)]
     if with_weights:
-        return kernel, outs + [f32(planes, ROWS, cols)], ()
+        return kernel, outs + [f32(planes, ROWS, cols)], [pltpu.VMEM((ROWS + SUMS, LANES), jnp.float32)]
     return kernel, outs, [pltpu.VMEM((planes, ROWS, cols), jnp.float32)]
 
 
-def mix_back(first, far, planes, levels, cols, tail):
+def mix_back(first, far, planes, levels, cols):
     base = planes * ROWS
     coefs = 2 * levels if first else 0
     fields = planes // levels
@@ -379,33 +397,23 @@
             out_three[sent:, :] = total
             return
         at, near_at = count * ROWS, count * 8
-        out_all[at : at + tail, :] = total
-        out_near[near_at : near_at + tail, :] = total
         if first:
             last = jnp.where(lax.axis_index("gy") == 0, LANES - 1, cols - 1)
             lane = lanes_of((ROWS, LANES))
             bottom = lax.broadcasted_iota(jnp.int32, (ROWS, LANES), 0) == ROWS - 1
-            wets = jnp.zeros((8, LANES), jnp.float32)
             for level in range(levels):
                 kx, ky, wet = (
                     with_edge(tile(raw, kind * levels + level), edge, planes + kind * levels + level, cols) for kind in range(3)
                 )
                 put(planes + level, kx * wet * jnp.where(bottom, 1.0, pltpu.roll(wet, ROWS - 1, 0)))
                 put(planes + levels + level, jnp.where(lane == last, 0.0, ky * wet * pltpu.roll(wet, LANES - 1, 1)))
-                wets = jnp.where(lax.broadcasted_iota(jnp.int32, (8, LANES), 0) == level, wet[:1], wets)
-            out_all[at + tail :, :] = wets
-            out_near[near_at + tail :, :] = wets
+                total = jnp.where(lax.broadcasted_iota(jnp.int32, total.shape, 0) == 1 + level, wet[:1], total)
+        out_all[at:, :] = total
+        out_near[near_at:, :] = total
 
     if not far:
-        return kernel, [f32(base, LANES)] + [f32(sent + tail, LANES)] * 2 + [f32(tail, LANES)]
-    tail_all = tail + (8 if first else 0)
-    return kernel, [f32(count * ROWS + tail_all, LANES), f32(count * 8 + tail_all, LANES)]
-
-
-def pass_on(*refs):
-    half = len(refs) // 2
-    for source, target in zip(refs[:half], refs[half:], strict=True):
-        target[...] = source[...]
+        return kernel, [f32(base, LANES)] + [f32(sent + SUMS, LANES)] * 2 + [f32(SUMS, LANES)]
+    return kernel, [f32(count * ROWS + SUMS, LANES), f32(count * 8 + SUMS, LANES)]
 
 
 def is_even():
@@ -469,10 +477,6 @@
     return over_rows(jnp.where(lanes_of(values.shape) < cols, values, 0.0))
 
 
-def spread(values):
-    return jnp.broadcast_to(jnp.sum(values, axis=1, keepdims=True), values.shape)
-
-
 def window_scratch(planes):
     return [pltpu.VMEM((planes, WIN, LANES), jnp.float32)] * 2
 
@@ -496,7 +500,7 @@
         for index in range(coefs):
             far_window(nat, index, own, first, near, third, planes + index)
             if index < levels:
-                row, near_row = at + ROWS + index, near_at + ROWS + index
+                row, near_row = at + 1 + index, near_at + 1 + index
                 one, three = first[row : row + 1, :], third[row : row + 1, :]
                 nat[index, 15:16, :] = nat[index, 15:16, :] * jnp.where(even, one, three)
                 nat[index, 31:32, :] = nat[index, 31:32, :] * near[near_row : near_row + 1, :]
@@ -512,8 +516,9 @@
         for plane in range(planes):
             far_window(nat, plane, own, first, near, third, plane)
             deal(buf, nat, plane, TILES)
-        sent = slice(at, at + ROWS)
-        weights[...] = spread((own[sent, :] + first[sent, :]) + (near[near_at : near_at + ROWS, :] + third[sent, :]))
+        sent = slice(at, at + 1)
+        total = (own[sent, :] + first[sent, :]) + (near[near_at : near_at + 1, :] + third[sent, :])
+        weights[...] = off_diagonal(total, ROWS)
         run_steps(buf, nat, coef, steps, planes, levels, TILES)
         squares = jnp.zeros((ROWS, LANES), jnp.float32)
         for plane in range(planes):
@@ -544,7 +549,9 @@
             far_window(nat, plane, own, first, near, third, plane)
             deal(buf, nat, plane, TILES)
         at, near_at = planes * ROWS, planes * 8
-        total = spread((own[at:, :] + first[at:, :]) + (near[near_at:, :] + third[at:, :]))
+        sent = slice(at, at + 1)
+        total = (own[sent, :] + first[sent, :]) + (near[near_at : near_at + 1, :] + third[sent, :])
+        total = off_diagonal(total, ROWS + SUMS)
         energy = total[ROWS : ROWS + 1]
         rr = total[ROWS + 4 : ROWS + 5] + over_rows(weights[...] * weights[...])
         step = rr / (rr + energy)
@@ -636,8 +643,7 @@
     kernel, outs = kernel_of
     args = (out_z, other, edge, edge_other, vert)
     if raw is not None:
-        own, raw = call(pass_on, [f32(*out_z.shape), f32(*raw.shape)], [VMEM] * 2, (out_z, raw))
-        args = (own, *args[1:], raw)
+        args += (raw,)
     return call(kernel, outs, [VMEM] * len(args), args)
 
 
@@ -659,15 +665,16 @@
 
     kernel, outs, scratch = start(planes, levels, cols, count)
     args = (innov, prec, scale, sea_mask, kappa_x, kappa_y, ens)
-    out_z, out_e, raw = call(kernel, outs, [HBM] * 7, args, scratch, 56)
-    parts = far_round(*mix_round(mix_back(True, True, planes, levels, cols, ROWS), out_z, out_e, vert, raw))
+    args = [pltpu.with_memory_space_constraint(a, pltpu.HBM) for a in args]
+    out_z, out_e, raw = call(kernel, outs, [HBM] * 7, args, scratch)
+    parts = far_round(*mix_round(mix_back(True, True, planes, levels, cols), out_z, out_e, vert, raw))
     kernel, outs, scratch = first_diffuse(planes, levels, cols)
     coef, coef_near, resid, weights, sums, out_g = call(kernel, outs, [VMEM] * 5, (*parts, steps), scratch)
 
     kernel, outs, scratch = observe(planes, levels, cols, count, True)
     args = (out_g, moved_to(out_g, 0, 0, 1), weights, sums, vert, prec, scale, sea_mask, ens)
     out_z, out_e, seen = call(kernel, outs, [VMEM] * 9, args, scratch)
-    parts = far_round(*mix_round(mix_back(False, True, planes, levels, cols, ROWS + SUMS), out_z, out_e, vert))
+    parts = far_round(*mix_round(mix_back(False, True, planes, levels, cols), out_z, out_e, vert))
     kernel, outs, scratch = second_diffuse(planes, levels, cols)
     args = (*parts, steps, coef, coef_near, resid, weights)
     image, new, new_w, sums, facts, out_g = call(kernel, outs, [VMEM] * 9, args, scratch)
@@ -675,7 +682,7 @@
     kernel, outs, scratch = observe(planes, levels, cols, count, False)
     args = (out_g, moved_to(out_g, 0, 0, 1), new_w, sums, vert, prec, scale, sea_mask, ens, seen)
     out_z, out_e = call(kernel, outs, [VMEM] * 10, args, scratch)
-    own, one, three, sums = mix_round(mix_back(False, False, planes, levels, cols, SUMS), out_z, out_e, vert)
+    own, one, three, sums = mix_round(mix_back(False, False, planes, levels, cols), out_z, out_e, vert)
     sums_two = moved_to(sums, 2, 0, 0)
     kernel, outs, scratch = last_diffuse(planes, levels, cols)
     args = (own, moved_to(one, 1, 0, 0), moved_to(three, 3, 0, 0), sums, steps, coef_near)

time: 58.7 us -> 57.1 us (0.973)
  local copies, waits for them, and re-layouts: 2.06 us -> 0.37 us
  waiting for transfers between devices: 24.3 us -> 25.1 us
    unnamed x17 -> x13, local copies, waits for them, and re-layouts: 1.82 us -> 0.14 us
    ppermute x20, waiting for transfers between devices: 24.3 us -> 25.1 us  [moved_to(): lax.ppermute(values, AXES, [(number[a, b, c], number[a ^ x, b ^ y, c ^ z]...]
    pallas_call x11 -> x10, Pallas kernels: 11.1 us -> 10.6 us  [call(): pl.pallas_call(kernel, out_shape=outs, in_specs=specs, out_specs=[VMEM] *...]
  transfers between devices with their start and end apart: 20 -> 20, of which waited for: 12 -> 14; matrix products, arithmetic and copies ran while one was open for 0% -> 0% of each run, Pallas kernels for 2% -> 2%
where the time goes in v7:
time: 57.1 us; the launch traced here: 56.9 us
  waiting for transfers between devices  25.1 us (44%)
  starting transfers between devices  20.1 us (35%)
  Pallas kernels  10.6 us (19%)
  between operations  0.77 us (1%)
    ppermute x20, waiting for transfers between devices, moved_to(): lax.ppermute(values, AXES, [(number[a, b, c], number[a ^ x, b ^ y, c ^ z]...  25.1 us
    ppermute x20, starting transfers between devices, moved_to(): lax.ppermute(values, AXES, [(number[a, b, c], number[a ^ x, b ^ y, c ^ z]...  20.1 us
    pallas_call x10, Pallas kernels, call(): pl.pallas_call(kernel, out_shape=outs, in_specs=specs, out_specs=[VMEM] *...  10.6 us
  transfers between devices with their start and end apart: 20, of which 14 were waited for; matrix products, arithmetic and copies ran while one was open for 0% of the time, Pallas kernels for 2%

profile of v7, /device:TPU:0, one launch (start us, length us, event | category | flops | bytes accessed | tf_op | source)
XLA Modules:
  0.0 56.9 jit_solution(10705807987704907344)
XLA Ops:
  0.6 0.0 copy-start.3
  0.6 0.0 copy-start
  0.7 0.0 copy-start.2
  0.7 0.0 copy-start.1
  0.7 0.0 copy-start.4
  0.7 0.0 copy-start.5
  0.7 1.7 %shard_map.112 = (f32[168,128]{1,0:T(8,128)S(1)}, f32[56,128]{1,0:T(8,128)S(1)}, f32[96,128]{1,0:T(8,128)S(1)}) custom-call(f32[10,16,108]{2,1,0:T(8,128)} %bitcast.16, f32[10,16,108]{2,1,0:T(8,128)} %bitcast.10, f32[10,16,108]{2,1,0:T(8,128)} %bitcast.13, s32[2,16,108]{2,1,0:T(8,128)} %refs_7_.3, f32[2,16,108]{2,1,0:T(8,128)} %refs_4_.1, ...), custom_call_target="tpu_custom_call" | custom-call | tf_op jit(solution)/shard_map/pallas_call | solution.py:165
  2.4 0.5 collective-permute-start
  2.9 2.6 %collective-permute-start.2 = (f32[56,128]{1,0:T(8,128)S(1)}, f32[56,128]{1,0:T(8,128)S(1)}, u32[]{:S(2)}, u32[]{:S(2)}) collective-permute-start(f32[56,128]{1,0:T(8,128)S(1)} %get-tuple-element.37), channel_id=1, source_target_pairs={{0,3},{1,2},{2,1},{3,0},{4,7},{5,6},{6,5},{7,4},{8,11},{9,10},{10,... | collective-permute-start | bytes 86024 | tf_op jit(solution)/shard_map/ppermute | solution.py:636
  5.6 0.0 collective-permute-start.1
  5.6 0.0 copy-done.4
  5.6 0.1 copy.13
  5.7 0.1 broadcast_in_dim.6
  5.8 1.3 %collective-permute-done.2.refs_3_ = f32[56,128]{1,0:T(8,128)S(1)} collective-permute-done((f32[56,128]{1,0:T(8,128)S(1)}, f32[56,128]{1,0:T(8,128)S(1)}, u32[]{:S(2)}, u32[]{:S(2)}) %collective-permute-start.2) | collective-permute-done | bytes 28704 | tf_op jit(solution)/shard_map/ppermute | solution.py:636
  7.1 2.3 %collective-permute-done.1.refs_2_ = f32[56,128]{1,0:T(8,128)S(1)} collective-permute-done((f32[56,128]{1,0:T(8,128)S(1)}, f32[56,128]{1,0:T(8,128)S(1)}, u32[]{:S(2)}, u32[]{:S(2)}) %collective-permute-start.1) | collective-permute-done | bytes 28704 | tf_op jit(solution)/shard_map/ppermute | solution.py:636
  9.4 0.0 collective-permute-done.refs_1_
  9.4 0.1 broadcast_in_dim.14.refs_4_
  9.5 0.1 shard_map.113
  9.7 3.7 %collective-permute-start.5 = (f32[232,128]{1,0:T(8,128)S(1)}, f32[232,128]{1,0:T(8,128)S(1)}, u32[]{:S(2)}, u32[]{:S(2)}) collective-permute-start(f32[232,128]{1,0:T(8,128)S(1)} %get-tuple-element.39.own), channel_id=1, source_target_pairs={{0,12},{1,13},{2,14},{3,15},{4,8},{5,9},{6,10},{7,11},{8,4},{9,5},... | collective-permute-start | bytes 356360 | tf_op jit(solution)/shard_map/ppermute | solution.py:636
  13.3 0.0 collective-permute-start.3
  13.3 0.8 %collective-permute-start.4 = (f32[120,128]{1,0:T(8,128)S(1)}, f32[120,128]{1,0:T(8,128)S(1)}, u32[]{:S(2)}, u32[]{:S(2)}) collective-permute-start(f32[120,128]{1,0:T(8,128)S(1)} %get-tuple-element.40), channel_id=1, source_target_pairs={{0,8},{1,9},{2,10},{3,11},{4,12},{5,13},{6,14},{7,15},{8,0},{9,1},... | collective-permute-start | bytes 184328 | tf_op jit(solution)/shard_map/ppermute | solution.py:636
  14.1 0.0 copy-done.5
  14.1 5.3 %collective-permute-done.4.near = f32[120,128]{1,0:T(8,128)S(1)} collective-permute-done((f32[120,128]{1,0:T(8,128)S(1)}, f32[120,128]{1,0:T(8,128)S(1)}, u32[]{:S(2)}, u32[]{:S(2)}) %collective-permute-start.4) | collective-permute-done | bytes 61472 | tf_op jit(solution)/shard_map/ppermute | solution.py:636
  19.4 0.0 collective-permute-done.5.third
  19.4 0.3 collective-permute-done.3.first
  19.7 0.1 broadcast_in_dim.15.steps
  19.7 2.8 %shard_map.114 = (f32[3,2,56,128]{3,2,1,0:T(8,128)S(1)}, f32[3,2,40,128]{3,2,1,0:T(8,128)S(1)}, f32[10,40,128]{2,1,0:T(8,128)S(1)}, f32[16,128]{1,0:T(8,128)S(1)...) custom-call(f32[232,128]{1,0:T(8,128)S(1)} %get-tuple-element.39.own, f32[232,128]{1,0:T(8,128)S(1)} %collective-permute-done.3.first, ...), custom_call_target="tpu_custom_call" | custom-call | tf_op jit(solution)/shard_map/pallas_call | solution.py:165
  22.6 0.1 collective-permute-start.6
  22.6 1.3 %collective-permute-done.6.refs_1_ = f32[160,128]{1,0:T(8,128)S(1)} collective-permute-done((f32[160,128]{1,0:T(8,128)S(1)}, f32[160,128]{1,0:T(8,128)S(1)}, u32[]{:S(2)}, u32[]{:S(2)}) %collective-permute-start.6) | collective-permute-done | bytes 81952 | tf_op jit(solution)/shard_map/ppermute | solution.py:636
  23.9 0.0 copy-done.3
  23.9 0.0 copy-done
  23.9 0.4 shard_map.115
  24.3 0.2 collective-permute-start.7
  24.5 1.2 %collective-permute-start.9 = (f32[40,128]{1,0:T(8,128)S(1)}, f32[40,128]{1,0:T(8,128)S(1)}, u32[]{:S(2)}, u32[]{:S(2)}) collective-permute-start(f32[40,128]{1,0:T(8,128)S(1)} %get-tuple-element.45), channel_id=1, source_target_pairs={{0,3},{1,2},{2,1},{3,0},{4,7},{5,6},{6,5},{7,4},{8,11},{9,10},{10,... | collective-permute-start | bytes 61448 | tf_op jit(solution)/shard_map/ppermute | solution.py:636
  25.7 0.8 %collective-permute-start.8 = (f32[40,128]{1,0:T(8,128)S(1)}, f32[40,128]{1,0:T(8,128)S(1)}, u32[]{:S(2)}, u32[]{:S(2)}) collective-permute-start(f32[40,128]{1,0:T(8,128)S(1)} %get-tuple-element.45), channel_id=1, source_target_pairs={{0,2},{1,3},{2,0},{3,1},{4,6},{5,7},{6,4},{7,5},{8,10},{9,11},{10,... | collective-permute-start | bytes 61448 | tf_op jit(solution)/shard_map/ppermute | solution.py:636
  26.5 1.2 %collective-permute-done.9.refs_3_ = f32[40,128]{1,0:T(8,128)S(1)} collective-permute-done((f32[40,128]{1,0:T(8,128)S(1)}, f32[40,128]{1,0:T(8,128)S(1)}, u32[]{:S(2)}, u32[]{:S(2)}) %collective-permute-start.9) | collective-permute-done | bytes 20512 | tf_op jit(solution)/shard_map/ppermute | solution.py:636
  27.8 1.7 %collective-permute-done.8.refs_2_ = f32[40,128]{1,0:T(8,128)S(1)} collective-permute-done((f32[40,128]{1,0:T(8,128)S(1)}, f32[40,128]{1,0:T(8,128)S(1)}, u32[]{:S(2)}, u32[]{:S(2)}) %collective-permute-start.8) | collective-permute-done | bytes 20512 | tf_op jit(solution)/shard_map/ppermute | solution.py:636
  29.5 0.0 collective-permute-done.7.refs_1_
  29.5 0.1 shard_map.116
  29.6 2.3 %collective-permute-start.12 = (f32[168,128]{1,0:T(8,128)S(1)}, f32[168,128]{1,0:T(8,128)S(1)}, u32[]{:S(2)}, u32[]{:S(2)}) collective-permute-start(f32[168,128]{1,0:T(8,128)S(1)} %get-tuple-element.46.own), channel_id=1, source_target_pairs={{0,12},{1,13},{2,14},{3,15},{4,8},{5,9},{6,10},{7,11},{8,4},{9,5},... | collective-permute-start | bytes 258056 | tf_op jit(solution)/shard_map/ppermute | solution.py:636
  31.9 0.6 collective-permute-start.10
  32.5 1.6 %collective-permute-start.11 = (f32[88,128]{1,0:T(8,128)S(1)}, f32[88,128]{1,0:T(8,128)S(1)}, u32[]{:S(2)}, u32[]{:S(2)}) collective-permute-start(f32[88,128]{1,0:T(8,128)S(1)} %get-tuple-element.47), channel_id=1, source_target_pairs={{0,8},{1,9},{2,10},{3,11},{4,12},{5,13},{6,14},{7,15},{8,0},{9,1},... | collective-permute-start | bytes 135176 | tf_op jit(solution)/shard_map/ppermute | solution.py:636
  34.1 3.4 %collective-permute-done.11.near = f32[88,128]{1,0:T(8,128)S(1)} collective-permute-done((f32[88,128]{1,0:T(8,128)S(1)}, f32[88,128]{1,0:T(8,128)S(1)}, u32[]{:S(2)}, u32[]{:S(2)}) %collective-permute-start.11) | collective-permute-done | bytes 45088 | tf_op jit(solution)/shard_map/ppermute | solution.py:636
  37.5 0.0 collective-permute-done.12.third
  37.5 0.3 collective-permute-done.10.first
  37.7 2.8 %shard_map.117 = (f32[10,16,128]{2,1,0:T(8,128)S(1)}, f32[10,16,128]{2,1,0:T(8,128)S(1)}, f32[16,128]{1,0:T(8,128)S(1)}, f32[8,128]{1,0:T(8,128)S(1)}, f32[8,128]{1,0:T(8,128)S(1)}, /*index=5*/f32[160,128]{1,0:T(8,128)S(1)}) custom-call(f32[168,128]{1,0:T(8,128)S(1)} %get-tuple-element.46.own, f32[168,128]{1,0:T(8,128)S(1)} %collective-permute-done.10.first, ...), custom_call_target="tpu_custom_call" | custom-call | tf_op jit(solution)/shard_map/pallas_call | solution.py:165
  40.6 0.1 collective-permute-start.13
  40.7 1.3 %collective-permute-done.13.refs_1_ = f32[160,128]{1,0:T(8,128)S(1)} collective-permute-done((f32[160,128]{1,0:T(8,128)S(1)}, f32[160,128]{1,0:T(8,128)S(1)}, u32[]{:S(2)}, u32[]{:S(2)}) %collective-permute-start.13) | collective-permute-done | bytes 81952 | tf_op jit(solution)/shard_map/ppermute | solution.py:636
  41.9 0.4 shard_map.118
  42.3 0.2 collective-permute-start.14
  42.5 1.0 %collective-permute-start.16 = (f32[40,128]{1,0:T(8,128)S(1)}, f32[40,128]{1,0:T(8,128)S(1)}, u32[]{:S(2)}, u32[]{:S(2)}) collective-permute-start(f32[40,128]{1,0:T(8,128)S(1)} %get-tuple-element.56), channel_id=1, source_target_pairs={{0,3},{1,2},{2,1},{3,0},{4,7},{5,6},{6,5},{7,4},{8,11},{9,10},{10,... | collective-permute-start | bytes 61448 | tf_op jit(solution)/shard_map/ppermute | solution.py:636
  43.5 1.0 %collective-permute-start.15 = (f32[40,128]{1,0:T(8,128)S(1)}, f32[40,128]{1,0:T(8,128)S(1)}, u32[]{:S(2)}, u32[]{:S(2)}) collective-permute-start(f32[40,128]{1,0:T(8,128)S(1)} %get-tuple-element.56), channel_id=1, source_target_pairs={{0,2},{1,3},{2,0},{3,1},{4,6},{5,7},{6,4},{7,5},{8,10},{9,11},{10,... | collective-permute-start | bytes 61448 | tf_op jit(solution)/shard_map/ppermute | solution.py:636
  44.5 1.2 %collective-permute-done.16.refs_3_ = f32[40,128]{1,0:T(8,128)S(1)} collective-permute-done((f32[40,128]{1,0:T(8,128)S(1)}, f32[40,128]{1,0:T(8,128)S(1)}, u32[]{:S(2)}, u32[]{:S(2)}) %collective-permute-start.16) | collective-permute-done | bytes 20512 | tf_op jit(solution)/shard_map/ppermute | solution.py:636
  45.7 1.6 %collective-permute-done.15.refs_2_ = f32[40,128]{1,0:T(8,128)S(1)} collective-permute-done((f32[40,128]{1,0:T(8,128)S(1)}, f32[40,128]{1,0:T(8,128)S(1)}, u32[]{:S(2)}, u32[]{:S(2)}) %collective-permute-start.15) | collective-permute-done | bytes 20512 | tf_op jit(solution)/shard_map/ppermute | solution.py:636
  47.2 0.0 collective-permute-done.14.refs_1_
  47.2 0.1 shard_map.119
  47.4 1.5 %collective-permute-start.17 = (f32[112,128]{1,0:T(8,128)S(1)}, f32[112,128]{1,0:T(8,128)S(1)}, u32[]{:S(2)}, u32[]{:S(2)}) collective-permute-start(f32[112,128]{1,0:T(8,128)S(1)} %get-tuple-element.58), channel_id=1, source_target_pairs={{0,4},{1,5},{2,6},{3,7},{4,0},{5,1},{6,2},{7,3},{8,12},{9,13},{10,... | collective-permute-start | bytes 172040 | tf_op jit(solution)/shard_map/ppermute | solution.py:636
  48.9 1.7 %collective-permute-start.18 = (f32[112,128]{1,0:T(8,128)S(1)}, f32[112,128]{1,0:T(8,128)S(1)}, u32[]{:S(2)}, u32[]{:S(2)}) collective-permute-start(f32[112,128]{1,0:T(8,128)S(1)} %get-tuple-element.59), channel_id=1, source_target_pairs={{0,12},{1,13},{2,14},{3,15},{4,8},{5,9},{6,10},{7,11},{8,4},{9,5},... | collective-permute-start | bytes 172040 | tf_op jit(solution)/shard_map/ppermute | solution.py:636
  50.6 0.3 collective-permute-start.19
  50.9 0.7 %collective-permute-done.17.one = f32[112,128]{1,0:T(8,128)S(1)} collective-permute-done((f32[112,128]{1,0:T(8,128)S(1)}, f32[112,128]{1,0:T(8,128)S(1)}, u32[]{:S(2)}, u32[]{:S(2)}) %collective-permute-start.17) | collective-permute-done | bytes 57376 | tf_op jit(solution)/shard_map/ppermute | solution.py:636
  51.6 3.3 %collective-permute-done.18.three = f32[112,128]{1,0:T(8,128)S(1)} collective-permute-done((f32[112,128]{1,0:T(8,128)S(1)}, f32[112,128]{1,0:T(8,128)S(1)}, u32[]{:S(2)}, u32[]{:S(2)}) %collective-permute-start.18) | collective-permute-done | bytes 57376 | tf_op jit(solution)/shard_map/ppermute | solution.py:636
  54.9 1.2 %shard_map.120 = (f32[10,16,128]{2,1,0:T(8,128)S(1)}, f32[2,8,128]{2,1,0:T(8,128)S(1)}) custom-call(f32[160,128]{1,0:T(8,128)S(1)} %get-tuple-element.57.own, f32[112,128]{1,0:T(8,128)S(1)} %collective-permute-done.17.one, f32[112,128]{1,0:T(8,128)S(1)} %collective-permute-done.18.three, f32[8,128]{1,0:T(8,128)S(1)} %get-tuple-element.60.sums, ...), custom_call_target="tpu_custom_call" | custom-call | tf_op jit(solution)/shard_map/pallas_call | solution.py:165
  56.1 0.0 collective-permute-done.19.sums_two
  56.1 0.9 %shard_map.121 = (f32[10,16,108]{2,1,0:T(8,128)}, f32[1,16]{1,0:T(1,128)}, f32[10,16,108]{2,1,0:T(8,128)}) custom-call(f32[10,16,128]{2,1,0:T(8,128)S(1)} %get-tuple-element.61.diffused, f32[2,8,128]{2,1,0:T(8,128)S(1)} %get-tuple-element.62.sums, f32[8,128]{1,0:T(8,128)S(1)} %collective-permute-done.19.sums_two, ...), custom_call_target="tpu_custom_call" | custom-call | tf_op jit(solution)/shard_map/pallas_call | solution.py:165
  (3 shorter events, 0.0 us)
Async XLA Ops:
  0.6 23.3 %copy-start.3 = (s32[2,16,108]{2,1,0:T(8,128)S(1)}, s32[2,16,108]{2,1,0:T(8,128)}, u32[]{:S(2)}) copy-start(s32[2,16,108]{2,1,0:T(8,128)} %refs_7_.3) | copy-start | bytes 41476
  0.6 23.3 %copy-start = (f32[16,5,2,16,108]{4,3,2,1,0:T(8,128)S(1)}, f32[16,5,2,16,108]{4,3,2,1,0:T(8,128)}, u32[]{:S(2)}) copy-start(f32[16,5,2,16,108]{4,3,2,1,0:T(8,128)} %param.15) | copy-start | bytes 3317764
  0.7 23.3 %copy-start.2 = (f32[5,2,16,108]{3,2,1,0:T(8,128)S(1)}, f32[5,2,16,108]{3,2,1,0:T(8,128)}, u32[]{:S(2)}) copy-start(f32[5,2,16,108]{3,2,1,0:T(8,128)} %param.11) | copy-start | bytes 207364
  0.7 23.3 %copy-start.1 = (f32[5,2,16,108]{3,2,1,0:T(8,128)S(1)}, f32[5,2,16,108]{3,2,1,0:T(8,128)}, u32[]{:S(2)}) copy-start(f32[5,2,16,108]{3,2,1,0:T(8,128)} %param.10) | copy-start | bytes 207364
  0.7 4.9 %copy-start.4 = (f32[5,4,4]{0,2,1:T(4,128)S(1)}, f32[5,4,4]{0,2,1:T(4,128)}, u32[]{:S(2)}) copy-start(f32[5,4,4]{0,2,1:T(4,128)} %param.16) | copy-start | bytes 964
  0.7 13.4 %copy-start.5 = (s32[5]{0:T(128)S(1)}, s32[5]{0:T(128)}, u32[]{:S(2)}) copy-start(s32[5]{0:T(128)} %param.17) | copy-start | bytes 64
  2.4 7.0 %collective-permute-start = (f32[168,128]{1,0:T(8,128)S(1)}, f32[168,128]{1,0:T(8,128)S(1)}, u32[]{:S(2)}, u32[]{:S(2)}) collective-permute-start(f32[168,128]{1,0:T(8,128)S(1)} %get-tuple-element.36.refs_0_), channel_id=1, source_target_pairs={{0,1},{1,0},{2,3},{3,2},{4,5},{5,4},{6,7},{7,6},{8,9},{9,8},{10,11... | collective-permute-start | bytes 258056 | tf_op jit(solution)/shard_map/ppermute | solution.py:636
  2.9 4.2 %collective-permute-start.2 = (f32[56,128]{1,0:T(8,128)S(1)}, f32[56,128]{1,0:T(8,128)S(1)}, u32[]{:S(2)}, u32[]{:S(2)}) collective-permute-start(f32[56,128]{1,0:T(8,128)S(1)} %get-tuple-element.37), channel_id=1, source_target_pairs={{0,3},{1,2},{2,1},{3,0},{4,7},{5,6},{6,5},{7,4},{8,11},{9,10},{10,... | collective-permute-start | bytes 86024 | tf_op jit(solution)/shard_map/ppermute | solution.py:636
  5.6 3.9 %collective-permute-start.1 = (f32[56,128]{1,0:T(8,128)S(1)}, f32[56,128]{1,0:T(8,128)S(1)}, u32[]{:S(2)}, u32[]{:S(2)}) collective-permute-start(f32[56,128]{1,0:T(8,128)S(1)} %get-tuple-element.37), channel_id=1, source_target_pairs={{0,2},{1,3},{2,0},{3,1},{4,6},{5,7},{6,4},{7,5},{8,10},{9,11},{10,... | collective-permute-start | bytes 86024 | tf_op jit(solution)/shard_map/ppermute | solution.py:636
  9.7 9.7 %collective-permute-start.5 = (f32[232,128]{1,0:T(8,128)S(1)}, f32[232,128]{1,0:T(8,128)S(1)}, u32[]{:S(2)}, u32[]{:S(2)}) collective-permute-start(f32[232,128]{1,0:T(8,128)S(1)} %get-tuple-element.39.own), channel_id=1, source_target_pairs={{0,12},{1,13},{2,14},{3,15},{4,8},{5,9},{6,10},{7,11},{8,4},{9,5},... | collective-permute-start | bytes 356360 | tf_op jit(solution)/shard_map/ppermute | solution.py:636
  13.3 6.4 %collective-permute-start.3 = (f32[232,128]{1,0:T(8,128)S(1)}, f32[232,128]{1,0:T(8,128)S(1)}, u32[]{:S(2)}, u32[]{:S(2)}) collective-permute-start(f32[232,128]{1,0:T(8,128)S(1)} %get-tuple-element.39.own), channel_id=1, source_target_pairs={{0,4},{1,5},{2,6},{3,7},{4,0},{5,1},{6,2},{7,3},{8,12},{9,13},{10,... | collective-permute-start | bytes 356360 | tf_op jit(solution)/shard_map/ppermute | solution.py:636
  13.3 6.0 %collective-permute-start.4 = (f32[120,128]{1,0:T(8,128)S(1)}, f32[120,128]{1,0:T(8,128)S(1)}, u32[]{:S(2)}, u32[]{:S(2)}) collective-permute-start(f32[120,128]{1,0:T(8,128)S(1)} %get-tuple-element.40), channel_id=1, source_target_pairs={{0,8},{1,9},{2,10},{3,11},{4,12},{5,13},{6,14},{7,15},{8,0},{9,1},... | collective-permute-start | bytes 184328 | tf_op jit(solution)/shard_map/ppermute | solution.py:636
  22.6 1.3 %collective-permute-start.6 = (f32[160,128]{1,0:T(8,128)S(1)}, f32[160,128]{1,0:T(8,128)S(1)}, u32[]{:S(2)}, u32[]{:S(2)}) collective-permute-start(f32[160,128]{1,0:T(8,128)S(1)} %get-tuple-element.41.refs_0_), channel_id=1, source_target_pairs={{0,1},{1,0},{2,3},{3,2},{4,5},{5,4},{6,7},{7,6},{8,9},{9,8},{10,11... | collective-permute-start | bytes 245768 | tf_op jit(solution)/shard_map/ppermute | solution.py:636
  24.3 5.2 %collective-permute-start.7 = (f32[168,128]{1,0:T(8,128)S(1)}, f32[168,128]{1,0:T(8,128)S(1)}, u32[]{:S(2)}, u32[]{:S(2)}) collective-permute-start(f32[168,128]{1,0:T(8,128)S(1)} %get-tuple-element.44.refs_0_), channel_id=1, source_target_pairs={{0,1},{1,0},{2,3},{3,2},{4,5},{5,4},{6,7},{7,6},{8,9},{9,8},{10,11... | collective-permute-start | bytes 258056 | tf_op jit(solution)/shard_map/ppermute | solution.py:636
  24.5 3.2 %collective-permute-start.9 = (f32[40,128]{1,0:T(8,128)S(1)}, f32[40,128]{1,0:T(8,128)S(1)}, u32[]{:S(2)}, u32[]{:S(2)}) collective-permute-start(f32[40,128]{1,0:T(8,128)S(1)} %get-tuple-element.45), channel_id=1, source_target_pairs={{0,3},{1,2},{2,1},{3,0},{4,7},{5,6},{6,5},{7,4},{8,11},{9,10},{10,... | collective-permute-start | bytes 61448 | tf_op jit(solution)/shard_map/ppermute | solution.py:636
  25.7 3.8 %collective-permute-start.8 = (f32[40,128]{1,0:T(8,128)S(1)}, f32[40,128]{1,0:T(8,128)S(1)}, u32[]{:S(2)}, u32[]{:S(2)}) collective-permute-start(f32[40,128]{1,0:T(8,128)S(1)} %get-tuple-element.45), channel_id=1, source_target_pairs={{0,2},{1,3},{2,0},{3,1},{4,6},{5,7},{6,4},{7,5},{8,10},{9,11},{10,... | collective-permute-start | bytes 61448 | tf_op jit(solution)/shard_map/ppermute | solution.py:636
  29.6 7.9 %collective-permute-start.12 = (f32[168,128]{1,0:T(8,128)S(1)}, f32[168,128]{1,0:T(8,128)S(1)}, u32[]{:S(2)}, u32[]{:S(2)}) collective-permute-start(f32[168,128]{1,0:T(8,128)S(1)} %get-tuple-element.46.own), channel_id=1, source_target_pairs={{0,12},{1,13},{2,14},{3,15},{4,8},{5,9},{6,10},{7,11},{8,4},{9,5},... | collective-permute-start | bytes 258056 | tf_op jit(solution)/shard_map/ppermute | solution.py:636
  31.9 5.8 %collective-permute-start.10 = (f32[168,128]{1,0:T(8,128)S(1)}, f32[168,128]{1,0:T(8,128)S(1)}, u32[]{:S(2)}, u32[]{:S(2)}) collective-permute-start(f32[168,128]{1,0:T(8,128)S(1)} %get-tuple-element.46.own), channel_id=1, source_target_pairs={{0,4},{1,5},{2,6},{3,7},{4,0},{5,1},{6,2},{7,3},{8,12},{9,13},{10,... | collective-permute-start | bytes 258056 | tf_op jit(solution)/shard_map/ppermute | solution.py:636
  32.5 5.0 %collective-permute-start.11 = (f32[88,128]{1,0:T(8,128)S(1)}, f32[88,128]{1,0:T(8,128)S(1)}, u32[]{:S(2)}, u32[]{:S(2)}) collective-permute-start(f32[88,128]{1,0:T(8,128)S(1)} %get-tuple-element.47), channel_id=1, source_target_pairs={{0,8},{1,9},{2,10},{3,11},{4,12},{5,13},{6,14},{7,15},{8,0},{9,1},... | collective-permute-start | bytes 135176 | tf_op jit(solution)/shard_map/ppermute | solution.py:636
  40.6 1.3 %collective-permute-start.13 = (f32[160,128]{1,0:T(8,128)S(1)}, f32[160,128]{1,0:T(8,128)S(1)}, u32[]{:S(2)}, u32[]{:S(2)}) collective-permute-start(f32[160,128]{1,0:T(8,128)S(1)} %get-tuple-element.51.refs_0_), channel_id=1, source_target_pairs={{0,1},{1,0},{2,3},{3,2},{4,5},{5,4},{6,7},{7,6},{8,9},{9,8},{10,11... | collective-permute-start | bytes 245768 | tf_op jit(solution)/shard_map/ppermute | solution.py:636
  42.3 4.9 %collective-permute-start.14 = (f32[168,128]{1,0:T(8,128)S(1)}, f32[168,128]{1,0:T(8,128)S(1)}, u32[]{:S(2)}, u32[]{:S(2)}) collective-permute-start(f32[168,128]{1,0:T(8,128)S(1)} %get-tuple-element.55.refs_0_), channel_id=1, source_target_pairs={{0,1},{1,0},{2,3},{3,2},{4,5},{5,4},{6,7},{7,6},{8,9},{9,8},{10,11... | collective-permute-start | bytes 258056 | tf_op jit(solution)/shard_map/ppermute | solution.py:636
  42.5 3.2 %collective-permute-start.16 = (f32[40,128]{1,0:T(8,128)S(1)}, f32[40,128]{1,0:T(8,128)S(1)}, u32[]{:S(2)}, u32[]{:S(2)}) collective-permute-start(f32[40,128]{1,0:T(8,128)S(1)} %get-tuple-element.56), channel_id=1, source_target_pairs={{0,3},{1,2},{2,1},{3,0},{4,7},{5,6},{6,5},{7,4},{8,11},{9,10},{10,... | collective-permute-start | bytes 61448 | tf_op jit(solution)/shard_map/ppermute | solution.py:636
  43.5 3.8 %collective-permute-start.15 = (f32[40,128]{1,0:T(8,128)S(1)}, f32[40,128]{1,0:T(8,128)S(1)}, u32[]{:S(2)}, u32[]{:S(2)}) collective-permute-start(f32[40,128]{1,0:T(8,128)S(1)} %get-tuple-element.56), channel_id=1, source_target_pairs={{0,2},{1,3},{2,0},{3,1},{4,6},{5,7},{6,4},{7,5},{8,10},{9,11},{10,... | collective-permute-start | bytes 61448 | tf_op jit(solution)/shard_map/ppermute | solution.py:636
  47.4 4.2 %collective-permute-start.17 = (f32[112,128]{1,0:T(8,128)S(1)}, f32[112,128]{1,0:T(8,128)S(1)}, u32[]{:S(2)}, u32[]{:S(2)}) collective-permute-start(f32[112,128]{1,0:T(8,128)S(1)} %get-tuple-element.58), channel_id=1, source_target_pairs={{0,4},{1,5},{2,6},{3,7},{4,0},{5,1},{6,2},{7,3},{8,12},{9,13},{10,... | collective-permute-start | bytes 172040 | tf_op jit(solution)/shard_map/ppermute | solution.py:636
  48.9 6.0 %collective-permute-start.18 = (f32[112,128]{1,0:T(8,128)S(1)}, f32[112,128]{1,0:T(8,128)S(1)}, u32[]{:S(2)}, u32[]{:S(2)}) collective-permute-start(f32[112,128]{1,0:T(8,128)S(1)} %get-tuple-element.59), channel_id=1, source_target_pairs={{0,12},{1,13},{2,14},{3,15},{4,8},{5,9},{6,10},{7,11},{8,4},{9,5},... | collective-permute-start | bytes 172040 | tf_op jit(solution)/shard_map/ppermute | solution.py:636
  50.6 5.4 %collective-permute-start.19 = (f32[8,128]{1,0:T(8,128)S(1)}, f32[8,128]{1,0:T(8,128)S(1)}, u32[]{:S(2)}, u32[]{:S(2)}) collective-permute-start(f32[8,128]{1,0:T(8,128)S(1)} %get-tuple-element.60.sums), channel_id=1, source_target_pairs={{0,8},{1,9},{2,10},{3,11},{4,12},{5,13},{6,14},{7,15},{8,0},{9,1},... | collective-permute-start | bytes 12296 | tf_op jit(solution)/shard_map/ppermute | solution.py:636

commit v8 on v7

--- a/solution.py
+++ b/solution.py
@@ -277,17 +277,35 @@
     return kernel, outs, scratch
 
 
+def tables(vert, steps, _, out_vert, out_steps):
+    out_vert[...] = vert[...]
+    out_steps[...] = steps[...]
+
+
+def ensemble_part(planes, cols, count):
+    ens_scale = math.sqrt(ensemble_share / (count - 1))
+
+    def kernel(weights, members, out):
+        for plane in range(planes):
+            total = jnp.zeros((ROWS, cols), jnp.float32)
+            for m in range(count):
+                total += weights[m : m + 1, :cols] * members[m, plane]
+            out[plane] = ens_scale * total
+
+    return kernel, [f32(planes, ROWS, cols)]
+
+
 def observe(planes, levels, cols, count, with_weights):
     ens_scale = math.sqrt(ensemble_share / (count - 1))
     base = planes * ROWS
     edge_rows = -(-planes // GROUP) * ROWS
 
     def kernel(*refs):
-        own, other, weights, sums, vert, prec, scale, mask, members = refs[:9]
+        own, other, ensemble, sums, vert, prec, scale, mask = refs[:8]
         if with_weights:
-            out_z, out_e, seen, stack = refs[9:]
+            members, out_z, out_e, seen, stack = refs[8:]
         else:
-            seen, out_z, out_e, now = refs[9:]
+            seen, out_z, out_e, now = refs[8:]
         out_z[...] = jnp.zeros(out_z.shape, jnp.float32)
         totals = [jnp.zeros((ROWS, cols), jnp.float32) for _ in range(count)]
         energy = jnp.zeros((ROWS, cols), jnp.float32)
@@ -302,10 +320,7 @@
                 row = (field * 2 * levels + here + level) * 2 * levels
                 static += vert[pl.ds(row + here + k, 1), :cols] * tile(own, field * levels + k)[:, :cols]
                 static += vert[pl.ds(row + there + k, 1), :cols] * tile(other, field * levels + k)[:, :cols]
-            ensemble = jnp.zeros((ROWS, cols), jnp.float32)
-            for m in range(count):
-                ensemble += weights[m : m + 1, :cols] * members[m, plane]
-            seen_now = wet * (SQRT_STATIC * (scale[plane] * static) + ens_scale * ensemble)
+            seen_now = wet * (SQRT_STATIC * (scale[plane] * static) + ensemble[plane])
             weighted = wet * (prec[plane] * seen_now)
             if with_weights:
                 seen[plane] = seen_now
@@ -667,21 +682,26 @@
     args = (innov, prec, scale, sea_mask, kappa_x, kappa_y, ens)
     args = [pltpu.with_memory_space_constraint(a, pltpu.HBM) for a in args]
     out_z, out_e, raw = call(kernel, outs, [HBM] * 7, args, scratch)
+    vert, steps = call(tables, [f32(*vert.shape), f32(*steps.shape)], [VMEM] * 3, (vert, steps, out_e))
     parts = far_round(*mix_round(mix_back(True, True, planes, levels, cols), out_z, out_e, vert, raw))
     kernel, outs, scratch = first_diffuse(planes, levels, cols)
     coef, coef_near, resid, weights, sums, out_g = call(kernel, outs, [VMEM] * 5, (*parts, steps), scratch)
 
+    kernel, outs = ensemble_part(planes, cols, count)
+    (part,) = call(kernel, outs, [VMEM] * 2, (weights, ens))
     kernel, outs, scratch = observe(planes, levels, cols, count, True)
-    args = (out_g, moved_to(out_g, 0, 0, 1), weights, sums, vert, prec, scale, sea_mask, ens)
+    args = (out_g, moved_to(out_g, 0, 0, 1), part, sums, vert, prec, scale, sea_mask, ens)
     out_z, out_e, seen = call(kernel, outs, [VMEM] * 9, args, scratch)
     parts = far_round(*mix_round(mix_back(False, True, planes, levels, cols), out_z, out_e, vert))
     kernel, outs, scratch = second_diffuse(planes, levels, cols)
     args = (*parts, steps, coef, coef_near, resid, weights)
     image, new, new_w, sums, facts, out_g = call(kernel, outs, [VMEM] * 9, args, scratch)
 
+    kernel, outs = ensemble_part(planes, cols, count)
+    (part,) = call(kernel, outs, [VMEM] * 2, (new_w, ens))
     kernel, outs, scratch = observe(planes, levels, cols, count, False)
-    args = (out_g, moved_to(out_g, 0, 0, 1), new_w, sums, vert, prec, scale, sea_mask, ens, seen)
-    out_z, out_e = call(kernel, outs, [VMEM] * 10, args, scratch)
+    args = (out_g, moved_to(out_g, 0, 0, 1), part, sums, vert, prec, scale, sea_mask, seen)
+    out_z, out_e = call(kernel, outs, [VMEM] * 9, args, scratch)
     own, one, three, sums = mix_round(mix_back(False, False, planes, levels, cols), out_z, out_e, vert)
     sums_two = moved_to(sums, 2, 0, 0)
     kernel, outs, scratch = last_diffuse(planes, levels, cols)

time: 57.1 us -> 56.7 us (level)
    pallas_call x10 -> x13, Pallas kernels: 10.6 us -> 10.5 us  [call(): pl.pallas_call(kernel, out_shape=outs, in_specs=specs, out_specs=[VMEM] *...]
  transfers between devices with their start and end apart: 20 -> 20, of which waited for: 14 -> 14; matrix products, arithmetic and copies ran while one was open for 0% -> 1% of each run, Pallas kernels for 2% -> 2%
where the time goes in v8:
time: 56.7 us; the launch traced here: 56.5 us
  waiting for transfers between devices  24.7 us (44%)
  starting transfers between devices  20.1 us (35%)
  Pallas kernels  10.5 us (19%)
  between operations  0.77 us (1%)
    ppermute x20, waiting for transfers between devices, moved_to(): lax.ppermute(values, AXES, [(number[a, b, c], number[a ^ x, b ^ y, c ^ z]...  24.7 us
    ppermute x20, starting transfers between devices, moved_to(): lax.ppermute(values, AXES, [(number[a, b, c], number[a ^ x, b ^ y, c ^ z]...  20.1 us
    pallas_call x13, Pallas kernels, call(): pl.pallas_call(kernel, out_shape=outs, in_specs=specs, out_specs=[VMEM] *...  10.5 us
  transfers between devices with their start and end apart: 20, of which 14 were waited for; matrix products, arithmetic and copies ran while one was open for 1% of the time, Pallas kernels for 2%

profile of v8, /device:TPU:0, one launch (start us, length us, event | category | flops | bytes accessed | tf_op | source)
XLA Modules:
  0.0 56.5 jit_solution(18347864809890974016)
XLA Ops:
  0.6 0.0 copy-start
  0.7 1.7 %shard_map.112 = (f32[168,128]{1,0:T(8,128)S(1)}, f32[56,128]{1,0:T(8,128)S(1)}, f32[96,128]{1,0:T(8,128)S(1)}) custom-call(f32[10,16,108]{2,1,0:T(8,128)} %bitcast.17, f32[10,16,108]{2,1,0:T(8,128)} %bitcast.11, f32[10,16,108]{2,1,0:T(8,128)} %bitcast.14, s32[2,16,108]{2,1,0:T(8,128)} %refs_7_.3, f32[2,16,108]{2,1,0:T(8,128)} %refs_4_.1, ...), custom_call_target="tpu_custom_call" | custom-call | tf_op jit(solution)/shard_map/pallas_call | solution.py:165
  2.4 0.0 copy-start.1
  2.4 0.0 copy-start.2
  2.4 0.0 copy-start.3
  2.4 0.5 collective-permute-start
  3.0 2.6 %collective-permute-start.2 = (f32[56,128]{1,0:T(8,128)S(1)}, f32[56,128]{1,0:T(8,128)S(1)}, u32[]{:S(2)}, u32[]{:S(2)}) collective-permute-start(f32[56,128]{1,0:T(8,128)S(1)} %get-tuple-element.39._), channel_id=1, source_target_pairs={{0,3},{1,2},{2,1},{3,0},{4,7},{5,6},{6,5},{7,4},{8,11},{9,10},{10,... | collective-permute-start | bytes 86024 | tf_op jit(solution)/shard_map/ppermute | solution.py:651
  5.6 0.0 collective-permute-start.1
  5.6 0.0 copy-done.4
  5.6 0.1 copy.13
  5.7 0.1 broadcast_in_dim.6
  5.8 0.1 broadcast_in_dim.15.steps
  5.9 0.1 broadcast_in_dim.14.vert
  6.0 1.2 %collective-permute-done.2.refs_3_ = f32[56,128]{1,0:T(8,128)S(1)} collective-permute-done((f32[56,128]{1,0:T(8,128)S(1)}, f32[56,128]{1,0:T(8,128)S(1)}, u32[]{:S(2)}, u32[]{:S(2)}) %collective-permute-start.2) | collective-permute-done | bytes 28704 | tf_op jit(solution)/shard_map/ppermute | solution.py:651
  7.2 2.3 %collective-permute-done.1.refs_2_ = f32[56,128]{1,0:T(8,128)S(1)} collective-permute-done((f32[56,128]{1,0:T(8,128)S(1)}, f32[56,128]{1,0:T(8,128)S(1)}, u32[]{:S(2)}, u32[]{:S(2)}) %collective-permute-start.1) | collective-permute-done | bytes 28704 | tf_op jit(solution)/shard_map/ppermute | solution.py:651
  9.4 0.0 collective-permute-done.refs_1_
  9.5 0.1 shard_map.114
  9.6 3.7 %collective-permute-start.5 = (f32[232,128]{1,0:T(8,128)S(1)}, f32[232,128]{1,0:T(8,128)S(1)}, u32[]{:S(2)}, u32[]{:S(2)}) collective-permute-start(f32[232,128]{1,0:T(8,128)S(1)} %get-tuple-element.42.own), channel_id=1, source_target_pairs={{0,12},{1,13},{2,14},{3,15},{4,8},{5,9},{6,10},{7,11},{8,4},{9,5},... | collective-permute-start | bytes 356360 | tf_op jit(solution)/shard_map/ppermute | solution.py:651
  13.3 0.0 collective-permute-start.3
  13.3 0.8 %collective-permute-start.4 = (f32[120,128]{1,0:T(8,128)S(1)}, f32[120,128]{1,0:T(8,128)S(1)}, u32[]{:S(2)}, u32[]{:S(2)}) collective-permute-start(f32[120,128]{1,0:T(8,128)S(1)} %get-tuple-element.43), channel_id=1, source_target_pairs={{0,8},{1,9},{2,10},{3,11},{4,12},{5,13},{6,14},{7,15},{8,0},{9,1},... | collective-permute-start | bytes 184328 | tf_op jit(solution)/shard_map/ppermute | solution.py:651
  14.0 5.3 %collective-permute-done.4.near = f32[120,128]{1,0:T(8,128)S(1)} collective-permute-done((f32[120,128]{1,0:T(8,128)S(1)}, f32[120,128]{1,0:T(8,128)S(1)}, u32[]{:S(2)}, u32[]{:S(2)}) %collective-permute-start.4) | collective-permute-done | bytes 61472 | tf_op jit(solution)/shard_map/ppermute | solution.py:651
  19.3 0.0 collective-permute-done.5.third
  19.3 0.3 collective-permute-done.3.first
  19.6 2.8 %shard_map.115 = (f32[3,2,56,128]{3,2,1,0:T(8,128)S(1)}, f32[3,2,40,128]{3,2,1,0:T(8,128)S(1)}, f32[10,40,128]{2,1,0:T(8,128)S(1)}, f32[16,128]{1,0:T(8,128)S(1)...) custom-call(f32[232,128]{1,0:T(8,128)S(1)} %get-tuple-element.42.own, f32[232,128]{1,0:T(8,128)S(1)} %collective-permute-done.3.first, ...), custom_call_target="tpu_custom_call" | custom-call | tf_op jit(solution)/shard_map/pallas_call | solution.py:165
  22.4 0.1 collective-permute-start.6
  22.5 0.0 copy-done
  22.5 0.1 shard_map.116.refs_2_
  22.6 1.1 %collective-permute-done.6.refs_1_ = f32[160,128]{1,0:T(8,128)S(1)} collective-permute-done((f32[160,128]{1,0:T(8,128)S(1)}, f32[160,128]{1,0:T(8,128)S(1)}, u32[]{:S(2)}, u32[]{:S(2)}) %collective-permute-start.6) | collective-permute-done | bytes 81952 | tf_op jit(solution)/shard_map/ppermute | solution.py:651
  23.8 0.0 copy-done.1
  23.8 0.0 copy-done.3
  23.8 0.3 shard_map.117
  24.0 0.2 collective-permute-start.7
  24.3 1.2 %collective-permute-start.9 = (f32[40,128]{1,0:T(8,128)S(1)}, f32[40,128]{1,0:T(8,128)S(1)}, u32[]{:S(2)}, u32[]{:S(2)}) collective-permute-start(f32[40,128]{1,0:T(8,128)S(1)} %get-tuple-element.49), channel_id=1, source_target_pairs={{0,3},{1,2},{2,1},{3,0},{4,7},{5,6},{6,5},{7,4},{8,11},{9,10},{10,... | collective-permute-start | bytes 61448 | tf_op jit(solution)/shard_map/ppermute | solution.py:651
  25.4 0.8 %collective-permute-start.8 = (f32[40,128]{1,0:T(8,128)S(1)}, f32[40,128]{1,0:T(8,128)S(1)}, u32[]{:S(2)}, u32[]{:S(2)}) collective-permute-start(f32[40,128]{1,0:T(8,128)S(1)} %get-tuple-element.49), channel_id=1, source_target_pairs={{0,2},{1,3},{2,0},{3,1},{4,6},{5,7},{6,4},{7,5},{8,10},{9,11},{10,... | collective-permute-start | bytes 61448 | tf_op jit(solution)/shard_map/ppermute | solution.py:651
  26.2 1.2 %collective-permute-done.9.refs_3_ = f32[40,128]{1,0:T(8,128)S(1)} collective-permute-done((f32[40,128]{1,0:T(8,128)S(1)}, f32[40,128]{1,0:T(8,128)S(1)}, u32[]{:S(2)}, u32[]{:S(2)}) %collective-permute-start.9) | collective-permute-done | bytes 20512 | tf_op jit(solution)/shard_map/ppermute | solution.py:651
  27.5 1.7 %collective-permute-done.8.refs_2_ = f32[40,128]{1,0:T(8,128)S(1)} collective-permute-done((f32[40,128]{1,0:T(8,128)S(1)}, f32[40,128]{1,0:T(8,128)S(1)}, u32[]{:S(2)}, u32[]{:S(2)}) %collective-permute-start.8) | collective-permute-done | bytes 20512 | tf_op jit(solution)/shard_map/ppermute | solution.py:651
  29.2 0.0 collective-permute-done.7.refs_1_
  29.2 0.1 shard_map.118
  29.3 2.3 %collective-permute-start.12 = (f32[168,128]{1,0:T(8,128)S(1)}, f32[168,128]{1,0:T(8,128)S(1)}, u32[]{:S(2)}, u32[]{:S(2)}) collective-permute-start(f32[168,128]{1,0:T(8,128)S(1)} %get-tuple-element.50.own), channel_id=1, source_target_pairs={{0,12},{1,13},{2,14},{3,15},{4,8},{5,9},{6,10},{7,11},{8,4},{9,5},... | collective-permute-start | bytes 258056 | tf_op jit(solution)/shard_map/ppermute | solution.py:651
  31.6 0.6 collective-permute-start.10
  32.2 1.6 %collective-permute-start.11 = (f32[88,128]{1,0:T(8,128)S(1)}, f32[88,128]{1,0:T(8,128)S(1)}, u32[]{:S(2)}, u32[]{:S(2)}) collective-permute-start(f32[88,128]{1,0:T(8,128)S(1)} %get-tuple-element.51), channel_id=1, source_target_pairs={{0,8},{1,9},{2,10},{3,11},{4,12},{5,13},{6,14},{7,15},{8,0},{9,1},... | collective-permute-start | bytes 135176 | tf_op jit(solution)/shard_map/ppermute | solution.py:651
  33.8 3.4 %collective-permute-done.11.near = f32[88,128]{1,0:T(8,128)S(1)} collective-permute-done((f32[88,128]{1,0:T(8,128)S(1)}, f32[88,128]{1,0:T(8,128)S(1)}, u32[]{:S(2)}, u32[]{:S(2)}) %collective-permute-start.11) | collective-permute-done | bytes 45088 | tf_op jit(solution)/shard_map/ppermute | solution.py:651
  37.2 0.0 collective-permute-done.12.third
  37.2 0.3 collective-permute-done.10.first
  37.4 2.8 %shard_map.119 = (f32[10,16,128]{2,1,0:T(8,128)S(1)}, f32[10,16,128]{2,1,0:T(8,128)S(1)}, f32[16,128]{1,0:T(8,128)S(1)}, f32[8,128]{1,0:T(8,128)S(1)}, f32[8,128]{1,0:T(8,128)S(1)}, /*index=5*/f32[160,128]{1,0:T(8,128)S(1)}) custom-call(f32[168,128]{1,0:T(8,128)S(1)} %get-tuple-element.50.own, f32[168,128]{1,0:T(8,128)S(1)} %collective-permute-done.10.first, ...), custom_call_target="tpu_custom_call" | custom-call | tf_op jit(solution)/shard_map/pallas_call | solution.py:165
  40.3 0.1 collective-permute-start.13
  40.4 0.1 shard_map.120.refs_2_
  40.5 1.2 %collective-permute-done.13.refs_1_ = f32[160,128]{1,0:T(8,128)S(1)} collective-permute-done((f32[160,128]{1,0:T(8,128)S(1)}, f32[160,128]{1,0:T(8,128)S(1)}, u32[]{:S(2)}, u32[]{:S(2)}) %collective-permute-start.13) | collective-permute-done | bytes 81952 | tf_op jit(solution)/shard_map/ppermute | solution.py:651
  41.6 0.3 shard_map.121
  41.9 0.2 collective-permute-start.14
  42.1 1.0 %collective-permute-start.16 = (f32[40,128]{1,0:T(8,128)S(1)}, f32[40,128]{1,0:T(8,128)S(1)}, u32[]{:S(2)}, u32[]{:S(2)}) collective-permute-start(f32[40,128]{1,0:T(8,128)S(1)} %get-tuple-element.60), channel_id=1, source_target_pairs={{0,3},{1,2},{2,1},{3,0},{4,7},{5,6},{6,5},{7,4},{8,11},{9,10},{10,... | collective-permute-start | bytes 61448 | tf_op jit(solution)/shard_map/ppermute | solution.py:651
  43.0 1.0 %collective-permute-start.15 = (f32[40,128]{1,0:T(8,128)S(1)}, f32[40,128]{1,0:T(8,128)S(1)}, u32[]{:S(2)}, u32[]{:S(2)}) collective-permute-start(f32[40,128]{1,0:T(8,128)S(1)} %get-tuple-element.60), channel_id=1, source_target_pairs={{0,2},{1,3},{2,0},{3,1},{4,6},{5,7},{6,4},{7,5},{8,10},{9,11},{10,... | collective-permute-start | bytes 61448 | tf_op jit(solution)/shard_map/ppermute | solution.py:651
  44.0 1.2 %collective-permute-done.16.refs_3_ = f32[40,128]{1,0:T(8,128)S(1)} collective-permute-done((f32[40,128]{1,0:T(8,128)S(1)}, f32[40,128]{1,0:T(8,128)S(1)}, u32[]{:S(2)}, u32[]{:S(2)}) %collective-permute-start.16) | collective-permute-done | bytes 20512 | tf_op jit(solution)/shard_map/ppermute | solution.py:651
  45.3 1.5 %collective-permute-done.15.refs_2_ = f32[40,128]{1,0:T(8,128)S(1)} collective-permute-done((f32[40,128]{1,0:T(8,128)S(1)}, f32[40,128]{1,0:T(8,128)S(1)}, u32[]{:S(2)}, u32[]{:S(2)}) %collective-permute-start.15) | collective-permute-done | bytes 20512 | tf_op jit(solution)/shard_map/ppermute | solution.py:651
  46.8 0.0 collective-permute-done.14.refs_1_
  46.8 0.1 shard_map.122
  47.0 1.5 %collective-permute-start.17 = (f32[112,128]{1,0:T(8,128)S(1)}, f32[112,128]{1,0:T(8,128)S(1)}, u32[]{:S(2)}, u32[]{:S(2)}) collective-permute-start(f32[112,128]{1,0:T(8,128)S(1)} %get-tuple-element.62), channel_id=1, source_target_pairs={{0,4},{1,5},{2,6},{3,7},{4,0},{5,1},{6,2},{7,3},{8,12},{9,13},{10,... | collective-permute-start | bytes 172040 | tf_op jit(solution)/shard_map/ppermute | solution.py:651
  48.5 1.7 %collective-permute-start.18 = (f32[112,128]{1,0:T(8,128)S(1)}, f32[112,128]{1,0:T(8,128)S(1)}, u32[]{:S(2)}, u32[]{:S(2)}) collective-permute-start(f32[112,128]{1,0:T(8,128)S(1)} %get-tuple-element.63), channel_id=1, source_target_pairs={{0,12},{1,13},{2,14},{3,15},{4,8},{5,9},{6,10},{7,11},{8,4},{9,5},... | collective-permute-start | bytes 172040 | tf_op jit(solution)/shard_map/ppermute | solution.py:651
  50.2 0.3 collective-permute-start.19
  50.5 0.7 %collective-permute-done.17.one = f32[112,128]{1,0:T(8,128)S(1)} collective-permute-done((f32[112,128]{1,0:T(8,128)S(1)}, f32[112,128]{1,0:T(8,128)S(1)}, u32[]{:S(2)}, u32[]{:S(2)}) %collective-permute-start.17) | collective-permute-done | bytes 57376 | tf_op jit(solution)/shard_map/ppermute | solution.py:651
  51.2 3.3 %collective-permute-done.18.three = f32[112,128]{1,0:T(8,128)S(1)} collective-permute-done((f32[112,128]{1,0:T(8,128)S(1)}, f32[112,128]{1,0:T(8,128)S(1)}, u32[]{:S(2)}, u32[]{:S(2)}) %collective-permute-start.18) | collective-permute-done | bytes 57376 | tf_op jit(solution)/shard_map/ppermute | solution.py:651
  54.5 1.2 %shard_map.123 = (f32[10,16,128]{2,1,0:T(8,128)S(1)}, f32[2,8,128]{2,1,0:T(8,128)S(1)}) custom-call(f32[160,128]{1,0:T(8,128)S(1)} %get-tuple-element.61.own, f32[112,128]{1,0:T(8,128)S(1)} %collective-permute-done.17.one, f32[112,128]{1,0:T(8,128)S(1)} %collective-permute-done.18.three, f32[8,128]{1,0:T(8,128)S(1)} %get-tuple-element.64.sums, ...), custom_call_target="tpu_custom_call" | custom-call | tf_op jit(solution)/shard_map/pallas_call | solution.py:165
  55.7 0.0 collective-permute-done.19.sums_two
  55.7 0.9 %shard_map.124 = (f32[10,16,108]{2,1,0:T(8,128)}, f32[1,16]{1,0:T(1,128)}, f32[10,16,108]{2,1,0:T(8,128)}) custom-call(f32[10,16,128]{2,1,0:T(8,128)S(1)} %get-tuple-element.65.diffused, f32[2,8,128]{2,1,0:T(8,128)S(1)} %get-tuple-element.66.sums, f32[8,128]{1,0:T(8,128)S(1)} %collective-permute-done.19.sums_two, ...), custom_call_target="tpu_custom_call" | custom-call | tf_op jit(solution)/shard_map/pallas_call | solution.py:165
  (6 shorter events, 0.0 us)
Async XLA Ops:
  0.6 21.9 %copy-start = (f32[16,5,2,16,108]{4,3,2,1,0:T(8,128)S(1)}, f32[16,5,2,16,108]{4,3,2,1,0:T(8,128)}, u32[]{:S(2)}) copy-start(f32[16,5,2,16,108]{4,3,2,1,0:T(8,128)} %param.15) | copy-start | bytes 3317764
  0.6 5.0 %copy-start.5 = (s32[5]{0:T(128)S(1)}, s32[5]{0:T(128)}, u32[]{:S(2)}) copy-start(s32[5]{0:T(128)} %param.17) | copy-start | bytes 64
  0.7 5.0 %copy-start.4 = (f32[5,4,4]{0,2,1:T(4,128)S(1)}, f32[5,4,4]{0,2,1:T(4,128)}, u32[]{:S(2)}) copy-start(f32[5,4,4]{0,2,1:T(4,128)} %param.16) | copy-start | bytes 964
  2.4 21.4 %copy-start.1 = (f32[5,2,16,108]{3,2,1,0:T(8,128)S(1)}, f32[5,2,16,108]{3,2,1,0:T(8,128)}, u32[]{:S(2)}) copy-start(f32[5,2,16,108]{3,2,1,0:T(8,128)} %param.10) | copy-start | bytes 207364
  2.4 21.3 %copy-start.2 = (f32[5,2,16,108]{3,2,1,0:T(8,128)S(1)}, f32[5,2,16,108]{3,2,1,0:T(8,128)}, u32[]{:S(2)}) copy-start(f32[5,2,16,108]{3,2,1,0:T(8,128)} %param.11) | copy-start | bytes 207364
  2.4 21.3 %copy-start.3 = (s32[2,16,108]{2,1,0:T(8,128)S(1)}, s32[2,16,108]{2,1,0:T(8,128)}, u32[]{:S(2)}) copy-start(s32[2,16,108]{2,1,0:T(8,128)} %refs_7_.3) | copy-start | bytes 41476
  2.4 7.0 %collective-permute-start = (f32[168,128]{1,0:T(8,128)S(1)}, f32[168,128]{1,0:T(8,128)S(1)}, u32[]{:S(2)}, u32[]{:S(2)}) collective-permute-start(f32[168,128]{1,0:T(8,128)S(1)} %get-tuple-element.38.refs_0_), channel_id=1, source_target_pairs={{0,1},{1,0},{2,3},{3,2},{4,5},{5,4},{6,7},{7,6},{8,9},{9,8},{10,11... | collective-permute-start | bytes 258056 | tf_op jit(solution)/shard_map/ppermute | solution.py:651
  3.0 4.2 %collective-permute-start.2 = (f32[56,128]{1,0:T(8,128)S(1)}, f32[56,128]{1,0:T(8,128)S(1)}, u32[]{:S(2)}, u32[]{:S(2)}) collective-permute-start(f32[56,128]{1,0:T(8,128)S(1)} %get-tuple-element.39._), channel_id=1, source_target_pairs={{0,3},{1,2},{2,1},{3,0},{4,7},{5,6},{6,5},{7,4},{8,11},{9,10},{10,... | collective-permute-start | bytes 86024 | tf_op jit(solution)/shard_map/ppermute | solution.py:651
  5.6 3.9 %collective-permute-start.1 = (f32[56,128]{1,0:T(8,128)S(1)}, f32[56,128]{1,0:T(8,128)S(1)}, u32[]{:S(2)}, u32[]{:S(2)}) collective-permute-start(f32[56,128]{1,0:T(8,128)S(1)} %get-tuple-element.39._), channel_id=1, source_target_pairs={{0,2},{1,3},{2,0},{3,1},{4,6},{5,7},{6,4},{7,5},{8,10},{9,11},{10,... | collective-permute-start | bytes 86024 | tf_op jit(solution)/shard_map/ppermute | solution.py:651
  9.6 9.7 %collective-permute-start.5 = (f32[232,128]{1,0:T(8,128)S(1)}, f32[232,128]{1,0:T(8,128)S(1)}, u32[]{:S(2)}, u32[]{:S(2)}) collective-permute-start(f32[232,128]{1,0:T(8,128)S(1)} %get-tuple-element.42.own), channel_id=1, source_target_pairs={{0,12},{1,13},{2,14},{3,15},{4,8},{5,9},{6,10},{7,11},{8,4},{9,5},... | collective-permute-start | bytes 356360 | tf_op jit(solution)/shard_map/ppermute | solution.py:651
  13.3 6.4 %collective-permute-start.3 = (f32[232,128]{1,0:T(8,128)S(1)}, f32[232,128]{1,0:T(8,128)S(1)}, u32[]{:S(2)}, u32[]{:S(2)}) collective-permute-start(f32[232,128]{1,0:T(8,128)S(1)} %get-tuple-element.42.own), channel_id=1, source_target_pairs={{0,4},{1,5},{2,6},{3,7},{4,0},{5,1},{6,2},{7,3},{8,12},{9,13},{10,... | collective-permute-start | bytes 356360 | tf_op jit(solution)/shard_map/ppermute | solution.py:651
  13.3 6.0 %collective-permute-start.4 = (f32[120,128]{1,0:T(8,128)S(1)}, f32[120,128]{1,0:T(8,128)S(1)}, u32[]{:S(2)}, u32[]{:S(2)}) collective-permute-start(f32[120,128]{1,0:T(8,128)S(1)} %get-tuple-element.43), channel_id=1, source_target_pairs={{0,8},{1,9},{2,10},{3,11},{4,12},{5,13},{6,14},{7,15},{8,0},{9,1},... | collective-permute-start | bytes 184328 | tf_op jit(solution)/shard_map/ppermute | solution.py:651
  22.4 1.3 %collective-permute-start.6 = (f32[160,128]{1,0:T(8,128)S(1)}, f32[160,128]{1,0:T(8,128)S(1)}, u32[]{:S(2)}, u32[]{:S(2)}) collective-permute-start(f32[160,128]{1,0:T(8,128)S(1)} %get-tuple-element.45.refs_0_), channel_id=1, source_target_pairs={{0,1},{1,0},{2,3},{3,2},{4,5},{5,4},{6,7},{7,6},{8,9},{9,8},{10,11... | collective-permute-start | bytes 245768 | tf_op jit(solution)/shard_map/ppermute | solution.py:651
  24.0 5.2 %collective-permute-start.7 = (f32[168,128]{1,0:T(8,128)S(1)}, f32[168,128]{1,0:T(8,128)S(1)}, u32[]{:S(2)}, u32[]{:S(2)}) collective-permute-start(f32[168,128]{1,0:T(8,128)S(1)} %get-tuple-element.48.refs_0_), channel_id=1, source_target_pairs={{0,1},{1,0},{2,3},{3,2},{4,5},{5,4},{6,7},{7,6},{8,9},{9,8},{10,11... | collective-permute-start | bytes 258056 | tf_op jit(solution)/shard_map/ppermute | solution.py:651
  24.3 3.2 %collective-permute-start.9 = (f32[40,128]{1,0:T(8,128)S(1)}, f32[40,128]{1,0:T(8,128)S(1)}, u32[]{:S(2)}, u32[]{:S(2)}) collective-permute-start(f32[40,128]{1,0:T(8,128)S(1)} %get-tuple-element.49), channel_id=1, source_target_pairs={{0,3},{1,2},{2,1},{3,0},{4,7},{5,6},{6,5},{7,4},{8,11},{9,10},{10,... | collective-permute-start | bytes 61448 | tf_op jit(solution)/shard_map/ppermute | solution.py:651
  25.4 3.8 %collective-permute-start.8 = (f32[40,128]{1,0:T(8,128)S(1)}, f32[40,128]{1,0:T(8,128)S(1)}, u32[]{:S(2)}, u32[]{:S(2)}) collective-permute-start(f32[40,128]{1,0:T(8,128)S(1)} %get-tuple-element.49), channel_id=1, source_target_pairs={{0,2},{1,3},{2,0},{3,1},{4,6},{5,7},{6,4},{7,5},{8,10},{9,11},{10,... | collective-permute-start | bytes 61448 | tf_op jit(solution)/shard_map/ppermute | solution.py:651
  29.3 7.8 %collective-permute-start.12 = (f32[168,128]{1,0:T(8,128)S(1)}, f32[168,128]{1,0:T(8,128)S(1)}, u32[]{:S(2)}, u32[]{:S(2)}) collective-permute-start(f32[168,128]{1,0:T(8,128)S(1)} %get-tuple-element.50.own), channel_id=1, source_target_pairs={{0,12},{1,13},{2,14},{3,15},{4,8},{5,9},{6,10},{7,11},{8,4},{9,5},... | collective-permute-start | bytes 258056 | tf_op jit(solution)/shard_map/ppermute | solution.py:651
  31.6 5.8 %collective-permute-start.10 = (f32[168,128]{1,0:T(8,128)S(1)}, f32[168,128]{1,0:T(8,128)S(1)}, u32[]{:S(2)}, u32[]{:S(2)}) collective-permute-start(f32[168,128]{1,0:T(8,128)S(1)} %get-tuple-element.50.own), channel_id=1, source_target_pairs={{0,4},{1,5},{2,6},{3,7},{4,0},{5,1},{6,2},{7,3},{8,12},{9,13},{10,... | collective-permute-start | bytes 258056 | tf_op jit(solution)/shard_map/ppermute | solution.py:651
  32.2 5.0 %collective-permute-start.11 = (f32[88,128]{1,0:T(8,128)S(1)}, f32[88,128]{1,0:T(8,128)S(1)}, u32[]{:S(2)}, u32[]{:S(2)}) collective-permute-start(f32[88,128]{1,0:T(8,128)S(1)} %get-tuple-element.51), channel_id=1, source_target_pairs={{0,8},{1,9},{2,10},{3,11},{4,12},{5,13},{6,14},{7,15},{8,0},{9,1},... | collective-permute-start | bytes 135176 | tf_op jit(solution)/shard_map/ppermute | solution.py:651
  40.3 1.3 %collective-permute-start.13 = (f32[160,128]{1,0:T(8,128)S(1)}, f32[160,128]{1,0:T(8,128)S(1)}, u32[]{:S(2)}, u32[]{:S(2)}) collective-permute-start(f32[160,128]{1,0:T(8,128)S(1)} %get-tuple-element.55.refs_0_), channel_id=1, source_target_pairs={{0,1},{1,0},{2,3},{3,2},{4,5},{5,4},{6,7},{7,6},{8,9},{9,8},{10,11... | collective-permute-start | bytes 245768 | tf_op jit(solution)/shard_map/ppermute | solution.py:651
  41.9 4.9 %collective-permute-start.14 = (f32[168,128]{1,0:T(8,128)S(1)}, f32[168,128]{1,0:T(8,128)S(1)}, u32[]{:S(2)}, u32[]{:S(2)}) collective-permute-start(f32[168,128]{1,0:T(8,128)S(1)} %get-tuple-element.59.refs_0_), channel_id=1, source_target_pairs={{0,1},{1,0},{2,3},{3,2},{4,5},{5,4},{6,7},{7,6},{8,9},{9,8},{10,11... | collective-permute-start | bytes 258056 | tf_op jit(solution)/shard_map/ppermute | solution.py:651
  42.1 3.2 %collective-permute-start.16 = (f32[40,128]{1,0:T(8,128)S(1)}, f32[40,128]{1,0:T(8,128)S(1)}, u32[]{:S(2)}, u32[]{:S(2)}) collective-permute-start(f32[40,128]{1,0:T(8,128)S(1)} %get-tuple-element.60), channel_id=1, source_target_pairs={{0,3},{1,2},{2,1},{3,0},{4,7},{5,6},{6,5},{7,4},{8,11},{9,10},{10,... | collective-permute-start | bytes 61448 | tf_op jit(solution)/shard_map/ppermute | solution.py:651
  43.0 3.8 %collective-permute-start.15 = (f32[40,128]{1,0:T(8,128)S(1)}, f32[40,128]{1,0:T(8,128)S(1)}, u32[]{:S(2)}, u32[]{:S(2)}) collective-permute-start(f32[40,128]{1,0:T(8,128)S(1)} %get-tuple-element.60), channel_id=1, source_target_pairs={{0,2},{1,3},{2,0},{3,1},{4,6},{5,7},{6,4},{7,5},{8,10},{9,11},{10,... | collective-permute-start | bytes 61448 | tf_op jit(solution)/shard_map/ppermute | solution.py:651
  47.0 4.2 %collective-permute-start.17 = (f32[112,128]{1,0:T(8,128)S(1)}, f32[112,128]{1,0:T(8,128)S(1)}, u32[]{:S(2)}, u32[]{:S(2)}) collective-permute-start(f32[112,128]{1,0:T(8,128)S(1)} %get-tuple-element.62), channel_id=1, source_target_pairs={{0,4},{1,5},{2,6},{3,7},{4,0},{5,1},{6,2},{7,3},{8,12},{9,13},{10,... | collective-permute-start | bytes 172040 | tf_op jit(solution)/shard_map/ppermute | solution.py:651
  48.5 6.0 %collective-permute-start.18 = (f32[112,128]{1,0:T(8,128)S(1)}, f32[112,128]{1,0:T(8,128)S(1)}, u32[]{:S(2)}, u32[]{:S(2)}) collective-permute-start(f32[112,128]{1,0:T(8,128)S(1)} %get-tuple-element.63), channel_id=1, source_target_pairs={{0,12},{1,13},{2,14},{3,15},{4,8},{5,9},{6,10},{7,11},{8,4},{9,5},... | collective-permute-start | bytes 172040 | tf_op jit(solution)/shard_map/ppermute | solution.py:651
  50.2 5.4 %collective-permute-start.19 = (f32[8,128]{1,0:T(8,128)S(1)}, f32[8,128]{1,0:T(8,128)S(1)}, u32[]{:S(2)}, u32[]{:S(2)}) collective-permute-start(f32[8,128]{1,0:T(8,128)S(1)} %get-tuple-element.64.sums), channel_id=1, source_target_pairs={{0,8},{1,9},{2,10},{3,11},{4,12},{5,13},{6,14},{7,15},{8,0},{9,1},... | collective-permute-start | bytes 12296 | tf_op jit(solution)/shard_map/ppermute | solution.py:651

commit v9 on v8

--- a/solution.py
+++ b/solution.py
@@ -598,7 +598,7 @@
 
 
 def last_diffuse(planes, levels, cols):
-    def kernel(own, one, three, sums, steps, coef, out_g, out_sums, buf, nat):
+    def kernel(own, three, one, sums, steps, coef, out_g, out_sums, buf, nat):
         even = is_even()
         gap_rows = jnp.zeros((4, LANES), jnp.float32)
         for plane in range(planes):
@@ -705,7 +705,7 @@
     own, one, three, sums = mix_round(mix_back(False, False, planes, levels, cols), out_z, out_e, vert)
     sums_two = moved_to(sums, 2, 0, 0)
     kernel, outs, scratch = last_diffuse(planes, levels, cols)
-    args = (own, moved_to(one, 1, 0, 0), moved_to(three, 3, 0, 0), sums, steps, coef_near)
+    args = (own, moved_to(three, 3, 0, 0), moved_to(one, 1, 0, 0), sums, steps, coef_near)
     diffused, sums = call(kernel, outs, [VMEM] * 6, args, scratch)
     kernel, outs = finish(planes, cols)
     args = (diffused, sums, sums_two, resid, weights, image, new, new_w, facts)

time: 56.7 us -> 55.9 us (0.986)
  waiting for transfers between devices: 24.7 us -> 23 us
  starting transfers between devices: 20.1 us -> 21 us
    ppermute x20, waiting for transfers between devices: 24.7 us -> 23 us  [moved_to(): lax.ppermute(values, AXES, [(number[a, b, c], number[a ^ x, b ^ y, c ^ z]...]
    ppermute x20, starting transfers between devices: 20.1 us -> 21 us  [moved_to(): lax.ppermute(values, AXES, [(number[a, b, c], number[a ^ x, b ^ y, c ^ z]...]
  transfers between devices with their start and end apart: 20 -> 20, of which waited for: 14 -> 14; matrix products, arithmetic and copies ran while one was open for 1% -> 1% of each run, Pallas kernels for 2% -> 3%
where the time goes in v9:
time: 55.9 us; the launch traced here: 55.7 us
  waiting for transfers between devices  23 us (41%)
  starting transfers between devices  21 us (38%)
  Pallas kernels  10.5 us (19%)
  between operations  0.77 us (1%)
    ppermute x20, waiting for transfers between devices, moved_to(): lax.ppermute(values, AXES, [(number[a, b, c], number[a ^ x, b ^ y, c ^ z]...  23 us
    ppermute x20, starting transfers between devices, moved_to(): lax.ppermute(values, AXES, [(number[a, b, c], number[a ^ x, b ^ y, c ^ z]...  21 us
    pallas_call x13, Pallas kernels, call(): pl.pallas_call(kernel, out_shape=outs, in_specs=specs, out_specs=[VMEM] *...  10.5 us
  transfers between devices with their start and end apart: 20, of which 14 were waited for; matrix products, arithmetic and copies ran while one was open for 1% of the time, Pallas kernels for 3%

profile of v9, /device:TPU:0, one launch (start us, length us, event | category | flops | bytes accessed | tf_op | source)
XLA Modules:
  0.0 55.7 jit_solution(8630667174524802370)
XLA Ops:
  0.6 0.0 copy-start
  0.6 0.0 copy-start.5
  0.7 0.0 copy-start.4
  0.7 1.7 %shard_map.112 = (f32[168,128]{1,0:T(8,128)S(1)}, f32[56,128]{1,0:T(8,128)S(1)}, f32[96,128]{1,0:T(8,128)S(1)}) custom-call(f32[10,16,108]{2,1,0:T(8,128)} %bitcast.17, f32[10,16,108]{2,1,0:T(8,128)} %bitcast.11, f32[10,16,108]{2,1,0:T(8,128)} %bitcast.14, s32[2,16,108]{2,1,0:T(8,128)} %refs_7_.3, f32[2,16,108]{2,1,0:T(8,128)} %refs_4_.1, ...), custom_call_target="tpu_custom_call" | custom-call | tf_op jit(solution)/shard_map/pallas_call | solution.py:165
  2.4 0.0 copy-start.1
  2.4 0.0 copy-start.2
  2.4 0.0 copy-start.3
  2.4 0.5 collective-permute-start
  3.0 2.6 %collective-permute-start.2 = (f32[56,128]{1,0:T(8,128)S(1)}, f32[56,128]{1,0:T(8,128)S(1)}, u32[]{:S(2)}, u32[]{:S(2)}) collective-permute-start(f32[56,128]{1,0:T(8,128)S(1)} %get-tuple-element.39._), channel_id=1, source_target_pairs={{0,3},{1,2},{2,1},{3,0},{4,7},{5,6},{6,5},{7,4},{8,11},{9,10},{10,... | collective-permute-start | bytes 86024 | tf_op jit(solution)/shard_map/ppermute | solution.py:651
  5.6 0.0 collective-permute-start.1
  5.6 0.0 copy-done.5
  5.6 0.1 copy.13
  5.7 0.1 broadcast_in_dim.6
  5.8 0.1 broadcast_in_dim.15.steps
  5.9 0.1 broadcast_in_dim.14.vert
  6.0 1.2 %collective-permute-done.2.refs_3_ = f32[56,128]{1,0:T(8,128)S(1)} collective-permute-done((f32[56,128]{1,0:T(8,128)S(1)}, f32[56,128]{1,0:T(8,128)S(1)}, u32[]{:S(2)}, u32[]{:S(2)}) %collective-permute-start.2) | collective-permute-done | bytes 28704 | tf_op jit(solution)/shard_map/ppermute | solution.py:651
  7.2 2.3 %collective-permute-done.1.refs_2_ = f32[56,128]{1,0:T(8,128)S(1)} collective-permute-done((f32[56,128]{1,0:T(8,128)S(1)}, f32[56,128]{1,0:T(8,128)S(1)}, u32[]{:S(2)}, u32[]{:S(2)}) %collective-permute-start.1) | collective-permute-done | bytes 28704 | tf_op jit(solution)/shard_map/ppermute | solution.py:651
  9.4 0.0 collective-permute-done.refs_1_
  9.5 0.1 shard_map.114
  9.6 3.7 %collective-permute-start.5 = (f32[232,128]{1,0:T(8,128)S(1)}, f32[232,128]{1,0:T(8,128)S(1)}, u32[]{:S(2)}, u32[]{:S(2)}) collective-permute-start(f32[232,128]{1,0:T(8,128)S(1)} %get-tuple-element.42.own), channel_id=1, source_target_pairs={{0,12},{1,13},{2,14},{3,15},{4,8},{5,9},{6,10},{7,11},{8,4},{9,5},... | collective-permute-start | bytes 356360 | tf_op jit(solution)/shard_map/ppermute | solution.py:651
  13.3 0.0 collective-permute-start.3
  13.3 0.8 %collective-permute-start.4 = (f32[120,128]{1,0:T(8,128)S(1)}, f32[120,128]{1,0:T(8,128)S(1)}, u32[]{:S(2)}, u32[]{:S(2)}) collective-permute-start(f32[120,128]{1,0:T(8,128)S(1)} %get-tuple-element.43), channel_id=1, source_target_pairs={{0,8},{1,9},{2,10},{3,11},{4,12},{5,13},{6,14},{7,15},{8,0},{9,1},... | collective-permute-start | bytes 184328 | tf_op jit(solution)/shard_map/ppermute | solution.py:651
  14.0 5.3 %collective-permute-done.4.near = f32[120,128]{1,0:T(8,128)S(1)} collective-permute-done((f32[120,128]{1,0:T(8,128)S(1)}, f32[120,128]{1,0:T(8,128)S(1)}, u32[]{:S(2)}, u32[]{:S(2)}) %collective-permute-start.4) | collective-permute-done | bytes 61472 | tf_op jit(solution)/shard_map/ppermute | solution.py:651
  19.3 0.0 collective-permute-done.5.third
  19.3 0.3 collective-permute-done.3.first
  19.6 2.8 %shard_map.115 = (f32[3,2,56,128]{3,2,1,0:T(8,128)S(1)}, f32[3,2,40,128]{3,2,1,0:T(8,128)S(1)}, f32[10,40,128]{2,1,0:T(8,128)S(1)}, f32[16,128]{1,0:T(8,128)S(1)...) custom-call(f32[232,128]{1,0:T(8,128)S(1)} %get-tuple-element.42.own, f32[232,128]{1,0:T(8,128)S(1)} %collective-permute-done.3.first, ...), custom_call_target="tpu_custom_call" | custom-call | tf_op jit(solution)/shard_map/pallas_call | solution.py:165
  22.4 0.1 collective-permute-start.6
  22.5 0.1 shard_map.116.refs_2_
  22.6 1.1 %collective-permute-done.6.refs_1_ = f32[160,128]{1,0:T(8,128)S(1)} collective-permute-done((f32[160,128]{1,0:T(8,128)S(1)}, f32[160,128]{1,0:T(8,128)S(1)}, u32[]{:S(2)}, u32[]{:S(2)}) %collective-permute-start.6) | collective-permute-done | bytes 81952 | tf_op jit(solution)/shard_map/ppermute | solution.py:651
  23.8 0.0 copy-done.2
  23.8 0.3 shard_map.117
  24.0 0.2 collective-permute-start.7
  24.3 1.2 %collective-permute-start.9 = (f32[40,128]{1,0:T(8,128)S(1)}, f32[40,128]{1,0:T(8,128)S(1)}, u32[]{:S(2)}, u32[]{:S(2)}) collective-permute-start(f32[40,128]{1,0:T(8,128)S(1)} %get-tuple-element.49), channel_id=1, source_target_pairs={{0,3},{1,2},{2,1},{3,0},{4,7},{5,6},{6,5},{7,4},{8,11},{9,10},{10,... | collective-permute-start | bytes 61448 | tf_op jit(solution)/shard_map/ppermute | solution.py:651
  25.4 0.8 %collective-permute-start.8 = (f32[40,128]{1,0:T(8,128)S(1)}, f32[40,128]{1,0:T(8,128)S(1)}, u32[]{:S(2)}, u32[]{:S(2)}) collective-permute-start(f32[40,128]{1,0:T(8,128)S(1)} %get-tuple-element.49), channel_id=1, source_target_pairs={{0,2},{1,3},{2,0},{3,1},{4,6},{5,7},{6,4},{7,5},{8,10},{9,11},{10,... | collective-permute-start | bytes 61448 | tf_op jit(solution)/shard_map/ppermute | solution.py:651
  26.2 1.2 %collective-permute-done.9.refs_3_ = f32[40,128]{1,0:T(8,128)S(1)} collective-permute-done((f32[40,128]{1,0:T(8,128)S(1)}, f32[40,128]{1,0:T(8,128)S(1)}, u32[]{:S(2)}, u32[]{:S(2)}) %collective-permute-start.9) | collective-permute-done | bytes 20512 | tf_op jit(solution)/shard_map/ppermute | solution.py:651
  27.5 1.7 %collective-permute-done.8.refs_2_ = f32[40,128]{1,0:T(8,128)S(1)} collective-permute-done((f32[40,128]{1,0:T(8,128)S(1)}, f32[40,128]{1,0:T(8,128)S(1)}, u32[]{:S(2)}, u32[]{:S(2)}) %collective-permute-start.8) | collective-permute-done | bytes 20512 | tf_op jit(solution)/shard_map/ppermute | solution.py:651
  29.2 0.0 collective-permute-done.7.refs_1_
  29.2 0.1 shard_map.118
  29.3 2.3 %collective-permute-start.12 = (f32[168,128]{1,0:T(8,128)S(1)}, f32[168,128]{1,0:T(8,128)S(1)}, u32[]{:S(2)}, u32[]{:S(2)}) collective-permute-start(f32[168,128]{1,0:T(8,128)S(1)} %get-tuple-element.50.own), channel_id=1, source_target_pairs={{0,12},{1,13},{2,14},{3,15},{4,8},{5,9},{6,10},{7,11},{8,4},{9,5},... | collective-permute-start | bytes 258056 | tf_op jit(solution)/shard_map/ppermute | solution.py:651
  31.6 0.6 %collective-permute-start.10 = (f32[168,128]{1,0:T(8,128)S(1)}, f32[168,128]{1,0:T(8,128)S(1)}, u32[]{:S(2)}, u32[]{:S(2)}) collective-permute-start(f32[168,128]{1,0:T(8,128)S(1)} %get-tuple-element.50.own), channel_id=1, source_target_pairs={{0,4},{1,5},{2,6},{3,7},{4,0},{5,1},{6,2},{7,3},{8,12},{9,13},{10,... | collective-permute-start | bytes 258056 | tf_op jit(solution)/shard_map/ppermute | solution.py:651
  32.2 1.6 %collective-permute-start.11 = (f32[88,128]{1,0:T(8,128)S(1)}, f32[88,128]{1,0:T(8,128)S(1)}, u32[]{:S(2)}, u32[]{:S(2)}) collective-permute-start(f32[88,128]{1,0:T(8,128)S(1)} %get-tuple-element.51), channel_id=1, source_target_pairs={{0,8},{1,9},{2,10},{3,11},{4,12},{5,13},{6,14},{7,15},{8,0},{9,1},... | collective-permute-start | bytes 135176 | tf_op jit(solution)/shard_map/ppermute | solution.py:651
  33.8 3.4 %collective-permute-done.11.near = f32[88,128]{1,0:T(8,128)S(1)} collective-permute-done((f32[88,128]{1,0:T(8,128)S(1)}, f32[88,128]{1,0:T(8,128)S(1)}, u32[]{:S(2)}, u32[]{:S(2)}) %collective-permute-start.11) | collective-permute-done | bytes 45088 | tf_op jit(solution)/shard_map/ppermute | solution.py:651
  37.2 0.0 collective-permute-done.12.third
  37.2 0.3 collective-permute-done.10.first
  37.4 2.8 %shard_map.119 = (f32[10,16,128]{2,1,0:T(8,128)S(1)}, f32[10,16,128]{2,1,0:T(8,128)S(1)}, f32[16,128]{1,0:T(8,128)S(1)}, f32[8,128]{1,0:T(8,128)S(1)}, f32[8,128]{1,0:T(8,128)S(1)}, /*index=5*/f32[160,128]{1,0:T(8,128)S(1)}) custom-call(f32[168,128]{1,0:T(8,128)S(1)} %get-tuple-element.50.own, f32[168,128]{1,0:T(8,128)S(1)} %collective-permute-done.10.first, ...), custom_call_target="tpu_custom_call" | custom-call | tf_op jit(solution)/shard_map/pallas_call | solution.py:165
  40.3 0.1 collective-permute-start.13
  40.4 0.1 shard_map.120.refs_2_
  40.5 1.2 %collective-permute-done.13.refs_1_ = f32[160,128]{1,0:T(8,128)S(1)} collective-permute-done((f32[160,128]{1,0:T(8,128)S(1)}, f32[160,128]{1,0:T(8,128)S(1)}, u32[]{:S(2)}, u32[]{:S(2)}) %collective-permute-start.13) | collective-permute-done | bytes 81952 | tf_op jit(solution)/shard_map/ppermute | solution.py:651
  41.6 0.3 shard_map.121
  41.9 0.2 collective-permute-start.14
  42.1 1.0 %collective-permute-start.16 = (f32[40,128]{1,0:T(8,128)S(1)}, f32[40,128]{1,0:T(8,128)S(1)}, u32[]{:S(2)}, u32[]{:S(2)}) collective-permute-start(f32[40,128]{1,0:T(8,128)S(1)} %get-tuple-element.60), channel_id=1, source_target_pairs={{0,3},{1,2},{2,1},{3,0},{4,7},{5,6},{6,5},{7,4},{8,11},{9,10},{10,... | collective-permute-start | bytes 61448 | tf_op jit(solution)/shard_map/ppermute | solution.py:651
  43.0 1.0 %collective-permute-start.15 = (f32[40,128]{1,0:T(8,128)S(1)}, f32[40,128]{1,0:T(8,128)S(1)}, u32[]{:S(2)}, u32[]{:S(2)}) collective-permute-start(f32[40,128]{1,0:T(8,128)S(1)} %get-tuple-element.60), channel_id=1, source_target_pairs={{0,2},{1,3},{2,0},{3,1},{4,6},{5,7},{6,4},{7,5},{8,10},{9,11},{10,... | collective-permute-start | bytes 61448 | tf_op jit(solution)/shard_map/ppermute | solution.py:651
  44.0 1.2 %collective-permute-done.16.refs_3_ = f32[40,128]{1,0:T(8,128)S(1)} collective-permute-done((f32[40,128]{1,0:T(8,128)S(1)}, f32[40,128]{1,0:T(8,128)S(1)}, u32[]{:S(2)}, u32[]{:S(2)}) %collective-permute-start.16) | collective-permute-done | bytes 20512 | tf_op jit(solution)/shard_map/ppermute | solution.py:651
  45.3 1.5 %collective-permute-done.15.refs_2_ = f32[40,128]{1,0:T(8,128)S(1)} collective-permute-done((f32[40,128]{1,0:T(8,128)S(1)}, f32[40,128]{1,0:T(8,128)S(1)}, u32[]{:S(2)}, u32[]{:S(2)}) %collective-permute-start.15) | collective-permute-done | bytes 20512 | tf_op jit(solution)/shard_map/ppermute | solution.py:651
  46.8 0.0 collective-permute-done.14.refs_1_
  46.8 0.1 shard_map.122
  47.0 2.2 %collective-permute-start.17 = (f32[112,128]{1,0:T(8,128)S(1)}, f32[112,128]{1,0:T(8,128)S(1)}, u32[]{:S(2)}, u32[]{:S(2)}) collective-permute-start(f32[112,128]{1,0:T(8,128)S(1)} %get-tuple-element.62), channel_id=1, source_target_pairs={{0,12},{1,13},{2,14},{3,15},{4,8},{5,9},{6,10},{7,11},{8,4},{9,5},... | collective-permute-start | bytes 172040 | tf_op jit(solution)/shard_map/ppermute | solution.py:651
  49.2 0.1 collective-permute-start.18
  49.3 2.1 %collective-permute-start.19 = (f32[8,128]{1,0:T(8,128)S(1)}, f32[8,128]{1,0:T(8,128)S(1)}, u32[]{:S(2)}, u32[]{:S(2)}) collective-permute-start(f32[8,128]{1,0:T(8,128)S(1)} %get-tuple-element.64.sums), channel_id=1, source_target_pairs={{0,8},{1,9},{2,10},{3,11},{4,12},{5,13},{6,14},{7,15},{8,0},{9,1},... | collective-permute-start | bytes 12296 | tf_op jit(solution)/shard_map/ppermute | solution.py:651
  51.4 1.7 %collective-permute-done.17.three = f32[112,128]{1,0:T(8,128)S(1)} collective-permute-done((f32[112,128]{1,0:T(8,128)S(1)}, f32[112,128]{1,0:T(8,128)S(1)}, u32[]{:S(2)}, u32[]{:S(2)}) %collective-permute-start.17) | collective-permute-done | bytes 57376 | tf_op jit(solution)/shard_map/ppermute | solution.py:651
  53.1 0.6 %collective-permute-done.18.one = f32[112,128]{1,0:T(8,128)S(1)} collective-permute-done((f32[112,128]{1,0:T(8,128)S(1)}, f32[112,128]{1,0:T(8,128)S(1)}, u32[]{:S(2)}, u32[]{:S(2)}) %collective-permute-start.18) | collective-permute-done | bytes 57376 | tf_op jit(solution)/shard_map/ppermute | solution.py:651
  53.7 1.2 %shard_map.123 = (f32[10,16,128]{2,1,0:T(8,128)S(1)}, f32[2,8,128]{2,1,0:T(8,128)S(1)}) custom-call(f32[160,128]{1,0:T(8,128)S(1)} %get-tuple-element.61.own, f32[112,128]{1,0:T(8,128)S(1)} %collective-permute-done.17.three, f32[112,128]{1,0:T(8,128)S(1)} %collective-permute-done.18.one, f32[8,128]{1,0:T(8,128)S(1)} %get-tuple-element.64.sums, ...), custom_call_target="tpu_custom_call" | custom-call | tf_op jit(solution)/shard_map/pallas_call | solution.py:165
  54.8 0.0 collective-permute-done.19.sums_two
  54.9 0.9 %shard_map.124 = (f32[10,16,108]{2,1,0:T(8,128)}, f32[1,16]{1,0:T(1,128)}, f32[10,16,108]{2,1,0:T(8,128)}) custom-call(f32[10,16,128]{2,1,0:T(8,128)S(1)} %get-tuple-element.65.diffused, f32[2,8,128]{2,1,0:T(8,128)S(1)} %get-tuple-element.66.sums, f32[8,128]{1,0:T(8,128)S(1)} %collective-permute-done.19.sums_two, ...), custom_call_target="tpu_custom_call" | custom-call | tf_op jit(solution)/shard_map/pallas_call | solution.py:165
  (6 shorter events, 0.0 us)
Async XLA Ops:
  0.6 21.9 %copy-start = (f32[16,5,2,16,108]{4,3,2,1,0:T(8,128)S(1)}, f32[16,5,2,16,108]{4,3,2,1,0:T(8,128)}, u32[]{:S(2)}) copy-start(f32[16,5,2,16,108]{4,3,2,1,0:T(8,128)} %param.15) | copy-start | bytes 3317764
  0.6 5.0 %copy-start.5 = (s32[5]{0:T(128)S(1)}, s32[5]{0:T(128)}, u32[]{:S(2)}) copy-start(s32[5]{0:T(128)} %param.17) | copy-start | bytes 64
  0.7 5.0 %copy-start.4 = (f32[5,4,4]{0,2,1:T(4,128)S(1)}, f32[5,4,4]{0,2,1:T(4,128)}, u32[]{:S(2)}) copy-start(f32[5,4,4]{0,2,1:T(4,128)} %param.16) | copy-start | bytes 964
  2.4 21.4 %copy-start.1 = (f32[5,2,16,108]{3,2,1,0:T(8,128)S(1)}, f32[5,2,16,108]{3,2,1,0:T(8,128)}, u32[]{:S(2)}) copy-start(f32[5,2,16,108]{3,2,1,0:T(8,128)} %param.10) | copy-start | bytes 207364
  2.4 21.3 %copy-start.2 = (f32[5,2,16,108]{3,2,1,0:T(8,128)S(1)}, f32[5,2,16,108]{3,2,1,0:T(8,128)}, u32[]{:S(2)}) copy-start(f32[5,2,16,108]{3,2,1,0:T(8,128)} %param.11) | copy-start | bytes 207364
  2.4 21.3 %copy-start.3 = (s32[2,16,108]{2,1,0:T(8,128)S(1)}, s32[2,16,108]{2,1,0:T(8,128)}, u32[]{:S(2)}) copy-start(s32[2,16,108]{2,1,0:T(8,128)} %refs_7_.3) | copy-start | bytes 41476
  2.4 7.0 %collective-permute-start = (f32[168,128]{1,0:T(8,128)S(1)}, f32[168,128]{1,0:T(8,128)S(1)}, u32[]{:S(2)}, u32[]{:S(2)}) collective-permute-start(f32[168,128]{1,0:T(8,128)S(1)} %get-tuple-element.38.refs_0_), channel_id=1, source_target_pairs={{0,1},{1,0},{2,3},{3,2},{4,5},{5,4},{6,7},{7,6},{8,9},{9,8},{10,11... | collective-permute-start | bytes 258056 | tf_op jit(solution)/shard_map/ppermute | solution.py:651
  3.0 4.2 %collective-permute-start.2 = (f32[56,128]{1,0:T(8,128)S(1)}, f32[56,128]{1,0:T(8,128)S(1)}, u32[]{:S(2)}, u32[]{:S(2)}) collective-permute-start(f32[56,128]{1,0:T(8,128)S(1)} %get-tuple-element.39._), channel_id=1, source_target_pairs={{0,3},{1,2},{2,1},{3,0},{4,7},{5,6},{6,5},{7,4},{8,11},{9,10},{10,... | collective-permute-start | bytes 86024 | tf_op jit(solution)/shard_map/ppermute | solution.py:651
  5.6 3.9 %collective-permute-start.1 = (f32[56,128]{1,0:T(8,128)S(1)}, f32[56,128]{1,0:T(8,128)S(1)}, u32[]{:S(2)}, u32[]{:S(2)}) collective-permute-start(f32[56,128]{1,0:T(8,128)S(1)} %get-tuple-element.39._), channel_id=1, source_target_pairs={{0,2},{1,3},{2,0},{3,1},{4,6},{5,7},{6,4},{7,5},{8,10},{9,11},{10,... | collective-permute-start | bytes 86024 | tf_op jit(solution)/shard_map/ppermute | solution.py:651
  9.6 9.7 %collective-permute-start.5 = (f32[232,128]{1,0:T(8,128)S(1)}, f32[232,128]{1,0:T(8,128)S(1)}, u32[]{:S(2)}, u32[]{:S(2)}) collective-permute-start(f32[232,128]{1,0:T(8,128)S(1)} %get-tuple-element.42.own), channel_id=1, source_target_pairs={{0,12},{1,13},{2,14},{3,15},{4,8},{5,9},{6,10},{7,11},{8,4},{9,5},... | collective-permute-start | bytes 356360 | tf_op jit(solution)/shard_map/ppermute | solution.py:651
  13.3 6.4 %collective-permute-start.3 = (f32[232,128]{1,0:T(8,128)S(1)}, f32[232,128]{1,0:T(8,128)S(1)}, u32[]{:S(2)}, u32[]{:S(2)}) collective-permute-start(f32[232,128]{1,0:T(8,128)S(1)} %get-tuple-element.42.own), channel_id=1, source_target_pairs={{0,4},{1,5},{2,6},{3,7},{4,0},{5,1},{6,2},{7,3},{8,12},{9,13},{10,... | collective-permute-start | bytes 356360 | tf_op jit(solution)/shard_map/ppermute | solution.py:651
  13.3 6.0 %collective-permute-start.4 = (f32[120,128]{1,0:T(8,128)S(1)}, f32[120,128]{1,0:T(8,128)S(1)}, u32[]{:S(2)}, u32[]{:S(2)}) collective-permute-start(f32[120,128]{1,0:T(8,128)S(1)} %get-tuple-element.43), channel_id=1, source_target_pairs={{0,8},{1,9},{2,10},{3,11},{4,12},{5,13},{6,14},{7,15},{8,0},{9,1},... | collective-permute-start | bytes 184328 | tf_op jit(solution)/shard_map/ppermute | solution.py:651
  22.4 1.3 %collective-permute-start.6 = (f32[160,128]{1,0:T(8,128)S(1)}, f32[160,128]{1,0:T(8,128)S(1)}, u32[]{:S(2)}, u32[]{:S(2)}) collective-permute-start(f32[160,128]{1,0:T(8,128)S(1)} %get-tuple-element.45.refs_0_), channel_id=1, source_target_pairs={{0,1},{1,0},{2,3},{3,2},{4,5},{5,4},{6,7},{7,6},{8,9},{9,8},{10,11... | collective-permute-start | bytes 245768 | tf_op jit(solution)/shard_map/ppermute | solution.py:651
  24.0 5.2 %collective-permute-start.7 = (f32[168,128]{1,0:T(8,128)S(1)}, f32[168,128]{1,0:T(8,128)S(1)}, u32[]{:S(2)}, u32[]{:S(2)}) collective-permute-start(f32[168,128]{1,0:T(8,128)S(1)} %get-tuple-element.48.refs_0_), channel_id=1, source_target_pairs={{0,1},{1,0},{2,3},{3,2},{4,5},{5,4},{6,7},{7,6},{8,9},{9,8},{10,11... | collective-permute-start | bytes 258056 | tf_op jit(solution)/shard_map/ppermute | solution.py:651
  24.3 3.2 %collective-permute-start.9 = (f32[40,128]{1,0:T(8,128)S(1)}, f32[40,128]{1,0:T(8,128)S(1)}, u32[]{:S(2)}, u32[]{:S(2)}) collective-permute-start(f32[40,128]{1,0:T(8,128)S(1)} %get-tuple-element.49), channel_id=1, source_target_pairs={{0,3},{1,2},{2,1},{3,0},{4,7},{5,6},{6,5},{7,4},{8,11},{9,10},{10,... | collective-permute-start | bytes 61448 | tf_op jit(solution)/shard_map/ppermute | solution.py:651
  25.4 3.8 %collective-permute-start.8 = (f32[40,128]{1,0:T(8,128)S(1)}, f32[40,128]{1,0:T(8,128)S(1)}, u32[]{:S(2)}, u32[]{:S(2)}) collective-permute-start(f32[40,128]{1,0:T(8,128)S(1)} %get-tuple-element.49), channel_id=1, source_target_pairs={{0,2},{1,3},{2,0},{3,1},{4,6},{5,7},{6,4},{7,5},{8,10},{9,11},{10,... | collective-permute-start | bytes 61448 | tf_op jit(solution)/shard_map/ppermute | solution.py:651
  29.3 7.8 %collective-permute-start.12 = (f32[168,128]{1,0:T(8,128)S(1)}, f32[168,128]{1,0:T(8,128)S(1)}, u32[]{:S(2)}, u32[]{:S(2)}) collective-permute-start(f32[168,128]{1,0:T(8,128)S(1)} %get-tuple-element.50.own), channel_id=1, source_target_pairs={{0,12},{1,13},{2,14},{3,15},{4,8},{5,9},{6,10},{7,11},{8,4},{9,5},... | collective-permute-start | bytes 258056 | tf_op jit(solution)/shard_map/ppermute | solution.py:651
  31.6 5.8 %collective-permute-start.10 = (f32[168,128]{1,0:T(8,128)S(1)}, f32[168,128]{1,0:T(8,128)S(1)}, u32[]{:S(2)}, u32[]{:S(2)}) collective-permute-start(f32[168,128]{1,0:T(8,128)S(1)} %get-tuple-element.50.own), channel_id=1, source_target_pairs={{0,4},{1,5},{2,6},{3,7},{4,0},{5,1},{6,2},{7,3},{8,12},{9,13},{10,... | collective-permute-start | bytes 258056 | tf_op jit(solution)/shard_map/ppermute | solution.py:651
  32.2 5.0 %collective-permute-start.11 = (f32[88,128]{1,0:T(8,128)S(1)}, f32[88,128]{1,0:T(8,128)S(1)}, u32[]{:S(2)}, u32[]{:S(2)}) collective-permute-start(f32[88,128]{1,0:T(8,128)S(1)} %get-tuple-element.51), channel_id=1, source_target_pairs={{0,8},{1,9},{2,10},{3,11},{4,12},{5,13},{6,14},{7,15},{8,0},{9,1},... | collective-permute-start | bytes 135176 | tf_op jit(solution)/shard_map/ppermute | solution.py:651
  40.3 1.3 %collective-permute-start.13 = (f32[160,128]{1,0:T(8,128)S(1)}, f32[160,128]{1,0:T(8,128)S(1)}, u32[]{:S(2)}, u32[]{:S(2)}) collective-permute-start(f32[160,128]{1,0:T(8,128)S(1)} %get-tuple-element.55.refs_0_), channel_id=1, source_target_pairs={{0,1},{1,0},{2,3},{3,2},{4,5},{5,4},{6,7},{7,6},{8,9},{9,8},{10,11... | collective-permute-start | bytes 245768 | tf_op jit(solution)/shard_map/ppermute | solution.py:651
  41.9 4.9 %collective-permute-start.14 = (f32[168,128]{1,0:T(8,128)S(1)}, f32[168,128]{1,0:T(8,128)S(1)}, u32[]{:S(2)}, u32[]{:S(2)}) collective-permute-start(f32[168,128]{1,0:T(8,128)S(1)} %get-tuple-element.59.refs_0_), channel_id=1, source_target_pairs={{0,1},{1,0},{2,3},{3,2},{4,5},{5,4},{6,7},{7,6},{8,9},{9,8},{10,11... | collective-permute-start | bytes 258056 | tf_op jit(solution)/shard_map/ppermute | solution.py:651
  42.1 3.2 %collective-permute-start.16 = (f32[40,128]{1,0:T(8,128)S(1)}, f32[40,128]{1,0:T(8,128)S(1)}, u32[]{:S(2)}, u32[]{:S(2)}) collective-permute-start(f32[40,128]{1,0:T(8,128)S(1)} %get-tuple-element.60), channel_id=1, source_target_pairs={{0,3},{1,2},{2,1},{3,0},{4,7},{5,6},{6,5},{7,4},{8,11},{9,10},{10,... | collective-permute-start | bytes 61448 | tf_op jit(solution)/shard_map/ppermute | solution.py:651
  43.0 3.8 %collective-permute-start.15 = (f32[40,128]{1,0:T(8,128)S(1)}, f32[40,128]{1,0:T(8,128)S(1)}, u32[]{:S(2)}, u32[]{:S(2)}) collective-permute-start(f32[40,128]{1,0:T(8,128)S(1)} %get-tuple-element.60), channel_id=1, source_target_pairs={{0,2},{1,3},{2,0},{3,1},{4,6},{5,7},{6,4},{7,5},{8,10},{9,11},{10,... | collective-permute-start | bytes 61448 | tf_op jit(solution)/shard_map/ppermute | solution.py:651
  47.0 6.1 %collective-permute-start.17 = (f32[112,128]{1,0:T(8,128)S(1)}, f32[112,128]{1,0:T(8,128)S(1)}, u32[]{:S(2)}, u32[]{:S(2)}) collective-permute-start(f32[112,128]{1,0:T(8,128)S(1)} %get-tuple-element.62), channel_id=1, source_target_pairs={{0,12},{1,13},{2,14},{3,15},{4,8},{5,9},{6,10},{7,11},{8,4},{9,5},... | collective-permute-start | bytes 172040 | tf_op jit(solution)/shard_map/ppermute | solution.py:651
  49.2 4.5 %collective-permute-start.18 = (f32[112,128]{1,0:T(8,128)S(1)}, f32[112,128]{1,0:T(8,128)S(1)}, u32[]{:S(2)}, u32[]{:S(2)}) collective-permute-start(f32[112,128]{1,0:T(8,128)S(1)} %get-tuple-element.63), channel_id=1, source_target_pairs={{0,4},{1,5},{2,6},{3,7},{4,0},{5,1},{6,2},{7,3},{8,12},{9,13},{10,... | collective-permute-start | bytes 172040 | tf_op jit(solution)/shard_map/ppermute | solution.py:651
  49.3 5.5 %collective-permute-start.19 = (f32[8,128]{1,0:T(8,128)S(1)}, f32[8,128]{1,0:T(8,128)S(1)}, u32[]{:S(2)}, u32[]{:S(2)}) collective-permute-start(f32[8,128]{1,0:T(8,128)S(1)} %get-tuple-element.64.sums), channel_id=1, source_target_pairs={{0,8},{1,9},{2,10},{3,11},{4,12},{5,13},{6,14},{7,15},{8,0},{9,1},... | collective-permute-start | bytes 12296 | tf_op jit(solution)/shard_map/ppermute | solution.py:651
